TPU v7x, 32 devices: a whole 2x2x4 slice. The times are simulated.
32 devices in a mesh: users: 32 (over z, y, x, core).
Axes of the slice: x: 2, y: 2, z: 4, core: 2. Of those that a mesh axis runs over, the one named last changes fastest.
Arguments:
- tile_owner: int32 [2048, 1], P('users'), may hold values from 0 to 31; in each aligned block of 64 rows (0 to 63, 64 to 127, ...) at most 2 rows name the same one
- tile_slot: int32 [2048], P('users'), may hold values from 0 to 15
- tile_cblock: int32 [2048], P('users'), may hold values from 0 to 63
- tile_context: int32 [2048, 512], P('users'), may hold values from 0 to 7
- tile_weights: bfloat16 [2048, 128, 512], P('users'), as said below
- item_factors: bfloat16 [512, 64, 128], P('users'), may hold values from -0.5 to 0.5
- context_factors: bfloat16 [8, 512], replicated, may hold values from -0.75 to 0.75
- user_basis: float32 [16384, 128], P('users'), may hold values from -6 to 6
- user_counts: int32 [32], P('users'), may hold values from 256 to 512, as said below
Outputs:
- basis: float32 [16384, 128], P('users')
- core_out: float32 [128, 512], replicated
Inputs may be any that keep to these rules, and one draw needn't show every extreme that they name: `tile_owner`: among the 64 tiles of one device (aligned blocks of 64 rows), at most 2 name the same owner, and this is reached. `user_counts`: rows of a device at and beyond its count carry no events; some device has 512 live rows and some 512 // 2. tile_weights[t, :, u] is zero for u >= user_counts[t // 64].
All inputs are finite; a program needn't handle non-finite values.
Results may differ from a plain program's by a relative error of at most 0.006.
Values may be sent and summed in bfloat16 or wider, within the bound.
No kernel may reach another device: no remote copies, remote signals or barrier semaphores. Data moves between devices by JAX's collectives and lax.ppermute only.
A program may use at most 128 MiB of HBM per device.

v0:
```python
import jax
import jax.numpy as jnp
from jax import lax
from jax.sharding import PartitionSpec as P

CB = 8
SLOTS = 2


HIGH = lax.Precision.HIGHEST


def cholesky_lower(gram_matrix):
    order = gram_matrix.shape[0]
    indices = jnp.arange(order, dtype=jnp.int32)

    def column_step(column, carry):
        remain, factor_low = carry
        marker = (indices == column).astype(jnp.float32)
        column_vals = jnp.dot(remain, marker, precision=HIGH)
        pivot = jnp.sqrt(jnp.dot(marker, column_vals, precision=HIGH))
        column_vals = jnp.where(indices >= column, column_vals / pivot, jnp.zeros_like(column_vals))
        remain = remain - column_vals[:, None] * column_vals[None, :]
        factor_low = factor_low + column_vals[:, None] * marker[None, :]
        return (remain, factor_low)

    start = (gram_matrix, jnp.zeros_like(gram_matrix))
    return lax.fori_loop(0, order, column_step, start)[1]


def inverse_lower(factor_low):
    order = factor_low.shape[0]
    indices = jnp.arange(order, dtype=jnp.int32)

    def row_step(row, inverse):
        marker = (indices == row).astype(jnp.float32)
        row_vals = jnp.dot(marker, factor_low, precision=HIGH)
        pivot = jnp.dot(row_vals, marker, precision=HIGH)
        new_row = (marker - jnp.dot(row_vals, inverse, precision=HIGH)) / pivot
        return inverse + marker[:, None] * new_row[None, :]

    return lax.fori_loop(0, order, row_step, jnp.zeros_like(factor_low))


def upper_of(gram_matrix):
    return cholesky_lower(gram_matrix).T


def body(
    tile_owner,
    tile_slot,
    tile_cblock,
    tile_context,
    tile_weights,
    item_factors,
    context_factors,
    user_basis,
    user_counts,
):
    devices = lax.axis_size("users")
    owners = tile_owner[:, 0]
    rank_c = context_factors.shape[0]
    rank_i = item_factors.shape[1]
    block_len = item_factors.shape[2]
    user_rows = tile_weights.shape[2]
    total_users = user_rows * devices
    ctx_block = tile_context.shape[0] * 0 + CB
    owner_hits = owners[:, None] == jnp.arange(devices, dtype=jnp.int32)[None, :]
    owner_ints = owner_hits.astype(jnp.int32)
    earlier = jnp.cumsum(owner_ints, axis=0) - owner_ints
    position = jnp.sum(earlier * owner_ints, axis=1)
    placed = owner_hits[:, :, None] & (
        position[:, None, None] == jnp.arange(SLOTS, dtype=jnp.int32)[None, None, :]
    )
    requests = jnp.sum(jnp.where(placed, tile_slot[:, None, None], 0), axis=0)
    found = item_factors[lax.all_to_all(requests, "users", split_axis=0, concat_axis=0, tiled=True)]
    fetched = lax.all_to_all(found, "users", split_axis=0, concat_axis=0, tiled=True)
    blocks = fetched.reshape(devices * SLOTS, rank_i, block_len)[owners * SLOTS + position]
    products = jnp.einsum(
        "tai,tiu->tau", blocks, tile_weights, preferred_element_type=jnp.float32
    ).astype(jnp.bfloat16)
    lookup = context_factors.astype(jnp.float32).reshape(rank_c, -1, ctx_block)
    chosen = (tile_cblock[:, None] == jnp.arange(lookup.shape[1], dtype=jnp.int32)[None, :]).astype(
        jnp.float32
    )
    block_values = jnp.einsum("rbk,tb->trk", lookup, chosen).astype(jnp.bfloat16)
    context_hits = (
        tile_context[:, None, :] == jnp.arange(ctx_block, dtype=jnp.int32)[None, :, None]
    ).astype(jnp.bfloat16)
    context_values = jnp.einsum(
        "trk,tku->tru", block_values, context_hits, preferred_element_type=jnp.float32
    ).astype(jnp.bfloat16)
    ytrans = jnp.einsum(
        "tru,tau->rau", context_values, products, preferred_element_type=jnp.float32
    )
    ytrans = ytrans.reshape(rank_c * rank_i, user_rows)
    living = jnp.arange(user_rows, dtype=jnp.int32) < user_counts[0]
    ytrans = jnp.where(living[None, :], ytrans, jnp.zeros_like(ytrans))
    local_projection = jnp.dot(ytrans, user_basis, precision=HIGH)
    scale_root = jnp.sqrt(jnp.float32(total_users))
    projection = lax.psum(local_projection, "users")
    projected = lax.dot_general(ytrans, projection, (((0,), (0,)), ((), ())), precision=HIGH)
    gram_matrix = lax.psum(jnp.dot(projected.T, projected, precision=HIGH), "users")
    inverse = inverse_lower(upper_of(gram_matrix).T)
    basis = jnp.dot(projected, inverse.T, precision=HIGH) * scale_root
    core_out = lax.psum(
        lax.dot_general(basis, ytrans, (((0,), (1,)), ((), ())), precision=HIGH), "users"
    ) / jnp.float32(total_users)
    return (basis, core_out)


def solution(mesh):
    return jax.shard_map(
        body,
        mesh=mesh,
        in_specs=(
            P("users", None),
            P("users"),
            P("users"),
            P("users", None),
            P("users", None, None),
            P("users", None, None),
            P(),
            P("users", None),
            P("users"),
        ),
        out_specs=(P("users", None), P()),
        check_vma=False,
    )
```

profile of v0, /device:TPU:0, one launch (start us, length us, event | category | flops | bytes accessed | tf_op | source)
XLA Modules:
  0.0 1185.1 jit_solution(8450169403604927145)
XLA Ops:
  9.9 14.2 %all_to_all.17 = s32[32,1,2]{2,1,0:T(1,128)S(1)} all-to-all(s32[32,1,2]{2,1,0:T(1,128)S(1)} %copy.23), channel_id=1, replica_groups=mesh['users'=32] {'users'}, dimensions={0} | all-to-all | bytes 512 | tf_op jit(solution)/shard_map/all_to_all | solution.py:76
  24.4 1.7 gather_fusion
  26.1 2.6 all-to-all-start.1
  32.0 2.0 copy.29
  35.4 19.6 %all-to-all-done.1 = bf16[32,2,64,128]{3,2,1,0:T(8,128)(2,1)S(1)} async-done(((bf16[32,2,64,128]{3,2,1,0:T(8,128)(2,1)}), bf16[32,2,64,128]{3,2,1,0:T(8,128)(2,1)S(1)}, u32[]{:S(2)}, u32[]{:S(2)}) %all-to-all-start.1) | async-done | bytes 1048608 | tf_op jit(solution)/shard_map/all_to_all | solution.py:77
  55.7 6.6 convolution_convert_fusion
  62.4 13.0 %copy.28 = bf16[64,64,512]{1,0,2:T(8,128)(2,1)} copy(bf16[64,64,512]{2,1,0:T(8,128)(2,1)} %convolution_convert_fusion) | data formatting | bytes 8388608 | tf_op jit(solution)/shard_map/convert_element_type | solution.py:81
  75.4 4.6 convolution_bitcast_fusion.2
  80.1 1.7 copy.30
  83.1 2.6 fusion.26
  85.8 124.1 %all-reduce.4.cloned.1.call-done = f32[512,128]{1,0:T(8,128)} async-done(((f32[512,128]{1,0:T(8,128)}), f32[512,128]{1,0:T(8,128)}) %all-reduce.4.cloned.1.call-update) | async-done | bytes 262160 | tf_op jit(solution)/shard_map/psum | solution.py:101
  209.9 2.7 fusion.27
  214.0 118.6 %all-reduce.6.cloned.1.call-done = f32[128,128]{1,0:T(8,128)} async-done(((f32[128,128]{1,0:T(8,128)}), f32[128,128]{1,0:T(8,128)}) %all-reduce.6.cloned.1.call-update) | async-done | bytes 65552 | tf_op jit(solution)/shard_map/psum | solution.py:103
  332.6 500.1 %while.32 = (s32[]{:T(128)}, f32[128,128]{1,0:T(8,128)}, f32[128,128]{1,0:T(8,128)S(1)}, s32[]{:T(128)}, s32[]{:T(128)}) while((s32[]{:T(128)}, f32[128,128]{1,0:T(8,128)}, f32[128,128]{1,0:T(8,128)S(1)}, s32[]{:T(128)}, s32[]{:T(128)}) %tuple.76), condition=%wide.region_6.7_spmd.clone.clone, body=%wide.region_5.6_spmd.clone.clone.sunk | while | flops 279682 | bytes 330851 | solution.py:28
  332.6 1.6 fusion.62
  336.5 1.6 fusion.62
  340.4 1.6 fusion.62
  344.3 1.6 fusion.62
  348.2 1.6 fusion.62
  352.1 1.6 fusion.62
  356.0 1.6 fusion.62
  359.9 1.6 fusion.62
  363.8 1.6 fusion.62
  367.7 1.6 fusion.62
  371.6 1.6 fusion.62
  375.5 1.6 fusion.62
  383.4 1.6 fusion.62
  387.3 1.6 fusion.62
  832.7 215.8 %while.31 = (s32[]{:T(128)}, f32[128,128]{1,0:T(8,128)S(1)}, f32[128,128]{1,0:T(8,128)S(1)}, s32[]{:T(128)}, s32[]{:T(128)}) while((s32[]{:T(128)}, f32[128,128]{1,0:T(8,128)S(1)}, f32[128,128]{1,0:T(8,128)S(1)}, s32[]{:T(128)}, s32[]{:T(128)}) %tuple.79), condition=%wide.region_8.9_spmd.clone, body=%wide.region_7.8_spmd.clone.sunk | while | flops 460034 | bytes 265308 | solution.py:42
  1049.0 2.0 fusion.29
  1050.9 126.0 %all-reduce.8.cloned.1.call-done = f32[128,512]{1,0:T(8,128)} async-done(((f32[128,512]{1,0:T(8,128)}), f32[128,512]{1,0:T(8,128)}) %all-reduce.8.cloned.1.call-update) | async-done | bytes 262160 | tf_op jit(solution)/shard_map/psum | solution.py:106
  1176.9 1.7 broadcast_multiply_fusion
  (1048 shorter events, 608.6 us)
Async XLA Ops:
  7.2 17.3 %copy-start = (bf16[16,64,128]{2,1,0:T(8,128)(2,1)S(1)}, bf16[16,64,128]{2,1,0:T(8,128)(2,1)}, u32[]{:S(2)}) copy-start(bf16[16,64,128]{2,1,0:T(8,128)(2,1)} %param.18) | copy-start | bytes 786436
  26.1 28.9 %all-to-all-start.1 = ((bf16[32,2,64,128]{3,2,1,0:T(8,128)(2,1)}), bf16[32,2,64,128]{3,2,1,0:T(8,128)(2,1)S(1)}, u32[]{:S(2)}, u32[]{:S(2)}) async-start(bf16[32,2,64,128]{3,2,1,0:T(8,128)(2,1)} %bitcast.4), calls=%async_computation.1 | async-start | bytes 2097152 | tf_op jit(solution)/shard_map/all_to_all | solution.py:77
  28.7 181.2 %all-reduce.4.cloned.1.call-start = ((), (), s32[]{:S(2)}) async-start(), calls=%async_computation.2 | async-start | bytes 524288 | tf_op jit(solution)/shard_map/psum | solution.py:101
  62.4 13.1 %copy-start.1 = (bf16[64,8,512]{0,1,2:T(8,128)(2,1)S(1)}, bf16[64,8,512]{0,1,2:T(8,128)(2,1)}, u32[]{:S(2)}) copy-start(bf16[64,8,512]{0,1,2:T(8,128)(2,1)} %copy.29) | copy-start | bytes 1572868
  85.7 246.8 %all-reduce.6.cloned.1.call-start = ((), (), s32[]{:S(2)}) async-start(), calls=%async_computation.3 | async-start | bytes 131072 | tf_op jit(solution)/shard_map/psum | solution.py:103
  213.9 963.0 %all-reduce.8.cloned.1.call-start = ((), (), s32[]{:S(2)}) async-start(), calls=%async_computation.4 | async-start | bytes 524288 | tf_op jit(solution)/shard_map/psum | solution.py:106
  1048.9 129.7 %copy-start.2 = (f32[512,128]{1,0:T(8,128)}, f32[512,128]{1,0:T(8,128)S(1)}, u32[]{:S(2)}) copy-start(f32[512,128]{1,0:T(8,128)S(1)} %convolution_multiply_fusion) | copy-start | bytes 786436
Sparse Core Ops, SparseCore 0:
  85.9 123.9 all-reduce.3
  216.1 116.4 all-reduce.5
  1051.1 125.8 all-reduce.7
where the time goes:
time: 1200 us; the launch traced here: 1190 us
  matrix products  430 us (36%)
  waiting for transfers between devices  388 us (32%)
  other arithmetic  219 us (18%)
  loops' own time  95.2 us (8%)
  local copies, waits for them, and re-layouts  20.8 us (2%)
  between operations  14.5 us (1%)
  blocking collectives  14.2 us (1%)
    dot_general x128, matrix products, column_step(): column_vals = jnp.dot(remain, marker, precision=HIGH)  209 us
    add x128, other arithmetic, column_step(): factor_low = factor_low + column_vals[:, None] * marker[None, :]  199 us
    psum x1, waiting for transfers between devices, body(): lax.psum(lax.dot_general(basis, ytrans, (((0,), (1,)), ((), ())), precisi...  126 us
    psum x1, waiting for transfers between devices, body(): projection = lax.psum(local_projection, 'users')  124 us
    psum x1, waiting for transfers between devices, body(): lax.psum(jnp.dot(projected.T, projected, precision=HIGH), 'users')  119 us
    dot_general x128, matrix products, row_step(): new_row = (marker - jnp.dot(row_vals, inverse, precision=HIGH)) / pivot  102 us
    dot_general x128, matrix products, row_step(): row_vals = jnp.dot(marker, factor_low, precision=HIGH)  96.5 us
    another operation x1, loops' own time, cholesky_lower(): return lax.fori_loop(0, order, column_step, start)[1]  91.4 us
  transfers between devices with their start and end apart: 4, of which 4 were waited for; matrix products, arithmetic and copies ran while one was open for 0% of the time, Pallas kernels for 0%

commit v1 on v0

v1 whole, which is shorter than its diff:
```python
import functools

import jax
import jax.numpy as jnp
from jax import lax
from jax.experimental import pallas as pl
from jax.experimental.pallas import tpu as pltpu
from jax.sharding import PartitionSpec as P

CB = 8
SLOTS = 2
HIGH = lax.Precision.HIGHEST
LANES = 128
ROWS = 8


def dot_f32(lhs, rhs, contract):
    return lax.dot_general(
        lhs, rhs, ((contract[:1], contract[1:]), ((), ())),
        precision=HIGH, preferred_element_type=jnp.float32,
    )


def route_kernel(tiles, devices, owner_ref, slot_ref, request_ref, where_ref, used_ref):
    def clear(place, _):
        used_ref[place] = 0
        for slot in range(SLOTS):
            request_ref[place * SLOTS + slot] = 0
        return 0

    lax.fori_loop(0, devices, clear, 0)

    def assign(tile, _):
        owner = owner_ref[tile]
        taken = used_ref[owner]
        used_ref[owner] = taken + 1
        place = owner * SLOTS + taken
        request_ref[place] = slot_ref[tile]
        where_ref[tile] = place
        return 0

    lax.fori_loop(0, tiles, assign, 0)


def route(owners, slots, devices):
    tiles = owners.shape[0]
    smem = pl.BlockSpec(memory_space=pltpu.SMEM)
    return pl.pallas_call(
        functools.partial(route_kernel, tiles, devices),
        out_shape=(
            jax.ShapeDtypeStruct((devices * SLOTS,), jnp.int32),
            jax.ShapeDtypeStruct((tiles,), jnp.int32),
        ),
        in_specs=[smem, smem],
        out_specs=(smem, smem),
        scratch_shapes=[pltpu.SMEM((devices,), jnp.int32)],
        name="route",
    )(owners, slots)


def context_kernel(tiles, cblock_ref, table_ref, context_ref, out_ref):
    users = context_ref.shape[1]

    def one(tile, _):
        table = table_ref[cblock_ref[tile]]
        marks = jnp.broadcast_to(context_ref[pl.ds(tile, 1), :], (ROWS, users))
        total = jnp.zeros((ROWS, users), jnp.float32)
        for k in range(CB):
            column = jnp.broadcast_to(table[:, k : k + 1], (ROWS, users))
            total = jnp.where(marks == k, column, total)
        out_ref[tile] = total
        return 0

    lax.fori_loop(0, tiles, one, 0)


def context_values(cblock, table, context):
    tiles, users = context.shape
    vmem = pl.BlockSpec(memory_space=pltpu.VMEM)
    return pl.pallas_call(
        functools.partial(context_kernel, tiles),
        out_shape=jax.ShapeDtypeStruct((tiles, ROWS, users), jnp.float32),
        in_specs=[pl.BlockSpec(memory_space=pltpu.SMEM), vmem, vmem],
        out_specs=vmem,
        name="contexts",
    )(cblock, table, context)


def tiles_kernel(
    step_tiles, where_ref, count_ref, core_ref,
    blocks_ref, weights_ref, context_ref, basis_ref,
    y_ref, keep_ref, send_ref, product_ref, pack_ref,
):
    step = pl.program_id(0)
    rank_i = blocks_ref.shape[1]
    users = weights_ref.shape[2]
    rank_c = context_ref.shape[1]

    @pl.when(step == 0)
    def _():
        y_ref[...] = jnp.zeros_like(y_ref)

    for tile in range(step_tiles):
        block = blocks_ref[where_ref[step * step_tiles + tile]]
        product = jnp.dot(block, weights_ref[tile], preferred_element_type=jnp.float32)
        product_ref[tile] = product.astype(jnp.bfloat16).astype(jnp.float32)

    half = rank_i // 2
    for lane in range(users // LANES):
        lanes = slice(lane * LANES, (lane + 1) * LANES)
        for part in range(2):
            rows = slice(part * half, (part + 1) * half)
            total = y_ref[:, rows, lanes]
            for tile in range(step_tiles):
                values = context_ref[tile, :, lanes]
                total = total + values[:, None, :] * product_ref[tile, rows, lanes][None]
            y_ref[:, rows, lanes] = total

    @pl.when(step == pl.num_programs(0) - 1)
    def _():
        living = lax.broadcasted_iota(jnp.int32, (rank_i, users), 1) < count_ref[0]
        for r in range(rank_c):
            y_ref[r] = jnp.where(living, y_ref[r], 0.0)
        ytrans = y_ref[...].reshape(rank_c * rank_i, users)
        groups = ytrans.shape[0] // LANES
        place = 0
        for i in range(groups):
            upper = ytrans[i * LANES : (i + 1) * LANES]
            for j in range(i, groups):
                pack_ref[place] = dot_f32(upper, ytrans[j * LANES : (j + 1) * LANES], (1, 1))
                place += 1
        for i in range(groups):
            pack_ref[place] = dot_f32(ytrans[i * LANES : (i + 1) * LANES], basis_ref[...], (1, 0))
            place += 1
        core = core_ref[0]
        part = place // 2
        for i in range(part):
            keep_ref[i] = pack_ref[core * part + i]
            send_ref[i] = pack_ref[(1 - core) * part + i]


def tile_sums(where, count, core, blocks, weights, contexts, user_basis):
    tiles, block_len, users = weights.shape
    rank_i = blocks.shape[1]
    rank_c = contexts.shape[1]
    rank_u = user_basis.shape[1]
    step_tiles = 8
    groups = rank_c * rank_i // LANES
    pack = groups * (groups + 1) // 2 + groups
    whole = lambda *shape: pl.BlockSpec(shape, lambda s, *_: (0,) * len(shape))
    return pl.pallas_call(
        functools.partial(tiles_kernel, step_tiles),
        out_shape=(
            jax.ShapeDtypeStruct((rank_c, rank_i, users), jnp.float32),
            jax.ShapeDtypeStruct((pack // 2, LANES, rank_u), jnp.float32),
            jax.ShapeDtypeStruct((pack // 2, LANES, rank_u), jnp.float32),
        ),
        grid_spec=pltpu.PrefetchScalarGridSpec(
            num_scalar_prefetch=3,
            grid=(tiles // step_tiles,),
            in_specs=[
                whole(*blocks.shape),
                pl.BlockSpec((step_tiles, block_len, users), lambda s, *_: (s, 0, 0)),
                pl.BlockSpec((step_tiles, rank_c, users), lambda s, *_: (s, 0, 0)),
                whole(*user_basis.shape),
            ],
            out_specs=(
                whole(rank_c, rank_i, users),
                whole(pack // 2, LANES, rank_u),
                whole(pack // 2, LANES, rank_u),
            ),
            scratch_shapes=[
                pltpu.VMEM((step_tiles, rank_i, users), jnp.float32),
                pltpu.VMEM((pack, LANES, rank_u), jnp.float32),
            ],
        ),
        compiler_params=pltpu.CompilerParams(vmem_limit_bytes=28 * 2**20),
        cost_estimate=pl.CostEstimate(flops=2 * 10**9, bytes_accessed=12 * 10**6, transcendentals=0),
        name="tile_sums",
    )(where, count, core, blocks, weights, contexts, user_basis)


def inverse_factor(gram):
    order = gram.shape[0]
    panels = order // ROWS
    sub = lax.broadcasted_iota(jnp.int32, (ROWS, order), 0)
    lane = lax.broadcasted_iota(jnp.int32, (ROWS, order), 1)
    left = [gram[ROWS * i : ROWS * (i + 1)] for i in range(panels)]
    right = [jnp.where(lane == sub + ROWS * i, 1.0, 0.0) for i in range(panels)]
    for k in range(panels):
        columns = {
            i: [
                jnp.broadcast_to(left[i][:, ROWS * k + j : ROWS * k + j + 1], (ROWS, order))
                for j in range(ROWS)
            ]
            for i in range(k, panels)
        }
        row, tail = left[k], right[k]
        scale = jnp.zeros((ROWS, order), jnp.float32)
        rows, tails = [], []
        for j in range(ROWS):
            head = columns[k][j]
            pivot = jnp.broadcast_to(head[j : j + 1], (ROWS, order))
            inverse = pl.reciprocal(pivot, approx=True)
            inverse = inverse * (2.0 - pivot * inverse)
            scale = jnp.where(sub == j, pivot, scale)
            rows.append(jnp.broadcast_to(row[j : j + 1], (ROWS, order)))
            tails.append(jnp.broadcast_to(tail[j : j + 1], (ROWS, order)))
            below = jnp.where(sub > j, head, 0.0) * inverse
            row = row - below * rows[j]
            tail = tail - below * tails[j]
            facts = {k: below}
            for i in range(k + 1, panels):
                facts[i] = columns[i][j] * inverse
            for c in range(j + 1, ROWS):
                crossing = jnp.broadcast_to(head[c : c + 1], (ROWS, order))
                for i in range(k, panels):
                    columns[i][c] = columns[i][c] - facts[i] * crossing
            for i in range(k + 1, panels):
                left[i] = left[i] - facts[i] * rows[j]
                right[i] = right[i] - facts[i] * tails[j]
        right[k] = tail * lax.rsqrt(scale)
    return jnp.concatenate(right, axis=0)


def finish_kernel(total_users, core_ref, mine_ref, other_ref, y_ref, basis_ref, core_out_ref, pack_ref, full_ref):
    core = core_ref[0]
    part = mine_ref.shape[0]
    for i in range(part):
        pack_ref[core * part + i] = mine_ref[i]
        pack_ref[(1 - core) * part + i] = other_ref[i]
    groups = full_ref.shape[0] // LANES
    place = 0
    for i in range(groups):
        for j in range(i, groups):
            block = pack_ref[place]
            full_ref[i * LANES : (i + 1) * LANES, j * LANES : (j + 1) * LANES] = block
            if i != j:
                full_ref[j * LANES : (j + 1) * LANES, i * LANES : (i + 1) * LANES] = block.T
            place += 1
    projection = pack_ref[place : place + groups].reshape(groups * LANES, LANES)
    crossed = dot_f32(full_ref[...], projection, (1, 0))
    gram = dot_f32(projection, crossed, (0, 0))
    projected = dot_f32(y_ref[...].reshape(full_ref.shape[0], -1), projection, (0, 0))
    inverse = inverse_factor(gram)
    root = total_users ** 0.5
    basis_ref[...] = dot_f32(projected, inverse, (1, 1)) * root
    core_out_ref[...] = dot_f32(inverse, crossed, (1, 1)) * (1.0 / root)


def finish(core, mine, other, ytrans, total_users):
    rank_c, rank_i, users = ytrans.shape
    ranks = rank_c * rank_i
    vmem = pl.BlockSpec(memory_space=pltpu.VMEM)
    return pl.pallas_call(
        functools.partial(finish_kernel, total_users),
        out_shape=(
            jax.ShapeDtypeStruct((users, LANES), jnp.float32),
            jax.ShapeDtypeStruct((LANES, ranks), jnp.float32),
        ),
        in_specs=[pl.BlockSpec(memory_space=pltpu.SMEM), vmem, vmem, vmem],
        out_specs=(vmem, vmem),
        scratch_shapes=[
            pltpu.VMEM((2 * mine.shape[0], LANES, LANES), jnp.float32),
            pltpu.VMEM((ranks, ranks), jnp.float32),
        ],
        compiler_params=pltpu.CompilerParams(vmem_limit_bytes=28 * 2**20),
        name="finish",
    )(core, mine, other, ytrans)


def body(
    tile_owner, tile_slot, tile_cblock, tile_context, tile_weights,
    item_factors, context_factors, user_basis, user_counts,
):
    devices = lax.axis_size("users")
    chips = devices // 2
    rank_c = context_factors.shape[0]
    rank_i, block_len = item_factors.shape[1:]
    users = tile_weights.shape[2]
    core = (lax.axis_index("users") % 2).astype(jnp.int32).reshape(1)

    requests, where = route(tile_owner[:, 0], tile_slot, devices)
    asked = lax.all_to_all(requests, "users", split_axis=0, concat_axis=0, tiled=True)
    found = item_factors[asked]
    blocks = lax.all_to_all(found, "users", split_axis=0, concat_axis=0, tiled=True)

    table = context_factors.astype(jnp.float32).reshape(rank_c, -1, CB).transpose(1, 0, 2)
    contexts = context_values(tile_cblock, table, tile_context)
    ytrans, keep, send = tile_sums(where, user_counts, core, blocks, tile_weights, contexts, user_basis)

    pairs = [(i, i ^ 1) for i in range(devices)]
    groups = [[2 * chip + c for chip in range(chips)] for c in range(2)]
    part, wide = keep.shape[0] * keep.shape[1], keep.shape[2]
    halved = (keep + lax.ppermute(send, "users", pairs)).reshape(chips, part // chips, wide)
    pieces = lax.all_to_all(halved, "users", 0, 0, axis_index_groups=groups, tiled=True)
    piece = jnp.sum(pieces, axis=0, keepdims=True)
    spread = jnp.broadcast_to(piece, pieces.shape)
    mine = lax.all_to_all(spread, "users", 0, 0, axis_index_groups=groups, tiled=True)
    mine = mine.reshape(keep.shape)
    other = lax.ppermute(mine, "users", pairs)
    return finish(core, mine, other, ytrans, users * devices)


def solution(mesh):
    return jax.shard_map(
        body,
        mesh=mesh,
        in_specs=(
            P("users", None), P("users"), P("users"), P("users", None), P("users", None, None),
            P("users", None, None), P(), P("users", None), P("users"),
        ),
        out_specs=(P("users", None), P()),
        check_vma=False,
    )
```

time: 1200 us -> 116 us (0.10); the launches traced: 1190 us -> 116 us
  matrix products: 430 us -> 0 us
  waiting for transfers between devices: 388 us -> 20.1 us
  other arithmetic: 219 us -> 0.79 us
  loops' own time: 95.2 us -> 0 us
  blocking collectives: 14.2 us -> 49.6 us
  Pallas kernels: 0 us -> 30 us
  between operations: 14.5 us -> 1.4 us
    dot_general x392 -> x0, matrix products: 429 us -> none  [the longest x128 209 us: column_step(): column_vals = jnp.dot(remain, marker, precision=HIGH)]
    psum x3 -> x0, waiting for transfers between devices: 369 us -> none  [the longest x1 126 us: body(): lax.psum(lax.dot_general(basis, ytrans, (((0,), (1,)), ((), ())), precisi...]
    add x256 -> x1, other arithmetic: 212 us -> 0.06 us  [body(): keep + lax.ppermute(send, 'users', pairs)]
    another operation x2 -> x0, loops' own time: 95.2 us -> none  [the longest x1 91.4 us: cholesky_lower(): return lax.fori_loop(0, order, column_step, start)[1]]
    all_to_all x0 -> x2, blocking collectives: none -> 35.3 us  [the longest x1 18.5 us: body(): lax.all_to_all(halved, 'users', 0, 0, axis_index_groups=groups, tiled=True)]
    pallas_call x0 -> x4, Pallas kernels: none -> 30 us  [the longest x1 12 us: tile_sums(): pl.pallas_call(functools.partial(tiles_kernel, step_tiles), out_shape=(ja...]
    convert_element_type x3 -> x0, local copies, waits for them, and re-layouts: 15.2 us -> none  [the longest x1 13 us: body(): products = jnp.einsum('tai,tiu->tau', blocks, tile_weights, preferred_ele...]
  transfers between devices with their start and end apart: 4 -> 3, of which waited for: 4 -> 3; matrix products, arithmetic and copies ran while one was open for 0% -> 1% of each run, Pallas kernels for 0% -> 6%
where the time goes in v1:
time: 116 us
  blocking collectives  49.6 us (43%)
  Pallas kernels  30 us (26%)
  waiting for transfers between devices  20.1 us (17%)
  local copies, waits for them, and re-layouts  11 us (9%)
  starting transfers between devices  2.72 us (2%)
  between operations  1.4 us (1%)
    all_to_all x1, blocking collectives, body(): lax.all_to_all(halved, 'users', 0, 0, axis_index_groups=groups, tiled=True)  18.5 us
    all_to_all x1, blocking collectives, body(): lax.all_to_all(spread, 'users', 0, 0, axis_index_groups=groups, tiled=True)  16.8 us
    all_to_all x1, waiting for transfers between devices, body(): lax.all_to_all(found, 'users', split_axis=0, concat_axis=0, tiled=True)  16.5 us
    all_to_all x1, blocking collectives, body(): lax.all_to_all(requests, 'users', split_axis=0, concat_axis=0, tiled=True)  14.3 us
    pallas_call x1, Pallas kernels, tile_sums(): pl.pallas_call(functools.partial(tiles_kernel, step_tiles), out_shape=(ja...  12 us
    pallas_call x1, Pallas kernels, finish(): pl.pallas_call(functools.partial(finish_kernel, total_users), out_shape=(...  8.58 us
    pallas_call x1, Pallas kernels, context_values(): pl.pallas_call(functools.partial(context_kernel, tiles), out_shape=jax.Sh...  7.34 us
    unnamed x10, local copies, waits for them, and re-layouts  6.22 us
  transfers between devices with their start and end apart: 3, of which 3 were waited for; matrix products, arithmetic and copies ran while one was open for 1% of the time, Pallas kernels for 6%

profile of v1, /device:TPU:0, one launch (start us, length us, event | category | flops | bytes accessed | tf_op | source)
XLA Modules:
  0.0 115.6 jit_solution(877591280161614990)
XLA Ops:
  0.6 0.0 copy-start
  0.6 2.1 %route.1 = (s32[64]{0:T(128)}, s32[64]{0:T(128)}) custom-call(s32[64]{0:T(128)} %bitcast.16, s32[64]{0:T(128)} %slot_ref.1), custom_call_target="tpu_custom_call" | custom-call | tf_op jit(solution)/shard_map/route/pallas_call | solution.py:48
  2.8 0.8 all_to_all.17
  3.5 14.3 %all_to_all.27 = s32[32,2,1]{1,2,0:T(1,128)S(1)} all-to-all(s32[32,2,1]{1,2,0:T(1,128)S(1)} %bitcast.15), channel_id=1, replica_groups=mesh['users'=32] {'users'}, dimensions={0} | all-to-all | bytes 512 | tf_op jit(solution)/shard_map/all_to_all | solution.py:284
  17.8 0.5 broadcast.23
  18.3 0.7 reduce.3
  19.0 0.1 all_to_all.19
  19.1 0.0 copy-done
  19.1 1.7 %gather_fusion = bf16[64,64,128]{2,1,0:T(8,128)(2,1)} fusion(bf16[16,64,128]{2,1,0:T(8,128)(2,1)S(1)} %copy-done, s32[1024]{0:T(1024)S(1)} %pad_clamp_fusion), kind=kCustom, calls=%fused_computation | custom fusion | bytes 2097408 | tf_op jit(solution)/shard_map/gather | solution.py:285
  20.8 2.6 %all-to-all-start.1 = ((bf16[64,64,128]{2,1,0:T(8,128)(2,1)}), bf16[64,64,128]{2,1,0:T(8,128)(2,1)S(1)}, u32[]{:S(2)}, u32[]{:S(2)}) async-start(bf16[64,64,128]{2,1,0:T(8,128)(2,1)} %gather_fusion), calls=%async_computation.1 | async-start | bytes 2097152 | tf_op jit(solution)/shard_map/all_to_all | solution.py:286
  24.1 0.9 reshape.52
  25.0 0.9 copy.15
  25.8 7.3 %contexts.1.context_ref = f32[64,8,512]{2,1,0:T(8,128)} custom-call(s32[64]{0:T(128)} %cblock_ref.1, f32[64,8,8]{2,1,0:T(8,128)} %bitcast.14, s32[64,512]{1,0:T(8,128)} %context_ref.1), custom_call_target="tpu_custom_call" | custom-call | tf_op jit(solution)/shard_map/contexts/pallas_call | solution.py:80
  33.1 16.5 %all-to-all-done.1.blocks_ref = bf16[64,64,128]{2,1,0:T(8,128)(2,1)S(1)} async-done(((bf16[64,64,128]{2,1,0:T(8,128)(2,1)}), bf16[64,64,128]{2,1,0:T(8,128)(2,1)S(1)}, u32[]{:S(2)}, u32[]{:S(2)}) %all-to-all-start.1) | async-done | bytes 1048608 | tf_op jit(solution)/shard_map/all_to_all | solution.py:286
  49.6 0.0 copy-start.1
  49.6 3.4 %copy-done.1 = bf16[64,128,512]{2,1,0:T(8,128)(2,1)S(1)} copy-done((bf16[64,128,512]{2,1,0:T(8,128)(2,1)S(1)}, bf16[64,128,512]{2,1,0:T(8,128)(2,1)}, u32[]{:S(2)}) %copy-start.1) | copy-done | bytes 8388632
  53.0 0.0 copy-start.2
  53.0 1.2 %copy-done.2 = f32[64,8,512]{2,1,0:T(8,128)S(1)} copy-done((f32[64,8,512]{2,1,0:T(8,128)S(1)}, f32[64,8,512]{2,1,0:T(8,128)}, u32[]{:S(2)}) %copy-start.2) | copy-done | bytes 1048600
  54.2 0.0 copy-start.3
  54.2 0.9 copy-done.3
  55.2 0.0 copy-start.4
  55.2 0.7 copy-done.4
  55.9 12.0 %tile_sums.1 = (f32[8,64,512]{2,1,0:T(8,128)S(1)}, f32[7,128,128]{2,1,0:T(8,128)S(1)}, f32[7,128,128]{2,1,0:T(8,128)S(1)}) custom-call(s32[64]{0:T(128)S(1)} %copy-done.4, s32[1]{0:T(128)S(6)} %copy.16.count_ref, s32[1]{0:T(128)} %bitcast.core_ref, bf16[64,64,128]{2,1,0:T(8,128)(2,1)S(1)} %all-to-all-done.1.blocks_ref, bf16[64,128,512]{2,1,0:T(8,128)(2,1)S(1)} %copy-done.1, ...), custom_call_target="tpu_custom_call" | custom-call | flops 2000000000 | bytes 12000000 | tf_op jit(solution)/shard_map/tile_sums/pallas_call | solution.py:151
  67.9 0.1 collective-permute-start
  67.9 1.8 %collective-permute-done = f32[7,128,128]{2,1,0:T(8,128)S(1)} collective-permute-done((f32[7,128,128]{2,1,0:T(8,128)S(1)}, f32[7,128,128]{2,1,0:T(8,128)S(1)}, u32[]{:S(2)}, u32[]{:S(2)}) %collective-permute-start) | collective-permute-done | bytes 458784 | tf_op jit(solution)/shard_map/ppermute | solution.py:295
  69.7 0.1 add.23
  69.8 18.5 %all_to_all.28 = f32[16,56,128]{2,1,0:T(8,128)S(1)} all-to-all(f32[16,56,128]{2,1,0:T(8,128)S(1)} %bitcast.13), channel_id=1, replica_groups={{0,2,4,6,8,10,12,14,16,18,20,22,24,26,28,30},{1,3,5,7,9,11,13,15,17,19,..., dimensions={0} | all-to-all | bytes 917504 | tf_op jit(solution)/shard_map/all_to_all | solution.py:296
  88.4 16.8 %all_to_all.29 = f32[16,56,128]{2,1,0:T(8,128)S(1)} all-to-all(f32[16,56,128]{2,1,0:T(8,128)S(1)} %broadcast_in_dim.2), channel_id=1, replica_groups={{0,2,4,6,8,10,12,14,16,18,20,22,24,26,28,30},{1,3,5,7,9,11,13,15,17,19,..., dimensions={0} | all-to-all | bytes 917504 | tf_op jit(solution)/shard_map/all_to_all | solution.py:299
  105.2 0.0 collective-permute-start.1
  105.2 1.8 %collective-permute-done.1.other_ref = f32[7,128,128]{2,1,0:T(8,128)S(1)} collective-permute-done((f32[7,128,128]{2,1,0:T(8,128)S(1)}, f32[7,128,128]{2,1,0:T(8,128)S(1)}, u32[]{:S(2)}, u32[]{:S(2)}) %collective-permute-start.1) | collective-permute-done | bytes 458784 | tf_op jit(solution)/shard_map/ppermute | solution.py:301
  107.0 8.6 %finish.1 = (f32[512,128]{1,0:T(8,128)}, f32[128,512]{1,0:T(8,128)}) custom-call(s32[1]{0:T(128)} %bitcast.core_ref, f32[7,128,128]{2,1,0:T(8,128)S(1)} %bitcast.12, f32[7,128,128]{2,1,0:T(8,128)S(1)} %collective-permute-done.1.other_ref, f32[8,64,512]{2,1,0:T(8,128)S(1)} %get-tuple-element.11.y_ref), custom_call_target="tpu_custom_call" | custom-call | tf_op jit(solution)/shard_map/finish/pallas_call | solution.py:255
  (4 shorter events, 0.1 us)
Async XLA Ops:
  0.6 18.5 %copy-start = (bf16[16,64,128]{2,1,0:T(8,128)(2,1)S(1)}, bf16[16,64,128]{2,1,0:T(8,128)(2,1)}, u32[]{:S(2)}) copy-start(bf16[16,64,128]{2,1,0:T(8,128)(2,1)} %param.14) | copy-start | bytes 786436
  20.8 28.9 %all-to-all-start.1 = ((bf16[64,64,128]{2,1,0:T(8,128)(2,1)}), bf16[64,64,128]{2,1,0:T(8,128)(2,1)S(1)}, u32[]{:S(2)}, u32[]{:S(2)}) async-start(bf16[64,64,128]{2,1,0:T(8,128)(2,1)} %gather_fusion), calls=%async_computation.1 | async-start | bytes 2097152 | tf_op jit(solution)/shard_map/all_to_all | solution.py:286
  49.6 3.4 %copy-start.1 = (bf16[64,128,512]{2,1,0:T(8,128)(2,1)S(1)}, bf16[64,128,512]{2,1,0:T(8,128)(2,1)}, u32[]{:S(2)}) copy-start(bf16[64,128,512]{2,1,0:T(8,128)(2,1)} %weights_ref.1) | copy-start | bytes 25165828
  53.0 1.2 %copy-start.2 = (f32[64,8,512]{2,1,0:T(8,128)S(1)}, f32[64,8,512]{2,1,0:T(8,128)}, u32[]{:S(2)}) copy-start(f32[64,8,512]{2,1,0:T(8,128)} %contexts.1.context_ref) | copy-start | bytes 3145732
  54.2 0.9 copy-start.3
  55.2 0.7 copy-start.4
  67.9 1.9 %collective-permute-start = (f32[7,128,128]{2,1,0:T(8,128)S(1)}, f32[7,128,128]{2,1,0:T(8,128)S(1)}, u32[]{:S(2)}, u32[]{:S(2)}) collective-permute-start(f32[7,128,128]{2,1,0:T(8,128)S(1)} %get-tuple-element.10), channel_id=1, source_target_pairs={{0,1},{1,0},{2,3},{3,2},{4,5},{5,4},{6,7},{7,6},{8,9},{9,8},{10,11... | collective-permute-start | bytes 1376264 | tf_op jit(solution)/shard_map/ppermute | solution.py:295
  105.2 1.8 %collective-permute-start.1 = (f32[7,128,128]{2,1,0:T(8,128)S(1)}, f32[7,128,128]{2,1,0:T(8,128)S(1)}, u32[]{:S(2)}, u32[]{:S(2)}) collective-permute-start(f32[7,128,128]{2,1,0:T(8,128)S(1)} %bitcast.11), channel_id=1, source_target_pairs={{0,1},{1,0},{2,3},{3,2},{4,5},{5,4},{6,7},{7,6},{8,9},{9,8},{10,11... | collective-permute-start | bytes 1376264 | tf_op jit(solution)/shard_map/ppermute | solution.py:301

commit v2 on v1

--- a/solution.py
+++ b/solution.py
@@ -12,6 +12,7 @@
 HIGH = lax.Precision.HIGHEST
 LANES = 128
 ROWS = 8
+VMEM_LIMIT = 56 * 2**20
 
 
 def dot_f32(lhs, rhs, contract):
@@ -21,41 +22,68 @@
     )
 
 
-def route_kernel(tiles, devices, owner_ref, slot_ref, request_ref, where_ref, used_ref):
+def route_kernel(half, me_ref, owner_ref, slot_ref, request_ref, where_ref, used_ref):
+    side = me_ref[0] // half
+    lane = lax.broadcasted_iota(jnp.int32, (1, LANES), 1)
+
     def clear(place, _):
         used_ref[place] = 0
-        for slot in range(SLOTS):
-            request_ref[place * SLOTS + slot] = 0
         return 0
 
-    lax.fori_loop(0, devices, clear, 0)
+    lax.fori_loop(0, 2 * half, clear, 0)
+    request_ref[...] = jnp.zeros_like(request_ref)
 
     def assign(tile, _):
         owner = owner_ref[tile]
         taken = used_ref[owner]
         used_ref[owner] = taken + 1
-        place = owner * SLOTS + taken
-        request_ref[place] = slot_ref[tile]
-        where_ref[tile] = place
+        low = lax.rem(owner, half)
+        mirrored = jnp.where(owner // half == side, 0, 1)
+        place = mirrored * SLOTS + taken
+        request_ref[low] = jnp.where(lane == place, slot_ref[tile], request_ref[low])
+        where_ref[tile] = low * 2 * SLOTS + place
         return 0
 
-    lax.fori_loop(0, tiles, assign, 0)
-
-
-def route(owners, slots, devices):
+    lax.fori_loop(0, owner_ref.shape[0], assign, 0)
+
+
+def route(me, owners, slots, half):
     tiles = owners.shape[0]
     smem = pl.BlockSpec(memory_space=pltpu.SMEM)
     return pl.pallas_call(
-        functools.partial(route_kernel, tiles, devices),
+        functools.partial(route_kernel, half),
         out_shape=(
-            jax.ShapeDtypeStruct((devices * SLOTS,), jnp.int32),
+            jax.ShapeDtypeStruct((half, 1, LANES), jnp.int32),
             jax.ShapeDtypeStruct((tiles,), jnp.int32),
         ),
-        in_specs=[smem, smem],
-        out_specs=(smem, smem),
-        scratch_shapes=[pltpu.SMEM((devices,), jnp.int32)],
+        in_specs=[smem, smem, smem],
+        out_specs=(pl.BlockSpec(memory_space=pltpu.VMEM), smem),
+        scratch_shapes=[pltpu.SMEM((2 * half,), jnp.int32)],
         name="route",
-    )(owners, slots)
+    )(me, owners, slots)
+
+
+def collect_kernel(asked_ref, own_ref, mirror_ref, out_ref):
+    def one(peer, _):
+        for place in range(2 * SLOTS):
+            block = asked_ref[peer, 0, place]
+            source = own_ref if place < SLOTS else mirror_ref
+            out_ref[peer * 2 * SLOTS + place] = source[block]
+        return 0
+
+    lax.fori_loop(0, asked_ref.shape[0], one, 0)
+
+
+def collect(asked, own, mirror):
+    vmem = pl.BlockSpec(memory_space=pltpu.VMEM)
+    peers = asked.shape[0]
+    return pl.pallas_call(
+        collect_kernel,
+        out_shape=jax.ShapeDtypeStruct((peers * 2 * SLOTS,) + own.shape[1:], own.dtype),
+        in_specs=[pl.BlockSpec(memory_space=pltpu.SMEM), vmem, vmem],
+        out_specs=vmem,
+        name="collect",
+    )(asked, own, mirror)
 
 
 def context_kernel(tiles, cblock_ref, table_ref, context_ref, out_ref):
@@ -86,15 +114,35 @@
     )(cblock, table, context)
 
 
+def piece_places(devices):
+    bits = devices.bit_length() - 1
+    rest = [r << 3 for r in range(1 << (bits - 4))]
+    places = {}
+    for top in range(2):
+        second, third = (1, 2) if top == 0 else (2, 1)
+        for second_set in range(2):
+            for core in range(2):
+                places[core, top, second_set] = [
+                    core + (top << (bits - 1)) + (second_set << second) + (third_set << third) + others
+                    for third_set in range(2)
+                    for others in rest
+                ]
+    return places
+
+
+PIECES = [(core, top, second) for core in (1, 0) for second in (1, 0) for top in (0, 1)]
+
+
 def tiles_kernel(
-    step_tiles, where_ref, count_ref, core_ref,
-    blocks_ref, weights_ref, context_ref, basis_ref,
-    y_ref, keep_ref, send_ref, product_ref, pack_ref,
+    step_tiles, places, where_ref, count_ref, me_ref,
+    blocks_ref, weights_ref, context_ref, basis_ref, *rest,
 ):
+    y_ref, piece_refs, product_ref, pack_ref = rest[0], rest[1:-2], rest[-2], rest[-1]
     step = pl.program_id(0)
     rank_i = blocks_ref.shape[1]
     users = weights_ref.shape[2]
     rank_c = context_ref.shape[1]
+    chunk = piece_refs[0].shape[1]
 
     @pl.when(step == 0)
     def _():
@@ -127,34 +175,43 @@
         for i in range(groups):
             upper = ytrans[i * LANES : (i + 1) * LANES]
             for j in range(i, groups):
-                pack_ref[place] = dot_f32(upper, ytrans[j * LANES : (j + 1) * LANES], (1, 1))
+                pack_ref[place * LANES : (place + 1) * LANES] = dot_f32(
+                    upper, ytrans[j * LANES : (j + 1) * LANES], (1, 1)
+                )
                 place += 1
         for i in range(groups):
-            pack_ref[place] = dot_f32(ytrans[i * LANES : (i + 1) * LANES], basis_ref[...], (1, 0))
+            pack_ref[place * LANES : (place + 1) * LANES] = dot_f32(
+                ytrans[i * LANES : (i + 1) * LANES], basis_ref[...], (1, 0)
+            )
             place += 1
-        core = core_ref[0]
-        part = place // 2
-        for i in range(part):
-            keep_ref[i] = pack_ref[core * part + i]
-            send_ref[i] = pack_ref[(1 - core) * part + i]
-
-
-def tile_sums(where, count, core, blocks, weights, contexts, user_basis):
+        if place * LANES < pack_ref.shape[0]:
+            pack_ref[place * LANES :] = jnp.zeros((pack_ref.shape[0] - place * LANES, LANES), jnp.float32)
+        me = me_ref[0]
+        for piece, ref in zip(PIECES, piece_refs):
+            for i, position in enumerate(places[piece]):
+                start = pl.multiple_of(jnp.bitwise_xor(me, position) * chunk, ROWS)
+                ref[i] = pack_ref[pl.ds(start, chunk)]
+
+
+def pack_rows(ranks, devices):
+    groups = ranks // LANES
+    rows = (groups * (groups + 1) // 2 + groups) * LANES
+    return -(-rows // (devices * ROWS)) * ROWS
+
+
+def tile_sums(where, count, me, blocks, weights, contexts, user_basis, devices):
     tiles, block_len, users = weights.shape
     rank_i = blocks.shape[1]
     rank_c = contexts.shape[1]
-    rank_u = user_basis.shape[1]
     step_tiles = 8
-    groups = rank_c * rank_i // LANES
-    pack = groups * (groups + 1) // 2 + groups
+    chunk = pack_rows(rank_c * rank_i, devices)
+    places = piece_places(devices)
+    piece_shape = (devices // 8, chunk, LANES)
     whole = lambda *shape: pl.BlockSpec(shape, lambda s, *_: (0,) * len(shape))
-    return pl.pallas_call(
-        functools.partial(tiles_kernel, step_tiles),
-        out_shape=(
-            jax.ShapeDtypeStruct((rank_c, rank_i, users), jnp.float32),
-            jax.ShapeDtypeStruct((pack // 2, LANES, rank_u), jnp.float32),
-            jax.ShapeDtypeStruct((pack // 2, LANES, rank_u), jnp.float32),
-        ),
+    out = pl.pallas_call(
+        functools.partial(tiles_kernel, step_tiles, places),
+        out_shape=(jax.ShapeDtypeStruct((rank_c, rank_i, users), jnp.float32),)
+        + (jax.ShapeDtypeStruct(piece_shape, jnp.float32),) * len(PIECES),
         grid_spec=pltpu.PrefetchScalarGridSpec(
             num_scalar_prefetch=3,
             grid=(tiles // step_tiles,),
@@ -164,20 +221,17 @@
                 pl.BlockSpec((step_tiles, rank_c, users), lambda s, *_: (s, 0, 0)),
                 whole(*user_basis.shape),
             ],
-            out_specs=(
-                whole(rank_c, rank_i, users),
-                whole(pack // 2, LANES, rank_u),
-                whole(pack // 2, LANES, rank_u),
-            ),
+            out_specs=(whole(rank_c, rank_i, users),) + (whole(*piece_shape),) * len(PIECES),
             scratch_shapes=[
                 pltpu.VMEM((step_tiles, rank_i, users), jnp.float32),
-                pltpu.VMEM((pack, LANES, rank_u), jnp.float32),
+                pltpu.VMEM((devices * chunk, LANES), jnp.float32),
             ],
         ),
-        compiler_params=pltpu.CompilerParams(vmem_limit_bytes=28 * 2**20),
+        compiler_params=pltpu.CompilerParams(vmem_limit_bytes=VMEM_LIMIT),
         cost_estimate=pl.CostEstimate(flops=2 * 10**9, bytes_accessed=12 * 10**6, transcendentals=0),
         name="tile_sums",
-    )(where, count, core, blocks, weights, contexts, user_basis)
+    )(where, count, me, blocks, weights, contexts, user_basis)
+    return out[0], dict(zip(PIECES, out[1:]))
 
 
 def inverse_factor(gram):
@@ -223,22 +277,24 @@
     return jnp.concatenate(right, axis=0)
 
 
-def finish_kernel(total_users, core_ref, mine_ref, other_ref, y_ref, basis_ref, core_out_ref, pack_ref, full_ref):
-    core = core_ref[0]
-    part = mine_ref.shape[0]
-    for i in range(part):
-        pack_ref[core * part + i] = mine_ref[i]
-        pack_ref[(1 - core) * part + i] = other_ref[i]
+def finish_kernel(total_users, places, me_ref, y_ref, *rest):
+    piece_refs, (basis_ref, core_out_ref, pack_ref, full_ref) = rest[: len(PIECES)], rest[len(PIECES) :]
+    me = me_ref[0]
+    chunk = piece_refs[0].shape[1]
+    for piece, ref in zip(PIECES, piece_refs):
+        for i, position in enumerate(places[piece]):
+            start = pl.multiple_of(jnp.bitwise_xor(me, position) * chunk, ROWS)
+            pack_ref[pl.ds(start, chunk)] = ref[i]
     groups = full_ref.shape[0] // LANES
     place = 0
     for i in range(groups):
         for j in range(i, groups):
-            block = pack_ref[place]
+            block = pack_ref[place * LANES : (place + 1) * LANES]
             full_ref[i * LANES : (i + 1) * LANES, j * LANES : (j + 1) * LANES] = block
             if i != j:
                 full_ref[j * LANES : (j + 1) * LANES, i * LANES : (i + 1) * LANES] = block.T
             place += 1
-    projection = pack_ref[place : place + groups].reshape(groups * LANES, LANES)
+    projection = pack_ref[place * LANES : (place + groups) * LANES]
     crossed = dot_f32(full_ref[...], projection, (1, 0))
     gram = dot_f32(projection, crossed, (0, 0))
     projected = dot_f32(y_ref[...].reshape(full_ref.shape[0], -1), projection, (0, 0))
@@ -248,25 +304,68 @@
     core_out_ref[...] = dot_f32(inverse, crossed, (1, 1)) * (1.0 / root)
 
 
-def finish(core, mine, other, ytrans, total_users):
+def finish(me, ytrans, pieces, devices):
     rank_c, rank_i, users = ytrans.shape
     ranks = rank_c * rank_i
+    chunk = pack_rows(ranks, devices)
     vmem = pl.BlockSpec(memory_space=pltpu.VMEM)
     return pl.pallas_call(
-        functools.partial(finish_kernel, total_users),
+        functools.partial(finish_kernel, users * devices, piece_places(devices)),
         out_shape=(
             jax.ShapeDtypeStruct((users, LANES), jnp.float32),
             jax.ShapeDtypeStruct((LANES, ranks), jnp.float32),
         ),
-        in_specs=[pl.BlockSpec(memory_space=pltpu.SMEM), vmem, vmem, vmem],
+        in_specs=[pl.BlockSpec(memory_space=pltpu.SMEM)] + [vmem] * (1 + len(PIECES)),
         out_specs=(vmem, vmem),
         scratch_shapes=[
-            pltpu.VMEM((2 * mine.shape[0], LANES, LANES), jnp.float32),
+            pltpu.VMEM((devices * chunk, LANES), jnp.float32),
             pltpu.VMEM((ranks, ranks), jnp.float32),
         ],
         compiler_params=pltpu.CompilerParams(vmem_limit_bytes=28 * 2**20),
         name="finish",
-    )(core, mine, other, ytrans)
+    )(me, ytrans, *[pieces[piece] for piece in PIECES])
+
+
+def swap(value, bit, devices):
+    return lax.ppermute(value, "users", [(i, i ^ (1 << bit)) for i in range(devices)])
+
+
+def reduce_pieces(pieces, devices):
+    top_bit = devices.bit_length() - 2
+    got = {}
+    for second in (1, 0):
+        for top in (0, 1):
+            got[top, second] = swap(pieces[1, top, second], 0, devices)
+    half = devices // 16
+    sums = []
+    for top in (0, 1):
+        away = swap(pieces[0, top, 1] + got[top, 1], 1 + top, devices)
+        sums.append((pieces[0, top, 0], got[top, 0], away))
+    lone = []
+    for top in (0, 1):
+        kept, near, away = sums[top]
+        further = swap(kept[half:] + near[half:] + away[half:], 2 - top, devices)
+        lone.append(kept[:half] + near[:half] + away[:half] + further)
+    for bit in range(top_bit - 1, 2, -1):
+        half = lone[0].shape[0] // 2
+        lone = [value[:half] + swap(value[half:], bit, devices) for value in lone]
+    return lone[0] + swap(lone[1], top_bit, devices)
+
+
+def spread_pieces(total, devices):
+    top_bit = devices.bit_length() - 2
+    lone = [total, swap(total, top_bit, devices)]
+    for bit in range(3, top_bit):
+        lone = [jnp.concatenate([value, swap(value, bit, devices)], axis=0) for value in lone]
+    pieces = {}
+    for top in (0, 1):
+        near = jnp.concatenate([lone[top], swap(lone[top], 2 - top, devices)], axis=0)
+        pieces[0, top, 0] = near
+        pieces[0, top, 1] = swap(near, 1 + top, devices)
+    for second in (0, 1):
+        for top in (0, 1):
+            pieces[1, top, second] = swap(pieces[0, top, second], 0, devices)
+    return pieces
 
 
 def body(
@@ -274,32 +373,24 @@
     item_factors, context_factors, user_basis, user_counts,
 ):
     devices = lax.axis_size("users")
-    chips = devices // 2
+    half = devices // 2
     rank_c = context_factors.shape[0]
-    rank_i, block_len = item_factors.shape[1:]
-    users = tile_weights.shape[2]
-    core = (lax.axis_index("users") % 2).astype(jnp.int32).reshape(1)
-
-    requests, where = route(tile_owner[:, 0], tile_slot, devices)
-    asked = lax.all_to_all(requests, "users", split_axis=0, concat_axis=0, tiled=True)
-    found = item_factors[asked]
-    blocks = lax.all_to_all(found, "users", split_axis=0, concat_axis=0, tiled=True)
+    me = lax.axis_index("users").astype(jnp.int32).reshape(1)
+
+    mirror = swap(item_factors, devices.bit_length() - 2, devices)
+    requests, where = route(me, tile_owner[:, 0], tile_slot, half)
+    sides = [list(range(half)), list(range(half, devices))]
+    asked = lax.all_to_all(requests, "users", 0, 0, axis_index_groups=sides, tiled=True)
+    found = collect(asked, item_factors, mirror)
+    blocks = lax.all_to_all(found, "users", 0, 0, axis_index_groups=sides, tiled=True)
 
     table = context_factors.astype(jnp.float32).reshape(rank_c, -1, CB).transpose(1, 0, 2)
     contexts = context_values(tile_cblock, table, tile_context)
-    ytrans, keep, send = tile_sums(where, user_counts, core, blocks, tile_weights, contexts, user_basis)
-
-    pairs = [(i, i ^ 1) for i in range(devices)]
-    groups = [[2 * chip + c for chip in range(chips)] for c in range(2)]
-    part, wide = keep.shape[0] * keep.shape[1], keep.shape[2]
-    halved = (keep + lax.ppermute(send, "users", pairs)).reshape(chips, part // chips, wide)
-    pieces = lax.all_to_all(halved, "users", 0, 0, axis_index_groups=groups, tiled=True)
-    piece = jnp.sum(pieces, axis=0, keepdims=True)
-    spread = jnp.broadcast_to(piece, pieces.shape)
-    mine = lax.all_to_all(spread, "users", 0, 0, axis_index_groups=groups, tiled=True)
-    mine = mine.reshape(keep.shape)
-    other = lax.ppermute(mine, "users", pairs)
-    return finish(core, mine, other, ytrans, users * devices)
+    ytrans, pieces = tile_sums(
+        where, user_counts, me, blocks, tile_weights, contexts, user_basis, devices
+    )
+    pieces = spread_pieces(reduce_pieces(pieces, devices), devices)
+    return finish(me, ytrans, pieces, devices)
 
 
 def solution(mesh):

time: 116 us -> 110 us (0.948)
  blocking collectives: 49.6 us -> 10.6 us
  starting transfers between devices: 2.72 us -> 25.6 us
  local copies, waits for them, and re-layouts: 11 us -> 4.63 us
  Pallas kernels: 30 us -> 36.3 us
  waiting for transfers between devices: 20.1 us -> 25.6 us
  other arithmetic: 0.79 us -> 5.19 us
    all_to_all x3 -> x1, blocking collectives: 49.6 us -> 10.6 us  [body(): lax.all_to_all(requests, 'users', 0, 0, axis_index_groups=sides, tiled=True)]
    ppermute x2 -> x23, starting transfers between devices: 0.07 us -> 21.9 us  [swap(): lax.ppermute(value, 'users', [(i, i ^ 1 << bit) for i in range(devices)])]
    ppermute x2 -> x23, waiting for transfers between devices: 3.62 us -> 19.2 us  [swap(): lax.ppermute(value, 'users', [(i, i ^ 1 << bit) for i in range(devices)])]
    all_to_all x1, waiting for transfers between devices: 16.5 us -> 6.44 us  [body(): lax.all_to_all(found, 'users', 0, 0, axis_index_groups=sides, tiled=True)]
    pallas_call x3 -> x4, Pallas kernels: 22.7 us -> 29 us  [the longest x1 15.8 us: tile_sums(): pl.pallas_call(functools.partial(tiles_kernel, step_tiles, places), out_s...]
    add x1 -> x8, other arithmetic: 0.06 us -> 5.17 us  [the longest x2 1.83 us: reduce_pieces(): away = swap(pieces[0, top, 1] + got[top, 1], 1 + top, devices)]
    unnamed x10 -> x8, local copies, waits for them, and re-layouts: 6.22 us -> 2.89 us
    gather x1 -> x0, local copies, waits for them, and re-layouts: 1.65 us -> none  [body(): found = item_factors[asked]]
  transfers between devices with their start and end apart: 3 -> 24, of which waited for: 3 -> 14; matrix products, arithmetic and copies ran while one was open for 1% -> 6% of each run, Pallas kernels for 6% -> 9%
where the time goes in v2:
time: 110 us; the launch traced here: 109 us
  Pallas kernels  36.3 us (33%)
  starting transfers between devices  25.6 us (23%)
  waiting for transfers between devices  25.6 us (23%)
  blocking collectives  10.6 us (10%)
  other arithmetic  5.19 us (5%)
  local copies, waits for them, and re-layouts  4.63 us (4%)
  between operations  1.4 us (1%)
    ppermute x23, starting transfers between devices, swap(): lax.ppermute(value, 'users', [(i, i ^ 1 << bit) for i in range(devices)])  21.9 us
    ppermute x23, waiting for transfers between devices, swap(): lax.ppermute(value, 'users', [(i, i ^ 1 << bit) for i in range(devices)])  19.2 us
    pallas_call x1, Pallas kernels, tile_sums(): pl.pallas_call(functools.partial(tiles_kernel, step_tiles, places), out_s...  15.8 us
    all_to_all x1, blocking collectives, body(): lax.all_to_all(requests, 'users', 0, 0, axis_index_groups=sides, tiled=True)  10.6 us
    pallas_call x1, Pallas kernels, finish(): pl.pallas_call(functools.partial(finish_kernel, users * devices, piece_pl...  8.58 us
    pallas_call x1, Pallas kernels, context_values(): pl.pallas_call(functools.partial(context_kernel, tiles), out_shape=jax.Sh...  7.31 us
    all_to_all x1, waiting for transfers between devices, body(): lax.all_to_all(found, 'users', 0, 0, axis_index_groups=sides, tiled=True)  6.44 us
    all_to_all x1, starting transfers between devices, body(): lax.all_to_all(found, 'users', 0, 0, axis_index_groups=sides, tiled=True)  3.65 us
  transfers between devices with their start and end apart: 24, of which 14 were waited for; matrix products, arithmetic and copies ran while one was open for 6% of the time, Pallas kernels for 9%

profile of v2, /device:TPU:0, one launch (start us, length us, event | category | flops | bytes accessed | tf_op | source)
XLA Modules:
  0.0 109.3 jit_solution(6201127227316708271)
XLA Ops:
  0.6 4.1 %collective-permute-start = (bf16[16,64,128]{2,1,0:T(8,128)(2,1)}, bf16[16,64,128]{2,1,0:T(8,128)(2,1)S(1)}, u32[]{:S(2)}, u32[]{:S(2)}) collective-permute-start(bf16[16,64,128]{2,1,0:T(8,128)(2,1)} %own_ref.1), channel_id=1, source_target_pairs={{0,16},{1,17},{2,18},{3,19},{4,20},{5,21},{6,22},{7,23},{8,24},{9,... | collective-permute-start | bytes 786440 | tf_op jit(solution)/shard_map/ppermute | solution.py:330
  4.7 2.5 %route.1 = (s32[16,1,128]{2,1,0:T(1,128)}, s32[64]{0:T(128)}) custom-call(s32[1]{0:T(128)} %bitcast.me_ref, s32[64]{0:T(128)} %bitcast.6, s32[64]{0:T(128)} %slot_ref.1), custom_call_target="tpu_custom_call" | custom-call | tf_op jit(solution)/shard_map/route/pallas_call | solution.py:53
  7.2 10.6 %all_to_all.10.asked_ref = s32[16,1,128]{2,1,0:T(1,128)} all-to-all(s32[16,1,128]{2,1,0:T(1,128)} %get-tuple-element.14), channel_id=1, replica_groups={{0,1,2,3,4,5,6,7,8,9,10,11,12,13,14,15},{16,17,18,19,20,21,22,23,24,25,..., dimensions={0} | all-to-all | bytes 16384 | tf_op jit(solution)/shard_map/all_to_all | solution.py:383
  18.5 2.2 %collect.1 = bf16[64,64,128]{2,1,0:T(8,128)(2,1)} custom-call(s32[16,1,128]{2,1,0:T(1,128)} %all_to_all.10.asked_ref, bf16[16,64,128]{2,1,0:T(8,128)(2,1)} %own_ref.1, bf16[16,64,128]{2,1,0:T(8,128)(2,1)} %copy-done.2), custom_call_target="tpu_custom_call" | custom-call | tf_op jit(solution)/shard_map/collect/pallas_call | solution.py:80
  20.7 3.7 %all-to-all-start.1 = ((bf16[64,64,128]{2,1,0:T(8,128)(2,1)}), bf16[64,64,128]{2,1,0:T(8,128)(2,1)S(1)}, u32[]{:S(2)}, u32[]{:S(2)}) async-start(bf16[64,64,128]{2,1,0:T(8,128)(2,1)} %collect.1), calls=%async_computation.1 | async-start | bytes 2097152 | tf_op jit(solution)/shard_map/all_to_all | solution.py:385
  25.0 0.9 reshape.13
  25.8 0.9 copy.13
  26.7 7.3 %contexts.1.context_ref = f32[64,8,512]{2,1,0:T(8,128)} custom-call(s32[64]{0:T(128)} %cblock_ref.1, f32[64,8,8]{2,1,0:T(8,128)} %bitcast.5, s32[64,512]{1,0:T(8,128)} %context_ref.1), custom_call_target="tpu_custom_call" | custom-call | tf_op jit(solution)/shard_map/contexts/pallas_call | solution.py:108
  34.0 6.4 %all-to-all-done.1.blocks_ref = bf16[64,64,128]{2,1,0:T(8,128)(2,1)S(1)} async-done(((bf16[64,64,128]{2,1,0:T(8,128)(2,1)}), bf16[64,64,128]{2,1,0:T(8,128)(2,1)S(1)}, u32[]{:S(2)}, u32[]{:S(2)}) %all-to-all-start.1) | async-done | bytes 1048608 | tf_op jit(solution)/shard_map/all_to_all | solution.py:385
  40.4 1.0 copy-done.1
  41.4 15.8 %tile_sums.1 = (f32[8,64,512]{2,1,0:T(8,128)}, f32[4,56,128]{2,1,0:T(8,128)}, f32[4,56,128]{2,1,0:T(8,128)}, f32[4,56,128]{2,1,0:T(8,128)}, f32[4,56,128]{2,1,0:...) custom-call(s32[64]{0:T(128)} %get-tuple-element.13.where_ref, ...), custom_call_target="tpu_custom_call" | custom-call | flops 2000000000 | bytes 12000000 | tf_op jit(solution)/shard_map/tile_sums/pallas_call | solution.py:211
  57.8 0.9 collective-permute-done.7
  58.7 0.9 add.53
  59.7 0.9 collective-permute-start.8
  60.6 0.9 add.46
  62.3 2.7 %collective-permute-done.8 = f32[4,56,128]{2,1,0:T(8,128)S(1)} collective-permute-done((f32[4,56,128]{2,1,0:T(8,128)S(1)}, f32[4,56,128]{2,1,0:T(8,128)S(1)}, u32[]{:S(2)}, u32[]{:S(2)}) %collective-permute-start.8) | collective-permute-done | bytes 114720 | tf_op jit(solution)/shard_map/ppermute | solution.py:330
  65.9 1.3 %collective-permute-done.3 = f32[4,56,128]{2,1,0:T(8,128)S(1)} collective-permute-done((f32[4,56,128]{2,1,0:T(8,128)S(1)}, f32[4,56,128]{2,1,0:T(8,128)S(1)}, u32[]{:S(2)}, u32[]{:S(2)}) %collective-permute-start.3) | collective-permute-done | bytes 114720 | tf_op jit(solution)/shard_map/ppermute | solution.py:330
  67.9 1.3 %collective-permute-start.4 = (f32[2,56,128]{2,1,0:T(8,128)S(1)}, f32[2,56,128]{2,1,0:T(8,128)S(1)}, u32[]{:S(2)}, u32[]{:S(2)}) collective-permute-start(f32[2,56,128]{2,1,0:T(8,128)S(1)} %slice_add_fusion.4), channel_id=1, source_target_pairs={{0,4},{1,5},{2,6},{3,7},{4,0},{5,1},{6,2},{7,3},{8,12},{9,13},{10,... | collective-permute-start | bytes 172040 | tf_op jit(solution)/shard_map/ppermute | solution.py:330
  73.9 1.0 collective-permute-done.10
  74.9 3.1 %collective-permute-start.11 = (f32[1,56,128]{2,1,0:T(8,128)S(1)}, f32[1,56,128]{2,1,0:T(8,128)S(1)}, u32[]{:S(2)}, u32[]{:S(2)}) collective-permute-start(f32[1,56,128]{2,1,0:T(8,128)S(1)} %slice_add_fusion.8), channel_id=1, source_target_pairs={{0,16},{1,17},{2,18},{3,19},{4,20},{5,21},{6,22},{7,23},{8,24},{9,... | collective-permute-start | bytes 86024 | tf_op jit(solution)/shard_map/ppermute | solution.py:330
  78.0 2.1 %collective-permute-done.11 = f32[1,56,128]{2,1,0:T(8,128)S(1)} collective-permute-done((f32[1,56,128]{2,1,0:T(8,128)S(1)}, f32[1,56,128]{2,1,0:T(8,128)S(1)}, u32[]{:S(2)}, u32[]{:S(2)}) %collective-permute-start.11) | collective-permute-done | bytes 28704 | tf_op jit(solution)/shard_map/ppermute | solution.py:330
  80.4 3.0 %collective-permute-start.16 = (f32[1,56,128]{2,1,0:T(8,128)S(1)}, f32[1,56,128]{2,1,0:T(8,128)S(1)}, u32[]{:S(2)}, u32[]{:S(2)}) collective-permute-start(f32[1,56,128]{2,1,0:T(8,128)S(1)} %fusion.2), channel_id=1, source_target_pairs={{0,16},{1,17},{2,18},{3,19},{4,20},{5,21},{6,22},{7,23},{8,24},{9,... | collective-permute-start | bytes 86024 | tf_op jit(solution)/shard_map/ppermute | solution.py:330
  84.0 0.9 collective-permute-start.13
  85.3 1.7 %collective-permute-start.17 = (f32[1,56,128]{2,1,0:T(8,128)S(1)}, f32[1,56,128]{2,1,0:T(8,128)S(1)}, u32[]{:S(2)}, u32[]{:S(2)}) collective-permute-start(f32[1,56,128]{2,1,0:T(8,128)S(1)} %collective-permute-done.16), channel_id=1, source_target_pairs={{0,8},{1,9},{2,10},{3,11},{4,12},{5,13},{6,14},{7,15},{8,0},{9,1},... | collective-permute-start | bytes 86024 | tf_op jit(solution)/shard_map/ppermute | solution.py:330
  87.0 2.1 %collective-permute-done.17 = f32[1,56,128]{2,1,0:T(8,128)S(1)} collective-permute-done((f32[1,56,128]{2,1,0:T(8,128)S(1)}, f32[1,56,128]{2,1,0:T(8,128)S(1)}, u32[]{:S(2)}, u32[]{:S(2)}) %collective-permute-start.17) | collective-permute-done | bytes 28704 | tf_op jit(solution)/shard_map/ppermute | solution.py:330
  89.8 1.5 %collective-permute-start.14 = (f32[4,56,128]{2,1,0:T(8,128)S(1)}, f32[4,56,128]{2,1,0:T(8,128)S(1)}, u32[]{:S(2)}, u32[]{:S(2)}) collective-permute-start(f32[4,56,128]{2,1,0:T(8,128)S(1)} %pad_maximum_fusion.rest_6_), channel_id=1, source_target_pairs={{0,2},{1,3},{2,0},{3,1},{4,6},{5,7},{6,4},{7,5},{8,10},{9,11},{10,... | collective-permute-start | bytes 344072 | tf_op jit(solution)/shard_map/ppermute | solution.py:330
  91.3 2.1 %collective-permute-done.18 = f32[2,56,128]{2,1,0:T(8,128)S(1)} collective-permute-done((f32[2,56,128]{2,1,0:T(8,128)S(1)}, f32[2,56,128]{2,1,0:T(8,128)S(1)}, u32[]{:S(2)}, u32[]{:S(2)}) %collective-permute-start.18) | collective-permute-done | bytes 57376 | tf_op jit(solution)/shard_map/ppermute | solution.py:330
  93.3 1.0 collective-permute-start.19
  94.9 3.2 %collective-permute-done.19.rest_5_ = f32[4,56,128]{2,1,0:T(8,128)S(1)} collective-permute-done((f32[4,56,128]{2,1,0:T(8,128)S(1)}, f32[4,56,128]{2,1,0:T(8,128)S(1)}, u32[]{:S(2)}, u32[]{:S(2)}) %collective-permute-start.19) | collective-permute-done | bytes 114720 | tf_op jit(solution)/shard_map/ppermute | solution.py:330
  98.2 1.3 %collective-permute-done.20.rest_1_ = f32[4,56,128]{2,1,0:T(8,128)S(1)} collective-permute-done((f32[4,56,128]{2,1,0:T(8,128)S(1)}, f32[4,56,128]{2,1,0:T(8,128)S(1)}, u32[]{:S(2)}, u32[]{:S(2)}) %collective-permute-start.20) | collective-permute-done | bytes 114720 | tf_op jit(solution)/shard_map/ppermute | solution.py:330
  99.5 1.2 %copy-done = f32[8,64,512]{2,1,0:T(8,128)S(1)} copy-done((f32[8,64,512]{2,1,0:T(8,128)S(1)}, f32[8,64,512]{2,1,0:T(8,128)}, u32[]{:S(2)}) %copy-start) | copy-done | bytes 1048600
  100.7 8.6 %finish.1 = (f32[512,128]{1,0:T(8,128)}, f32[128,512]{1,0:T(8,128)}) custom-call(s32[1]{0:T(128)} %bitcast.me_ref, f32[8,64,512]{2,1,0:T(8,128)S(1)} %copy-done, f32[4,56,128]{2,1,0:T(8,128)S(1)} %collective-permute-done.15.rest_0_, f32[4,56,128]{2,1,0:T(8,128)S(1)} %collective-permute-done.20.rest_1_, f32[4,56,128]{2,1,0:T(8,128)S(1)} %collective-permute-done.21.rest_2_, ...), custom_call_target="tpu_custom_call" | custom-call | tf_op jit(solution)/shard_map/finish/pallas_call | solution.py:312
  (46 shorter events, 11.0 us)
Async XLA Ops:
  0.6 17.2 %collective-permute-start = (bf16[16,64,128]{2,1,0:T(8,128)(2,1)}, bf16[16,64,128]{2,1,0:T(8,128)(2,1)S(1)}, u32[]{:S(2)}, u32[]{:S(2)}) collective-permute-start(bf16[16,64,128]{2,1,0:T(8,128)(2,1)} %own_ref.1), channel_id=1, source_target_pairs={{0,16},{1,17},{2,18},{3,19},{4,20},{5,21},{6,22},{7,23},{8,24},{9,... | collective-permute-start | bytes 786440 | tf_op jit(solution)/shard_map/ppermute | solution.py:330
  17.8 0.7 copy-start.2
  20.7 19.8 %all-to-all-start.1 = ((bf16[64,64,128]{2,1,0:T(8,128)(2,1)}), bf16[64,64,128]{2,1,0:T(8,128)(2,1)S(1)}, u32[]{:S(2)}, u32[]{:S(2)}) async-start(bf16[64,64,128]{2,1,0:T(8,128)(2,1)} %collect.1), calls=%async_computation.1 | async-start | bytes 2097152 | tf_op jit(solution)/shard_map/all_to_all | solution.py:385
  40.4 1.0 copy-start.1
  57.2 1.6 %collective-permute-start.7 = (f32[4,56,128]{2,1,0:T(8,128)}, f32[4,56,128]{2,1,0:T(8,128)S(1)}, u32[]{:S(2)}, u32[]{:S(2)}) collective-permute-start(f32[4,56,128]{2,1,0:T(8,128)} %get-tuple-element.23), channel_id=1, source_target_pairs={{0,1},{1,0},{2,3},{3,2},{4,5},{5,4},{6,7},{7,6},{8,9},{9,8},{10,11... | collective-permute-start | bytes 344072 | tf_op jit(solution)/shard_map/ppermute | solution.py:330
  57.2 3.3 %collective-permute-start.2 = (f32[4,56,128]{2,1,0:T(8,128)}, f32[4,56,128]{2,1,0:T(8,128)S(1)}, u32[]{:S(2)}, u32[]{:S(2)}) collective-permute-start(f32[4,56,128]{2,1,0:T(8,128)} %get-tuple-element.19), channel_id=1, source_target_pairs={{0,1},{1,0},{2,3},{3,2},{4,5},{5,4},{6,7},{7,6},{8,9},{9,8},{10,11... | collective-permute-start | bytes 344072 | tf_op jit(solution)/shard_map/ppermute | solution.py:330
  57.7 4.5 %collective-permute-start.6 = (f32[4,56,128]{2,1,0:T(8,128)}, f32[4,56,128]{2,1,0:T(8,128)S(1)}, u32[]{:S(2)}, u32[]{:S(2)}) collective-permute-start(f32[4,56,128]{2,1,0:T(8,128)} %get-tuple-element.21), channel_id=1, source_target_pairs={{0,1},{1,0},{2,3},{3,2},{4,5},{5,4},{6,7},{7,6},{8,9},{9,8},{10,11... | collective-permute-start | bytes 344072 | tf_op jit(solution)/shard_map/ppermute | solution.py:330
  59.7 5.3 %collective-permute-start.8 = (f32[4,56,128]{2,1,0:T(8,128)S(1)}, f32[4,56,128]{2,1,0:T(8,128)S(1)}, u32[]{:S(2)}, u32[]{:S(2)}) collective-permute-start(f32[4,56,128]{2,1,0:T(8,128)S(1)} %add.53), channel_id=1, source_target_pairs={{0,4},{1,5},{2,6},{3,7},{4,0},{5,1},{6,2},{7,3},{8,12},{9,13},{10,... | collective-permute-start | bytes 344072 | tf_op jit(solution)/shard_map/ppermute | solution.py:330
  60.6 5.3 %collective-permute-start.1 = (f32[4,56,128]{2,1,0:T(8,128)}, f32[4,56,128]{2,1,0:T(8,128)S(1)}, u32[]{:S(2)}, u32[]{:S(2)}) collective-permute-start(f32[4,56,128]{2,1,0:T(8,128)} %get-tuple-element.17), channel_id=1, source_target_pairs={{0,1},{1,0},{2,3},{3,2},{4,5},{5,4},{6,7},{7,6},{8,9},{9,8},{10,11... | collective-permute-start | bytes 344072 | tf_op jit(solution)/shard_map/ppermute | solution.py:330
  61.5 5.6 %collective-permute-start.3 = (f32[4,56,128]{2,1,0:T(8,128)S(1)}, f32[4,56,128]{2,1,0:T(8,128)S(1)}, u32[]{:S(2)}, u32[]{:S(2)}) collective-permute-start(f32[4,56,128]{2,1,0:T(8,128)S(1)} %add.46), channel_id=1, source_target_pairs={{0,2},{1,3},{2,0},{3,1},{4,6},{5,7},{6,4},{7,5},{8,10},{9,11},{10,... | collective-permute-start | bytes 344072 | tf_op jit(solution)/shard_map/ppermute | solution.py:330
  65.8 4.2 %collective-permute-start.9 = (f32[2,56,128]{2,1,0:T(8,128)S(1)}, f32[2,56,128]{2,1,0:T(8,128)S(1)}, u32[]{:S(2)}, u32[]{:S(2)}) collective-permute-start(f32[2,56,128]{2,1,0:T(8,128)S(1)} %slice_add_fusion), channel_id=1, source_target_pairs={{0,2},{1,3},{2,0},{3,1},{4,6},{5,7},{6,4},{7,5},{8,10},{9,11},{10,... | collective-permute-start | bytes 172040 | tf_op jit(solution)/shard_map/ppermute | solution.py:330
  67.9 4.2 %collective-permute-start.4 = (f32[2,56,128]{2,1,0:T(8,128)S(1)}, f32[2,56,128]{2,1,0:T(8,128)S(1)}, u32[]{:S(2)}, u32[]{:S(2)}) collective-permute-start(f32[2,56,128]{2,1,0:T(8,128)S(1)} %slice_add_fusion.4), channel_id=1, source_target_pairs={{0,4},{1,5},{2,6},{3,7},{4,0},{5,1},{6,2},{7,3},{8,12},{9,13},{10,... | collective-permute-start | bytes 172040 | tf_op jit(solution)/shard_map/ppermute | solution.py:330
  70.9 4.0 %collective-permute-start.10 = (f32[1,56,128]{2,1,0:T(8,128)S(1)}, f32[1,56,128]{2,1,0:T(8,128)S(1)}, u32[]{:S(2)}, u32[]{:S(2)}) collective-permute-start(f32[1,56,128]{2,1,0:T(8,128)S(1)} %slice.75), channel_id=1, source_target_pairs={{0,8},{1,9},{2,10},{3,11},{4,12},{5,13},{6,14},{7,15},{8,0},{9,1},... | collective-permute-start | bytes 86024 | tf_op jit(solution)/shard_map/ppermute | solution.py:330
  73.0 5.0 %collective-permute-start.5 = (f32[1,56,128]{2,1,0:T(8,128)S(1)}, f32[1,56,128]{2,1,0:T(8,128)S(1)}, u32[]{:S(2)}, u32[]{:S(2)}) collective-permute-start(f32[1,56,128]{2,1,0:T(8,128)S(1)} %slice.69), channel_id=1, source_target_pairs={{0,8},{1,9},{2,10},{3,11},{4,12},{5,13},{6,14},{7,15},{8,0},{9,1},... | collective-permute-start | bytes 86024 | tf_op jit(solution)/shard_map/ppermute | solution.py:330
  74.9 5.2 %collective-permute-start.11 = (f32[1,56,128]{2,1,0:T(8,128)S(1)}, f32[1,56,128]{2,1,0:T(8,128)S(1)}, u32[]{:S(2)}, u32[]{:S(2)}) collective-permute-start(f32[1,56,128]{2,1,0:T(8,128)S(1)} %slice_add_fusion.8), channel_id=1, source_target_pairs={{0,16},{1,17},{2,18},{3,19},{4,20},{5,21},{6,22},{7,23},{8,24},{9,... | collective-permute-start | bytes 86024 | tf_op jit(solution)/shard_map/ppermute | solution.py:330
  80.1 3.9 %collective-permute-start.12 = (f32[1,56,128]{2,1,0:T(8,128)S(1)}, f32[1,56,128]{2,1,0:T(8,128)S(1)}, u32[]{:S(2)}, u32[]{:S(2)}) collective-permute-start(f32[1,56,128]{2,1,0:T(8,128)S(1)} %fusion.2), channel_id=1, source_target_pairs={{0,8},{1,9},{2,10},{3,11},{4,12},{5,13},{6,14},{7,15},{8,0},{9,1},... | collective-permute-start | bytes 86024 | tf_op jit(solution)/shard_map/ppermute | solution.py:330
  80.4 4.8 %collective-permute-start.16 = (f32[1,56,128]{2,1,0:T(8,128)S(1)}, f32[1,56,128]{2,1,0:T(8,128)S(1)}, u32[]{:S(2)}, u32[]{:S(2)}) collective-permute-start(f32[1,56,128]{2,1,0:T(8,128)S(1)} %fusion.2), channel_id=1, source_target_pairs={{0,16},{1,17},{2,18},{3,19},{4,20},{5,21},{6,22},{7,23},{8,24},{9,... | collective-permute-start | bytes 86024 | tf_op jit(solution)/shard_map/ppermute | solution.py:330
  84.0 5.7 %collective-permute-start.13 = (f32[2,56,128]{2,1,0:T(8,128)S(1)}, f32[2,56,128]{2,1,0:T(8,128)S(1)}, u32[]{:S(2)}, u32[]{:S(2)}) collective-permute-start(f32[2,56,128]{2,1,0:T(8,128)S(1)} %pad_maximum_fusion.1), channel_id=1, source_target_pairs={{0,4},{1,5},{2,6},{3,7},{4,0},{5,1},{6,2},{7,3},{8,12},{9,13},{10,... | collective-permute-start | bytes 172040 | tf_op jit(solution)/shard_map/ppermute | solution.py:330
  85.3 3.9 %collective-permute-start.17 = (f32[1,56,128]{2,1,0:T(8,128)S(1)}, f32[1,56,128]{2,1,0:T(8,128)S(1)}, u32[]{:S(2)}, u32[]{:S(2)}) collective-permute-start(f32[1,56,128]{2,1,0:T(8,128)S(1)} %collective-permute-done.16), channel_id=1, source_target_pairs={{0,8},{1,9},{2,10},{3,11},{4,12},{5,13},{6,14},{7,15},{8,0},{9,1},... | collective-permute-start | bytes 86024 | tf_op jit(solution)/shard_map/ppermute | solution.py:330
  89.2 4.2 %collective-permute-start.18 = (f32[2,56,128]{2,1,0:T(8,128)S(1)}, f32[2,56,128]{2,1,0:T(8,128)S(1)}, u32[]{:S(2)}, u32[]{:S(2)}) collective-permute-start(f32[2,56,128]{2,1,0:T(8,128)S(1)} %pad_maximum_fusion.2), channel_id=1, source_target_pairs={{0,2},{1,3},{2,0},{3,1},{4,6},{5,7},{6,4},{7,5},{8,10},{9,11},{10,... | collective-permute-start | bytes 172040 | tf_op jit(solution)/shard_map/ppermute | solution.py:330
  89.8 5.1 %collective-permute-start.14 = (f32[4,56,128]{2,1,0:T(8,128)S(1)}, f32[4,56,128]{2,1,0:T(8,128)S(1)}, u32[]{:S(2)}, u32[]{:S(2)}) collective-permute-start(f32[4,56,128]{2,1,0:T(8,128)S(1)} %pad_maximum_fusion.rest_6_), channel_id=1, source_target_pairs={{0,2},{1,3},{2,0},{3,1},{4,6},{5,7},{6,4},{7,5},{8,10},{9,11},{10,... | collective-permute-start | bytes 344072 | tf_op jit(solution)/shard_map/ppermute | solution.py:330
  93.3 4.8 %collective-permute-start.19 = (f32[4,56,128]{2,1,0:T(8,128)S(1)}, f32[4,56,128]{2,1,0:T(8,128)S(1)}, u32[]{:S(2)}, u32[]{:S(2)}) collective-permute-start(f32[4,56,128]{2,1,0:T(8,128)S(1)} %constant_dynamic-update-slice_fusion.rest_7_), channel_id=1, source_target_pairs={{0,4},{1,5},{2,6},{3,7},{4,0},{5,1},{6,2},{7,3},{8,12},{9,13},{10,... | collective-permute-start | bytes 344072 | tf_op jit(solution)/shard_map/ppermute | solution.py:330
  94.4 3.8 %collective-permute-start.21 = (f32[4,56,128]{2,1,0:T(8,128)S(1)}, f32[4,56,128]{2,1,0:T(8,128)S(1)}, u32[]{:S(2)}, u32[]{:S(2)}) collective-permute-start(f32[4,56,128]{2,1,0:T(8,128)S(1)} %pad_maximum_fusion.rest_6_), channel_id=1, source_target_pairs={{0,1},{1,0},{2,3},{3,2},{4,5},{5,4},{6,7},{7,6},{8,9},{9,8},{10,11... | collective-permute-start | bytes 344072 | tf_op jit(solution)/shard_map/ppermute | solution.py:330
  94.4 3.8 %collective-permute-start.22 = (f32[4,56,128]{2,1,0:T(8,128)S(1)}, f32[4,56,128]{2,1,0:T(8,128)S(1)}, u32[]{:S(2)}, u32[]{:S(2)}) collective-permute-start(f32[4,56,128]{2,1,0:T(8,128)S(1)} %constant_dynamic-update-slice_fusion.rest_7_), channel_id=1, source_target_pairs={{0,1},{1,0},{2,3},{3,2},{4,5},{5,4},{6,7},{7,6},{8,9},{9,8},{10,11... | collective-permute-start | bytes 344072 | tf_op jit(solution)/shard_map/ppermute | solution.py:330
  94.9 3.3 %collective-permute-start.15 = (f32[4,56,128]{2,1,0:T(8,128)S(1)}, f32[4,56,128]{2,1,0:T(8,128)S(1)}, u32[]{:S(2)}, u32[]{:S(2)}) collective-permute-start(f32[4,56,128]{2,1,0:T(8,128)S(1)} %collective-permute-done.14.rest_4_), channel_id=1, source_target_pairs={{0,1},{1,0},{2,3},{3,2},{4,5},{5,4},{6,7},{7,6},{8,9},{9,8},{10,11... | collective-permute-start | bytes 344072 | tf_op jit(solution)/shard_map/ppermute | solution.py:330
  98.1 1.3 %collective-permute-start.20 = (f32[4,56,128]{2,1,0:T(8,128)S(1)}, f32[4,56,128]{2,1,0:T(8,128)S(1)}, u32[]{:S(2)}, u32[]{:S(2)}) collective-permute-start(f32[4,56,128]{2,1,0:T(8,128)S(1)} %collective-permute-done.19.rest_5_), channel_id=1, source_target_pairs={{0,1},{1,0},{2,3},{3,2},{4,5},{5,4},{6,7},{7,6},{8,9},{9,8},{10,11... | collective-permute-start | bytes 344072 | tf_op jit(solution)/shard_map/ppermute | solution.py:330
  99.5 1.2 %copy-start = (f32[8,64,512]{2,1,0:T(8,128)S(1)}, f32[8,64,512]{2,1,0:T(8,128)}, u32[]{:S(2)}) copy-start(f32[8,64,512]{2,1,0:T(8,128)} %get-tuple-element.15.y_ref) | copy-start | bytes 3145732

commit v3 on v2

v3 whole, which is shorter than its diff:
```python
import functools

import jax
import jax.numpy as jnp
from jax import lax
from jax.experimental import pallas as pl
from jax.experimental.pallas import tpu as pltpu
from jax.sharding import PartitionSpec as P

CB = 8
SLOTS = 2
PLACES = 2 * SLOTS
HIGH = lax.Precision.HIGHEST
LANES = 128
ROWS = 8
MASKS = 4
BATCH = 8
MIB = 2**20

SMEM = pl.BlockSpec(memory_space=pltpu.SMEM)
VMEM = pl.BlockSpec(memory_space=pltpu.VMEM)


def limit(mib):
    return pltpu.CompilerParams(vmem_limit_bytes=mib * MIB)


def dot(lhs, rhs):
    return jnp.dot(lhs, rhs, preferred_element_type=jnp.float32)


def dot_nt(lhs, rhs):
    return lax.dot_general(lhs, rhs, (((1,), (1,)), ((), ())), preferred_element_type=jnp.float32)


def split(value):
    high = value.astype(jnp.bfloat16)
    return high, (value - high.astype(jnp.float32)).astype(jnp.bfloat16)


def route_kernel(half, me_ref, owner_ref, slot_ref, request_ref, tile_ref, used_ref):
    side = me_ref[0] // half
    low_me = lax.rem(me_ref[0], half)
    lane = lax.broadcasted_iota(jnp.int32, (1, LANES), 1)

    def clear(place, _):
        used_ref[place] = 0
        tile_ref[SLOTS * place] = -1
        tile_ref[SLOTS * place + 1] = -1
        return 0

    lax.fori_loop(0, 2 * half, clear, 0)
    request_ref[...] = jnp.zeros_like(request_ref)

    def assign(tile, _):
        owner = owner_ref[tile]
        taken = used_ref[owner]
        used_ref[owner] = taken + 1
        low = lax.rem(owner, half)
        place = jnp.where(owner // half == side, 0, SLOTS) + taken
        request_ref[low] = jnp.where(lane == place, slot_ref[tile], request_ref[low])
        tile_ref[jnp.bitwise_xor(low, low_me) * PLACES + place] = tile
        return 0

    lax.fori_loop(0, owner_ref.shape[0], assign, 0)


def route(me, owners, slots, half):
    return pl.pallas_call(
        functools.partial(route_kernel, half),
        out_shape=(
            jax.ShapeDtypeStruct((half, 1, LANES), jnp.int32),
            jax.ShapeDtypeStruct((half * PLACES,), jnp.int32),
        ),
        in_specs=[SMEM, SMEM, SMEM],
        out_specs=(VMEM, SMEM),
        scratch_shapes=[pltpu.SMEM((2 * half,), jnp.int32)],
        compiler_params=limit(2),
        name="route",
    )(me, owners, slots)


def collect_kernel(me_ref, asked_ref, own_ref, mirror_ref, *out_refs):
    low_me = lax.rem(me_ref[0], len(out_refs))
    for mask, out_ref in enumerate(out_refs):
        peer = jnp.bitwise_xor(low_me, mask)
        for place in range(PLACES):
            source = own_ref if place < SLOTS else mirror_ref
            out_ref[place] = source[asked_ref[peer, 0, place]]


def collect(me, asked, own, mirror):
    half = asked.shape[0]
    return pl.pallas_call(
        collect_kernel,
        out_shape=(jax.ShapeDtypeStruct((PLACES,) + own.shape[1:], own.dtype),) * half,
        in_specs=[SMEM, SMEM, VMEM, VMEM],
        out_specs=(VMEM,) * half,
        compiler_params=limit(8),
        name="collect",
    )(me, asked, own, mirror)


def piece_places(devices):
    return {
        (core, plane): [core + 2 * plane + 8 * rest for rest in range(devices // 8)]
        for core in range(2)
        for plane in range(4)
    }


PIECES = [(core, plane) for core in (1, 0) for plane in (3, 1, 2, 0)]


def pack_rows(ranks, devices):
    groups = ranks // LANES
    rows = (groups * (groups + 1) // 2 + groups) * LANES
    return -(-rows // (devices * ROWS)) * ROWS


def tiles_kernel(group, last, places, *refs):
    tile_ref, cblock_ref, count_ref, me_ref = refs[:4]
    block_refs = refs[4 : 4 + MASKS]
    weights_ref, marks_ref, factors_ref = refs[4 + MASKS : 7 + MASKS]
    refs = refs[7 + MASKS :]
    before_ref = basis_ref = None
    if group:
        before_ref, refs = refs[0], refs[1:]
    if last:
        basis_ref, refs = refs[0], refs[1:]
        piece_refs, refs = refs[: len(PIECES)], refs[len(PIECES) :]
        high_ref, low_ref, refs = refs[0], refs[1], refs[2:]
        y_ref, pack_ref, refs = refs[0], refs[1], refs[2:]
    else:
        y_ref, refs = refs[0], refs[1:]
    held_ref, sem_ref, product_ref, context_ref = refs
    rank_c, rank_i, users = y_ref.shape
    slots = MASKS * PLACES

    tiles = [tile_ref[group * slots + slot] for slot in range(slots)]
    copies = []
    for slot in range(slots):
        copy = pltpu.make_async_copy(
            weights_ref.at[jnp.maximum(tiles[slot], 0)], held_ref.at[slot], sem_ref.at[slot]
        )
        copy.start()
        copies.append(copy)

    for first in range(0, slots, BATCH):
        for place in range(BATCH):
            tile = jnp.maximum(tiles[first + place], 0)
            used = tiles[first + place] >= 0
            cblock = cblock_ref[tile]
            per = LANES // CB
            start = pl.multiple_of(cblock // per * LANES, LANES)
            table = factors_ref[:, pl.ds(start, LANES)].astype(jnp.float32)
            table = jnp.where(used, table, 0.0)
            marks = marks_ref[pl.ds(tile, 1), :] + lax.rem(cblock, per) * CB
            for lane in range(users // LANES):
                index = jnp.broadcast_to(marks[:, lane * LANES : (lane + 1) * LANES], (rank_c, LANES))
                context_ref[place, :, lane * LANES : (lane + 1) * LANES] = jnp.take_along_axis(
                    table, index, axis=1, mode="promise_in_bounds"
                )
        for place in range(BATCH):
            slot = first + place
            copies[slot].wait()
            product = dot(block_refs[slot // PLACES][slot % PLACES], held_ref[slot])
            product_ref[place] = product.astype(jnp.bfloat16).astype(jnp.float32)
        half = rank_i // 2
        for lane in range(users // LANES):
            lanes = slice(lane * LANES, (lane + 1) * LANES)
            for part in range(2):
                rows = slice(part * half, (part + 1) * half)
                if first:
                    total = y_ref[:, rows, lanes]
                elif group:
                    total = before_ref[:, rows, lanes]
                else:
                    total = jnp.zeros((rank_c, half, LANES), jnp.float32)
                for place in range(BATCH):
                    values = context_ref[place, :, lanes]
                    total = total + values[:, None, :] * product_ref[place, rows, lanes][None]
                y_ref[:, rows, lanes] = total

    if not last:
        return
    living = lax.broadcasted_iota(jnp.int32, (rank_i, users), 1) < count_ref[0]
    for r in range(rank_c):
        high, low = split(jnp.where(living, y_ref[r], 0.0))
        high_ref[r * rank_i : (r + 1) * rank_i] = high
        low_ref[r * rank_i : (r + 1) * rank_i] = low
    ranks = rank_c * rank_i
    groups = ranks // LANES
    place = 0
    for i in range(groups):
        rows = slice(i * LANES, (i + 1) * LANES)
        strip = dot_nt(high_ref[rows], high_ref[i * LANES :])
        strip = strip + dot_nt(high_ref[rows], low_ref[i * LANES :])
        strip = strip + dot_nt(low_ref[rows], high_ref[i * LANES :])
        for j in range(groups - i):
            pack_ref[place * LANES : (place + 1) * LANES] = strip[:, j * LANES : (j + 1) * LANES]
            place += 1
    basis_high, basis_low = split(basis_ref[...])
    projection = dot(high_ref[...], basis_high) + dot(high_ref[...], basis_low) + dot(low_ref[...], basis_high)
    pack_ref[place * LANES : (place + groups) * LANES] = projection
    place += groups
    if place * LANES < pack_ref.shape[0]:
        pack_ref[place * LANES :] = jnp.zeros((pack_ref.shape[0] - place * LANES, LANES), jnp.float32)
    me = me_ref[0]
    chunk = piece_refs[0].shape[1]
    for piece, ref in zip(PIECES, piece_refs):
        for i, position in enumerate(places[piece]):
            start = pl.multiple_of(jnp.bitwise_xor(me, position) * chunk, ROWS)
            ref[i] = pack_ref[pl.ds(start, chunk)]


def tile_sums(tile_of, cblock, count, me, blocks, weights, marks, factors, user_basis, devices):
    block_len, users = weights.shape[1:]
    rank_i = blocks[0].shape[1]
    rank_c = factors.shape[0]
    ranks = rank_c * rank_i
    slots = MASKS * PLACES
    chunk = pack_rows(ranks, devices)
    calls = len(blocks) // MASKS
    y_shape = (rank_c, rank_i, users)
    y_type = jax.ShapeDtypeStruct(y_shape, jnp.float32)
    y = None
    for group in range(calls):
        last = group == calls - 1
        operands = [tile_of, cblock, count, me, *blocks[group * MASKS : (group + 1) * MASKS], weights, marks, factors]
        in_specs = [SMEM] * 4 + [VMEM] * MASKS + [pl.BlockSpec(memory_space=pltpu.HBM), VMEM, VMEM]
        aliases = {}
        if group:
            if not last:
                aliases = {len(operands): 0}
            operands.append(y)
            in_specs.append(VMEM)
        scratch = [
            pltpu.VMEM((slots, block_len, users), jnp.bfloat16),
            pltpu.SemaphoreType.DMA((slots,)),
            pltpu.VMEM((BATCH, rank_i, users), jnp.float32),
            pltpu.VMEM((BATCH, rank_c, users), jnp.float32),
        ]
        if last:
            operands.append(user_basis)
            in_specs.append(VMEM)
            out_shape = (jax.ShapeDtypeStruct((devices // 8, chunk, LANES), jnp.float32),) * len(PIECES)
            out_shape += (jax.ShapeDtypeStruct((ranks, users), jnp.bfloat16),) * 2
            out_specs = (VMEM,) * len(out_shape)
            scratch = [pltpu.VMEM(y_shape, jnp.float32), pltpu.VMEM((devices * chunk, LANES), jnp.float32)] + scratch
        else:
            out_shape, out_specs = y_type, VMEM
        y = pl.pallas_call(
            functools.partial(tiles_kernel, group, last, piece_places(devices)),
            out_shape=out_shape,
            in_specs=in_specs,
            out_specs=out_specs,
            input_output_aliases=aliases,
            scratch_shapes=scratch,
            compiler_params=limit(16),
            cost_estimate=pl.CostEstimate(flops=5 * 10**8, bytes_accessed=4 * 10**6, transcendentals=0),
            name="tile_sums",
        )(*operands)
    return dict(zip(PIECES, y[:-2])), y[-2], y[-1]


def inverse_factor(gram):
    order = gram.shape[0]
    panels = order // ROWS
    sub = lax.broadcasted_iota(jnp.int32, (ROWS, order), 0)
    lane = lax.broadcasted_iota(jnp.int32, (ROWS, order), 1)
    left = [gram[ROWS * i : ROWS * (i + 1)] for i in range(panels)]
    right = [jnp.where(lane == sub + ROWS * i, 1.0, 0.0) for i in range(panels)]
    for k in range(panels):
        columns = {
            i: [
                jnp.broadcast_to(left[i][:, ROWS * k + j : ROWS * k + j + 1], (ROWS, order))
                for j in range(ROWS)
            ]
            for i in range(k, panels)
        }
        row, tail = left[k], right[k]
        scale = jnp.zeros((ROWS, order), jnp.float32)
        rows, tails = [], []
        for j in range(ROWS):
            head = columns[k][j]
            pivot = jnp.broadcast_to(head[j : j + 1], (ROWS, order))
            inverse = pl.reciprocal(pivot, approx=True)
            inverse = inverse * (2.0 - pivot * inverse)
            scale = jnp.where(sub == j, pivot, scale)
            rows.append(jnp.broadcast_to(row[j : j + 1], (ROWS, order)))
            tails.append(jnp.broadcast_to(tail[j : j + 1], (ROWS, order)))
            below = jnp.where(sub > j, head, 0.0) * inverse
            row = row - below * rows[j]
            tail = tail - below * tails[j]
            facts = {k: below}
            for i in range(k + 1, panels):
                facts[i] = columns[i][j] * inverse
            for c in range(j + 1, ROWS):
                crossing = jnp.broadcast_to(head[c : c + 1], (ROWS, order))
                for i in range(k, panels):
                    columns[i][c] = columns[i][c] - facts[i] * crossing
            for i in range(k + 1, panels):
                left[i] = left[i] - facts[i] * rows[j]
                right[i] = right[i] - facts[i] * tails[j]
        right[k] = tail * lax.rsqrt(scale)
    return jnp.concatenate(right, axis=0)


def finish_kernel(total_users, places, me_ref, high_ref, low_ref, *rest):
    piece_refs, (basis_ref, core_out_ref, pack_ref, full_ref) = rest[: len(PIECES)], rest[len(PIECES) :]
    me = me_ref[0]
    chunk = piece_refs[0].shape[1]
    for piece, ref in zip(PIECES, piece_refs):
        for i, position in enumerate(places[piece]):
            start = pl.multiple_of(jnp.bitwise_xor(me, position) * chunk, ROWS)
            pack_ref[pl.ds(start, chunk)] = ref[i]
    groups = full_ref.shape[0] // LANES
    place = 0
    for i in range(groups):
        for j in range(i, groups):
            block = pack_ref[place * LANES : (place + 1) * LANES]
            full_ref[i * LANES : (i + 1) * LANES, j * LANES : (j + 1) * LANES] = block
            if i != j:
                full_ref[j * LANES : (j + 1) * LANES, i * LANES : (i + 1) * LANES] = block.T
            place += 1
    projection = pack_ref[place * LANES : (place + groups) * LANES]
    turned = jnp.concatenate(
        [projection[i * LANES : (i + 1) * LANES].T for i in range(groups)], axis=1
    )
    turned_high, turned_low = split(turned)
    full_high, full_low = split(full_ref[...])
    crossed = dot(turned_high, full_high) + dot(turned_high, full_low) + dot(turned_low, full_high)
    gram = jnp.dot(crossed, projection, precision=HIGH, preferred_element_type=jnp.float32)
    projected = (
        dot(turned_high, high_ref[...]) + dot(turned_high, low_ref[...]) + dot(turned_low, high_ref[...])
    )
    inverse = inverse_factor(gram)
    root = total_users ** 0.5
    scaled = jnp.dot(inverse * root, projected, precision=HIGH, preferred_element_type=jnp.float32)
    for i in range(scaled.shape[1] // LANES):
        basis_ref[i * LANES : (i + 1) * LANES] = scaled[:, i * LANES : (i + 1) * LANES].T
    core_out_ref[...] = jnp.dot(
        inverse * (1.0 / root), crossed, precision=HIGH, preferred_element_type=jnp.float32
    )


def finish(me, high, low, pieces, devices):
    ranks, users = high.shape
    chunk = pack_rows(ranks, devices)
    return pl.pallas_call(
        functools.partial(finish_kernel, users * devices, piece_places(devices)),
        out_shape=(
            jax.ShapeDtypeStruct((users, LANES), jnp.float32),
            jax.ShapeDtypeStruct((LANES, ranks), jnp.float32),
        ),
        in_specs=[SMEM] + [VMEM] * (2 + len(PIECES)),
        out_specs=(VMEM, VMEM),
        scratch_shapes=[
            pltpu.VMEM((devices * chunk, LANES), jnp.float32),
            pltpu.VMEM((ranks, ranks), jnp.float32),
        ],
        compiler_params=limit(16),
        name="finish",
    )(me, high, low, *[pieces[piece] for piece in PIECES])


def swap(value, mask, devices):
    return lax.ppermute(value, "users", [(i, i ^ mask) for i in range(devices)])


def reduce_pieces(pieces, devices):
    got = {plane: swap(pieces[1, plane], 1, devices) for plane in (3, 1, 2, 0)}
    away = [swap(pieces[0, plane] + got[plane], 2 * plane, devices) for plane in (3, 1, 2)]
    rest = devices // 8
    total = None
    far = []
    for position in list(range(rest - 1, -1, -1)):
        rows = slice(position, position + 1)
        value = pieces[0, 0][rows] + got[0][rows] + away[0][rows] + away[1][rows] + away[2][rows]
        if position:
            far.append(swap(value, 8 * position, devices))
        else:
            total = value
    for value in far:
        total = total + value
    return total


def spread_pieces(total, devices):
    near = [total] + [swap(total, 8 * position, devices) for position in range(1, devices // 8)]
    near = jnp.concatenate(near, axis=0)
    pieces = {(0, 0): near}
    for plane in (3, 1, 2):
        pieces[0, plane] = swap(near, 2 * plane, devices)
    for plane in (0, 3, 1, 2):
        pieces[1, plane] = swap(pieces[0, plane], 1, devices)
    return pieces


def body(
    tile_owner, tile_slot, tile_cblock, tile_context, tile_weights,
    item_factors, context_factors, user_basis, user_counts,
):
    devices = lax.axis_size("users")
    half = devices // 2
    me = lax.axis_index("users").astype(jnp.int32).reshape(1)

    mirror = swap(item_factors, half, devices)
    requests, tile_of = route(me, tile_owner[:, 0], tile_slot, half)
    sides = [list(range(half)), list(range(half, devices))]
    asked = lax.all_to_all(requests, "users", 0, 0, axis_index_groups=sides, tiled=True)
    found = collect(me, asked, item_factors, mirror)
    blocks = [found[0]] + [swap(found[mask], mask, devices) for mask in range(1, half)]
    pieces, high, low = tile_sums(
        tile_of, tile_cblock, user_counts, me, blocks, tile_weights, tile_context,
        context_factors, user_basis, devices,
    )
    pieces = spread_pieces(reduce_pieces(pieces, devices), devices)
    return finish(me, high, low, pieces, devices)


def solution(mesh):
    return jax.shard_map(
        body,
        mesh=mesh,
        in_specs=(
            P("users", None), P("users"), P("users"), P("users", None), P("users", None, None),
            P("users", None, None), P(), P("users", None), P("users"),
        ),
        out_specs=(P("users", None), P()),
        check_vma=False,
    )
```

time: 110 us -> 117 us (1.064)
  starting transfers between devices: 25.6 us -> 36.1 us
  waiting for transfers between devices: 25.6 us -> 19.7 us
  Pallas kernels: 36.3 us -> 41.5 us
  other arithmetic: 5.19 us -> 0.12 us
  local copies, waits for them, and re-layouts: 4.63 us -> 7.91 us
    ppermute x23 -> x36, starting transfers between devices: 21.9 us -> 36.1 us  [swap(): return lax.ppermute(value, 'users', [(i, i ^ mask) for i in range(devices)])]
    pallas_call x3 -> x5, Pallas kernels: 25.2 us -> 32.4 us  [the longest x4 31.7 us: tile_sums(): pl.pallas_call(functools.partial(tiles_kernel, group, last, piece_places(...]
    all_to_all x1 -> x0, waiting for transfers between devices: 6.44 us -> none  [body(): lax.all_to_all(found, 'users', 0, 0, axis_index_groups=sides, tiled=True)]
    add x8 -> x5, other arithmetic: 5.17 us -> 0.1 us  [the longest x3 0.05 us: reduce_pieces(): pieces[0, plane] + got[plane]]
    unnamed x8 -> x20, local copies, waits for them, and re-layouts: 2.89 us -> 7.91 us
    all_to_all x1 -> x0, starting transfers between devices: 3.65 us -> none  [body(): lax.all_to_all(found, 'users', 0, 0, axis_index_groups=sides, tiled=True)]
    pallas_call x1, Pallas kernels: 8.58 us -> 6.48 us  [finish(): pl.pallas_call(functools.partial(finish_kernel, users * devices, piece_pl...]
    transpose x2 -> x0, local copies, waits for them, and re-layouts: 1.73 us -> none  [body(): context_factors.astype(jnp.float32).reshape(rank_c, -1, CB)]
  transfers between devices with their start and end apart: 24 -> 36, of which waited for: 14 -> 15; matrix products, arithmetic and copies ran while one was open for 6% -> 0% of each run, Pallas kernels for 9% -> 21%
where the time goes in v3:
time: 117 us
  Pallas kernels  41.5 us (35%)
  starting transfers between devices  36.1 us (31%)
  waiting for transfers between devices  19.7 us (17%)
  blocking collectives  10.2 us (9%)
  local copies, waits for them, and re-layouts  7.91 us (7%)
  between operations  1.46 us (1%)
    ppermute x36, starting transfers between devices, swap(): return lax.ppermute(value, 'users', [(i, i ^ mask) for i in range(devices)])  36.1 us
    pallas_call x4, Pallas kernels, tile_sums(): pl.pallas_call(functools.partial(tiles_kernel, group, last, piece_places(...  31.7 us
    ppermute x36, waiting for transfers between devices, swap(): return lax.ppermute(value, 'users', [(i, i ^ mask) for i in range(devices)])  19.7 us
    all_to_all x1, blocking collectives, body(): lax.all_to_all(requests, 'users', 0, 0, axis_index_groups=sides, tiled=True)  10.2 us
    unnamed x20, local copies, waits for them, and re-layouts  7.91 us
    pallas_call x1, Pallas kernels, finish(): pl.pallas_call(functools.partial(finish_kernel, users * devices, piece_pl...  6.48 us
    pallas_call x1, Pallas kernels, route(): pl.pallas_call(functools.partial(route_kernel, half), out_shape=(jax.Shap...  2.6 us
  transfers between devices with their start and end apart: 36, of which 15 were waited for; matrix products, arithmetic and copies ran while one was open for 0% of the time, Pallas kernels for 21%

profile of v3, /device:TPU:0, one launch (start us, length us, event | category | flops | bytes accessed | tf_op | source)
XLA Modules:
  0.0 117.1 jit_solution(17343708240499462529)
XLA Ops:
  0.6 4.1 %collective-permute-start = (bf16[16,64,128]{2,1,0:T(8,128)(2,1)}, bf16[16,64,128]{2,1,0:T(8,128)(2,1)S(1)}, u32[]{:S(2)}, u32[]{:S(2)}) collective-permute-start(bf16[16,64,128]{2,1,0:T(8,128)(2,1)} %own_ref.1), channel_id=1, source_target_pairs={{0,16},{1,17},{2,18},{3,19},{4,20},{5,21},{6,22},{7,23},{8,24},{9,... | collective-permute-start | bytes 786440 | tf_op jit(solution)/shard_map/ppermute | solution.py:369
  6.1 2.6 %route.1 = (s32[16,1,128]{2,1,0:T(1,128)S(1)}, s32[64]{0:T(128)S(1)}) custom-call(s32[1]{0:T(128)} %bitcast.me_ref.refs_3_, s32[64]{0:T(128)S(1)} %bitcast.2, s32[64]{0:T(128)S(1)} %copy-done.9), custom_call_target="tpu_custom_call" | custom-call | tf_op jit(solution)/shard_map/route/pallas_call | solution.py:69
  8.7 10.2 %all_to_all.5.asked_ref = s32[16,1,128]{2,1,0:T(1,128)S(1)} all-to-all(s32[16,1,128]{2,1,0:T(1,128)S(1)} %get-tuple-element.31), channel_id=1, replica_groups={{0,1,2,3,4,5,6,7,8,9,10,11,12,13,14,15},{16,17,18,19,20,21,22,23,24,25,..., dimensions={0} | all-to-all | bytes 16384 | tf_op jit(solution)/shard_map/all_to_all | solution.py:412
  23.0 1.5 %collective-permute-start.14 = (bf16[4,64,128]{2,1,0:T(8,128)(2,1)S(1)}, bf16[4,64,128]{2,1,0:T(8,128)(2,1)S(1)}, u32[]{:S(2)}, u32[]{:S(2)}) collective-permute-start(bf16[4,64,128]{2,1,0:T(8,128)(2,1)S(1)} %get-tuple-element.46), channel_id=1, source_target_pairs={{0,2},{1,3},{2,0},{3,1},{4,6},{5,7},{6,4},{7,5},{8,10},{9,11},{10,... | collective-permute-start | bytes 196616 | tf_op jit(solution)/shard_map/ppermute | solution.py:369
  24.5 1.2 collective-permute-done.5.refs_4_
  26.1 1.6 %collective-permute-done.7.refs_6_ = bf16[4,64,128]{2,1,0:T(8,128)(2,1)S(1)} collective-permute-done((bf16[4,64,128]{2,1,0:T(8,128)(2,1)S(1)}, bf16[4,64,128]{2,1,0:T(8,128)(2,1)S(1)}, u32[]{:S(2)}, u32[]{:S(2)}) %collective-permute-start.7) | collective-permute-done | bytes 65568 | tf_op jit(solution)/shard_map/ppermute | solution.py:369
  29.2 1.5 %collective-permute-start.12 = (bf16[4,64,128]{2,1,0:T(8,128)(2,1)S(1)}, bf16[4,64,128]{2,1,0:T(8,128)(2,1)S(1)}, u32[]{:S(2)}, u32[]{:S(2)}) collective-permute-start(bf16[4,64,128]{2,1,0:T(8,128)(2,1)S(1)} %get-tuple-element.43), channel_id=1, source_target_pairs={{0,7},{1,6},{2,5},{3,4},{4,3},{5,2},{6,1},{7,0},{8,15},{9,14},{10,... | collective-permute-start | bytes 196616 | tf_op jit(solution)/shard_map/ppermute | solution.py:369
  31.4 1.2 collective-permute-start.8
  32.6 3.4 %copy-done = bf16[64,128,512]{2,1,0:T(8,128)(2,1)S(1)} copy-done((bf16[64,128,512]{2,1,0:T(8,128)(2,1)S(1)}, bf16[64,128,512]{2,1,0:T(8,128)(2,1)}, u32[]{:S(2)}) %copy-start) | copy-done | bytes 8388632
  38.2 7.4 %tile_sums.4.refs_11_ = f32[8,64,512]{2,1,0:T(8,128)S(1)} custom-call(s32[64]{0:T(128)S(1)} %get-tuple-element.30.refs_0_, s32[64]{0:T(128)S(1)} %copy-done.6, s32[1]{0:T(128)S(6)} %copy.15.refs_2_, s32[1]{0:T(128)} %bitcast.me_ref.refs_3_, bf16[4,64,128]{2,1,0:T(8,128)(2,1)S(1)} %get-tuple-element.44.refs_4_, ...), custom_call_target="tpu_custom_call" | custom-call | flops 500000000 | bytes 4000000 | tf_op jit(solution)/shard_map/tile_sums/pallas_call | solution.py:253
  45.6 1.5 %collective-permute-start.1 = (bf16[4,64,128]{2,1,0:T(8,128)(2,1)S(1)}, bf16[4,64,128]{2,1,0:T(8,128)(2,1)S(1)}, u32[]{:S(2)}, u32[]{:S(2)}) collective-permute-start(bf16[4,64,128]{2,1,0:T(8,128)(2,1)S(1)} %get-tuple-element.32), channel_id=1, source_target_pairs={{0,12},{1,13},{2,14},{3,15},{4,8},{5,9},{6,10},{7,11},{8,4},{9,5},... | collective-permute-start | bytes 196616 | tf_op jit(solution)/shard_map/ppermute | solution.py:369
  48.2 2.6 %collective-permute-start.3 = (bf16[4,64,128]{2,1,0:T(8,128)(2,1)S(1)}, bf16[4,64,128]{2,1,0:T(8,128)(2,1)S(1)}, u32[]{:S(2)}, u32[]{:S(2)}) collective-permute-start(bf16[4,64,128]{2,1,0:T(8,128)(2,1)S(1)} %get-tuple-element.34), channel_id=1, source_target_pairs={{0,14},{1,15},{2,12},{3,13},{4,10},{5,11},{6,8},{7,9},{8,6},{9,7},... | collective-permute-start | bytes 196616 | tf_op jit(solution)/shard_map/ppermute | solution.py:369
  50.7 1.2 collective-permute-start.4
  51.9 7.5 %tile_sums.5.refs_11_ = f32[8,64,512]{2,1,0:T(8,128)S(1)} custom-call(s32[64]{0:T(128)S(1)} %get-tuple-element.30.refs_0_, s32[64]{0:T(128)S(1)} %copy-done.7, s32[1]{0:T(128)S(6)} %copy.15.refs_2_, s32[1]{0:T(128)} %bitcast.me_ref.refs_3_, bf16[4,64,128]{2,1,0:T(8,128)(2,1)S(1)} %collective-permute-done.9.refs_4_, ...), custom_call_target="tpu_custom_call", output_to_operand_aliasing={{}: (11, {})} | custom-call | flops 500000000 | bytes 4000000 | tf_op jit(solution)/shard_map/tile_sums/pallas_call | solution.py:253
  59.4 7.5 %tile_sums.6.refs_11_ = f32[8,64,512]{2,1,0:T(8,128)S(1)} custom-call(s32[64]{0:T(128)S(1)} %get-tuple-element.30.refs_0_, s32[64]{0:T(128)S(1)} %copy-done.7, s32[1]{0:T(128)S(6)} %copy.15.refs_2_, s32[1]{0:T(128)} %bitcast.me_ref.refs_3_, bf16[4,64,128]{2,1,0:T(8,128)(2,1)S(1)} %collective-permute-done.5.refs_4_, ...), custom_call_target="tpu_custom_call", output_to_operand_aliasing={{}: (11, {})} | custom-call | flops 500000000 | bytes 4000000 | tf_op jit(solution)/shard_map/tile_sums/pallas_call | solution.py:253
  66.9 9.3 %tile_sums.7 = (f32[4,56,128]{2,1,0:T(8,128)S(1)}, f32[4,56,128]{2,1,0:T(8,128)S(1)}, f32[4,56,128]{2,1,0:T(8,128)S(1)}, f32[4,56,128]{2,1,0:T(8,128)S(1)}, f32[...) custom-call(s32[64]{0:T(128)S(1)} %get-tuple-element.30.refs_0_, ...), custom_call_target="tpu_custom_call" | custom-call | flops 500000000 | bytes 4000000 | tf_op jit(solution)/shard_map/tile_sums/pallas_call | solution.py:253
  77.7 1.6 %collective-permute-start.18 = (f32[4,56,128]{2,1,0:T(8,128)S(1)}, f32[4,56,128]{2,1,0:T(8,128)S(1)}, u32[]{:S(2)}, u32[]{:S(2)}) collective-permute-start(f32[4,56,128]{2,1,0:T(8,128)S(1)} %add.67), channel_id=1, source_target_pairs={{0,6},{1,7},{2,4},{3,5},{4,2},{5,3},{6,0},{7,1},{8,14},{9,15},{10,... | collective-permute-start | bytes 344072 | tf_op jit(solution)/shard_map/ppermute | solution.py:369
  79.3 1.5 %collective-permute-start.20 = (f32[4,56,128]{2,1,0:T(8,128)S(1)}, f32[4,56,128]{2,1,0:T(8,128)S(1)}, u32[]{:S(2)}, u32[]{:S(2)}) collective-permute-start(f32[4,56,128]{2,1,0:T(8,128)S(1)} %add.69), channel_id=1, source_target_pairs={{0,2},{1,3},{2,0},{3,1},{4,6},{5,7},{6,4},{7,5},{8,10},{9,11},{10,... | collective-permute-start | bytes 344072 | tf_op jit(solution)/shard_map/ppermute | solution.py:369
  81.4 3.2 %collective-permute-done.18 = f32[4,56,128]{2,1,0:T(8,128)S(1)} collective-permute-done((f32[4,56,128]{2,1,0:T(8,128)S(1)}, f32[4,56,128]{2,1,0:T(8,128)S(1)}, u32[]{:S(2)}, u32[]{:S(2)}) %collective-permute-start.18) | collective-permute-done | bytes 114720 | tf_op jit(solution)/shard_map/ppermute | solution.py:369
  84.6 1.7 %collective-permute-done.20 = f32[4,56,128]{2,1,0:T(8,128)S(1)} collective-permute-done((f32[4,56,128]{2,1,0:T(8,128)S(1)}, f32[4,56,128]{2,1,0:T(8,128)S(1)}, u32[]{:S(2)}, u32[]{:S(2)}) %collective-permute-start.20) | collective-permute-done | bytes 114720 | tf_op jit(solution)/shard_map/ppermute | solution.py:369
  86.4 3.0 %collective-permute-start.23 = (f32[1,56,128]{2,1,0:T(8,128)S(1)}, f32[1,56,128]{2,1,0:T(8,128)S(1)}, u32[]{:S(2)}, u32[]{:S(2)}) collective-permute-start(f32[1,56,128]{2,1,0:T(8,128)S(1)} %get-tuple-element.58), channel_id=1, source_target_pairs={{0,24},{1,25},{2,26},{3,27},{4,28},{5,29},{6,30},{7,31},{8,16},{9,... | collective-permute-start | bytes 86024 | tf_op jit(solution)/shard_map/ppermute | solution.py:369
  90.9 1.4 %collective-permute-done.23 = f32[1,56,128]{2,1,0:T(8,128)S(1)} collective-permute-done((f32[1,56,128]{2,1,0:T(8,128)S(1)}, f32[1,56,128]{2,1,0:T(8,128)S(1)}, u32[]{:S(2)}, u32[]{:S(2)}) %collective-permute-start.23) | collective-permute-done | bytes 28704 | tf_op jit(solution)/shard_map/ppermute | solution.py:369
  93.4 1.3 %collective-permute-done.24 = f32[1,56,128]{2,1,0:T(8,128)S(1)} collective-permute-done((f32[1,56,128]{2,1,0:T(8,128)S(1)}, f32[1,56,128]{2,1,0:T(8,128)S(1)}, u32[]{:S(2)}, u32[]{:S(2)}) %collective-permute-start.24) | collective-permute-done | bytes 28704 | tf_op jit(solution)/shard_map/ppermute | solution.py:369
  94.7 1.3 %collective-permute-start.28 = (f32[1,56,128]{2,1,0:T(8,128)S(1)}, f32[1,56,128]{2,1,0:T(8,128)S(1)}, u32[]{:S(2)}, u32[]{:S(2)}) collective-permute-start(f32[1,56,128]{2,1,0:T(8,128)S(1)} %fusion.2), channel_id=1, source_target_pairs={{0,24},{1,25},{2,26},{3,27},{4,28},{5,29},{6,30},{7,31},{8,16},{9,... | collective-permute-start | bytes 86024 | tf_op jit(solution)/shard_map/ppermute | solution.py:369
  95.9 1.8 %collective-permute-start.27 = (f32[1,56,128]{2,1,0:T(8,128)S(1)}, f32[1,56,128]{2,1,0:T(8,128)S(1)}, u32[]{:S(2)}, u32[]{:S(2)}) collective-permute-start(f32[1,56,128]{2,1,0:T(8,128)S(1)} %fusion.2), channel_id=1, source_target_pairs={{0,16},{1,17},{2,18},{3,19},{4,20},{5,21},{6,22},{7,23},{8,24},{9,... | collective-permute-start | bytes 86024 | tf_op jit(solution)/shard_map/ppermute | solution.py:369
  97.7 1.4 %collective-permute-start.26 = (f32[1,56,128]{2,1,0:T(8,128)S(1)}, f32[1,56,128]{2,1,0:T(8,128)S(1)}, u32[]{:S(2)}, u32[]{:S(2)}) collective-permute-start(f32[1,56,128]{2,1,0:T(8,128)S(1)} %fusion.2), channel_id=1, source_target_pairs={{0,8},{1,9},{2,10},{3,11},{4,12},{5,13},{6,14},{7,15},{8,0},{9,1},... | collective-permute-start | bytes 86024 | tf_op jit(solution)/shard_map/ppermute | solution.py:369
  99.1 1.3 %collective-permute-done.28 = f32[1,56,128]{2,1,0:T(8,128)S(1)} collective-permute-done((f32[1,56,128]{2,1,0:T(8,128)S(1)}, f32[1,56,128]{2,1,0:T(8,128)S(1)}, u32[]{:S(2)}, u32[]{:S(2)}) %collective-permute-start.28) | collective-permute-done | bytes 28704 | tf_op jit(solution)/shard_map/ppermute | solution.py:369
  103.6 1.6 %collective-permute-start.29 = (f32[4,56,128]{2,1,0:T(8,128)S(1)}, f32[4,56,128]{2,1,0:T(8,128)S(1)}, u32[]{:S(2)}, u32[]{:S(2)}) collective-permute-start(f32[4,56,128]{2,1,0:T(8,128)S(1)} %pad_maximum_fusion.rest_7_), channel_id=1, source_target_pairs={{0,6},{1,7},{2,4},{3,5},{4,2},{5,3},{6,0},{7,1},{8,14},{9,15},{10,... | collective-permute-start | bytes 344072 | tf_op jit(solution)/shard_map/ppermute | solution.py:369
  105.2 1.3 %collective-permute-done.33.rest_6_ = f32[4,56,128]{2,1,0:T(8,128)S(1)} collective-permute-done((f32[4,56,128]{2,1,0:T(8,128)S(1)}, f32[4,56,128]{2,1,0:T(8,128)S(1)}, u32[]{:S(2)}, u32[]{:S(2)}) %collective-permute-start.33) | collective-permute-done | bytes 114720 | tf_op jit(solution)/shard_map/ppermute | solution.py:369
  107.4 1.9 %collective-permute-done.29.rest_4_ = f32[4,56,128]{2,1,0:T(8,128)S(1)} collective-permute-done((f32[4,56,128]{2,1,0:T(8,128)S(1)}, f32[4,56,128]{2,1,0:T(8,128)S(1)}, u32[]{:S(2)}, u32[]{:S(2)}) %collective-permute-start.29) | collective-permute-done | bytes 114720 | tf_op jit(solution)/shard_map/ppermute | solution.py:369
  109.3 1.3 %collective-permute-done.30.rest_0_ = f32[4,56,128]{2,1,0:T(8,128)S(1)} collective-permute-done((f32[4,56,128]{2,1,0:T(8,128)S(1)}, f32[4,56,128]{2,1,0:T(8,128)S(1)}, u32[]{:S(2)}, u32[]{:S(2)}) %collective-permute-start.30) | collective-permute-done | bytes 114720 | tf_op jit(solution)/shard_map/ppermute | solution.py:369
  110.6 6.5 %finish.1 = (f32[512,128]{1,0:T(8,128)}, f32[128,512]{1,0:T(8,128)}) custom-call(s32[1]{0:T(128)} %bitcast.me_ref.refs_3_, bf16[512,512]{1,0:T(8,128)(2,1)S(1)} %get-tuple-element.48.high_ref, bf16[512,512]{1,0:T(8,128)(2,1)S(1)} %get-tuple-element.49.low_ref, f32[4,56,128]{2,1,0:T(8,128)S(1)} %collective-permute-done.30.rest_0_, ...), custom_call_target="tpu_custom_call" | custom-call | tf_op jit(solution)/shard_map/finish/pallas_call | solution.py:351
  (74 shorter events, 19.6 us)
Async XLA Ops:
  0.6 18.2 %collective-permute-start = (bf16[16,64,128]{2,1,0:T(8,128)(2,1)}, bf16[16,64,128]{2,1,0:T(8,128)(2,1)S(1)}, u32[]{:S(2)}, u32[]{:S(2)}) collective-permute-start(bf16[16,64,128]{2,1,0:T(8,128)(2,1)} %own_ref.1), channel_id=1, source_target_pairs={{0,16},{1,17},{2,18},{3,19},{4,20},{5,21},{6,22},{7,23},{8,24},{9,... | collective-permute-start | bytes 786440 | tf_op jit(solution)/shard_map/ppermute | solution.py:369
  20.6 5.0 %collective-permute-start.5 = (bf16[4,64,128]{2,1,0:T(8,128)(2,1)S(1)}, bf16[4,64,128]{2,1,0:T(8,128)(2,1)S(1)}, u32[]{:S(2)}, u32[]{:S(2)}) collective-permute-start(bf16[4,64,128]{2,1,0:T(8,128)(2,1)S(1)} %get-tuple-element.36), channel_id=1, source_target_pairs={{0,8},{1,9},{2,10},{3,11},{4,12},{5,13},{6,14},{7,15},{8,0},{9,1},... | collective-permute-start | bytes 196616 | tf_op jit(solution)/shard_map/ppermute | solution.py:369
  21.1 4.5 %collective-permute-start.6 = (bf16[4,64,128]{2,1,0:T(8,128)(2,1)S(1)}, bf16[4,64,128]{2,1,0:T(8,128)(2,1)S(1)}, u32[]{:S(2)}, u32[]{:S(2)}) collective-permute-start(bf16[4,64,128]{2,1,0:T(8,128)(2,1)S(1)} %get-tuple-element.37), channel_id=1, source_target_pairs={{0,9},{1,8},{2,11},{3,10},{4,13},{5,12},{6,15},{7,14},{8,1},{9,0},... | collective-permute-start | bytes 196616 | tf_op jit(solution)/shard_map/ppermute | solution.py:369
  21.8 5.9 %collective-permute-start.7 = (bf16[4,64,128]{2,1,0:T(8,128)(2,1)S(1)}, bf16[4,64,128]{2,1,0:T(8,128)(2,1)S(1)}, u32[]{:S(2)}, u32[]{:S(2)}) collective-permute-start(bf16[4,64,128]{2,1,0:T(8,128)(2,1)S(1)} %get-tuple-element.38), channel_id=1, source_target_pairs={{0,10},{1,11},{2,8},{3,9},{4,14},{5,15},{6,12},{7,13},{8,2},{9,3},... | collective-permute-start | bytes 196616 | tf_op jit(solution)/shard_map/ppermute | solution.py:369
  22.6 5.8 %collective-permute-start.13 = (bf16[4,64,128]{2,1,0:T(8,128)(2,1)S(1)}, bf16[4,64,128]{2,1,0:T(8,128)(2,1)S(1)}, u32[]{:S(2)}, u32[]{:S(2)}) collective-permute-start(bf16[4,64,128]{2,1,0:T(8,128)(2,1)S(1)} %get-tuple-element.45), channel_id=1, source_target_pairs={{0,1},{1,0},{2,3},{3,2},{4,5},{5,4},{6,7},{7,6},{8,9},{9,8},{10,11... | collective-permute-start | bytes 196616 | tf_op jit(solution)/shard_map/ppermute | solution.py:369
  23.0 6.2 %collective-permute-start.14 = (bf16[4,64,128]{2,1,0:T(8,128)(2,1)S(1)}, bf16[4,64,128]{2,1,0:T(8,128)(2,1)S(1)}, u32[]{:S(2)}, u32[]{:S(2)}) collective-permute-start(bf16[4,64,128]{2,1,0:T(8,128)(2,1)S(1)} %get-tuple-element.46), channel_id=1, source_target_pairs={{0,2},{1,3},{2,0},{3,1},{4,6},{5,7},{6,4},{7,5},{8,10},{9,11},{10,... | collective-permute-start | bytes 196616 | tf_op jit(solution)/shard_map/ppermute | solution.py:369
  25.6 5.8 %collective-permute-start.15 = (bf16[4,64,128]{2,1,0:T(8,128)(2,1)S(1)}, bf16[4,64,128]{2,1,0:T(8,128)(2,1)S(1)}, u32[]{:S(2)}, u32[]{:S(2)}) collective-permute-start(bf16[4,64,128]{2,1,0:T(8,128)(2,1)S(1)} %get-tuple-element.47), channel_id=1, source_target_pairs={{0,3},{1,2},{2,1},{3,0},{4,7},{5,6},{6,5},{7,4},{8,11},{9,10},{10,... | collective-permute-start | bytes 196616 | tf_op jit(solution)/shard_map/ppermute | solution.py:369
  25.6 20.0 %collective-permute-start.9 = (bf16[4,64,128]{2,1,0:T(8,128)(2,1)S(1)}, bf16[4,64,128]{2,1,0:T(8,128)(2,1)S(1)}, u32[]{:S(2)}, u32[]{:S(2)}) collective-permute-start(bf16[4,64,128]{2,1,0:T(8,128)(2,1)S(1)} %get-tuple-element.40), channel_id=1, source_target_pairs={{0,4},{1,5},{2,6},{3,7},{4,0},{5,1},{6,2},{7,3},{8,12},{9,13},{10,... | collective-permute-start | bytes 196616 | tf_op jit(solution)/shard_map/ppermute | solution.py:369
  27.7 19.4 %collective-permute-start.10 = (bf16[4,64,128]{2,1,0:T(8,128)(2,1)S(1)}, bf16[4,64,128]{2,1,0:T(8,128)(2,1)S(1)}, u32[]{:S(2)}, u32[]{:S(2)}) collective-permute-start(bf16[4,64,128]{2,1,0:T(8,128)(2,1)S(1)} %get-tuple-element.41), channel_id=1, source_target_pairs={{0,5},{1,4},{2,7},{3,6},{4,1},{5,0},{6,3},{7,2},{8,13},{9,12},{10,... | collective-permute-start | bytes 196616 | tf_op jit(solution)/shard_map/ppermute | solution.py:369
  28.4 19.7 %collective-permute-start.11 = (bf16[4,64,128]{2,1,0:T(8,128)(2,1)S(1)}, bf16[4,64,128]{2,1,0:T(8,128)(2,1)S(1)}, u32[]{:S(2)}, u32[]{:S(2)}) collective-permute-start(bf16[4,64,128]{2,1,0:T(8,128)(2,1)S(1)} %get-tuple-element.42), channel_id=1, source_target_pairs={{0,6},{1,7},{2,4},{3,5},{4,2},{5,3},{6,0},{7,1},{8,14},{9,15},{10,... | collective-permute-start | bytes 196616 | tf_op jit(solution)/shard_map/ppermute | solution.py:369
  29.2 21.5 %collective-permute-start.12 = (bf16[4,64,128]{2,1,0:T(8,128)(2,1)S(1)}, bf16[4,64,128]{2,1,0:T(8,128)(2,1)S(1)}, u32[]{:S(2)}, u32[]{:S(2)}) collective-permute-start(bf16[4,64,128]{2,1,0:T(8,128)(2,1)S(1)} %get-tuple-element.43), channel_id=1, source_target_pairs={{0,7},{1,6},{2,5},{3,4},{4,3},{5,2},{6,1},{7,0},{8,15},{9,14},{10,... | collective-permute-start | bytes 196616 | tf_op jit(solution)/shard_map/ppermute | solution.py:369
  31.4 27.9 %collective-permute-start.8 = (bf16[4,64,128]{2,1,0:T(8,128)(2,1)S(1)}, bf16[4,64,128]{2,1,0:T(8,128)(2,1)S(1)}, u32[]{:S(2)}, u32[]{:S(2)}) collective-permute-start(bf16[4,64,128]{2,1,0:T(8,128)(2,1)S(1)} %get-tuple-element.39), channel_id=1, source_target_pairs={{0,11},{1,10},{2,9},{3,8},{4,15},{5,14},{6,13},{7,12},{8,3},{9,2},... | collective-permute-start | bytes 196616 | tf_op jit(solution)/shard_map/ppermute | solution.py:369
  45.6 21.3 %collective-permute-start.1 = (bf16[4,64,128]{2,1,0:T(8,128)(2,1)S(1)}, bf16[4,64,128]{2,1,0:T(8,128)(2,1)S(1)}, u32[]{:S(2)}, u32[]{:S(2)}) collective-permute-start(bf16[4,64,128]{2,1,0:T(8,128)(2,1)S(1)} %get-tuple-element.32), channel_id=1, source_target_pairs={{0,12},{1,13},{2,14},{3,15},{4,8},{5,9},{6,10},{7,11},{8,4},{9,5},... | collective-permute-start | bytes 196616 | tf_op jit(solution)/shard_map/ppermute | solution.py:369
  47.2 19.7 %collective-permute-start.2 = (bf16[4,64,128]{2,1,0:T(8,128)(2,1)S(1)}, bf16[4,64,128]{2,1,0:T(8,128)(2,1)S(1)}, u32[]{:S(2)}, u32[]{:S(2)}) collective-permute-start(bf16[4,64,128]{2,1,0:T(8,128)(2,1)S(1)} %get-tuple-element.33), channel_id=1, source_target_pairs={{0,13},{1,12},{2,15},{3,14},{4,9},{5,8},{6,11},{7,10},{8,5},{9,4},... | collective-permute-start | bytes 196616 | tf_op jit(solution)/shard_map/ppermute | solution.py:369
  48.2 18.7 %collective-permute-start.3 = (bf16[4,64,128]{2,1,0:T(8,128)(2,1)S(1)}, bf16[4,64,128]{2,1,0:T(8,128)(2,1)S(1)}, u32[]{:S(2)}, u32[]{:S(2)}) collective-permute-start(bf16[4,64,128]{2,1,0:T(8,128)(2,1)S(1)} %get-tuple-element.34), channel_id=1, source_target_pairs={{0,14},{1,15},{2,12},{3,13},{4,10},{5,11},{6,8},{7,9},{8,6},{9,7},... | collective-permute-start | bytes 196616 | tf_op jit(solution)/shard_map/ppermute | solution.py:369
  50.7 16.2 %collective-permute-start.4 = (bf16[4,64,128]{2,1,0:T(8,128)(2,1)S(1)}, bf16[4,64,128]{2,1,0:T(8,128)(2,1)S(1)}, u32[]{:S(2)}, u32[]{:S(2)}) collective-permute-start(bf16[4,64,128]{2,1,0:T(8,128)(2,1)S(1)} %get-tuple-element.35), channel_id=1, source_target_pairs={{0,15},{1,14},{2,13},{3,12},{4,11},{5,10},{6,9},{7,8},{8,7},{9,6},... | collective-permute-start | bytes 196616 | tf_op jit(solution)/shard_map/ppermute | solution.py:369
  76.8 3.9 %collective-permute-start.21 = (f32[4,56,128]{2,1,0:T(8,128)S(1)}, f32[4,56,128]{2,1,0:T(8,128)S(1)}, u32[]{:S(2)}, u32[]{:S(2)}) collective-permute-start(f32[4,56,128]{2,1,0:T(8,128)S(1)} %get-tuple-element.57), channel_id=1, source_target_pairs={{0,1},{1,0},{2,3},{3,2},{4,5},{5,4},{6,7},{7,6},{8,9},{9,8},{10,11... | collective-permute-start | bytes 344072 | tf_op jit(solution)/shard_map/ppermute | solution.py:369
  77.1 4.3 %collective-permute-start.16 = (f32[4,56,128]{2,1,0:T(8,128)S(1)}, f32[4,56,128]{2,1,0:T(8,128)S(1)}, u32[]{:S(2)}, u32[]{:S(2)}) collective-permute-start(f32[4,56,128]{2,1,0:T(8,128)S(1)} %get-tuple-element.51), channel_id=1, source_target_pairs={{0,1},{1,0},{2,3},{3,2},{4,5},{5,4},{6,7},{7,6},{8,9},{9,8},{10,11... | collective-permute-start | bytes 344072 | tf_op jit(solution)/shard_map/ppermute | solution.py:369
  77.7 6.9 %collective-permute-start.18 = (f32[4,56,128]{2,1,0:T(8,128)S(1)}, f32[4,56,128]{2,1,0:T(8,128)S(1)}, u32[]{:S(2)}, u32[]{:S(2)}) collective-permute-start(f32[4,56,128]{2,1,0:T(8,128)S(1)} %add.67), channel_id=1, source_target_pairs={{0,6},{1,7},{2,4},{3,5},{4,2},{5,3},{6,0},{7,1},{8,14},{9,15},{10,... | collective-permute-start | bytes 344072 | tf_op jit(solution)/shard_map/ppermute | solution.py:369
  79.3 7.1 %collective-permute-start.20 = (f32[4,56,128]{2,1,0:T(8,128)S(1)}, f32[4,56,128]{2,1,0:T(8,128)S(1)}, u32[]{:S(2)}, u32[]{:S(2)}) collective-permute-start(f32[4,56,128]{2,1,0:T(8,128)S(1)} %add.69), channel_id=1, source_target_pairs={{0,2},{1,3},{2,0},{3,1},{4,6},{5,7},{6,4},{7,5},{8,10},{9,11},{10,... | collective-permute-start | bytes 344072 | tf_op jit(solution)/shard_map/ppermute | solution.py:369
  80.8 5.6 %collective-permute-start.22 = (f32[4,56,128]{2,1,0:T(8,128)S(1)}, f32[4,56,128]{2,1,0:T(8,128)S(1)}, u32[]{:S(2)}, u32[]{:S(2)}) collective-permute-start(f32[4,56,128]{2,1,0:T(8,128)S(1)} %add.71), channel_id=1, source_target_pairs={{0,4},{1,5},{2,6},{3,7},{4,0},{5,1},{6,2},{7,3},{8,12},{9,13},{10,... | collective-permute-start | bytes 344072 | tf_op jit(solution)/shard_map/ppermute | solution.py:369
  86.4 5.8 %collective-permute-start.23 = (f32[1,56,128]{2,1,0:T(8,128)S(1)}, f32[1,56,128]{2,1,0:T(8,128)S(1)}, u32[]{:S(2)}, u32[]{:S(2)}) collective-permute-start(f32[1,56,128]{2,1,0:T(8,128)S(1)} %get-tuple-element.58), channel_id=1, source_target_pairs={{0,24},{1,25},{2,26},{3,27},{4,28},{5,29},{6,30},{7,31},{8,16},{9,... | collective-permute-start | bytes 86024 | tf_op jit(solution)/shard_map/ppermute | solution.py:369
  89.4 4.0 %collective-permute-start.25 = (f32[1,56,128]{2,1,0:T(8,128)S(1)}, f32[1,56,128]{2,1,0:T(8,128)S(1)}, u32[]{:S(2)}, u32[]{:S(2)}) collective-permute-start(f32[1,56,128]{2,1,0:T(8,128)S(1)} %get-tuple-element.59), channel_id=1, source_target_pairs={{0,8},{1,9},{2,10},{3,11},{4,12},{5,13},{6,14},{7,15},{8,0},{9,1},... | collective-permute-start | bytes 86024 | tf_op jit(solution)/shard_map/ppermute | solution.py:369
  89.9 4.8 %collective-permute-start.24 = (f32[1,56,128]{2,1,0:T(8,128)S(1)}, f32[1,56,128]{2,1,0:T(8,128)S(1)}, u32[]{:S(2)}, u32[]{:S(2)}) collective-permute-start(f32[1,56,128]{2,1,0:T(8,128)S(1)} %get-tuple-element.60), channel_id=1, source_target_pairs={{0,16},{1,17},{2,18},{3,19},{4,20},{5,21},{6,22},{7,23},{8,24},{9,... | collective-permute-start | bytes 86024 | tf_op jit(solution)/shard_map/ppermute | solution.py:369
  94.7 5.7 %collective-permute-start.28 = (f32[1,56,128]{2,1,0:T(8,128)S(1)}, f32[1,56,128]{2,1,0:T(8,128)S(1)}, u32[]{:S(2)}, u32[]{:S(2)}) collective-permute-start(f32[1,56,128]{2,1,0:T(8,128)S(1)} %fusion.2), channel_id=1, source_target_pairs={{0,24},{1,25},{2,26},{3,27},{4,28},{5,29},{6,30},{7,31},{8,16},{9,... | collective-permute-start | bytes 86024 | tf_op jit(solution)/shard_map/ppermute | solution.py:369
  95.9 5.1 %collective-permute-start.27 = (f32[1,56,128]{2,1,0:T(8,128)S(1)}, f32[1,56,128]{2,1,0:T(8,128)S(1)}, u32[]{:S(2)}, u32[]{:S(2)}) collective-permute-start(f32[1,56,128]{2,1,0:T(8,128)S(1)} %fusion.2), channel_id=1, source_target_pairs={{0,16},{1,17},{2,18},{3,19},{4,20},{5,21},{6,22},{7,23},{8,24},{9,... | collective-permute-start | bytes 86024 | tf_op jit(solution)/shard_map/ppermute | solution.py:369
  97.7 3.9 %collective-permute-start.26 = (f32[1,56,128]{2,1,0:T(8,128)S(1)}, f32[1,56,128]{2,1,0:T(8,128)S(1)}, u32[]{:S(2)}, u32[]{:S(2)}) collective-permute-start(f32[1,56,128]{2,1,0:T(8,128)S(1)} %fusion.2), channel_id=1, source_target_pairs={{0,8},{1,9},{2,10},{3,11},{4,12},{5,13},{6,14},{7,15},{8,0},{9,1},... | collective-permute-start | bytes 86024 | tf_op jit(solution)/shard_map/ppermute | solution.py:369
  101.6 4.9 %collective-permute-start.33 = (f32[4,56,128]{2,1,0:T(8,128)S(1)}, f32[4,56,128]{2,1,0:T(8,128)S(1)}, u32[]{:S(2)}, u32[]{:S(2)}) collective-permute-start(f32[4,56,128]{2,1,0:T(8,128)S(1)} %pad_maximum_fusion.rest_7_), channel_id=1, source_target_pairs={{0,4},{1,5},{2,6},{3,7},{4,0},{5,1},{6,2},{7,3},{8,12},{9,13},{10,... | collective-permute-start | bytes 344072 | tf_op jit(solution)/shard_map/ppermute | solution.py:369
  102.6 4.8 %collective-permute-start.31 = (f32[4,56,128]{2,1,0:T(8,128)S(1)}, f32[4,56,128]{2,1,0:T(8,128)S(1)}, u32[]{:S(2)}, u32[]{:S(2)}) collective-permute-start(f32[4,56,128]{2,1,0:T(8,128)S(1)} %pad_maximum_fusion.rest_7_), channel_id=1, source_target_pairs={{0,2},{1,3},{2,0},{3,1},{4,6},{5,7},{6,4},{7,5},{8,10},{9,11},{10,... | collective-permute-start | bytes 344072 | tf_op jit(solution)/shard_map/ppermute | solution.py:369
  103.6 5.7 %collective-permute-start.29 = (f32[4,56,128]{2,1,0:T(8,128)S(1)}, f32[4,56,128]{2,1,0:T(8,128)S(1)}, u32[]{:S(2)}, u32[]{:S(2)}) collective-permute-start(f32[4,56,128]{2,1,0:T(8,128)S(1)} %pad_maximum_fusion.rest_7_), channel_id=1, source_target_pairs={{0,6},{1,7},{2,4},{3,5},{4,2},{5,3},{6,0},{7,1},{8,14},{9,15},{10,... | collective-permute-start | bytes 344072 | tf_op jit(solution)/shard_map/ppermute | solution.py:369
  105.2 4.1 %collective-permute-start.35 = (f32[4,56,128]{2,1,0:T(8,128)S(1)}, f32[4,56,128]{2,1,0:T(8,128)S(1)}, u32[]{:S(2)}, u32[]{:S(2)}) collective-permute-start(f32[4,56,128]{2,1,0:T(8,128)S(1)} %pad_maximum_fusion.rest_7_), channel_id=1, source_target_pairs={{0,1},{1,0},{2,3},{3,2},{4,5},{5,4},{6,7},{7,6},{8,9},{9,8},{10,11... | collective-permute-start | bytes 344072 | tf_op jit(solution)/shard_map/ppermute | solution.py:369
  106.5 2.8 %collective-permute-start.34 = (f32[4,56,128]{2,1,0:T(8,128)S(1)}, f32[4,56,128]{2,1,0:T(8,128)S(1)}, u32[]{:S(2)}, u32[]{:S(2)}) collective-permute-start(f32[4,56,128]{2,1,0:T(8,128)S(1)} %collective-permute-done.33.rest_6_), channel_id=1, source_target_pairs={{0,1},{1,0},{2,3},{3,2},{4,5},{5,4},{6,7},{7,6},{8,9},{9,8},{10,11... | collective-permute-start | bytes 344072 | tf_op jit(solution)/shard_map/ppermute | solution.py:369
  (14 other events, 96.3 us)

commit v4 on v3

--- a/solution.py
+++ b/solution.py
@@ -13,12 +13,16 @@
 HIGH = lax.Precision.HIGHEST
 LANES = 128
 ROWS = 8
-MASKS = 4
 BATCH = 8
 MIB = 2**20
 
 SMEM = pl.BlockSpec(memory_space=pltpu.SMEM)
 VMEM = pl.BlockSpec(memory_space=pltpu.VMEM)
+ANY = pl.BlockSpec(memory_space=pl.ANY)
+
+
+def in_hbm(value):
+    return pltpu.with_memory_space_constraint(value, pltpu.HBM)
 
 
 def limit(mib):
@@ -38,18 +42,17 @@
     return high, (value - high.astype(jnp.float32)).astype(jnp.bfloat16)
 
 
-def route_kernel(half, me_ref, owner_ref, slot_ref, request_ref, tile_ref, used_ref):
+def route_kernel(half, me_ref, owner_ref, slot_ref, own_ref, request_ref, where_ref, held_ref, used_ref, sem_ref):
+    copy = pltpu.make_async_copy(own_ref, held_ref, sem_ref)
+    copy.start()
     side = me_ref[0] // half
-    low_me = lax.rem(me_ref[0], half)
     lane = lax.broadcasted_iota(jnp.int32, (1, LANES), 1)
 
     def clear(place, _):
         used_ref[place] = 0
-        tile_ref[SLOTS * place] = -1
-        tile_ref[SLOTS * place + 1] = -1
-        return 0
-
-    lax.fori_loop(0, 2 * half, clear, 0)
+        return 0
+
+    lax.fori_loop(0, 2 * half, clear, 0, unroll=8)
     request_ref[...] = jnp.zeros_like(request_ref)
 
     def assign(tile, _):
@@ -59,46 +62,84 @@
         low = lax.rem(owner, half)
         place = jnp.where(owner // half == side, 0, SLOTS) + taken
         request_ref[low] = jnp.where(lane == place, slot_ref[tile], request_ref[low])
-        tile_ref[jnp.bitwise_xor(low, low_me) * PLACES + place] = tile
-        return 0
-
-    lax.fori_loop(0, owner_ref.shape[0], assign, 0)
-
-
-def route(me, owners, slots, half):
+        where_ref[tile] = low * PLACES + place
+        return 0
+
+    lax.fori_loop(0, owner_ref.shape[0], assign, 0, unroll=4)
+    copy.wait()
+
+
+def route(me, owners, slots, own, half):
     return pl.pallas_call(
         functools.partial(route_kernel, half),
         out_shape=(
             jax.ShapeDtypeStruct((half, 1, LANES), jnp.int32),
-            jax.ShapeDtypeStruct((half * PLACES,), jnp.int32),
+            jax.ShapeDtypeStruct(owners.shape, jnp.int32),
+            jax.ShapeDtypeStruct(own.shape, own.dtype),
         ),
-        in_specs=[SMEM, SMEM, SMEM],
-        out_specs=(VMEM, SMEM),
-        scratch_shapes=[pltpu.SMEM((2 * half,), jnp.int32)],
-        compiler_params=limit(2),
+        in_specs=[SMEM, SMEM, SMEM, ANY],
+        out_specs=(VMEM, SMEM, VMEM),
+        scratch_shapes=[pltpu.SMEM((2 * half,), jnp.int32), pltpu.SemaphoreType.DMA],
+        compiler_params=limit(4),
         name="route",
-    )(me, owners, slots)
-
-
-def collect_kernel(me_ref, asked_ref, own_ref, mirror_ref, *out_refs):
-    low_me = lax.rem(me_ref[0], len(out_refs))
-    for mask, out_ref in enumerate(out_refs):
-        peer = jnp.bitwise_xor(low_me, mask)
+    )(me, in_hbm(owners), in_hbm(slots), in_hbm(own))
+
+
+def collect_kernel(asked_ref, own_ref, mirror_ref, out_ref):
+    def one(peer, _):
         for place in range(PLACES):
             source = own_ref if place < SLOTS else mirror_ref
-            out_ref[place] = source[asked_ref[peer, 0, place]]
-
-
-def collect(me, asked, own, mirror):
-    half = asked.shape[0]
+            out_ref[peer * PLACES + place] = source[asked_ref[peer, 0, place]]
+        return 0
+
+    lax.fori_loop(0, asked_ref.shape[0], one, 0, unroll=4)
+
+
+def collect(asked, own, mirror):
     return pl.pallas_call(
         collect_kernel,
-        out_shape=(jax.ShapeDtypeStruct((PLACES,) + own.shape[1:], own.dtype),) * half,
-        in_specs=[SMEM, SMEM, VMEM, VMEM],
-        out_specs=(VMEM,) * half,
-        compiler_params=limit(8),
+        out_shape=jax.ShapeDtypeStruct((asked.shape[0] * PLACES,) + own.shape[1:], own.dtype),
+        in_specs=[SMEM, VMEM, VMEM],
+        out_specs=VMEM,
+        compiler_params=limit(4),
         name="collect",
-    )(me, asked, own, mirror)
+    )(asked, own, mirror)
+
+
+def stage_kernel(cblock_ref, table_ref, marks_ref, weights_ref, context_ref, held_ref, sem_ref):
+    copy = pltpu.make_async_copy(weights_ref, held_ref, sem_ref)
+    copy.start()
+    tiles, users = marks_ref.shape
+
+    def one(tile, _):
+        table = table_ref[cblock_ref[tile]]
+        marks = jnp.broadcast_to(marks_ref[pl.ds(tile, 1), :], (ROWS, users))
+        total = jnp.zeros((ROWS, users), jnp.float32)
+        for k in range(CB):
+            column = jnp.broadcast_to(table[:, k : k + 1], (ROWS, users))
+            total = jnp.where(marks == k, column, total)
+        context_ref[tile] = total
+        return 0
+
+    lax.fori_loop(0, tiles, one, 0, unroll=2)
+    copy.wait()
+
+
+def stage(cblock, table, marks, weights):
+    tiles, users = marks.shape
+    return pl.pallas_call(
+        stage_kernel,
+        out_shape=(
+            jax.ShapeDtypeStruct((tiles, ROWS, users), jnp.float32),
+            jax.ShapeDtypeStruct(weights.shape, weights.dtype),
+        ),
+        in_specs=[SMEM, VMEM, VMEM, ANY],
+        out_specs=(VMEM, VMEM),
+        scratch_shapes=[pltpu.SemaphoreType.DMA],
+        compiler_params=limit(4),
+        cost_estimate=pl.CostEstimate(flops=10**7, bytes_accessed=2 * 10**7, transcendentals=0),
+        name="stage",
+    )(in_hbm(cblock), table, marks, in_hbm(weights))
 
 
 def piece_places(devices):
@@ -118,72 +159,40 @@
     return -(-rows // (devices * ROWS)) * ROWS
 
 
-def tiles_kernel(group, last, places, *refs):
-    tile_ref, cblock_ref, count_ref, me_ref = refs[:4]
-    block_refs = refs[4 : 4 + MASKS]
-    weights_ref, marks_ref, factors_ref = refs[4 + MASKS : 7 + MASKS]
-    refs = refs[7 + MASKS :]
-    before_ref = basis_ref = None
-    if group:
-        before_ref, refs = refs[0], refs[1:]
-    if last:
-        basis_ref, refs = refs[0], refs[1:]
-        piece_refs, refs = refs[: len(PIECES)], refs[len(PIECES) :]
-        high_ref, low_ref, refs = refs[0], refs[1], refs[2:]
-        y_ref, pack_ref, refs = refs[0], refs[1], refs[2:]
-    else:
-        y_ref, refs = refs[0], refs[1:]
-    held_ref, sem_ref, product_ref, context_ref = refs
+def tiles_kernel(places, where_ref, count_ref, me_ref, blocks_ref, weights_ref, context_ref, basis_ref, *refs):
+    piece_refs, refs = refs[: len(PIECES)], refs[len(PIECES) :]
+    high_ref, low_ref, y_ref, pack_ref, product_ref = refs
     rank_c, rank_i, users = y_ref.shape
-    slots = MASKS * PLACES
-
-    tiles = [tile_ref[group * slots + slot] for slot in range(slots)]
-    copies = []
-    for slot in range(slots):
-        copy = pltpu.make_async_copy(
-            weights_ref.at[jnp.maximum(tiles[slot], 0)], held_ref.at[slot], sem_ref.at[slot]
-        )
-        copy.start()
-        copies.append(copy)
-
-    for first in range(0, slots, BATCH):
+    tiles = weights_ref.shape[0]
+    batches = tiles // BATCH
+    half = rank_i * users // LANES // BATCH
+
+    def multiply(tile, bank, place):
+        product = dot(blocks_ref[where_ref[tile]], weights_ref[tile])
+        product_ref[bank, place] = product.astype(jnp.bfloat16).astype(jnp.float32)
+
+    def first(place, _):
+        multiply(place, 0, place)
+        return 0
+
+    lax.fori_loop(0, BATCH, first, 0)
+    y_ref[...] = jnp.zeros_like(y_ref)
+
+    def step(index, _):
+        batch, part = index // BATCH, lax.rem(index, BATCH)
+        bank = lax.rem(batch, 2)
+        multiply(jnp.minimum(index + BATCH, tiles - 1), 1 - bank, part)
+        lanes = pl.ds(pl.multiple_of(part // (rank_i // half) * LANES, LANES), LANES)
+        rows = pl.ds(pl.multiple_of(lax.rem(part, rank_i // half) * half, ROWS), half)
+        total = y_ref[:, rows, lanes]
         for place in range(BATCH):
-            tile = jnp.maximum(tiles[first + place], 0)
-            used = tiles[first + place] >= 0
-            cblock = cblock_ref[tile]
-            per = LANES // CB
-            start = pl.multiple_of(cblock // per * LANES, LANES)
-            table = factors_ref[:, pl.ds(start, LANES)].astype(jnp.float32)
-            table = jnp.where(used, table, 0.0)
-            marks = marks_ref[pl.ds(tile, 1), :] + lax.rem(cblock, per) * CB
-            for lane in range(users // LANES):
-                index = jnp.broadcast_to(marks[:, lane * LANES : (lane + 1) * LANES], (rank_c, LANES))
-                context_ref[place, :, lane * LANES : (lane + 1) * LANES] = jnp.take_along_axis(
-                    table, index, axis=1, mode="promise_in_bounds"
-                )
-        for place in range(BATCH):
-            slot = first + place
-            copies[slot].wait()
-            product = dot(block_refs[slot // PLACES][slot % PLACES], held_ref[slot])
-            product_ref[place] = product.astype(jnp.bfloat16).astype(jnp.float32)
-        half = rank_i // 2
-        for lane in range(users // LANES):
-            lanes = slice(lane * LANES, (lane + 1) * LANES)
-            for part in range(2):
-                rows = slice(part * half, (part + 1) * half)
-                if first:
-                    total = y_ref[:, rows, lanes]
-                elif group:
-                    total = before_ref[:, rows, lanes]
-                else:
-                    total = jnp.zeros((rank_c, half, LANES), jnp.float32)
-                for place in range(BATCH):
-                    values = context_ref[place, :, lanes]
-                    total = total + values[:, None, :] * product_ref[place, rows, lanes][None]
-                y_ref[:, rows, lanes] = total
-
-    if not last:
-        return
+            values = context_ref[batch * BATCH + place, :, lanes]
+            total = total + values[:, None, :] * product_ref[bank, place, rows, lanes][None]
+        y_ref[:, rows, lanes] = total
+        return 0
+
+    lax.fori_loop(0, batches * BATCH, step, 0)
+
     living = lax.broadcasted_iota(jnp.int32, (rank_i, users), 1) < count_ref[0]
     for r in range(rank_c):
         high, low = split(jnp.where(living, y_ref[r], 0.0))
@@ -214,54 +223,29 @@
             ref[i] = pack_ref[pl.ds(start, chunk)]
 
 
-def tile_sums(tile_of, cblock, count, me, blocks, weights, marks, factors, user_basis, devices):
-    block_len, users = weights.shape[1:]
-    rank_i = blocks[0].shape[1]
-    rank_c = factors.shape[0]
+def tile_sums(where, count, me, blocks, weights, contexts, user_basis, devices):
+    users = weights.shape[2]
+    rank_i = blocks.shape[1]
+    rank_c = contexts.shape[1]
     ranks = rank_c * rank_i
-    slots = MASKS * PLACES
     chunk = pack_rows(ranks, devices)
-    calls = len(blocks) // MASKS
-    y_shape = (rank_c, rank_i, users)
-    y_type = jax.ShapeDtypeStruct(y_shape, jnp.float32)
-    y = None
-    for group in range(calls):
-        last = group == calls - 1
-        operands = [tile_of, cblock, count, me, *blocks[group * MASKS : (group + 1) * MASKS], weights, marks, factors]
-        in_specs = [SMEM] * 4 + [VMEM] * MASKS + [pl.BlockSpec(memory_space=pltpu.HBM), VMEM, VMEM]
-        aliases = {}
-        if group:
-            if not last:
-                aliases = {len(operands): 0}
-            operands.append(y)
-            in_specs.append(VMEM)
-        scratch = [
-            pltpu.VMEM((slots, block_len, users), jnp.bfloat16),
-            pltpu.SemaphoreType.DMA((slots,)),
-            pltpu.VMEM((BATCH, rank_i, users), jnp.float32),
-            pltpu.VMEM((BATCH, rank_c, users), jnp.float32),
-        ]
-        if last:
-            operands.append(user_basis)
-            in_specs.append(VMEM)
-            out_shape = (jax.ShapeDtypeStruct((devices // 8, chunk, LANES), jnp.float32),) * len(PIECES)
-            out_shape += (jax.ShapeDtypeStruct((ranks, users), jnp.bfloat16),) * 2
-            out_specs = (VMEM,) * len(out_shape)
-            scratch = [pltpu.VMEM(y_shape, jnp.float32), pltpu.VMEM((devices * chunk, LANES), jnp.float32)] + scratch
-        else:
-            out_shape, out_specs = y_type, VMEM
-        y = pl.pallas_call(
-            functools.partial(tiles_kernel, group, last, piece_places(devices)),
-            out_shape=out_shape,
-            in_specs=in_specs,
-            out_specs=out_specs,
-            input_output_aliases=aliases,
-            scratch_shapes=scratch,
-            compiler_params=limit(16),
-            cost_estimate=pl.CostEstimate(flops=5 * 10**8, bytes_accessed=4 * 10**6, transcendentals=0),
-            name="tile_sums",
-        )(*operands)
-    return dict(zip(PIECES, y[:-2])), y[-2], y[-1]
+    out_shape = (jax.ShapeDtypeStruct((devices // 8, chunk, LANES), jnp.float32),) * len(PIECES)
+    out_shape += (jax.ShapeDtypeStruct((ranks, users), jnp.bfloat16),) * 2
+    out = pl.pallas_call(
+        functools.partial(tiles_kernel, piece_places(devices)),
+        out_shape=out_shape,
+        in_specs=[SMEM] * 3 + [VMEM] * 4,
+        out_specs=(VMEM,) * len(out_shape),
+        scratch_shapes=[
+            pltpu.VMEM((rank_c, rank_i, users), jnp.float32),
+            pltpu.VMEM((devices * chunk, LANES), jnp.float32),
+            pltpu.VMEM((2, BATCH, rank_i, users), jnp.float32),
+        ],
+        compiler_params=limit(12),
+        cost_estimate=pl.CostEstimate(flops=2 * 10**9, bytes_accessed=12 * 10**6, transcendentals=0),
+        name="tile_sums",
+    )(where, count, me, blocks, weights, contexts, user_basis)
+    return dict(zip(PIECES, out[:-2])), out[-2], out[-1]
 
 
 def inverse_factor(gram):
@@ -404,17 +388,21 @@
 ):
     devices = lax.axis_size("users")
     half = devices // 2
+    rank_c = context_factors.shape[0]
     me = lax.axis_index("users").astype(jnp.int32).reshape(1)
 
     mirror = swap(item_factors, half, devices)
-    requests, tile_of = route(me, tile_owner[:, 0], tile_slot, half)
+    requests, where, own = route(me, tile_owner[:, 0], tile_slot, item_factors, half)
     sides = [list(range(half)), list(range(half, devices))]
     asked = lax.all_to_all(requests, "users", 0, 0, axis_index_groups=sides, tiled=True)
-    found = collect(me, asked, item_factors, mirror)
-    blocks = [found[0]] + [swap(found[mask], mask, devices) for mask in range(1, half)]
+    found = collect(asked, own, mirror)
+    found, cblock, factors = lax.optimization_barrier((found, tile_cblock, context_factors))
+    blocks = lax.all_to_all(found, "users", 0, 0, axis_index_groups=sides, tiled=True)
+
+    table = factors.astype(jnp.float32).reshape(rank_c, -1, CB).transpose(1, 0, 2)
+    contexts, weights = stage(cblock, table, tile_context, tile_weights)
     pieces, high, low = tile_sums(
-        tile_of, tile_cblock, user_counts, me, blocks, tile_weights, tile_context,
-        context_factors, user_basis, devices,
+        where, user_counts, me, blocks, weights, contexts, user_basis, devices
     )
     pieces = spread_pieces(reduce_pieces(pieces, devices), devices)
     return finish(me, high, low, pieces, devices)

time: 117 us -> 105 us (0.90)
  starting transfers between devices: 36.1 us -> 25 us
  Pallas kernels: 41.5 us -> 35.4 us
  waiting for transfers between devices: 19.7 us -> 24.1 us
    ppermute x36 -> x21, starting transfers between devices: 36.1 us -> 21.3 us  [swap(): return lax.ppermute(value, 'users', [(i, i ^ mask) for i in range(devices)])]
    all_to_all x0 -> x1, waiting for transfers between devices: none -> 6.2 us  [body(): lax.all_to_all(found, 'users', 0, 0, axis_index_groups=sides, tiled=True)]
    pallas_call x5 -> x3, Pallas kernels: 32.4 us -> 26.7 us  [the longest x1 20.8 us: tile_sums(): pl.pallas_call(functools.partial(tiles_kernel, piece_places(devices)), ou...]
    all_to_all x0 -> x1, starting transfers between devices: none -> 3.65 us  [body(): lax.all_to_all(found, 'users', 0, 0, axis_index_groups=sides, tiled=True)]
    ppermute x36 -> x21, waiting for transfers between devices: 19.7 us -> 17.9 us  [swap(): return lax.ppermute(value, 'users', [(i, i ^ mask) for i in range(devices)])]
    unnamed x20 -> x8, local copies, waits for them, and re-layouts: 7.91 us -> 7.55 us
  transfers between devices with their start and end apart: 36 -> 22, of which waited for: 15 -> 15; matrix products, arithmetic and copies ran while one was open for 0% -> 1% of each run, Pallas kernels for 21% -> 6%
where the time goes in v4:
time: 105 us
  Pallas kernels  35.4 us (34%)
  starting transfers between devices  25 us (24%)
  waiting for transfers between devices  24.1 us (23%)
  blocking collectives  10.5 us (10%)
  local copies, waits for them, and re-layouts  8.58 us (8%)
  between operations  1.41 us (1%)
    ppermute x21, starting transfers between devices, swap(): return lax.ppermute(value, 'users', [(i, i ^ mask) for i in range(devices)])  21.3 us
    pallas_call x1, Pallas kernels, tile_sums(): pl.pallas_call(functools.partial(tiles_kernel, piece_places(devices)), ou...  20.8 us
    ppermute x21, waiting for transfers between devices, swap(): return lax.ppermute(value, 'users', [(i, i ^ mask) for i in range(devices)])  17.9 us
    all_to_all x1, blocking collectives, body(): lax.all_to_all(requests, 'users', 0, 0, axis_index_groups=sides, tiled=True)  10.5 us
    unnamed x8, local copies, waits for them, and re-layouts  7.55 us
    pallas_call x1, Pallas kernels, finish(): pl.pallas_call(functools.partial(finish_kernel, users * devices, piece_pl...  6.46 us
    all_to_all x1, waiting for transfers between devices, body(): lax.all_to_all(found, 'users', 0, 0, axis_index_groups=sides, tiled=True)  6.2 us
    pallas_call x1, Pallas kernels, stage(): pl.pallas_call(stage_kernel, out_shape=(jax.ShapeDtypeStruct((tiles, ROWS...  4.05 us
  transfers between devices with their start and end apart: 22, of which 15 were waited for; matrix products, arithmetic and copies ran while one was open for 1% of the time, Pallas kernels for 6%

profile of v4, /device:TPU:0, one launch (start us, length us, event | category | flops | bytes accessed | tf_op | source)
XLA Modules:
  0.0 105.0 jit_solution(14361991185807258899)
XLA Ops:
  0.6 4.1 %collective-permute-start = (bf16[16,64,128]{2,1,0:T(8,128)(2,1)}, bf16[16,64,128]{2,1,0:T(8,128)(2,1)S(1)}, u32[]{:S(2)}, u32[]{:S(2)}) collective-permute-start(bf16[16,64,128]{2,1,0:T(8,128)(2,1)} %own_ref.1), channel_id=1, source_target_pairs={{0,16},{1,17},{2,18},{3,19},{4,20},{5,21},{6,22},{7,23},{8,24},{9,... | collective-permute-start | bytes 786440 | tf_op jit(solution)/shard_map/ppermute | solution.py:353
  4.7 2.2 %route.1 = (s32[16,1,128]{2,1,0:T(1,128)S(1)}, s32[64]{0:T(128)S(1)}, bf16[16,64,128]{2,1,0:T(8,128)(2,1)S(1)}) custom-call(s32[1]{0:T(128)} %bitcast.me_ref, s32[64]{0:T(128)} %bitcast.6, s32[64]{0:T(128)} %slot_ref.1, bf16[16,64,128]{2,1,0:T(8,128)(2,1)} %own_ref.1), custom_call_target="tpu_custom_call" | custom-call | tf_op jit(solution)/shard_map/route/pallas_call | solution.py:73
  7.0 10.5 %all_to_all.10.asked_ref = s32[16,1,128]{2,1,0:T(1,128)S(1)} all-to-all(s32[16,1,128]{2,1,0:T(1,128)S(1)} %get-tuple-element.21), channel_id=1, replica_groups={{0,1,2,3,4,5,6,7,8,9,10,11,12,13,14,15},{16,17,18,19,20,21,22,23,24,25,..., dimensions={0} | all-to-all | bytes 16384 | tf_op jit(solution)/shard_map/all_to_all | solution.py:397
  17.4 1.8 %collect.1 = bf16[64,64,128]{2,1,0:T(8,128)(2,1)} custom-call(s32[16,1,128]{2,1,0:T(1,128)S(1)} %all_to_all.10.asked_ref, bf16[16,64,128]{2,1,0:T(8,128)(2,1)S(1)} %get-tuple-element.22.own_ref, bf16[16,64,128]{2,1,0:T(8,128)(2,1)S(1)} %collective-permute-done.mirror_ref), custom_call_target="tpu_custom_call" | custom-call | tf_op jit(solution)/shard_map/collect/pallas_call | solution.py:99
  19.3 3.7 %all-to-all-start.1 = ((bf16[64,64,128]{2,1,0:T(8,128)(2,1)}), bf16[64,64,128]{2,1,0:T(8,128)(2,1)S(1)}, u32[]{:S(2)}, u32[]{:S(2)}) async-start(bf16[64,64,128]{2,1,0:T(8,128)(2,1)} %collect.1), calls=%async_computation.1 | async-start | bytes 2097152 | tf_op jit(solution)/shard_map/all_to_all | solution.py:400
  24.6 0.9 copy-done.3
  25.5 4.1 %stage.1 = (f32[64,8,512]{2,1,0:T(8,128)S(1)}, bf16[64,128,512]{2,1,0:T(8,128)(2,1)S(1)}) custom-call(s32[64]{0:T(128)} %cblock_ref, f32[64,8,8]{2,1,0:T(8,128)S(1)} %bitcast.5, s32[64,512]{1,0:T(8,128)S(1)} %copy-done.3, bf16[64,128,512]{2,1,0:T(8,128)(2,1)} %weights_ref.1), custom_call_target="tpu_custom_call" | custom-call | flops 10000000 | bytes 20000000 | tf_op jit(solution)/shard_map/stage/pallas_call | solution.py:130
  29.6 3.3 %copy-done = bf16[64,128,512]{2,1,0:T(8,128)(2,1)} copy-done((bf16[64,128,512]{2,1,0:T(8,128)(2,1)}, bf16[64,128,512]{2,1,0:T(8,128)(2,1)S(1)}, u32[]{:S(2)}) %copy-start) | copy-done | bytes 8388632
  32.8 6.2 %all-to-all-done.1.blocks_ref = bf16[64,64,128]{2,1,0:T(8,128)(2,1)S(1)} async-done(((bf16[64,64,128]{2,1,0:T(8,128)(2,1)}), bf16[64,64,128]{2,1,0:T(8,128)(2,1)S(1)}, u32[]{:S(2)}, u32[]{:S(2)}) %all-to-all-start.1) | async-done | bytes 1048608 | tf_op jit(solution)/shard_map/all_to_all | solution.py:400
  39.0 3.4 %copy-done.1 = bf16[64,128,512]{2,1,0:T(8,128)(2,1)S(1)} copy-done((bf16[64,128,512]{2,1,0:T(8,128)(2,1)S(1)}, bf16[64,128,512]{2,1,0:T(8,128)(2,1)}, u32[]{:S(2)}) %copy-start.1) | copy-done | bytes 8388632
  42.4 20.8 %tile_sums.1 = (f32[4,56,128]{2,1,0:T(8,128)S(1)}, f32[4,56,128]{2,1,0:T(8,128)S(1)}, f32[4,56,128]{2,1,0:T(8,128)S(1)}, f32[4,56,128]{2,1,0:T(8,128)S(1)}, f32[...) custom-call(s32[64]{0:T(128)S(1)} %get-tuple-element.20.where_ref, ...), custom_call_target="tpu_custom_call" | custom-call | flops 2000000000 | bytes 12000000 | tf_op jit(solution)/shard_map/tile_sums/pallas_call | solution.py:234
  64.7 1.0 collective-permute-start.3
  65.7 1.4 %collective-permute-start.5 = (f32[4,56,128]{2,1,0:T(8,128)S(1)}, f32[4,56,128]{2,1,0:T(8,128)S(1)}, u32[]{:S(2)}, u32[]{:S(2)}) collective-permute-start(f32[4,56,128]{2,1,0:T(8,128)S(1)} %add.69), channel_id=1, source_target_pairs={{0,2},{1,3},{2,0},{3,1},{4,6},{5,7},{6,4},{7,5},{8,10},{9,11},{10,... | collective-permute-start | bytes 344072 | tf_op jit(solution)/shard_map/ppermute | solution.py:353
  67.2 1.2 %collective-permute-start.7 = (f32[4,56,128]{2,1,0:T(8,128)S(1)}, f32[4,56,128]{2,1,0:T(8,128)S(1)}, u32[]{:S(2)}, u32[]{:S(2)}) collective-permute-start(f32[4,56,128]{2,1,0:T(8,128)S(1)} %add.71), channel_id=1, source_target_pairs={{0,4},{1,5},{2,6},{3,7},{4,0},{5,1},{6,2},{7,3},{8,12},{9,13},{10,... | collective-permute-start | bytes 344072 | tf_op jit(solution)/shard_map/ppermute | solution.py:353
  68.4 3.2 %collective-permute-done.3 = f32[4,56,128]{2,1,0:T(8,128)S(1)} collective-permute-done((f32[4,56,128]{2,1,0:T(8,128)S(1)}, f32[4,56,128]{2,1,0:T(8,128)S(1)}, u32[]{:S(2)}, u32[]{:S(2)}) %collective-permute-start.3) | collective-permute-done | bytes 114720 | tf_op jit(solution)/shard_map/ppermute | solution.py:353
  71.6 1.1 collective-permute-done.5
  73.3 3.4 %collective-permute-start.8 = (f32[1,56,128]{2,1,0:T(8,128)S(1)}, f32[1,56,128]{2,1,0:T(8,128)S(1)}, u32[]{:S(2)}, u32[]{:S(2)}) collective-permute-start(f32[1,56,128]{2,1,0:T(8,128)S(1)} %get-tuple-element.38), channel_id=1, source_target_pairs={{0,24},{1,25},{2,26},{3,27},{4,28},{5,29},{6,30},{7,31},{8,16},{9,... | collective-permute-start | bytes 86024 | tf_op jit(solution)/shard_map/ppermute | solution.py:353
  77.8 1.4 %collective-permute-done.8 = f32[1,56,128]{2,1,0:T(8,128)S(1)} collective-permute-done((f32[1,56,128]{2,1,0:T(8,128)S(1)}, f32[1,56,128]{2,1,0:T(8,128)S(1)}, u32[]{:S(2)}, u32[]{:S(2)}) %collective-permute-start.8) | collective-permute-done | bytes 28704 | tf_op jit(solution)/shard_map/ppermute | solution.py:353
  79.2 1.4 %collective-permute-done.10 = f32[1,56,128]{2,1,0:T(8,128)S(1)} collective-permute-done((f32[1,56,128]{2,1,0:T(8,128)S(1)}, f32[1,56,128]{2,1,0:T(8,128)S(1)}, u32[]{:S(2)}, u32[]{:S(2)}) %collective-permute-start.10) | collective-permute-done | bytes 28704 | tf_op jit(solution)/shard_map/ppermute | solution.py:353
  80.6 1.4 %collective-permute-done.9 = f32[1,56,128]{2,1,0:T(8,128)S(1)} collective-permute-done((f32[1,56,128]{2,1,0:T(8,128)S(1)}, f32[1,56,128]{2,1,0:T(8,128)S(1)}, u32[]{:S(2)}, u32[]{:S(2)}) %collective-permute-start.9) | collective-permute-done | bytes 28704 | tf_op jit(solution)/shard_map/ppermute | solution.py:353
  82.0 1.1 %collective-permute-start.13 = (f32[1,56,128]{2,1,0:T(8,128)S(1)}, f32[1,56,128]{2,1,0:T(8,128)S(1)}, u32[]{:S(2)}, u32[]{:S(2)}) collective-permute-start(f32[1,56,128]{2,1,0:T(8,128)S(1)} %fusion.2), channel_id=1, source_target_pairs={{0,24},{1,25},{2,26},{3,27},{4,28},{5,29},{6,30},{7,31},{8,16},{9,... | collective-permute-start | bytes 86024 | tf_op jit(solution)/shard_map/ppermute | solution.py:353
  83.1 2.0 %collective-permute-start.12 = (f32[1,56,128]{2,1,0:T(8,128)S(1)}, f32[1,56,128]{2,1,0:T(8,128)S(1)}, u32[]{:S(2)}, u32[]{:S(2)}) collective-permute-start(f32[1,56,128]{2,1,0:T(8,128)S(1)} %fusion.2), channel_id=1, source_target_pairs={{0,16},{1,17},{2,18},{3,19},{4,20},{5,21},{6,22},{7,23},{8,24},{9,... | collective-permute-start | bytes 86024 | tf_op jit(solution)/shard_map/ppermute | solution.py:353
  85.1 1.4 %collective-permute-start.11 = (f32[1,56,128]{2,1,0:T(8,128)S(1)}, f32[1,56,128]{2,1,0:T(8,128)S(1)}, u32[]{:S(2)}, u32[]{:S(2)}) collective-permute-start(f32[1,56,128]{2,1,0:T(8,128)S(1)} %fusion.2), channel_id=1, source_target_pairs={{0,8},{1,9},{2,10},{3,11},{4,12},{5,13},{6,14},{7,15},{8,0},{9,1},... | collective-permute-start | bytes 86024 | tf_op jit(solution)/shard_map/ppermute | solution.py:353
  86.5 1.3 %collective-permute-done.13 = f32[1,56,128]{2,1,0:T(8,128)S(1)} collective-permute-done((f32[1,56,128]{2,1,0:T(8,128)S(1)}, f32[1,56,128]{2,1,0:T(8,128)S(1)}, u32[]{:S(2)}, u32[]{:S(2)}) %collective-permute-start.13) | collective-permute-done | bytes 28704 | tf_op jit(solution)/shard_map/ppermute | solution.py:353
  89.0 0.9 collective-permute-start.18
  90.0 1.6 %collective-permute-start.16 = (f32[4,56,128]{2,1,0:T(8,128)S(1)}, f32[4,56,128]{2,1,0:T(8,128)S(1)}, u32[]{:S(2)}, u32[]{:S(2)}) collective-permute-start(f32[4,56,128]{2,1,0:T(8,128)S(1)} %pad_maximum_fusion.rest_7_), channel_id=1, source_target_pairs={{0,2},{1,3},{2,0},{3,1},{4,6},{5,7},{6,4},{7,5},{8,10},{9,11},{10,... | collective-permute-start | bytes 344072 | tf_op jit(solution)/shard_map/ppermute | solution.py:353
  91.6 1.0 collective-permute-start.14
  92.6 1.3 %collective-permute-done.18.rest_6_ = f32[4,56,128]{2,1,0:T(8,128)S(1)} collective-permute-done((f32[4,56,128]{2,1,0:T(8,128)S(1)}, f32[4,56,128]{2,1,0:T(8,128)S(1)}, u32[]{:S(2)}, u32[]{:S(2)}) %collective-permute-start.18) | collective-permute-done | bytes 114720 | tf_op jit(solution)/shard_map/ppermute | solution.py:353
  93.9 0.9 collective-permute-done.16.rest_5_
  94.7 2.5 %collective-permute-done.14.rest_4_ = f32[4,56,128]{2,1,0:T(8,128)S(1)} collective-permute-done((f32[4,56,128]{2,1,0:T(8,128)S(1)}, f32[4,56,128]{2,1,0:T(8,128)S(1)}, u32[]{:S(2)}, u32[]{:S(2)}) %collective-permute-start.14) | collective-permute-done | bytes 114720 | tf_op jit(solution)/shard_map/ppermute | solution.py:353
  97.3 1.3 %collective-permute-done.15.rest_0_ = f32[4,56,128]{2,1,0:T(8,128)S(1)} collective-permute-done((f32[4,56,128]{2,1,0:T(8,128)S(1)}, f32[4,56,128]{2,1,0:T(8,128)S(1)}, u32[]{:S(2)}, u32[]{:S(2)}) %collective-permute-start.15) | collective-permute-done | bytes 114720 | tf_op jit(solution)/shard_map/ppermute | solution.py:353
  98.6 6.5 %finish.1 = (f32[512,128]{1,0:T(8,128)}, f32[128,512]{1,0:T(8,128)}) custom-call(s32[1]{0:T(128)} %bitcast.me_ref, bf16[512,512]{1,0:T(8,128)(2,1)S(1)} %get-tuple-element.28.high_ref, bf16[512,512]{1,0:T(8,128)(2,1)S(1)} %get-tuple-element.29.low_ref, f32[4,56,128]{2,1,0:T(8,128)S(1)} %collective-permute-done.15.rest_0_, ...), custom_call_target="tpu_custom_call" | custom-call | tf_op jit(solution)/shard_map/finish/pallas_call | solution.py:335
  (34 shorter events, 5.4 us)
Async XLA Ops:
  0.6 38.4 %copy-start.2 = (f32[512,128]{1,0:T(8,128)S(1)}, f32[512,128]{1,0:T(8,128)}, u32[]{:S(2)}) copy-start(f32[512,128]{1,0:T(8,128)} %basis_ref.1) | copy-start | bytes 786436
  0.6 16.8 %collective-permute-start = (bf16[16,64,128]{2,1,0:T(8,128)(2,1)}, bf16[16,64,128]{2,1,0:T(8,128)(2,1)S(1)}, u32[]{:S(2)}, u32[]{:S(2)}) collective-permute-start(bf16[16,64,128]{2,1,0:T(8,128)(2,1)} %own_ref.1), channel_id=1, source_target_pairs={{0,16},{1,17},{2,18},{3,19},{4,20},{5,21},{6,22},{7,23},{8,24},{9,... | collective-permute-start | bytes 786440 | tf_op jit(solution)/shard_map/ppermute | solution.py:353
  19.3 19.8 %all-to-all-start.1 = ((bf16[64,64,128]{2,1,0:T(8,128)(2,1)}), bf16[64,64,128]{2,1,0:T(8,128)(2,1)S(1)}, u32[]{:S(2)}, u32[]{:S(2)}) async-start(bf16[64,64,128]{2,1,0:T(8,128)(2,1)} %collect.1), calls=%async_computation.1 | async-start | bytes 2097152 | tf_op jit(solution)/shard_map/all_to_all | solution.py:400
  24.6 0.9 copy-start.3
  29.6 3.3 %copy-start = (bf16[64,128,512]{2,1,0:T(8,128)(2,1)}, bf16[64,128,512]{2,1,0:T(8,128)(2,1)S(1)}, u32[]{:S(2)}) copy-start(bf16[64,128,512]{2,1,0:T(8,128)(2,1)S(1)} %get-tuple-element.26.weights_ref) | copy-start | bytes 25165828
  39.0 3.4 %copy-start.1 = (bf16[64,128,512]{2,1,0:T(8,128)(2,1)S(1)}, bf16[64,128,512]{2,1,0:T(8,128)(2,1)}, u32[]{:S(2)}) copy-start(bf16[64,128,512]{2,1,0:T(8,128)(2,1)} %copy-done) | copy-start | bytes 25165828
  63.3 1.4 %collective-permute-start.2 = (f32[4,56,128]{2,1,0:T(8,128)S(1)}, f32[4,56,128]{2,1,0:T(8,128)S(1)}, u32[]{:S(2)}, u32[]{:S(2)}) collective-permute-start(f32[4,56,128]{2,1,0:T(8,128)S(1)} %get-tuple-element.33), channel_id=1, source_target_pairs={{0,1},{1,0},{2,3},{3,2},{4,5},{5,4},{6,7},{7,6},{8,9},{9,8},{10,11... | collective-permute-start | bytes 344072 | tf_op jit(solution)/shard_map/ppermute | solution.py:353
  63.3 2.3 %collective-permute-start.4 = (f32[4,56,128]{2,1,0:T(8,128)S(1)}, f32[4,56,128]{2,1,0:T(8,128)S(1)}, u32[]{:S(2)}, u32[]{:S(2)}) collective-permute-start(f32[4,56,128]{2,1,0:T(8,128)S(1)} %get-tuple-element.35), channel_id=1, source_target_pairs={{0,1},{1,0},{2,3},{3,2},{4,5},{5,4},{6,7},{7,6},{8,9},{9,8},{10,11... | collective-permute-start | bytes 344072 | tf_op jit(solution)/shard_map/ppermute | solution.py:353
  63.8 3.3 %collective-permute-start.6 = (f32[4,56,128]{2,1,0:T(8,128)S(1)}, f32[4,56,128]{2,1,0:T(8,128)S(1)}, u32[]{:S(2)}, u32[]{:S(2)}) collective-permute-start(f32[4,56,128]{2,1,0:T(8,128)S(1)} %get-tuple-element.37), channel_id=1, source_target_pairs={{0,1},{1,0},{2,3},{3,2},{4,5},{5,4},{6,7},{7,6},{8,9},{9,8},{10,11... | collective-permute-start | bytes 344072 | tf_op jit(solution)/shard_map/ppermute | solution.py:353
  63.9 4.5 %collective-permute-start.1 = (f32[4,56,128]{2,1,0:T(8,128)S(1)}, f32[4,56,128]{2,1,0:T(8,128)S(1)}, u32[]{:S(2)}, u32[]{:S(2)}) collective-permute-start(f32[4,56,128]{2,1,0:T(8,128)S(1)} %get-tuple-element.31), channel_id=1, source_target_pairs={{0,1},{1,0},{2,3},{3,2},{4,5},{5,4},{6,7},{7,6},{8,9},{9,8},{10,11... | collective-permute-start | bytes 344072 | tf_op jit(solution)/shard_map/ppermute | solution.py:353
  64.7 7.0 %collective-permute-start.3 = (f32[4,56,128]{2,1,0:T(8,128)S(1)}, f32[4,56,128]{2,1,0:T(8,128)S(1)}, u32[]{:S(2)}, u32[]{:S(2)}) collective-permute-start(f32[4,56,128]{2,1,0:T(8,128)S(1)} %add.67), channel_id=1, source_target_pairs={{0,6},{1,7},{2,4},{3,5},{4,2},{5,3},{6,0},{7,1},{8,14},{9,15},{10,... | collective-permute-start | bytes 344072 | tf_op jit(solution)/shard_map/ppermute | solution.py:353
  65.7 7.0 %collective-permute-start.5 = (f32[4,56,128]{2,1,0:T(8,128)S(1)}, f32[4,56,128]{2,1,0:T(8,128)S(1)}, u32[]{:S(2)}, u32[]{:S(2)}) collective-permute-start(f32[4,56,128]{2,1,0:T(8,128)S(1)} %add.69), channel_id=1, source_target_pairs={{0,2},{1,3},{2,0},{3,1},{4,6},{5,7},{6,4},{7,5},{8,10},{9,11},{10,... | collective-permute-start | bytes 344072 | tf_op jit(solution)/shard_map/ppermute | solution.py:353
  67.2 6.1 %collective-permute-start.7 = (f32[4,56,128]{2,1,0:T(8,128)S(1)}, f32[4,56,128]{2,1,0:T(8,128)S(1)}, u32[]{:S(2)}, u32[]{:S(2)}) collective-permute-start(f32[4,56,128]{2,1,0:T(8,128)S(1)} %add.71), channel_id=1, source_target_pairs={{0,4},{1,5},{2,6},{3,7},{4,0},{5,1},{6,2},{7,3},{8,12},{9,13},{10,... | collective-permute-start | bytes 344072 | tf_op jit(solution)/shard_map/ppermute | solution.py:353
  73.3 5.9 %collective-permute-start.8 = (f32[1,56,128]{2,1,0:T(8,128)S(1)}, f32[1,56,128]{2,1,0:T(8,128)S(1)}, u32[]{:S(2)}, u32[]{:S(2)}) collective-permute-start(f32[1,56,128]{2,1,0:T(8,128)S(1)} %get-tuple-element.38), channel_id=1, source_target_pairs={{0,24},{1,25},{2,26},{3,27},{4,28},{5,29},{6,30},{7,31},{8,16},{9,... | collective-permute-start | bytes 86024 | tf_op jit(solution)/shard_map/ppermute | solution.py:353
  76.8 3.9 %collective-permute-start.10 = (f32[1,56,128]{2,1,0:T(8,128)S(1)}, f32[1,56,128]{2,1,0:T(8,128)S(1)}, u32[]{:S(2)}, u32[]{:S(2)}) collective-permute-start(f32[1,56,128]{2,1,0:T(8,128)S(1)} %get-tuple-element.39), channel_id=1, source_target_pairs={{0,8},{1,9},{2,10},{3,11},{4,12},{5,13},{6,14},{7,15},{8,0},{9,1},... | collective-permute-start | bytes 86024 | tf_op jit(solution)/shard_map/ppermute | solution.py:353
  77.2 4.8 %collective-permute-start.9 = (f32[1,56,128]{2,1,0:T(8,128)S(1)}, f32[1,56,128]{2,1,0:T(8,128)S(1)}, u32[]{:S(2)}, u32[]{:S(2)}) collective-permute-start(f32[1,56,128]{2,1,0:T(8,128)S(1)} %get-tuple-element.40), channel_id=1, source_target_pairs={{0,16},{1,17},{2,18},{3,19},{4,20},{5,21},{6,22},{7,23},{8,24},{9,... | collective-permute-start | bytes 86024 | tf_op jit(solution)/shard_map/ppermute | solution.py:353
  82.0 5.8 %collective-permute-start.13 = (f32[1,56,128]{2,1,0:T(8,128)S(1)}, f32[1,56,128]{2,1,0:T(8,128)S(1)}, u32[]{:S(2)}, u32[]{:S(2)}) collective-permute-start(f32[1,56,128]{2,1,0:T(8,128)S(1)} %fusion.2), channel_id=1, source_target_pairs={{0,24},{1,25},{2,26},{3,27},{4,28},{5,29},{6,30},{7,31},{8,16},{9,... | collective-permute-start | bytes 86024 | tf_op jit(solution)/shard_map/ppermute | solution.py:353
  83.1 5.3 %collective-permute-start.12 = (f32[1,56,128]{2,1,0:T(8,128)S(1)}, f32[1,56,128]{2,1,0:T(8,128)S(1)}, u32[]{:S(2)}, u32[]{:S(2)}) collective-permute-start(f32[1,56,128]{2,1,0:T(8,128)S(1)} %fusion.2), channel_id=1, source_target_pairs={{0,16},{1,17},{2,18},{3,19},{4,20},{5,21},{6,22},{7,23},{8,24},{9,... | collective-permute-start | bytes 86024 | tf_op jit(solution)/shard_map/ppermute | solution.py:353
  85.1 3.9 %collective-permute-start.11 = (f32[1,56,128]{2,1,0:T(8,128)S(1)}, f32[1,56,128]{2,1,0:T(8,128)S(1)}, u32[]{:S(2)}, u32[]{:S(2)}) collective-permute-start(f32[1,56,128]{2,1,0:T(8,128)S(1)} %fusion.2), channel_id=1, source_target_pairs={{0,8},{1,9},{2,10},{3,11},{4,12},{5,13},{6,14},{7,15},{8,0},{9,1},... | collective-permute-start | bytes 86024 | tf_op jit(solution)/shard_map/ppermute | solution.py:353
  89.0 4.9 %collective-permute-start.18 = (f32[4,56,128]{2,1,0:T(8,128)S(1)}, f32[4,56,128]{2,1,0:T(8,128)S(1)}, u32[]{:S(2)}, u32[]{:S(2)}) collective-permute-start(f32[4,56,128]{2,1,0:T(8,128)S(1)} %pad_maximum_fusion.rest_7_), channel_id=1, source_target_pairs={{0,4},{1,5},{2,6},{3,7},{4,0},{5,1},{6,2},{7,3},{8,12},{9,13},{10,... | collective-permute-start | bytes 344072 | tf_op jit(solution)/shard_map/ppermute | solution.py:353
  90.0 4.8 %collective-permute-start.16 = (f32[4,56,128]{2,1,0:T(8,128)S(1)}, f32[4,56,128]{2,1,0:T(8,128)S(1)}, u32[]{:S(2)}, u32[]{:S(2)}) collective-permute-start(f32[4,56,128]{2,1,0:T(8,128)S(1)} %pad_maximum_fusion.rest_7_), channel_id=1, source_target_pairs={{0,2},{1,3},{2,0},{3,1},{4,6},{5,7},{6,4},{7,5},{8,10},{9,11},{10,... | collective-permute-start | bytes 344072 | tf_op jit(solution)/shard_map/ppermute | solution.py:353
  91.6 5.7 %collective-permute-start.14 = (f32[4,56,128]{2,1,0:T(8,128)S(1)}, f32[4,56,128]{2,1,0:T(8,128)S(1)}, u32[]{:S(2)}, u32[]{:S(2)}) collective-permute-start(f32[4,56,128]{2,1,0:T(8,128)S(1)} %pad_maximum_fusion.rest_7_), channel_id=1, source_target_pairs={{0,6},{1,7},{2,4},{3,5},{4,2},{5,3},{6,0},{7,1},{8,14},{9,15},{10,... | collective-permute-start | bytes 344072 | tf_op jit(solution)/shard_map/ppermute | solution.py:353
  92.6 4.7 %collective-permute-start.20 = (f32[4,56,128]{2,1,0:T(8,128)S(1)}, f32[4,56,128]{2,1,0:T(8,128)S(1)}, u32[]{:S(2)}, u32[]{:S(2)}) collective-permute-start(f32[4,56,128]{2,1,0:T(8,128)S(1)} %pad_maximum_fusion.rest_7_), channel_id=1, source_target_pairs={{0,1},{1,0},{2,3},{3,2},{4,5},{5,4},{6,7},{7,6},{8,9},{9,8},{10,11... | collective-permute-start | bytes 344072 | tf_op jit(solution)/shard_map/ppermute | solution.py:353
  93.9 3.4 %collective-permute-start.19 = (f32[4,56,128]{2,1,0:T(8,128)S(1)}, f32[4,56,128]{2,1,0:T(8,128)S(1)}, u32[]{:S(2)}, u32[]{:S(2)}) collective-permute-start(f32[4,56,128]{2,1,0:T(8,128)S(1)} %collective-permute-done.18.rest_6_), channel_id=1, source_target_pairs={{0,1},{1,0},{2,3},{3,2},{4,5},{5,4},{6,7},{7,6},{8,9},{9,8},{10,11... | collective-permute-start | bytes 344072 | tf_op jit(solution)/shard_map/ppermute | solution.py:353
  94.7 2.5 %collective-permute-start.17 = (f32[4,56,128]{2,1,0:T(8,128)S(1)}, f32[4,56,128]{2,1,0:T(8,128)S(1)}, u32[]{:S(2)}, u32[]{:S(2)}) collective-permute-start(f32[4,56,128]{2,1,0:T(8,128)S(1)} %collective-permute-done.16.rest_5_), channel_id=1, source_target_pairs={{0,1},{1,0},{2,3},{3,2},{4,5},{5,4},{6,7},{7,6},{8,9},{9,8},{10,11... | collective-permute-start | bytes 344072 | tf_op jit(solution)/shard_map/ppermute | solution.py:353
  97.2 1.3 %collective-permute-start.15 = (f32[4,56,128]{2,1,0:T(8,128)S(1)}, f32[4,56,128]{2,1,0:T(8,128)S(1)}, u32[]{:S(2)}, u32[]{:S(2)}) collective-permute-start(f32[4,56,128]{2,1,0:T(8,128)S(1)} %collective-permute-done.14.rest_4_), channel_id=1, source_target_pairs={{0,1},{1,0},{2,3},{3,2},{4,5},{5,4},{6,7},{7,6},{8,9},{9,8},{10,11... | collective-permute-start | bytes 344072 | tf_op jit(solution)/shard_map/ppermute | solution.py:353

commit v5 on v4

--- a/solution.py
+++ b/solution.py
@@ -14,6 +14,7 @@
 LANES = 128
 ROWS = 8
 BATCH = 8
+CHUNKS = 8
 MIB = 2**20
 
 SMEM = pl.BlockSpec(memory_space=pltpu.SMEM)
@@ -86,13 +87,10 @@
 
 
 def collect_kernel(asked_ref, own_ref, mirror_ref, out_ref):
-    def one(peer, _):
+    for peer in range(asked_ref.shape[0]):
         for place in range(PLACES):
             source = own_ref if place < SLOTS else mirror_ref
             out_ref[peer * PLACES + place] = source[asked_ref[peer, 0, place]]
-        return 0
-
-    lax.fori_loop(0, asked_ref.shape[0], one, 0, unroll=4)
 
 
 def collect(asked, own, mirror):
@@ -106,9 +104,7 @@
     )(asked, own, mirror)
 
 
-def stage_kernel(cblock_ref, table_ref, marks_ref, weights_ref, context_ref, held_ref, sem_ref):
-    copy = pltpu.make_async_copy(weights_ref, held_ref, sem_ref)
-    copy.start()
+def context_kernel(cblock_ref, table_ref, marks_ref, context_ref):
     tiles, users = marks_ref.shape
 
     def one(tile, _):
@@ -122,29 +118,24 @@
         return 0
 
     lax.fori_loop(0, tiles, one, 0, unroll=2)
-    copy.wait()
-
-
-def stage(cblock, table, marks, weights):
+
+
+def context_values(cblock, table, marks):
     tiles, users = marks.shape
     return pl.pallas_call(
-        stage_kernel,
-        out_shape=(
-            jax.ShapeDtypeStruct((tiles, ROWS, users), jnp.float32),
-            jax.ShapeDtypeStruct(weights.shape, weights.dtype),
-        ),
-        in_specs=[SMEM, VMEM, VMEM, ANY],
-        out_specs=(VMEM, VMEM),
-        scratch_shapes=[pltpu.SemaphoreType.DMA],
+        context_kernel,
+        out_shape=jax.ShapeDtypeStruct((tiles, ROWS, users), jnp.float32),
+        in_specs=[SMEM, VMEM, VMEM],
+        out_specs=VMEM,
         compiler_params=limit(4),
         cost_estimate=pl.CostEstimate(flops=10**7, bytes_accessed=2 * 10**7, transcendentals=0),
-        name="stage",
-    )(in_hbm(cblock), table, marks, in_hbm(weights))
-
-
-def piece_places(devices):
+        name="contexts",
+    )(in_hbm(cblock), table, marks)
+
+
+def pack_places(me):
     return {
-        (core, plane): [core + 2 * plane + 8 * rest for rest in range(devices // 8)]
+        (core, plane): jnp.bitwise_xor(lax.rem(me, CHUNKS), core + 2 * plane)
         for core in range(2)
         for plane in range(4)
     }
@@ -153,45 +144,71 @@
 PIECES = [(core, plane) for core in (1, 0) for plane in (3, 1, 2, 0)]
 
 
-def pack_rows(ranks, devices):
+def pack_rows(ranks):
     groups = ranks // LANES
-    rows = (groups * (groups + 1) // 2 + groups) * LANES
-    return -(-rows // (devices * ROWS)) * ROWS
-
-
-def tiles_kernel(places, where_ref, count_ref, me_ref, blocks_ref, weights_ref, context_ref, basis_ref, *refs):
+    return (groups * (groups + 1) // 2 + groups) * LANES
+
+
+def tiles_kernel(
+    where_ref, count_ref, me_ref, blocks_ref, weights_ref, context_ref, basis_ref, *refs
+):
     piece_refs, refs = refs[: len(PIECES)], refs[len(PIECES) :]
-    high_ref, low_ref, y_ref, pack_ref, product_ref = refs
+    high_ref, low_ref, y_ref, pack_ref, even_ref, odd_ref = refs[:6]
+    weights_held, context_held, basis_held, weights_sem, context_sem, basis_sem = refs[6:]
     rank_c, rank_i, users = y_ref.shape
-    tiles = weights_ref.shape[0]
-    batches = tiles // BATCH
-    half = rank_i * users // LANES // BATCH
-
-    def multiply(tile, bank, place):
-        product = dot(blocks_ref[where_ref[tile]], weights_ref[tile])
-        product_ref[bank, place] = product.astype(jnp.bfloat16).astype(jnp.float32)
-
-    def first(place, _):
-        multiply(place, 0, place)
+    batches = weights_ref.shape[0] // BATCH
+    half = rank_c // 2
+
+    def weights_copy(batch):
+        rows = pl.ds(batch * BATCH, BATCH)
+        return pltpu.make_async_copy(weights_ref.at[rows], weights_held.at[rows], weights_sem.at[batch])
+
+    weights_copy(0).start()
+    contexts_copy = pltpu.make_async_copy(context_ref, context_held, context_sem)
+    contexts_copy.start()
+    for batch in range(1, batches):
+        weights_copy(batch).start()
+    basis_copy = pltpu.make_async_copy(basis_ref, basis_held, basis_sem)
+    basis_copy.start()
+
+    def multiply(batch, place, into_ref):
+        tile = batch * BATCH + place
+        product = dot(blocks_ref[where_ref[tile]], weights_held[tile])
+        into_ref[place] = product.astype(jnp.bfloat16).astype(jnp.float32)
+
+    def add(batch, part, from_ref):
+        lanes = slice(part // 2 * LANES, (part // 2 + 1) * LANES)
+        ranks = slice(part % 2 * half, (part % 2 + 1) * half)
+        total = y_ref[ranks, :, lanes]
+        for place in range(BATCH):
+            values = context_held[batch * BATCH + place, ranks, lanes]
+            total = total + values[:, None, :] * from_ref[place, :, lanes][None]
+        y_ref[ranks, :, lanes] = total
+
+    y_ref[...] = jnp.zeros_like(y_ref)
+    parts = 2 * users // LANES
+    weights_copy(0).wait()
+    for place in range(BATCH):
+        multiply(0, place, even_ref)
+    contexts_copy.wait()
+
+    def turn(batch, from_ref, into_ref):
+        weights_copy(batch + 1).wait()
+        for part in range(max(parts, BATCH)):
+            if part < BATCH:
+                multiply(batch + 1, part, into_ref)
+            if part < parts:
+                add(batch, part, from_ref)
+
+    def pair(index, _):
+        turn(2 * index, even_ref, odd_ref)
+        turn(2 * index + 1, odd_ref, even_ref)
         return 0
 
-    lax.fori_loop(0, BATCH, first, 0)
-    y_ref[...] = jnp.zeros_like(y_ref)
-
-    def step(index, _):
-        batch, part = index // BATCH, lax.rem(index, BATCH)
-        bank = lax.rem(batch, 2)
-        multiply(jnp.minimum(index + BATCH, tiles - 1), 1 - bank, part)
-        lanes = pl.ds(pl.multiple_of(part // (rank_i // half) * LANES, LANES), LANES)
-        rows = pl.ds(pl.multiple_of(lax.rem(part, rank_i // half) * half, ROWS), half)
-        total = y_ref[:, rows, lanes]
-        for place in range(BATCH):
-            values = context_ref[batch * BATCH + place, :, lanes]
-            total = total + values[:, None, :] * product_ref[bank, place, rows, lanes][None]
-        y_ref[:, rows, lanes] = total
-        return 0
-
-    lax.fori_loop(0, batches * BATCH, step, 0)
+    lax.fori_loop(0, batches // 2 - 1, pair, 0)
+    turn(batches - 2, even_ref, odd_ref)
+    for part in range(parts):
+        add(batches - 1, part, odd_ref)
 
     living = lax.broadcasted_iota(jnp.int32, (rank_i, users), 1) < count_ref[0]
     for r in range(rank_c):
@@ -209,42 +226,46 @@
         for j in range(groups - i):
             pack_ref[place * LANES : (place + 1) * LANES] = strip[:, j * LANES : (j + 1) * LANES]
             place += 1
-    basis_high, basis_low = split(basis_ref[...])
+    basis_copy.wait()
+    basis_high, basis_low = split(basis_held[...])
     projection = dot(high_ref[...], basis_high) + dot(high_ref[...], basis_low) + dot(low_ref[...], basis_high)
     pack_ref[place * LANES : (place + groups) * LANES] = projection
-    place += groups
-    if place * LANES < pack_ref.shape[0]:
-        pack_ref[place * LANES :] = jnp.zeros((pack_ref.shape[0] - place * LANES, LANES), jnp.float32)
-    me = me_ref[0]
-    chunk = piece_refs[0].shape[1]
+    chunk = piece_refs[0].shape[0]
+    places = pack_places(me_ref[0])
     for piece, ref in zip(PIECES, piece_refs):
-        for i, position in enumerate(places[piece]):
-            start = pl.multiple_of(jnp.bitwise_xor(me, position) * chunk, ROWS)
-            ref[i] = pack_ref[pl.ds(start, chunk)]
-
-
-def tile_sums(where, count, me, blocks, weights, contexts, user_basis, devices):
-    users = weights.shape[2]
+        ref[...] = pack_ref[pl.ds(pl.multiple_of(places[piece] * chunk, ROWS), chunk)]
+
+
+def tile_sums(where, count, me, blocks, weights, contexts, user_basis):
+    tiles, _, users = weights.shape
     rank_i = blocks.shape[1]
     rank_c = contexts.shape[1]
     ranks = rank_c * rank_i
-    chunk = pack_rows(ranks, devices)
-    out_shape = (jax.ShapeDtypeStruct((devices // 8, chunk, LANES), jnp.float32),) * len(PIECES)
+    rows = pack_rows(ranks)
+    out_shape = (jax.ShapeDtypeStruct((rows // CHUNKS, LANES), jnp.float32),) * len(PIECES)
     out_shape += (jax.ShapeDtypeStruct((ranks, users), jnp.bfloat16),) * 2
+    held = 3 * weights.size * 2 // (2 * MIB)
     out = pl.pallas_call(
-        functools.partial(tiles_kernel, piece_places(devices)),
+        tiles_kernel,
         out_shape=out_shape,
-        in_specs=[SMEM] * 3 + [VMEM] * 4,
+        in_specs=[SMEM] * 3 + [VMEM] + [ANY] * 3,
         out_specs=(VMEM,) * len(out_shape),
         scratch_shapes=[
             pltpu.VMEM((rank_c, rank_i, users), jnp.float32),
-            pltpu.VMEM((devices * chunk, LANES), jnp.float32),
-            pltpu.VMEM((2, BATCH, rank_i, users), jnp.float32),
+            pltpu.VMEM((rows, LANES), jnp.float32),
+            pltpu.VMEM((BATCH, rank_i, users), jnp.float32),
+            pltpu.VMEM((BATCH, rank_i, users), jnp.float32),
+            pltpu.VMEM(weights.shape, weights.dtype),
+            pltpu.VMEM(contexts.shape, contexts.dtype),
+            pltpu.VMEM(user_basis.shape, user_basis.dtype),
+            pltpu.SemaphoreType.DMA((tiles // BATCH,)),
+            pltpu.SemaphoreType.DMA,
+            pltpu.SemaphoreType.DMA,
         ],
-        compiler_params=limit(12),
+        compiler_params=limit(8 + held),
         cost_estimate=pl.CostEstimate(flops=2 * 10**9, bytes_accessed=12 * 10**6, transcendentals=0),
         name="tile_sums",
-    )(where, count, me, blocks, weights, contexts, user_basis)
+    )(where, count, me, blocks, in_hbm(weights), in_hbm(contexts), in_hbm(user_basis))
     return dict(zip(PIECES, out[:-2])), out[-2], out[-1]
 
 
@@ -291,14 +312,12 @@
     return jnp.concatenate(right, axis=0)
 
 
-def finish_kernel(total_users, places, me_ref, high_ref, low_ref, *rest):
+def finish_kernel(total_users, me_ref, high_ref, low_ref, *rest):
     piece_refs, (basis_ref, core_out_ref, pack_ref, full_ref) = rest[: len(PIECES)], rest[len(PIECES) :]
-    me = me_ref[0]
-    chunk = piece_refs[0].shape[1]
+    chunk = piece_refs[0].shape[0]
+    places = pack_places(me_ref[0])
     for piece, ref in zip(PIECES, piece_refs):
-        for i, position in enumerate(places[piece]):
-            start = pl.multiple_of(jnp.bitwise_xor(me, position) * chunk, ROWS)
-            pack_ref[pl.ds(start, chunk)] = ref[i]
+        pack_ref[pl.ds(pl.multiple_of(places[piece] * chunk, ROWS), chunk)] = ref[...]
     groups = full_ref.shape[0] // LANES
     place = 0
     for i in range(groups):
@@ -331,9 +350,8 @@
 
 def finish(me, high, low, pieces, devices):
     ranks, users = high.shape
-    chunk = pack_rows(ranks, devices)
     return pl.pallas_call(
-        functools.partial(finish_kernel, users * devices, piece_places(devices)),
+        functools.partial(finish_kernel, users * devices),
         out_shape=(
             jax.ShapeDtypeStruct((users, LANES), jnp.float32),
             jax.ShapeDtypeStruct((LANES, ranks), jnp.float32),
@@ -341,7 +359,7 @@
         in_specs=[SMEM] + [VMEM] * (2 + len(PIECES)),
         out_specs=(VMEM, VMEM),
         scratch_shapes=[
-            pltpu.VMEM((devices * chunk, LANES), jnp.float32),
+            pltpu.VMEM((pack_rows(ranks), LANES), jnp.float32),
             pltpu.VMEM((ranks, ranks), jnp.float32),
         ],
         compiler_params=limit(16),
@@ -355,28 +373,20 @@
 
 def reduce_pieces(pieces, devices):
     got = {plane: swap(pieces[1, plane], 1, devices) for plane in (3, 1, 2, 0)}
-    away = [swap(pieces[0, plane] + got[plane], 2 * plane, devices) for plane in (3, 1, 2)]
-    rest = devices // 8
-    total = None
-    far = []
-    for position in list(range(rest - 1, -1, -1)):
-        rows = slice(position, position + 1)
-        value = pieces[0, 0][rows] + got[0][rows] + away[0][rows] + away[1][rows] + away[2][rows]
-        if position:
-            far.append(swap(value, 8 * position, devices))
-        else:
-            total = value
-    for value in far:
-        total = total + value
+    total = pieces[0, 0] + got[0]
+    for plane in (3, 1, 2):
+        total = total + swap(pieces[0, plane] + got[plane], 2 * plane, devices)
+    mask = CHUNKS
+    while mask < devices:
+        total = total + swap(total, mask, devices)
+        mask *= 2
     return total
 
 
 def spread_pieces(total, devices):
-    near = [total] + [swap(total, 8 * position, devices) for position in range(1, devices // 8)]
-    near = jnp.concatenate(near, axis=0)
-    pieces = {(0, 0): near}
+    pieces = {(0, 0): total}
     for plane in (3, 1, 2):
-        pieces[0, plane] = swap(near, 2 * plane, devices)
+        pieces[0, plane] = swap(total, 2 * plane, devices)
     for plane in (0, 3, 1, 2):
         pieces[1, plane] = swap(pieces[0, plane], 1, devices)
     return pieces
@@ -400,9 +410,9 @@
     blocks = lax.all_to_all(found, "users", 0, 0, axis_index_groups=sides, tiled=True)
 
     table = factors.astype(jnp.float32).reshape(rank_c, -1, CB).transpose(1, 0, 2)
-    contexts, weights = stage(cblock, table, tile_context, tile_weights)
+    contexts = context_values(cblock, table, tile_context)
     pieces, high, low = tile_sums(
-        where, user_counts, me, blocks, weights, contexts, user_basis, devices
+        where, user_counts, me, blocks, tile_weights, contexts, user_basis
     )
     pieces = spread_pieces(reduce_pieces(pieces, devices), devices)
     return finish(me, high, low, pieces, devices)

time: 105 us -> 92.4 us (0.88)
  Pallas kernels: 35.4 us -> 28.5 us
  local copies, waits for them, and re-layouts: 8.58 us -> 2.89 us
  starting transfers between devices: 25 us -> 20.1 us
  waiting for transfers between devices: 24.1 us -> 28.7 us
    pallas_call x3, Pallas kernels: 31.4 us -> 24.5 us  [the longest x1 14.3 us: tile_sums(): pl.pallas_call(tiles_kernel, out_shape=out_shape, in_specs=[SMEM] * 3 + [...]
    unnamed x8 -> x4, local copies, waits for them, and re-layouts: 7.55 us -> 1.86 us
    ppermute x21 -> x17, starting transfers between devices: 21.3 us -> 16.4 us  [swap(): return lax.ppermute(value, 'users', [(i, i ^ mask) for i in range(devices)])]
    all_to_all x1, waiting for transfers between devices: 6.2 us -> 8.85 us  [body(): lax.all_to_all(found, 'users', 0, 0, axis_index_groups=sides, tiled=True)]
    ppermute x21 -> x17, waiting for transfers between devices: 17.9 us -> 19.8 us  [swap(): return lax.ppermute(value, 'users', [(i, i ^ mask) for i in range(devices)])]
  transfers between devices with their start and end apart: 22 -> 18, of which waited for: 15 -> 11; matrix products, arithmetic and copies ran while one was open for 1% -> 1% of each run, Pallas kernels for 6% -> 6%
where the time goes in v5:
time: 92.4 us; the launch traced here: 92.1 us
  waiting for transfers between devices  28.7 us (31%)
  Pallas kernels  28.5 us (31%)
  starting transfers between devices  20.1 us (22%)
  blocking collectives  10.5 us (11%)
  local copies, waits for them, and re-layouts  2.89 us (3%)
  between operations  1.4 us (2%)
    ppermute x17, waiting for transfers between devices, swap(): return lax.ppermute(value, 'users', [(i, i ^ mask) for i in range(devices)])  19.8 us
    ppermute x17, starting transfers between devices, swap(): return lax.ppermute(value, 'users', [(i, i ^ mask) for i in range(devices)])  16.4 us
    pallas_call x1, Pallas kernels, tile_sums(): pl.pallas_call(tiles_kernel, out_shape=out_shape, in_specs=[SMEM] * 3 + [...  14.3 us
    all_to_all x1, blocking collectives, body(): lax.all_to_all(requests, 'users', 0, 0, axis_index_groups=sides, tiled=True)  10.5 us
    all_to_all x1, waiting for transfers between devices, body(): lax.all_to_all(found, 'users', 0, 0, axis_index_groups=sides, tiled=True)  8.85 us
    pallas_call x1, Pallas kernels, finish(): pl.pallas_call(functools.partial(finish_kernel, users * devices), out_sha...  6.46 us
    pallas_call x1, Pallas kernels, context_values(): pl.pallas_call(context_kernel, out_shape=jax.ShapeDtypeStruct((tiles, ROW...  3.71 us
    all_to_all x1, starting transfers between devices, body(): lax.all_to_all(found, 'users', 0, 0, axis_index_groups=sides, tiled=True)  3.65 us
  transfers between devices with their start and end apart: 18, of which 11 were waited for; matrix products, arithmetic and copies ran while one was open for 1% of the time, Pallas kernels for 6%

profile of v5, /device:TPU:0, one launch (start us, length us, event | category | flops | bytes accessed | tf_op | source)
XLA Modules:
  0.0 92.1 jit_solution(4261080237018836177)
XLA Ops:
  0.6 4.1 %collective-permute-start = (bf16[16,64,128]{2,1,0:T(8,128)(2,1)}, bf16[16,64,128]{2,1,0:T(8,128)(2,1)S(1)}, u32[]{:S(2)}, u32[]{:S(2)}) collective-permute-start(bf16[16,64,128]{2,1,0:T(8,128)(2,1)} %own_ref.1), channel_id=1, source_target_pairs={{0,16},{1,17},{2,18},{3,19},{4,20},{5,21},{6,22},{7,23},{8,24},{9,... | collective-permute-start | bytes 786440 | tf_op jit(solution)/shard_map/ppermute | solution.py:371
  4.7 2.2 %route.1 = (s32[16,1,128]{2,1,0:T(1,128)S(1)}, s32[64]{0:T(128)S(1)}, bf16[16,64,128]{2,1,0:T(8,128)(2,1)S(1)}) custom-call(s32[1]{0:T(128)} %bitcast.me_ref, s32[64]{0:T(128)} %bitcast.6, s32[64]{0:T(128)} %slot_ref.1, bf16[16,64,128]{2,1,0:T(8,128)(2,1)} %own_ref.1), custom_call_target="tpu_custom_call" | custom-call | tf_op jit(solution)/shard_map/route/pallas_call | solution.py:74
  7.0 10.5 %all_to_all.10.asked_ref = s32[16,1,128]{2,1,0:T(1,128)S(1)} all-to-all(s32[16,1,128]{2,1,0:T(1,128)S(1)} %get-tuple-element.19), channel_id=1, replica_groups={{0,1,2,3,4,5,6,7,8,9,10,11,12,13,14,15},{16,17,18,19,20,21,22,23,24,25,..., dimensions={0} | all-to-all | bytes 16384 | tf_op jit(solution)/shard_map/all_to_all | solution.py:407
  17.4 1.7 %collect.1 = bf16[64,64,128]{2,1,0:T(8,128)(2,1)} custom-call(s32[16,1,128]{2,1,0:T(1,128)S(1)} %all_to_all.10.asked_ref, bf16[16,64,128]{2,1,0:T(8,128)(2,1)S(1)} %get-tuple-element.20.own_ref, bf16[16,64,128]{2,1,0:T(8,128)(2,1)S(1)} %collective-permute-done.mirror_ref), custom_call_target="tpu_custom_call" | custom-call | tf_op jit(solution)/shard_map/collect/pallas_call | solution.py:97
  19.2 3.7 %all-to-all-start.1 = ((bf16[64,64,128]{2,1,0:T(8,128)(2,1)}), bf16[64,64,128]{2,1,0:T(8,128)(2,1)S(1)}, u32[]{:S(2)}, u32[]{:S(2)}) async-start(bf16[64,64,128]{2,1,0:T(8,128)(2,1)} %collect.1), calls=%async_computation.1 | async-start | bytes 2097152 | tf_op jit(solution)/shard_map/all_to_all | solution.py:410
  23.5 0.9 reshape.13
  24.5 0.9 copy-done.1
  25.4 3.7 %contexts.1.context_ref = f32[64,8,512]{2,1,0:T(8,128)S(1)} custom-call(s32[64]{0:T(128)} %cblock_ref, f32[64,8,8]{2,1,0:T(8,128)S(1)} %bitcast.5, s32[64,512]{1,0:T(8,128)S(1)} %copy-done.1), custom_call_target="tpu_custom_call" | custom-call | flops 10000000 | bytes 20000000 | tf_op jit(solution)/shard_map/contexts/pallas_call | solution.py:125
  29.2 1.0 %copy-done = f32[64,8,512]{2,1,0:T(8,128)} copy-done((f32[64,8,512]{2,1,0:T(8,128)}, f32[64,8,512]{2,1,0:T(8,128)S(1)}, u32[]{:S(2)}) %copy-start) | copy-done | bytes 1048600
  30.1 8.8 %all-to-all-done.1.blocks_ref = bf16[64,64,128]{2,1,0:T(8,128)(2,1)S(1)} async-done(((bf16[64,64,128]{2,1,0:T(8,128)(2,1)}), bf16[64,64,128]{2,1,0:T(8,128)(2,1)S(1)}, u32[]{:S(2)}, u32[]{:S(2)}) %all-to-all-start.1) | async-done | bytes 1048608 | tf_op jit(solution)/shard_map/all_to_all | solution.py:410
  39.0 14.3 %tile_sums.1 = (f32[224,128]{1,0:T(8,128)S(1)}, f32[224,128]{1,0:T(8,128)S(1)}, f32[224,128]{1,0:T(8,128)S(1)}, f32[224,128]{1,0:T(8,128)S(1)}, f32[224,128]{1,0...) custom-call(s32[64]{0:T(128)S(1)} %get-tuple-element.18.where_ref, ...), custom_call_target="tpu_custom_call" | custom-call | flops 2000000000 | bytes 12000000 | tf_op jit(solution)/shard_map/tile_sums/pallas_call | solution.py:248
  53.4 0.5 collective-permute-start.4
  54.0 0.4 collective-permute-start.1
  54.4 0.3 collective-permute-done.2
  54.7 1.0 %collective-permute-start.3 = (f32[224,128]{1,0:T(8,128)S(1)}, f32[224,128]{1,0:T(8,128)S(1)}, u32[]{:S(2)}, u32[]{:S(2)}) collective-permute-start(f32[224,128]{1,0:T(8,128)S(1)} %add.28), channel_id=1, source_target_pairs={{0,6},{1,7},{2,4},{3,5},{4,2},{5,3},{6,0},{7,1},{8,14},{9,15},{10,... | collective-permute-start | bytes 344072 | tf_op jit(solution)/shard_map/ppermute | solution.py:371
  55.7 1.4 %collective-permute-start.5 = (f32[224,128]{1,0:T(8,128)S(1)}, f32[224,128]{1,0:T(8,128)S(1)}, u32[]{:S(2)}, u32[]{:S(2)}) collective-permute-start(f32[224,128]{1,0:T(8,128)S(1)} %add.30), channel_id=1, source_target_pairs={{0,2},{1,3},{2,0},{3,1},{4,6},{5,7},{6,4},{7,5},{8,10},{9,11},{10,... | collective-permute-start | bytes 344072 | tf_op jit(solution)/shard_map/ppermute | solution.py:371
  57.2 1.2 %collective-permute-start.7 = (f32[224,128]{1,0:T(8,128)S(1)}, f32[224,128]{1,0:T(8,128)S(1)}, u32[]{:S(2)}, u32[]{:S(2)}) collective-permute-start(f32[224,128]{1,0:T(8,128)S(1)} %add.32), channel_id=1, source_target_pairs={{0,4},{1,5},{2,6},{3,7},{4,0},{5,1},{6,2},{7,3},{8,12},{9,13},{10,... | collective-permute-start | bytes 344072 | tf_op jit(solution)/shard_map/ppermute | solution.py:371
  58.4 3.2 %collective-permute-done.3 = f32[224,128]{1,0:T(8,128)S(1)} collective-permute-done((f32[224,128]{1,0:T(8,128)S(1)}, f32[224,128]{1,0:T(8,128)S(1)}, u32[]{:S(2)}, u32[]{:S(2)}) %collective-permute-start.3) | collective-permute-done | bytes 114720 | tf_op jit(solution)/shard_map/ppermute | solution.py:371
  61.7 1.0 %collective-permute-done.5 = f32[224,128]{1,0:T(8,128)S(1)} collective-permute-done((f32[224,128]{1,0:T(8,128)S(1)}, f32[224,128]{1,0:T(8,128)S(1)}, u32[]{:S(2)}, u32[]{:S(2)}) %collective-permute-start.5) | collective-permute-done | bytes 114720 | tf_op jit(solution)/shard_map/ppermute | solution.py:371
  62.7 0.6 collective-permute-done.7
  63.4 0.7 collective-permute-start.8
  64.0 4.2 %collective-permute-done.8 = f32[224,128]{1,0:T(8,128)S(1)} collective-permute-done((f32[224,128]{1,0:T(8,128)S(1)}, f32[224,128]{1,0:T(8,128)S(1)}, u32[]{:S(2)}, u32[]{:S(2)}) %collective-permute-start.8) | collective-permute-done | bytes 114720 | tf_op jit(solution)/shard_map/ppermute | solution.py:371
  68.2 3.3 %collective-permute-start.9 = (f32[224,128]{1,0:T(8,128)S(1)}, f32[224,128]{1,0:T(8,128)S(1)}, u32[]{:S(2)}, u32[]{:S(2)}) collective-permute-start(f32[224,128]{1,0:T(8,128)S(1)} %add.34), channel_id=1, source_target_pairs={{0,16},{1,17},{2,18},{3,19},{4,20},{5,21},{6,22},{7,23},{8,24},{9,... | collective-permute-start | bytes 344072 | tf_op jit(solution)/shard_map/ppermute | solution.py:371
  71.6 4.3 %collective-permute-done.9 = f32[224,128]{1,0:T(8,128)S(1)} collective-permute-done((f32[224,128]{1,0:T(8,128)S(1)}, f32[224,128]{1,0:T(8,128)S(1)}, u32[]{:S(2)}, u32[]{:S(2)}) %collective-permute-start.9) | collective-permute-done | bytes 114720 | tf_op jit(solution)/shard_map/ppermute | solution.py:371
  75.9 0.8 collective-permute-start.14
  76.7 1.9 %collective-permute-start.12 = (f32[224,128]{1,0:T(8,128)S(1)}, f32[224,128]{1,0:T(8,128)S(1)}, u32[]{:S(2)}, u32[]{:S(2)}) collective-permute-start(f32[224,128]{1,0:T(8,128)S(1)} %add.35.rest_7_), channel_id=1, source_target_pairs={{0,2},{1,3},{2,0},{3,1},{4,6},{5,7},{6,4},{7,5},{8,10},{9,11},{10,... | collective-permute-start | bytes 344072 | tf_op jit(solution)/shard_map/ppermute | solution.py:371
  78.6 0.9 collective-permute-start.10
  79.5 1.7 %collective-permute-done.14.rest_6_ = f32[224,128]{1,0:T(8,128)S(1)} collective-permute-done((f32[224,128]{1,0:T(8,128)S(1)}, f32[224,128]{1,0:T(8,128)S(1)}, u32[]{:S(2)}, u32[]{:S(2)}) %collective-permute-start.14) | collective-permute-done | bytes 114720 | tf_op jit(solution)/shard_map/ppermute | solution.py:371
  81.2 0.8 collective-permute-done.12.rest_5_
  82.0 2.3 %collective-permute-done.10.rest_4_ = f32[224,128]{1,0:T(8,128)S(1)} collective-permute-done((f32[224,128]{1,0:T(8,128)S(1)}, f32[224,128]{1,0:T(8,128)S(1)}, u32[]{:S(2)}, u32[]{:S(2)}) %collective-permute-start.10) | collective-permute-done | bytes 114720 | tf_op jit(solution)/shard_map/ppermute | solution.py:371
  84.3 1.3 %collective-permute-done.11.rest_0_ = f32[224,128]{1,0:T(8,128)S(1)} collective-permute-done((f32[224,128]{1,0:T(8,128)S(1)}, f32[224,128]{1,0:T(8,128)S(1)}, u32[]{:S(2)}, u32[]{:S(2)}) %collective-permute-start.11) | collective-permute-done | bytes 114720 | tf_op jit(solution)/shard_map/ppermute | solution.py:371
  85.6 6.5 %finish.1 = (f32[512,128]{1,0:T(8,128)}, f32[128,512]{1,0:T(8,128)}) custom-call(s32[1]{0:T(128)} %bitcast.me_ref, bf16[512,512]{1,0:T(8,128)(2,1)S(1)} %get-tuple-element.24.high_ref, bf16[512,512]{1,0:T(8,128)(2,1)S(1)} %get-tuple-element.25.low_ref, f32[224,128]{1,0:T(8,128)S(1)} %collective-permute-done.11.rest_0_, ...), custom_call_target="tpu_custom_call" | custom-call | tf_op jit(solution)/shard_map/finish/pallas_call | solution.py:353
  (22 shorter events, 0.4 us)
Async XLA Ops:
  0.6 16.8 %collective-permute-start = (bf16[16,64,128]{2,1,0:T(8,128)(2,1)}, bf16[16,64,128]{2,1,0:T(8,128)(2,1)S(1)}, u32[]{:S(2)}, u32[]{:S(2)}) collective-permute-start(bf16[16,64,128]{2,1,0:T(8,128)(2,1)} %own_ref.1), channel_id=1, source_target_pairs={{0,16},{1,17},{2,18},{3,19},{4,20},{5,21},{6,22},{7,23},{8,24},{9,... | collective-permute-start | bytes 786440 | tf_op jit(solution)/shard_map/ppermute | solution.py:371
  19.2 19.8 %all-to-all-start.1 = ((bf16[64,64,128]{2,1,0:T(8,128)(2,1)}), bf16[64,64,128]{2,1,0:T(8,128)(2,1)S(1)}, u32[]{:S(2)}, u32[]{:S(2)}) async-start(bf16[64,64,128]{2,1,0:T(8,128)(2,1)} %collect.1), calls=%async_computation.1 | async-start | bytes 2097152 | tf_op jit(solution)/shard_map/all_to_all | solution.py:410
  24.5 0.9 copy-start.1
  29.1 1.0 %copy-start = (f32[64,8,512]{2,1,0:T(8,128)}, f32[64,8,512]{2,1,0:T(8,128)S(1)}, u32[]{:S(2)}) copy-start(f32[64,8,512]{2,1,0:T(8,128)S(1)} %contexts.1.context_ref) | copy-start | bytes 3145732
  53.3 1.4 %collective-permute-start.2 = (f32[224,128]{1,0:T(8,128)S(1)}, f32[224,128]{1,0:T(8,128)S(1)}, u32[]{:S(2)}, u32[]{:S(2)}) collective-permute-start(f32[224,128]{1,0:T(8,128)S(1)} %get-tuple-element.29), channel_id=1, source_target_pairs={{0,1},{1,0},{2,3},{3,2},{4,5},{5,4},{6,7},{7,6},{8,9},{9,8},{10,11... | collective-permute-start | bytes 344072 | tf_op jit(solution)/shard_map/ppermute | solution.py:371
  53.4 2.3 %collective-permute-start.4 = (f32[224,128]{1,0:T(8,128)S(1)}, f32[224,128]{1,0:T(8,128)S(1)}, u32[]{:S(2)}, u32[]{:S(2)}) collective-permute-start(f32[224,128]{1,0:T(8,128)S(1)} %get-tuple-element.31), channel_id=1, source_target_pairs={{0,1},{1,0},{2,3},{3,2},{4,5},{5,4},{6,7},{7,6},{8,9},{9,8},{10,11... | collective-permute-start | bytes 344072 | tf_op jit(solution)/shard_map/ppermute | solution.py:371
  53.9 3.3 %collective-permute-start.6 = (f32[224,128]{1,0:T(8,128)S(1)}, f32[224,128]{1,0:T(8,128)S(1)}, u32[]{:S(2)}, u32[]{:S(2)}) collective-permute-start(f32[224,128]{1,0:T(8,128)S(1)} %get-tuple-element.33), channel_id=1, source_target_pairs={{0,1},{1,0},{2,3},{3,2},{4,5},{5,4},{6,7},{7,6},{8,9},{9,8},{10,11... | collective-permute-start | bytes 344072 | tf_op jit(solution)/shard_map/ppermute | solution.py:371
  54.0 4.5 %collective-permute-start.1 = (f32[224,128]{1,0:T(8,128)S(1)}, f32[224,128]{1,0:T(8,128)S(1)}, u32[]{:S(2)}, u32[]{:S(2)}) collective-permute-start(f32[224,128]{1,0:T(8,128)S(1)} %get-tuple-element.27), channel_id=1, source_target_pairs={{0,1},{1,0},{2,3},{3,2},{4,5},{5,4},{6,7},{7,6},{8,9},{9,8},{10,11... | collective-permute-start | bytes 344072 | tf_op jit(solution)/shard_map/ppermute | solution.py:371
  54.7 7.0 %collective-permute-start.3 = (f32[224,128]{1,0:T(8,128)S(1)}, f32[224,128]{1,0:T(8,128)S(1)}, u32[]{:S(2)}, u32[]{:S(2)}) collective-permute-start(f32[224,128]{1,0:T(8,128)S(1)} %add.28), channel_id=1, source_target_pairs={{0,6},{1,7},{2,4},{3,5},{4,2},{5,3},{6,0},{7,1},{8,14},{9,15},{10,... | collective-permute-start | bytes 344072 | tf_op jit(solution)/shard_map/ppermute | solution.py:371
  55.7 7.0 %collective-permute-start.5 = (f32[224,128]{1,0:T(8,128)S(1)}, f32[224,128]{1,0:T(8,128)S(1)}, u32[]{:S(2)}, u32[]{:S(2)}) collective-permute-start(f32[224,128]{1,0:T(8,128)S(1)} %add.30), channel_id=1, source_target_pairs={{0,2},{1,3},{2,0},{3,1},{4,6},{5,7},{6,4},{7,5},{8,10},{9,11},{10,... | collective-permute-start | bytes 344072 | tf_op jit(solution)/shard_map/ppermute | solution.py:371
  57.2 6.1 %collective-permute-start.7 = (f32[224,128]{1,0:T(8,128)S(1)}, f32[224,128]{1,0:T(8,128)S(1)}, u32[]{:S(2)}, u32[]{:S(2)}) collective-permute-start(f32[224,128]{1,0:T(8,128)S(1)} %add.32), channel_id=1, source_target_pairs={{0,4},{1,5},{2,6},{3,7},{4,0},{5,1},{6,2},{7,3},{8,12},{9,13},{10,... | collective-permute-start | bytes 344072 | tf_op jit(solution)/shard_map/ppermute | solution.py:371
  63.4 4.9 %collective-permute-start.8 = (f32[224,128]{1,0:T(8,128)S(1)}, f32[224,128]{1,0:T(8,128)S(1)}, u32[]{:S(2)}, u32[]{:S(2)}) collective-permute-start(f32[224,128]{1,0:T(8,128)S(1)} %add_add_fusion), channel_id=1, source_target_pairs={{0,8},{1,9},{2,10},{3,11},{4,12},{5,13},{6,14},{7,15},{8,0},{9,1},... | collective-permute-start | bytes 344072 | tf_op jit(solution)/shard_map/ppermute | solution.py:371
  68.2 7.6 %collective-permute-start.9 = (f32[224,128]{1,0:T(8,128)S(1)}, f32[224,128]{1,0:T(8,128)S(1)}, u32[]{:S(2)}, u32[]{:S(2)}) collective-permute-start(f32[224,128]{1,0:T(8,128)S(1)} %add.34), channel_id=1, source_target_pairs={{0,16},{1,17},{2,18},{3,19},{4,20},{5,21},{6,22},{7,23},{8,24},{9,... | collective-permute-start | bytes 344072 | tf_op jit(solution)/shard_map/ppermute | solution.py:371
  75.9 5.3 %collective-permute-start.14 = (f32[224,128]{1,0:T(8,128)S(1)}, f32[224,128]{1,0:T(8,128)S(1)}, u32[]{:S(2)}, u32[]{:S(2)}) collective-permute-start(f32[224,128]{1,0:T(8,128)S(1)} %add.35.rest_7_), channel_id=1, source_target_pairs={{0,4},{1,5},{2,6},{3,7},{4,0},{5,1},{6,2},{7,3},{8,12},{9,13},{10,... | collective-permute-start | bytes 344072 | tf_op jit(solution)/shard_map/ppermute | solution.py:371
  76.7 5.3 %collective-permute-start.12 = (f32[224,128]{1,0:T(8,128)S(1)}, f32[224,128]{1,0:T(8,128)S(1)}, u32[]{:S(2)}, u32[]{:S(2)}) collective-permute-start(f32[224,128]{1,0:T(8,128)S(1)} %add.35.rest_7_), channel_id=1, source_target_pairs={{0,2},{1,3},{2,0},{3,1},{4,6},{5,7},{6,4},{7,5},{8,10},{9,11},{10,... | collective-permute-start | bytes 344072 | tf_op jit(solution)/shard_map/ppermute | solution.py:371
  78.6 5.7 %collective-permute-start.10 = (f32[224,128]{1,0:T(8,128)S(1)}, f32[224,128]{1,0:T(8,128)S(1)}, u32[]{:S(2)}, u32[]{:S(2)}) collective-permute-start(f32[224,128]{1,0:T(8,128)S(1)} %add.35.rest_7_), channel_id=1, source_target_pairs={{0,6},{1,7},{2,4},{3,5},{4,2},{5,3},{6,0},{7,1},{8,14},{9,15},{10,... | collective-permute-start | bytes 344072 | tf_op jit(solution)/shard_map/ppermute | solution.py:371
  79.5 4.9 %collective-permute-start.16 = (f32[224,128]{1,0:T(8,128)S(1)}, f32[224,128]{1,0:T(8,128)S(1)}, u32[]{:S(2)}, u32[]{:S(2)}) collective-permute-start(f32[224,128]{1,0:T(8,128)S(1)} %add.35.rest_7_), channel_id=1, source_target_pairs={{0,1},{1,0},{2,3},{3,2},{4,5},{5,4},{6,7},{7,6},{8,9},{9,8},{10,11... | collective-permute-start | bytes 344072 | tf_op jit(solution)/shard_map/ppermute | solution.py:371
  81.2 3.1 %collective-permute-start.15 = (f32[224,128]{1,0:T(8,128)S(1)}, f32[224,128]{1,0:T(8,128)S(1)}, u32[]{:S(2)}, u32[]{:S(2)}) collective-permute-start(f32[224,128]{1,0:T(8,128)S(1)} %collective-permute-done.14.rest_6_), channel_id=1, source_target_pairs={{0,1},{1,0},{2,3},{3,2},{4,5},{5,4},{6,7},{7,6},{8,9},{9,8},{10,11... | collective-permute-start | bytes 344072 | tf_op jit(solution)/shard_map/ppermute | solution.py:371
  82.0 2.3 %collective-permute-start.13 = (f32[224,128]{1,0:T(8,128)S(1)}, f32[224,128]{1,0:T(8,128)S(1)}, u32[]{:S(2)}, u32[]{:S(2)}) collective-permute-start(f32[224,128]{1,0:T(8,128)S(1)} %collective-permute-done.12.rest_5_), channel_id=1, source_target_pairs={{0,1},{1,0},{2,3},{3,2},{4,5},{5,4},{6,7},{7,6},{8,9},{9,8},{10,11... | collective-permute-start | bytes 344072 | tf_op jit(solution)/shard_map/ppermute | solution.py:371
  84.3 1.3 %collective-permute-start.11 = (f32[224,128]{1,0:T(8,128)S(1)}, f32[224,128]{1,0:T(8,128)S(1)}, u32[]{:S(2)}, u32[]{:S(2)}) collective-permute-start(f32[224,128]{1,0:T(8,128)S(1)} %collective-permute-done.10.rest_4_), channel_id=1, source_target_pairs={{0,1},{1,0},{2,3},{3,2},{4,5},{5,4},{6,7},{7,6},{8,9},{9,8},{10,11... | collective-permute-start | bytes 344072 | tf_op jit(solution)/shard_map/ppermute | solution.py:371

commit v6 on v5

--- a/solution.py
+++ b/solution.py
@@ -178,12 +178,19 @@
 
     def add(batch, part, from_ref):
         lanes = slice(part // 2 * LANES, (part // 2 + 1) * LANES)
-        ranks = slice(part % 2 * half, (part % 2 + 1) * half)
-        total = y_ref[ranks, :, lanes]
+        ranks = range(part % 2 * half, (part % 2 + 1) * half)
+        strips = [slice(i, i + ROWS) for i in range(0, rank_i, ROWS)]
+        totals = [[y_ref[r, strip, lanes] for strip in strips] for r in ranks]
         for place in range(BATCH):
-            values = context_held[batch * BATCH + place, ranks, lanes]
-            total = total + values[:, None, :] * from_ref[place, :, lanes][None]
-        y_ref[ranks, :, lanes] = total
+            parts_of = [from_ref[place, strip, lanes] for strip in strips]
+            for i, r in enumerate(ranks):
+                values = context_held[batch * BATCH + place, r : r + 1, lanes]
+                values = jnp.broadcast_to(values, (ROWS, LANES))
+                for j in range(len(strips)):
+                    totals[i][j] = totals[i][j] + values * parts_of[j]
+        for i, r in enumerate(ranks):
+            for strip, total in zip(strips, totals[i]):
+                y_ref[r, strip, lanes] = total
 
     y_ref[...] = jnp.zeros_like(y_ref)
     parts = 2 * users // LANES

time: 92.4 us -> 91.4 us (0.989)
  Pallas kernels: 28.5 us -> 27.4 us
    pallas_call x1, Pallas kernels: 14.3 us -> 13.3 us  [tile_sums(): pl.pallas_call(tiles_kernel, out_shape=out_shape, in_specs=[SMEM] * 3 + [...]
  transfers between devices with their start and end apart: 18 -> 18, of which waited for: 11 -> 11; matrix products, arithmetic and copies ran while one was open for 1% -> 1% of each run, Pallas kernels for 6% -> 7%
where the time goes in v6:
time: 91.4 us; the launch traced here: 91 us
  waiting for transfers between devices  28.7 us (31%)
  Pallas kernels  27.4 us (30%)
  starting transfers between devices  20.1 us (22%)
  blocking collectives  10.5 us (11%)
  local copies, waits for them, and re-layouts  2.89 us (3%)
  between operations  1.4 us (2%)
    ppermute x17, waiting for transfers between devices, swap(): return lax.ppermute(value, 'users', [(i, i ^ mask) for i in range(devices)])  19.8 us
    ppermute x17, starting transfers between devices, swap(): return lax.ppermute(value, 'users', [(i, i ^ mask) for i in range(devices)])  16.5 us
    pallas_call x1, Pallas kernels, tile_sums(): pl.pallas_call(tiles_kernel, out_shape=out_shape, in_specs=[SMEM] * 3 + [...  13.3 us
    all_to_all x1, blocking collectives, body(): lax.all_to_all(requests, 'users', 0, 0, axis_index_groups=sides, tiled=True)  10.5 us
    all_to_all x1, waiting for transfers between devices, body(): lax.all_to_all(found, 'users', 0, 0, axis_index_groups=sides, tiled=True)  8.84 us
    pallas_call x1, Pallas kernels, finish(): pl.pallas_call(functools.partial(finish_kernel, users * devices), out_sha...  6.46 us
    pallas_call x1, Pallas kernels, context_values(): pl.pallas_call(context_kernel, out_shape=jax.ShapeDtypeStruct((tiles, ROW...  3.72 us
    all_to_all x1, starting transfers between devices, body(): lax.all_to_all(found, 'users', 0, 0, axis_index_groups=sides, tiled=True)  3.65 us
  transfers between devices with their start and end apart: 18, of which 11 were waited for; matrix products, arithmetic and copies ran while one was open for 1% of the time, Pallas kernels for 7%

profile of v6, /device:TPU:0, one launch (start us, length us, event | category | flops | bytes accessed | tf_op | source)
XLA Modules:
  0.0 91.0 jit_solution(14814378662291226117)
XLA Ops:
  0.6 4.1 %collective-permute-start = (bf16[16,64,128]{2,1,0:T(8,128)(2,1)}, bf16[16,64,128]{2,1,0:T(8,128)(2,1)S(1)}, u32[]{:S(2)}, u32[]{:S(2)}) collective-permute-start(bf16[16,64,128]{2,1,0:T(8,128)(2,1)} %own_ref.1), channel_id=1, source_target_pairs={{0,16},{1,17},{2,18},{3,19},{4,20},{5,21},{6,22},{7,23},{8,24},{9,... | collective-permute-start | bytes 786440 | tf_op jit(solution)/shard_map/ppermute | solution.py:378
  4.7 2.2 %route.1 = (s32[16,1,128]{2,1,0:T(1,128)S(1)}, s32[64]{0:T(128)S(1)}, bf16[16,64,128]{2,1,0:T(8,128)(2,1)S(1)}) custom-call(s32[1]{0:T(128)} %bitcast.me_ref, s32[64]{0:T(128)} %bitcast.6, s32[64]{0:T(128)} %slot_ref.1, bf16[16,64,128]{2,1,0:T(8,128)(2,1)} %own_ref.1), custom_call_target="tpu_custom_call" | custom-call | tf_op jit(solution)/shard_map/route/pallas_call | solution.py:74
  7.0 10.5 %all_to_all.10.asked_ref = s32[16,1,128]{2,1,0:T(1,128)S(1)} all-to-all(s32[16,1,128]{2,1,0:T(1,128)S(1)} %get-tuple-element.19), channel_id=1, replica_groups={{0,1,2,3,4,5,6,7,8,9,10,11,12,13,14,15},{16,17,18,19,20,21,22,23,24,25,..., dimensions={0} | all-to-all | bytes 16384 | tf_op jit(solution)/shard_map/all_to_all | solution.py:414
  17.4 1.7 %collect.1 = bf16[64,64,128]{2,1,0:T(8,128)(2,1)} custom-call(s32[16,1,128]{2,1,0:T(1,128)S(1)} %all_to_all.10.asked_ref, bf16[16,64,128]{2,1,0:T(8,128)(2,1)S(1)} %get-tuple-element.20.own_ref, bf16[16,64,128]{2,1,0:T(8,128)(2,1)S(1)} %collective-permute-done.mirror_ref), custom_call_target="tpu_custom_call" | custom-call | tf_op jit(solution)/shard_map/collect/pallas_call | solution.py:97
  19.2 3.7 %all-to-all-start.1 = ((bf16[64,64,128]{2,1,0:T(8,128)(2,1)}), bf16[64,64,128]{2,1,0:T(8,128)(2,1)S(1)}, u32[]{:S(2)}, u32[]{:S(2)}) async-start(bf16[64,64,128]{2,1,0:T(8,128)(2,1)} %collect.1), calls=%async_computation.1 | async-start | bytes 2097152 | tf_op jit(solution)/shard_map/all_to_all | solution.py:417
  23.5 0.9 reshape.13
  24.5 0.9 copy-done.1
  25.4 3.7 %contexts.1.context_ref = f32[64,8,512]{2,1,0:T(8,128)S(1)} custom-call(s32[64]{0:T(128)} %cblock_ref, f32[64,8,8]{2,1,0:T(8,128)S(1)} %bitcast.5, s32[64,512]{1,0:T(8,128)S(1)} %copy-done.1), custom_call_target="tpu_custom_call" | custom-call | flops 10000000 | bytes 20000000 | tf_op jit(solution)/shard_map/contexts/pallas_call | solution.py:125
  29.2 1.0 %copy-done = f32[64,8,512]{2,1,0:T(8,128)} copy-done((f32[64,8,512]{2,1,0:T(8,128)}, f32[64,8,512]{2,1,0:T(8,128)S(1)}, u32[]{:S(2)}) %copy-start) | copy-done | bytes 1048600
  30.1 8.8 %all-to-all-done.1.blocks_ref = bf16[64,64,128]{2,1,0:T(8,128)(2,1)S(1)} async-done(((bf16[64,64,128]{2,1,0:T(8,128)(2,1)}), bf16[64,64,128]{2,1,0:T(8,128)(2,1)S(1)}, u32[]{:S(2)}, u32[]{:S(2)}) %all-to-all-start.1) | async-done | bytes 1048608 | tf_op jit(solution)/shard_map/all_to_all | solution.py:417
  39.0 13.3 %tile_sums.1 = (f32[224,128]{1,0:T(8,128)S(1)}, f32[224,128]{1,0:T(8,128)S(1)}, f32[224,128]{1,0:T(8,128)S(1)}, f32[224,128]{1,0:T(8,128)S(1)}, f32[224,128]{1,0...) custom-call(s32[64]{0:T(128)S(1)} %get-tuple-element.18.where_ref, ...), custom_call_target="tpu_custom_call" | custom-call | flops 2000000000 | bytes 12000000 | tf_op jit(solution)/shard_map/tile_sums/pallas_call | solution.py:255
  52.3 0.5 collective-permute-start.4
  52.9 0.4 collective-permute-start.1
  53.3 0.3 collective-permute-done.2
  53.6 1.0 %collective-permute-start.3 = (f32[224,128]{1,0:T(8,128)S(1)}, f32[224,128]{1,0:T(8,128)S(1)}, u32[]{:S(2)}, u32[]{:S(2)}) collective-permute-start(f32[224,128]{1,0:T(8,128)S(1)} %add.28), channel_id=1, source_target_pairs={{0,6},{1,7},{2,4},{3,5},{4,2},{5,3},{6,0},{7,1},{8,14},{9,15},{10,... | collective-permute-start | bytes 344072 | tf_op jit(solution)/shard_map/ppermute | solution.py:378
  54.7 1.4 %collective-permute-start.5 = (f32[224,128]{1,0:T(8,128)S(1)}, f32[224,128]{1,0:T(8,128)S(1)}, u32[]{:S(2)}, u32[]{:S(2)}) collective-permute-start(f32[224,128]{1,0:T(8,128)S(1)} %add.30), channel_id=1, source_target_pairs={{0,2},{1,3},{2,0},{3,1},{4,6},{5,7},{6,4},{7,5},{8,10},{9,11},{10,... | collective-permute-start | bytes 344072 | tf_op jit(solution)/shard_map/ppermute | solution.py:378
  56.1 1.2 %collective-permute-start.7 = (f32[224,128]{1,0:T(8,128)S(1)}, f32[224,128]{1,0:T(8,128)S(1)}, u32[]{:S(2)}, u32[]{:S(2)}) collective-permute-start(f32[224,128]{1,0:T(8,128)S(1)} %add.32), channel_id=1, source_target_pairs={{0,4},{1,5},{2,6},{3,7},{4,0},{5,1},{6,2},{7,3},{8,12},{9,13},{10,... | collective-permute-start | bytes 344072 | tf_op jit(solution)/shard_map/ppermute | solution.py:378
  57.4 3.2 %collective-permute-done.3 = f32[224,128]{1,0:T(8,128)S(1)} collective-permute-done((f32[224,128]{1,0:T(8,128)S(1)}, f32[224,128]{1,0:T(8,128)S(1)}, u32[]{:S(2)}, u32[]{:S(2)}) %collective-permute-start.3) | collective-permute-done | bytes 114720 | tf_op jit(solution)/shard_map/ppermute | solution.py:378
  60.6 1.1 %collective-permute-done.5 = f32[224,128]{1,0:T(8,128)S(1)} collective-permute-done((f32[224,128]{1,0:T(8,128)S(1)}, f32[224,128]{1,0:T(8,128)S(1)}, u32[]{:S(2)}, u32[]{:S(2)}) %collective-permute-start.5) | collective-permute-done | bytes 114720 | tf_op jit(solution)/shard_map/ppermute | solution.py:378
  61.6 0.6 collective-permute-done.7
  62.3 0.7 collective-permute-start.8
  63.0 4.2 %collective-permute-done.8 = f32[224,128]{1,0:T(8,128)S(1)} collective-permute-done((f32[224,128]{1,0:T(8,128)S(1)}, f32[224,128]{1,0:T(8,128)S(1)}, u32[]{:S(2)}, u32[]{:S(2)}) %collective-permute-start.8) | collective-permute-done | bytes 114720 | tf_op jit(solution)/shard_map/ppermute | solution.py:378
  67.2 3.4 %collective-permute-start.9 = (f32[224,128]{1,0:T(8,128)S(1)}, f32[224,128]{1,0:T(8,128)S(1)}, u32[]{:S(2)}, u32[]{:S(2)}) collective-permute-start(f32[224,128]{1,0:T(8,128)S(1)} %add.34), channel_id=1, source_target_pairs={{0,16},{1,17},{2,18},{3,19},{4,20},{5,21},{6,22},{7,23},{8,24},{9,... | collective-permute-start | bytes 344072 | tf_op jit(solution)/shard_map/ppermute | solution.py:378
  70.5 4.3 %collective-permute-done.9 = f32[224,128]{1,0:T(8,128)S(1)} collective-permute-done((f32[224,128]{1,0:T(8,128)S(1)}, f32[224,128]{1,0:T(8,128)S(1)}, u32[]{:S(2)}, u32[]{:S(2)}) %collective-permute-start.9) | collective-permute-done | bytes 114720 | tf_op jit(solution)/shard_map/ppermute | solution.py:378
  74.9 0.8 collective-permute-start.14
  75.6 1.9 %collective-permute-start.12 = (f32[224,128]{1,0:T(8,128)S(1)}, f32[224,128]{1,0:T(8,128)S(1)}, u32[]{:S(2)}, u32[]{:S(2)}) collective-permute-start(f32[224,128]{1,0:T(8,128)S(1)} %add.35.rest_7_), channel_id=1, source_target_pairs={{0,2},{1,3},{2,0},{3,1},{4,6},{5,7},{6,4},{7,5},{8,10},{9,11},{10,... | collective-permute-start | bytes 344072 | tf_op jit(solution)/shard_map/ppermute | solution.py:378
  77.5 0.9 collective-permute-start.10
  78.4 1.7 %collective-permute-done.14.rest_6_ = f32[224,128]{1,0:T(8,128)S(1)} collective-permute-done((f32[224,128]{1,0:T(8,128)S(1)}, f32[224,128]{1,0:T(8,128)S(1)}, u32[]{:S(2)}, u32[]{:S(2)}) %collective-permute-start.14) | collective-permute-done | bytes 114720 | tf_op jit(solution)/shard_map/ppermute | solution.py:378
  80.1 0.8 collective-permute-done.12.rest_5_
  80.9 2.3 %collective-permute-done.10.rest_4_ = f32[224,128]{1,0:T(8,128)S(1)} collective-permute-done((f32[224,128]{1,0:T(8,128)S(1)}, f32[224,128]{1,0:T(8,128)S(1)}, u32[]{:S(2)}, u32[]{:S(2)}) %collective-permute-start.10) | collective-permute-done | bytes 114720 | tf_op jit(solution)/shard_map/ppermute | solution.py:378
  83.3 1.3 %collective-permute-done.11.rest_0_ = f32[224,128]{1,0:T(8,128)S(1)} collective-permute-done((f32[224,128]{1,0:T(8,128)S(1)}, f32[224,128]{1,0:T(8,128)S(1)}, u32[]{:S(2)}, u32[]{:S(2)}) %collective-permute-start.11) | collective-permute-done | bytes 114720 | tf_op jit(solution)/shard_map/ppermute | solution.py:378
  84.6 6.5 %finish.1 = (f32[512,128]{1,0:T(8,128)}, f32[128,512]{1,0:T(8,128)}) custom-call(s32[1]{0:T(128)} %bitcast.me_ref, bf16[512,512]{1,0:T(8,128)(2,1)S(1)} %get-tuple-element.24.high_ref, bf16[512,512]{1,0:T(8,128)(2,1)S(1)} %get-tuple-element.25.low_ref, f32[224,128]{1,0:T(8,128)S(1)} %collective-permute-done.11.rest_0_, ...), custom_call_target="tpu_custom_call" | custom-call | tf_op jit(solution)/shard_map/finish/pallas_call | solution.py:360
  (22 shorter events, 0.4 us)
Async XLA Ops:
  0.6 16.8 %collective-permute-start = (bf16[16,64,128]{2,1,0:T(8,128)(2,1)}, bf16[16,64,128]{2,1,0:T(8,128)(2,1)S(1)}, u32[]{:S(2)}, u32[]{:S(2)}) collective-permute-start(bf16[16,64,128]{2,1,0:T(8,128)(2,1)} %own_ref.1), channel_id=1, source_target_pairs={{0,16},{1,17},{2,18},{3,19},{4,20},{5,21},{6,22},{7,23},{8,24},{9,... | collective-permute-start | bytes 786440 | tf_op jit(solution)/shard_map/ppermute | solution.py:378
  19.2 19.8 %all-to-all-start.1 = ((bf16[64,64,128]{2,1,0:T(8,128)(2,1)}), bf16[64,64,128]{2,1,0:T(8,128)(2,1)S(1)}, u32[]{:S(2)}, u32[]{:S(2)}) async-start(bf16[64,64,128]{2,1,0:T(8,128)(2,1)} %collect.1), calls=%async_computation.1 | async-start | bytes 2097152 | tf_op jit(solution)/shard_map/all_to_all | solution.py:417
  24.5 0.9 copy-start.1
  29.2 1.0 %copy-start = (f32[64,8,512]{2,1,0:T(8,128)}, f32[64,8,512]{2,1,0:T(8,128)S(1)}, u32[]{:S(2)}) copy-start(f32[64,8,512]{2,1,0:T(8,128)S(1)} %contexts.1.context_ref) | copy-start | bytes 3145732
  52.2 1.4 %collective-permute-start.2 = (f32[224,128]{1,0:T(8,128)S(1)}, f32[224,128]{1,0:T(8,128)S(1)}, u32[]{:S(2)}, u32[]{:S(2)}) collective-permute-start(f32[224,128]{1,0:T(8,128)S(1)} %get-tuple-element.29), channel_id=1, source_target_pairs={{0,1},{1,0},{2,3},{3,2},{4,5},{5,4},{6,7},{7,6},{8,9},{9,8},{10,11... | collective-permute-start | bytes 344072 | tf_op jit(solution)/shard_map/ppermute | solution.py:378
  52.3 2.4 %collective-permute-start.4 = (f32[224,128]{1,0:T(8,128)S(1)}, f32[224,128]{1,0:T(8,128)S(1)}, u32[]{:S(2)}, u32[]{:S(2)}) collective-permute-start(f32[224,128]{1,0:T(8,128)S(1)} %get-tuple-element.31), channel_id=1, source_target_pairs={{0,1},{1,0},{2,3},{3,2},{4,5},{5,4},{6,7},{7,6},{8,9},{9,8},{10,11... | collective-permute-start | bytes 344072 | tf_op jit(solution)/shard_map/ppermute | solution.py:378
  52.8 3.3 %collective-permute-start.6 = (f32[224,128]{1,0:T(8,128)S(1)}, f32[224,128]{1,0:T(8,128)S(1)}, u32[]{:S(2)}, u32[]{:S(2)}) collective-permute-start(f32[224,128]{1,0:T(8,128)S(1)} %get-tuple-element.33), channel_id=1, source_target_pairs={{0,1},{1,0},{2,3},{3,2},{4,5},{5,4},{6,7},{7,6},{8,9},{9,8},{10,11... | collective-permute-start | bytes 344072 | tf_op jit(solution)/shard_map/ppermute | solution.py:378
  52.9 4.5 %collective-permute-start.1 = (f32[224,128]{1,0:T(8,128)S(1)}, f32[224,128]{1,0:T(8,128)S(1)}, u32[]{:S(2)}, u32[]{:S(2)}) collective-permute-start(f32[224,128]{1,0:T(8,128)S(1)} %get-tuple-element.27), channel_id=1, source_target_pairs={{0,1},{1,0},{2,3},{3,2},{4,5},{5,4},{6,7},{7,6},{8,9},{9,8},{10,11... | collective-permute-start | bytes 344072 | tf_op jit(solution)/shard_map/ppermute | solution.py:378
  53.6 7.0 %collective-permute-start.3 = (f32[224,128]{1,0:T(8,128)S(1)}, f32[224,128]{1,0:T(8,128)S(1)}, u32[]{:S(2)}, u32[]{:S(2)}) collective-permute-start(f32[224,128]{1,0:T(8,128)S(1)} %add.28), channel_id=1, source_target_pairs={{0,6},{1,7},{2,4},{3,5},{4,2},{5,3},{6,0},{7,1},{8,14},{9,15},{10,... | collective-permute-start | bytes 344072 | tf_op jit(solution)/shard_map/ppermute | solution.py:378
  54.7 7.0 %collective-permute-start.5 = (f32[224,128]{1,0:T(8,128)S(1)}, f32[224,128]{1,0:T(8,128)S(1)}, u32[]{:S(2)}, u32[]{:S(2)}) collective-permute-start(f32[224,128]{1,0:T(8,128)S(1)} %add.30), channel_id=1, source_target_pairs={{0,2},{1,3},{2,0},{3,1},{4,6},{5,7},{6,4},{7,5},{8,10},{9,11},{10,... | collective-permute-start | bytes 344072 | tf_op jit(solution)/shard_map/ppermute | solution.py:378
  56.1 6.1 %collective-permute-start.7 = (f32[224,128]{1,0:T(8,128)S(1)}, f32[224,128]{1,0:T(8,128)S(1)}, u32[]{:S(2)}, u32[]{:S(2)}) collective-permute-start(f32[224,128]{1,0:T(8,128)S(1)} %add.32), channel_id=1, source_target_pairs={{0,4},{1,5},{2,6},{3,7},{4,0},{5,1},{6,2},{7,3},{8,12},{9,13},{10,... | collective-permute-start | bytes 344072 | tf_op jit(solution)/shard_map/ppermute | solution.py:378
  62.3 4.9 %collective-permute-start.8 = (f32[224,128]{1,0:T(8,128)S(1)}, f32[224,128]{1,0:T(8,128)S(1)}, u32[]{:S(2)}, u32[]{:S(2)}) collective-permute-start(f32[224,128]{1,0:T(8,128)S(1)} %add_add_fusion), channel_id=1, source_target_pairs={{0,8},{1,9},{2,10},{3,11},{4,12},{5,13},{6,14},{7,15},{8,0},{9,1},... | collective-permute-start | bytes 344072 | tf_op jit(solution)/shard_map/ppermute | solution.py:378
  67.2 7.7 %collective-permute-start.9 = (f32[224,128]{1,0:T(8,128)S(1)}, f32[224,128]{1,0:T(8,128)S(1)}, u32[]{:S(2)}, u32[]{:S(2)}) collective-permute-start(f32[224,128]{1,0:T(8,128)S(1)} %add.34), channel_id=1, source_target_pairs={{0,16},{1,17},{2,18},{3,19},{4,20},{5,21},{6,22},{7,23},{8,24},{9,... | collective-permute-start | bytes 344072 | tf_op jit(solution)/shard_map/ppermute | solution.py:378
  74.9 5.3 %collective-permute-start.14 = (f32[224,128]{1,0:T(8,128)S(1)}, f32[224,128]{1,0:T(8,128)S(1)}, u32[]{:S(2)}, u32[]{:S(2)}) collective-permute-start(f32[224,128]{1,0:T(8,128)S(1)} %add.35.rest_7_), channel_id=1, source_target_pairs={{0,4},{1,5},{2,6},{3,7},{4,0},{5,1},{6,2},{7,3},{8,12},{9,13},{10,... | collective-permute-start | bytes 344072 | tf_op jit(solution)/shard_map/ppermute | solution.py:378
  75.6 5.3 %collective-permute-start.12 = (f32[224,128]{1,0:T(8,128)S(1)}, f32[224,128]{1,0:T(8,128)S(1)}, u32[]{:S(2)}, u32[]{:S(2)}) collective-permute-start(f32[224,128]{1,0:T(8,128)S(1)} %add.35.rest_7_), channel_id=1, source_target_pairs={{0,2},{1,3},{2,0},{3,1},{4,6},{5,7},{6,4},{7,5},{8,10},{9,11},{10,... | collective-permute-start | bytes 344072 | tf_op jit(solution)/shard_map/ppermute | solution.py:378
  77.5 5.7 %collective-permute-start.10 = (f32[224,128]{1,0:T(8,128)S(1)}, f32[224,128]{1,0:T(8,128)S(1)}, u32[]{:S(2)}, u32[]{:S(2)}) collective-permute-start(f32[224,128]{1,0:T(8,128)S(1)} %add.35.rest_7_), channel_id=1, source_target_pairs={{0,6},{1,7},{2,4},{3,5},{4,2},{5,3},{6,0},{7,1},{8,14},{9,15},{10,... | collective-permute-start | bytes 344072 | tf_op jit(solution)/shard_map/ppermute | solution.py:378
  78.4 4.8 %collective-permute-start.16 = (f32[224,128]{1,0:T(8,128)S(1)}, f32[224,128]{1,0:T(8,128)S(1)}, u32[]{:S(2)}, u32[]{:S(2)}) collective-permute-start(f32[224,128]{1,0:T(8,128)S(1)} %add.35.rest_7_), channel_id=1, source_target_pairs={{0,1},{1,0},{2,3},{3,2},{4,5},{5,4},{6,7},{7,6},{8,9},{9,8},{10,11... | collective-permute-start | bytes 344072 | tf_op jit(solution)/shard_map/ppermute | solution.py:378
  80.1 3.1 %collective-permute-start.15 = (f32[224,128]{1,0:T(8,128)S(1)}, f32[224,128]{1,0:T(8,128)S(1)}, u32[]{:S(2)}, u32[]{:S(2)}) collective-permute-start(f32[224,128]{1,0:T(8,128)S(1)} %collective-permute-done.14.rest_6_), channel_id=1, source_target_pairs={{0,1},{1,0},{2,3},{3,2},{4,5},{5,4},{6,7},{7,6},{8,9},{9,8},{10,11... | collective-permute-start | bytes 344072 | tf_op jit(solution)/shard_map/ppermute | solution.py:378
  80.9 2.3 %collective-permute-start.13 = (f32[224,128]{1,0:T(8,128)S(1)}, f32[224,128]{1,0:T(8,128)S(1)}, u32[]{:S(2)}, u32[]{:S(2)}) collective-permute-start(f32[224,128]{1,0:T(8,128)S(1)} %collective-permute-done.12.rest_5_), channel_id=1, source_target_pairs={{0,1},{1,0},{2,3},{3,2},{4,5},{5,4},{6,7},{7,6},{8,9},{9,8},{10,11... | collective-permute-start | bytes 344072 | tf_op jit(solution)/shard_map/ppermute | solution.py:378
  83.3 1.3 %collective-permute-start.11 = (f32[224,128]{1,0:T(8,128)S(1)}, f32[224,128]{1,0:T(8,128)S(1)}, u32[]{:S(2)}, u32[]{:S(2)}) collective-permute-start(f32[224,128]{1,0:T(8,128)S(1)} %collective-permute-done.10.rest_4_), channel_id=1, source_target_pairs={{0,1},{1,0},{2,3},{3,2},{4,5},{5,4},{6,7},{7,6},{8,9},{9,8},{10,11... | collective-permute-start | bytes 344072 | tf_op jit(solution)/shard_map/ppermute | solution.py:378

commit v7 on v6

--- a/solution.py
+++ b/solution.py
@@ -10,7 +10,6 @@
 CB = 8
 SLOTS = 2
 PLACES = 2 * SLOTS
-HIGH = lax.Precision.HIGHEST
 LANES = 128
 ROWS = 8
 BATCH = 8
@@ -41,6 +40,17 @@
 def split(value):
     high = value.astype(jnp.bfloat16)
     return high, (value - high.astype(jnp.float32)).astype(jnp.bfloat16)
+
+
+def quarters(value):
+    rows, lanes = value.shape[0] // 2, value.shape[1] // 2
+    return (value[:rows, :lanes] + value[:rows, lanes:]) + (value[rows:, :lanes] + value[rows:, lanes:])
+
+
+def thrice(stack, high, low, product):
+    rows = stack.shape[0] // 2
+    first = product(stack, high)
+    return first[:rows] + (first[rows:] + product(stack[:rows], low))
 
 
 def route_kernel(half, me_ref, owner_ref, slot_ref, own_ref, request_ref, where_ref, held_ref, used_ref, sem_ref):
@@ -153,7 +163,7 @@
     where_ref, count_ref, me_ref, blocks_ref, weights_ref, context_ref, basis_ref, *refs
 ):
     piece_refs, refs = refs[: len(PIECES)], refs[len(PIECES) :]
-    high_ref, low_ref, y_ref, pack_ref, even_ref, odd_ref = refs[:6]
+    stack_ref, y_ref, square_ref, pack_ref, even_ref, odd_ref = refs[:6]
     weights_held, context_held, basis_held, weights_sem, context_sem, basis_sem = refs[6:]
     rank_c, rank_i, users = y_ref.shape
     batches = weights_ref.shape[0] // BATCH
@@ -218,25 +228,26 @@
         add(batches - 1, part, odd_ref)
 
     living = lax.broadcasted_iota(jnp.int32, (rank_i, users), 1) < count_ref[0]
+    ranks = rank_c * rank_i
     for r in range(rank_c):
         high, low = split(jnp.where(living, y_ref[r], 0.0))
-        high_ref[r * rank_i : (r + 1) * rank_i] = high
-        low_ref[r * rank_i : (r + 1) * rank_i] = low
-    ranks = rank_c * rank_i
+        stack_ref[r * rank_i : (r + 1) * rank_i] = high
+        stack_ref[ranks + r * rank_i : ranks + (r + 1) * rank_i] = low
+    square_ref[...] = dot_nt(stack_ref[...], stack_ref[:ranks])
+    basis_copy.wait()
+    projection = dot(stack_ref[...], jnp.concatenate(split(basis_held[...]), axis=1))
     groups = ranks // LANES
     place = 0
     for i in range(groups):
         rows = slice(i * LANES, (i + 1) * LANES)
-        strip = dot_nt(high_ref[rows], high_ref[i * LANES :])
-        strip = strip + dot_nt(high_ref[rows], low_ref[i * LANES :])
-        strip = strip + dot_nt(low_ref[rows], high_ref[i * LANES :])
-        for j in range(groups - i):
-            pack_ref[place * LANES : (place + 1) * LANES] = strip[:, j * LANES : (j + 1) * LANES]
+        low_rows = slice(ranks + i * LANES, ranks + (i + 1) * LANES)
+        for j in range(i, groups):
+            lanes = slice(j * LANES, (j + 1) * LANES)
+            low_lanes = slice(ranks + j * LANES, ranks + (j + 1) * LANES)
+            block = square_ref[rows, lanes] + square_ref[low_rows, lanes] + square_ref[low_lanes, rows].T
+            pack_ref[place * LANES : (place + 1) * LANES] = block
             place += 1
-    basis_copy.wait()
-    basis_high, basis_low = split(basis_held[...])
-    projection = dot(high_ref[...], basis_high) + dot(high_ref[...], basis_low) + dot(low_ref[...], basis_high)
-    pack_ref[place * LANES : (place + groups) * LANES] = projection
+    pack_ref[place * LANES : (place + groups) * LANES] = quarters(projection)
     chunk = piece_refs[0].shape[0]
     places = pack_places(me_ref[0])
     for piece, ref in zip(PIECES, piece_refs):
@@ -250,7 +261,7 @@
     ranks = rank_c * rank_i
     rows = pack_rows(ranks)
     out_shape = (jax.ShapeDtypeStruct((rows // CHUNKS, LANES), jnp.float32),) * len(PIECES)
-    out_shape += (jax.ShapeDtypeStruct((ranks, users), jnp.bfloat16),) * 2
+    out_shape += (jax.ShapeDtypeStruct((2 * ranks, users), jnp.bfloat16),)
     held = 3 * weights.size * 2 // (2 * MIB)
     out = pl.pallas_call(
         tiles_kernel,
@@ -259,6 +270,7 @@
         out_specs=(VMEM,) * len(out_shape),
         scratch_shapes=[
             pltpu.VMEM((rank_c, rank_i, users), jnp.float32),
+            pltpu.VMEM((2 * ranks, ranks), jnp.float32),
             pltpu.VMEM((rows, LANES), jnp.float32),
             pltpu.VMEM((BATCH, rank_i, users), jnp.float32),
             pltpu.VMEM((BATCH, rank_i, users), jnp.float32),
@@ -269,11 +281,11 @@
             pltpu.SemaphoreType.DMA,
             pltpu.SemaphoreType.DMA,
         ],
-        compiler_params=limit(8 + held),
+        compiler_params=limit(12 + held),
         cost_estimate=pl.CostEstimate(flops=2 * 10**9, bytes_accessed=12 * 10**6, transcendentals=0),
         name="tile_sums",
     )(where, count, me, blocks, in_hbm(weights), in_hbm(contexts), in_hbm(user_basis))
-    return dict(zip(PIECES, out[:-2])), out[-2], out[-1]
+    return dict(zip(PIECES, out[:-1])), out[-1]
 
 
 def inverse_factor(gram):
@@ -319,59 +331,58 @@
     return jnp.concatenate(right, axis=0)
 
 
-def finish_kernel(total_users, me_ref, high_ref, low_ref, *rest):
+def finish_kernel(total_users, me_ref, stack_ref, *rest):
     piece_refs, (basis_ref, core_out_ref, pack_ref, full_ref) = rest[: len(PIECES)], rest[len(PIECES) :]
     chunk = piece_refs[0].shape[0]
     places = pack_places(me_ref[0])
     for piece, ref in zip(PIECES, piece_refs):
         pack_ref[pl.ds(pl.multiple_of(places[piece] * chunk, ROWS), chunk)] = ref[...]
-    groups = full_ref.shape[0] // LANES
+    ranks = full_ref.shape[1]
+    groups = ranks // LANES
     place = 0
     for i in range(groups):
         for j in range(i, groups):
             block = pack_ref[place * LANES : (place + 1) * LANES]
-            full_ref[i * LANES : (i + 1) * LANES, j * LANES : (j + 1) * LANES] = block
-            if i != j:
-                full_ref[j * LANES : (j + 1) * LANES, i * LANES : (i + 1) * LANES] = block.T
+            for row, lane, part in ((i, j, block), (j, i, block.T))[: 1 if i == j else 2]:
+                lanes = slice(lane * LANES, (lane + 1) * LANES)
+                high, low = split(part)
+                full_ref[row * LANES : (row + 1) * LANES, lanes] = high
+                full_ref[ranks + row * LANES : ranks + (row + 1) * LANES, lanes] = low
             place += 1
     projection = pack_ref[place * LANES : (place + groups) * LANES]
+    crossed = quarters(dot(full_ref[...], jnp.concatenate(split(projection), axis=1)))
+    crossed_high, crossed_low = split(crossed)
     turned = jnp.concatenate(
         [projection[i * LANES : (i + 1) * LANES].T for i in range(groups)], axis=1
     )
-    turned_high, turned_low = split(turned)
-    full_high, full_low = split(full_ref[...])
-    crossed = dot(turned_high, full_high) + dot(turned_high, full_low) + dot(turned_low, full_high)
-    gram = jnp.dot(crossed, projection, precision=HIGH, preferred_element_type=jnp.float32)
-    projected = (
-        dot(turned_high, high_ref[...]) + dot(turned_high, low_ref[...]) + dot(turned_low, high_ref[...])
-    )
-    inverse = inverse_factor(gram)
+    turned_stack = jnp.concatenate(split(turned), axis=0)
+    gram = quarters(dot(turned_stack, jnp.concatenate([crossed_high, crossed_low], axis=1)))
+    projected_high, projected_low = split(thrice(turned_stack, stack_ref[:ranks], stack_ref[ranks:], dot))
+    inverse_stack = jnp.concatenate(split(inverse_factor(gram)), axis=0)
     root = total_users ** 0.5
-    scaled = jnp.dot(inverse * root, projected, precision=HIGH, preferred_element_type=jnp.float32)
+    scaled = thrice(inverse_stack, projected_high, projected_low, dot) * root
     for i in range(scaled.shape[1] // LANES):
         basis_ref[i * LANES : (i + 1) * LANES] = scaled[:, i * LANES : (i + 1) * LANES].T
-    core_out_ref[...] = jnp.dot(
-        inverse * (1.0 / root), crossed, precision=HIGH, preferred_element_type=jnp.float32
-    )
-
-
-def finish(me, high, low, pieces, devices):
-    ranks, users = high.shape
+    core_out_ref[...] = thrice(inverse_stack, crossed_high, crossed_low, dot_nt) * (1.0 / root)
+
+
+def finish(me, stack, pieces, devices):
+    ranks, users = stack.shape[0] // 2, stack.shape[1]
     return pl.pallas_call(
         functools.partial(finish_kernel, users * devices),
         out_shape=(
             jax.ShapeDtypeStruct((users, LANES), jnp.float32),
             jax.ShapeDtypeStruct((LANES, ranks), jnp.float32),
         ),
-        in_specs=[SMEM] + [VMEM] * (2 + len(PIECES)),
+        in_specs=[SMEM] + [VMEM] * (1 + len(PIECES)),
         out_specs=(VMEM, VMEM),
         scratch_shapes=[
             pltpu.VMEM((pack_rows(ranks), LANES), jnp.float32),
-            pltpu.VMEM((ranks, ranks), jnp.float32),
+            pltpu.VMEM((2 * ranks, ranks), jnp.bfloat16),
         ],
         compiler_params=limit(16),
         name="finish",
-    )(me, high, low, *[pieces[piece] for piece in PIECES])
+    )(me, stack, *[pieces[piece] for piece in PIECES])
 
 
 def swap(value, mask, devices):
@@ -418,11 +429,11 @@
 
     table = factors.astype(jnp.float32).reshape(rank_c, -1, CB).transpose(1, 0, 2)
     contexts = context_values(cblock, table, tile_context)
-    pieces, high, low = tile_sums(
+    pieces, stack = tile_sums(
         where, user_counts, me, blocks, tile_weights, contexts, user_basis
     )
     pieces = spread_pieces(reduce_pieces(pieces, devices), devices)
-    return finish(me, high, low, pieces, devices)
+    return finish(me, stack, pieces, devices)
 
 
 def solution(mesh):

time: 91.4 us -> 91.2 us (level)
  no operation moved by 1% of the time
where the time goes in v7:
time: 91.2 us; the launch traced here: 90.9 us
  waiting for transfers between devices  28.7 us (31%)
  Pallas kernels  27.2 us (30%)
  starting transfers between devices  20.1 us (22%)
  blocking collectives  10.5 us (12%)
  local copies, waits for them, and re-layouts  2.89 us (3%)
  between operations  1.39 us (2%)
    ppermute x17, waiting for transfers between devices, swap(): return lax.ppermute(value, 'users', [(i, i ^ mask) for i in range(devices)])  19.8 us
    ppermute x17, starting transfers between devices, swap(): return lax.ppermute(value, 'users', [(i, i ^ mask) for i in range(devices)])  16.5 us
    pallas_call x1, Pallas kernels, tile_sums(): pl.pallas_call(tiles_kernel, out_shape=out_shape, in_specs=[SMEM] * 3 + [...  13.1 us
    all_to_all x1, blocking collectives, body(): lax.all_to_all(requests, 'users', 0, 0, axis_index_groups=sides, tiled=True)  10.5 us
    all_to_all x1, waiting for transfers between devices, body(): lax.all_to_all(found, 'users', 0, 0, axis_index_groups=sides, tiled=True)  8.84 us
    pallas_call x1, Pallas kernels, finish(): pl.pallas_call(functools.partial(finish_kernel, users * devices), out_sha...  6.42 us
    pallas_call x1, Pallas kernels, context_values(): pl.pallas_call(context_kernel, out_shape=jax.ShapeDtypeStruct((tiles, ROW...  3.72 us
    all_to_all x1, starting transfers between devices, body(): lax.all_to_all(found, 'users', 0, 0, axis_index_groups=sides, tiled=True)  3.65 us
  transfers between devices with their start and end apart: 18, of which 11 were waited for; matrix products, arithmetic and copies ran while one was open for 1% of the time, Pallas kernels for 7%

profile of v7, /device:TPU:0, one launch (start us, length us, event | category | flops | bytes accessed | tf_op | source)
XLA Modules:
  0.0 90.9 jit_solution(6367625341950519906)
XLA Ops:
  0.6 4.1 %collective-permute-start = (bf16[16,64,128]{2,1,0:T(8,128)(2,1)}, bf16[16,64,128]{2,1,0:T(8,128)(2,1)S(1)}, u32[]{:S(2)}, u32[]{:S(2)}) collective-permute-start(bf16[16,64,128]{2,1,0:T(8,128)(2,1)} %own_ref.1), channel_id=1, source_target_pairs={{0,16},{1,17},{2,18},{3,19},{4,20},{5,21},{6,22},{7,23},{8,24},{9,... | collective-permute-start | bytes 786440 | tf_op jit(solution)/shard_map/ppermute | solution.py:389
  4.7 2.2 %route.1 = (s32[16,1,128]{2,1,0:T(1,128)S(1)}, s32[64]{0:T(128)S(1)}, bf16[16,64,128]{2,1,0:T(8,128)(2,1)S(1)}) custom-call(s32[1]{0:T(128)} %bitcast.me_ref, s32[64]{0:T(128)} %bitcast.6, s32[64]{0:T(128)} %slot_ref.1, bf16[16,64,128]{2,1,0:T(8,128)(2,1)} %own_ref.1), custom_call_target="tpu_custom_call" | custom-call | tf_op jit(solution)/shard_map/route/pallas_call | solution.py:84
  7.0 10.5 %all_to_all.10.asked_ref = s32[16,1,128]{2,1,0:T(1,128)S(1)} all-to-all(s32[16,1,128]{2,1,0:T(1,128)S(1)} %get-tuple-element.18), channel_id=1, replica_groups={{0,1,2,3,4,5,6,7,8,9,10,11,12,13,14,15},{16,17,18,19,20,21,22,23,24,25,..., dimensions={0} | all-to-all | bytes 16384 | tf_op jit(solution)/shard_map/all_to_all | solution.py:425
  17.4 1.7 %collect.1 = bf16[64,64,128]{2,1,0:T(8,128)(2,1)} custom-call(s32[16,1,128]{2,1,0:T(1,128)S(1)} %all_to_all.10.asked_ref, bf16[16,64,128]{2,1,0:T(8,128)(2,1)S(1)} %get-tuple-element.19.own_ref, bf16[16,64,128]{2,1,0:T(8,128)(2,1)S(1)} %collective-permute-done.mirror_ref), custom_call_target="tpu_custom_call" | custom-call | tf_op jit(solution)/shard_map/collect/pallas_call | solution.py:107
  19.2 3.7 %all-to-all-start.1 = ((bf16[64,64,128]{2,1,0:T(8,128)(2,1)}), bf16[64,64,128]{2,1,0:T(8,128)(2,1)S(1)}, u32[]{:S(2)}, u32[]{:S(2)}) async-start(bf16[64,64,128]{2,1,0:T(8,128)(2,1)} %collect.1), calls=%async_computation.1 | async-start | bytes 2097152 | tf_op jit(solution)/shard_map/all_to_all | solution.py:428
  23.5 0.9 reshape.13
  24.5 0.9 copy-done.1
  25.4 3.7 %contexts.1.context_ref = f32[64,8,512]{2,1,0:T(8,128)S(1)} custom-call(s32[64]{0:T(128)} %cblock_ref, f32[64,8,8]{2,1,0:T(8,128)S(1)} %bitcast.5, s32[64,512]{1,0:T(8,128)S(1)} %copy-done.1), custom_call_target="tpu_custom_call" | custom-call | flops 10000000 | bytes 20000000 | tf_op jit(solution)/shard_map/contexts/pallas_call | solution.py:135
  29.2 1.0 %copy-done = f32[64,8,512]{2,1,0:T(8,128)} copy-done((f32[64,8,512]{2,1,0:T(8,128)}, f32[64,8,512]{2,1,0:T(8,128)S(1)}, u32[]{:S(2)}) %copy-start) | copy-done | bytes 1048600
  30.1 8.8 %all-to-all-done.1.blocks_ref = bf16[64,64,128]{2,1,0:T(8,128)(2,1)S(1)} async-done(((bf16[64,64,128]{2,1,0:T(8,128)(2,1)}), bf16[64,64,128]{2,1,0:T(8,128)(2,1)S(1)}, u32[]{:S(2)}, u32[]{:S(2)}) %all-to-all-start.1) | async-done | bytes 1048608 | tf_op jit(solution)/shard_map/all_to_all | solution.py:428
  39.0 13.1 %tile_sums.1 = (f32[224,128]{1,0:T(8,128)S(1)}, f32[224,128]{1,0:T(8,128)S(1)}, f32[224,128]{1,0:T(8,128)S(1)}, f32[224,128]{1,0:T(8,128)S(1)}, f32[224,128]{1,0...) custom-call(s32[64]{0:T(128)S(1)} %get-tuple-element.17.where_ref, ...), custom_call_target="tpu_custom_call" | custom-call | flops 2000000000 | bytes 12000000 | tf_op jit(solution)/shard_map/tile_sums/pallas_call | solution.py:266
  52.2 0.5 collective-permute-start.4
  52.7 0.4 collective-permute-start.1
  53.2 0.3 collective-permute-done.2
  53.5 1.0 %collective-permute-start.3 = (f32[224,128]{1,0:T(8,128)S(1)}, f32[224,128]{1,0:T(8,128)S(1)}, u32[]{:S(2)}, u32[]{:S(2)}) collective-permute-start(f32[224,128]{1,0:T(8,128)S(1)} %add.28), channel_id=1, source_target_pairs={{0,6},{1,7},{2,4},{3,5},{4,2},{5,3},{6,0},{7,1},{8,14},{9,15},{10,... | collective-permute-start | bytes 344072 | tf_op jit(solution)/shard_map/ppermute | solution.py:389
  54.5 1.4 %collective-permute-start.5 = (f32[224,128]{1,0:T(8,128)S(1)}, f32[224,128]{1,0:T(8,128)S(1)}, u32[]{:S(2)}, u32[]{:S(2)}) collective-permute-start(f32[224,128]{1,0:T(8,128)S(1)} %add.30), channel_id=1, source_target_pairs={{0,2},{1,3},{2,0},{3,1},{4,6},{5,7},{6,4},{7,5},{8,10},{9,11},{10,... | collective-permute-start | bytes 344072 | tf_op jit(solution)/shard_map/ppermute | solution.py:389
  56.0 1.2 %collective-permute-start.7 = (f32[224,128]{1,0:T(8,128)S(1)}, f32[224,128]{1,0:T(8,128)S(1)}, u32[]{:S(2)}, u32[]{:S(2)}) collective-permute-start(f32[224,128]{1,0:T(8,128)S(1)} %add.32), channel_id=1, source_target_pairs={{0,4},{1,5},{2,6},{3,7},{4,0},{5,1},{6,2},{7,3},{8,12},{9,13},{10,... | collective-permute-start | bytes 344072 | tf_op jit(solution)/shard_map/ppermute | solution.py:389
  57.2 3.2 %collective-permute-done.3 = f32[224,128]{1,0:T(8,128)S(1)} collective-permute-done((f32[224,128]{1,0:T(8,128)S(1)}, f32[224,128]{1,0:T(8,128)S(1)}, u32[]{:S(2)}, u32[]{:S(2)}) %collective-permute-start.3) | collective-permute-done | bytes 114720 | tf_op jit(solution)/shard_map/ppermute | solution.py:389
  60.5 1.1 %collective-permute-done.5 = f32[224,128]{1,0:T(8,128)S(1)} collective-permute-done((f32[224,128]{1,0:T(8,128)S(1)}, f32[224,128]{1,0:T(8,128)S(1)}, u32[]{:S(2)}, u32[]{:S(2)}) %collective-permute-start.5) | collective-permute-done | bytes 114720 | tf_op jit(solution)/shard_map/ppermute | solution.py:389
  61.5 0.6 collective-permute-done.7
  62.2 0.7 collective-permute-start.8
  62.8 4.2 %collective-permute-done.8 = f32[224,128]{1,0:T(8,128)S(1)} collective-permute-done((f32[224,128]{1,0:T(8,128)S(1)}, f32[224,128]{1,0:T(8,128)S(1)}, u32[]{:S(2)}, u32[]{:S(2)}) %collective-permute-start.8) | collective-permute-done | bytes 114720 | tf_op jit(solution)/shard_map/ppermute | solution.py:389
  67.0 3.4 %collective-permute-start.9 = (f32[224,128]{1,0:T(8,128)S(1)}, f32[224,128]{1,0:T(8,128)S(1)}, u32[]{:S(2)}, u32[]{:S(2)}) collective-permute-start(f32[224,128]{1,0:T(8,128)S(1)} %add.34), channel_id=1, source_target_pairs={{0,16},{1,17},{2,18},{3,19},{4,20},{5,21},{6,22},{7,23},{8,24},{9,... | collective-permute-start | bytes 344072 | tf_op jit(solution)/shard_map/ppermute | solution.py:389
  70.4 4.3 %collective-permute-done.9 = f32[224,128]{1,0:T(8,128)S(1)} collective-permute-done((f32[224,128]{1,0:T(8,128)S(1)}, f32[224,128]{1,0:T(8,128)S(1)}, u32[]{:S(2)}, u32[]{:S(2)}) %collective-permute-start.9) | collective-permute-done | bytes 114720 | tf_op jit(solution)/shard_map/ppermute | solution.py:389
  74.7 0.8 collective-permute-start.14
  75.5 1.9 %collective-permute-start.12 = (f32[224,128]{1,0:T(8,128)S(1)}, f32[224,128]{1,0:T(8,128)S(1)}, u32[]{:S(2)}, u32[]{:S(2)}) collective-permute-start(f32[224,128]{1,0:T(8,128)S(1)} %add.35.rest_7_), channel_id=1, source_target_pairs={{0,2},{1,3},{2,0},{3,1},{4,6},{5,7},{6,4},{7,5},{8,10},{9,11},{10,... | collective-permute-start | bytes 344072 | tf_op jit(solution)/shard_map/ppermute | solution.py:389
  77.4 0.9 collective-permute-start.10
  78.3 1.7 %collective-permute-done.14.rest_6_ = f32[224,128]{1,0:T(8,128)S(1)} collective-permute-done((f32[224,128]{1,0:T(8,128)S(1)}, f32[224,128]{1,0:T(8,128)S(1)}, u32[]{:S(2)}, u32[]{:S(2)}) %collective-permute-start.14) | collective-permute-done | bytes 114720 | tf_op jit(solution)/shard_map/ppermute | solution.py:389
  80.0 0.8 collective-permute-done.12.rest_5_
  80.8 2.3 %collective-permute-done.10.rest_4_ = f32[224,128]{1,0:T(8,128)S(1)} collective-permute-done((f32[224,128]{1,0:T(8,128)S(1)}, f32[224,128]{1,0:T(8,128)S(1)}, u32[]{:S(2)}, u32[]{:S(2)}) %collective-permute-start.10) | collective-permute-done | bytes 114720 | tf_op jit(solution)/shard_map/ppermute | solution.py:389
  83.1 1.3 %collective-permute-done.11.rest_0_ = f32[224,128]{1,0:T(8,128)S(1)} collective-permute-done((f32[224,128]{1,0:T(8,128)S(1)}, f32[224,128]{1,0:T(8,128)S(1)}, u32[]{:S(2)}, u32[]{:S(2)}) %collective-permute-start.11) | collective-permute-done | bytes 114720 | tf_op jit(solution)/shard_map/ppermute | solution.py:389
  84.5 6.4 %finish.1 = (f32[512,128]{1,0:T(8,128)}, f32[128,512]{1,0:T(8,128)}) custom-call(s32[1]{0:T(128)} %bitcast.me_ref, bf16[1024,512]{1,0:T(8,128)(2,1)S(1)} %get-tuple-element.23.stack_ref, f32[224,128]{1,0:T(8,128)S(1)} %collective-permute-done.11.rest_0_, f32[224,128]{1,0:T(8,128)S(1)} %collective-permute-done.13.rest_1_, ...), custom_call_target="tpu_custom_call" | custom-call | tf_op jit(solution)/shard_map/finish/pallas_call | solution.py:371
  (22 shorter events, 0.5 us)
Async XLA Ops:
  0.6 16.8 %collective-permute-start = (bf16[16,64,128]{2,1,0:T(8,128)(2,1)}, bf16[16,64,128]{2,1,0:T(8,128)(2,1)S(1)}, u32[]{:S(2)}, u32[]{:S(2)}) collective-permute-start(bf16[16,64,128]{2,1,0:T(8,128)(2,1)} %own_ref.1), channel_id=1, source_target_pairs={{0,16},{1,17},{2,18},{3,19},{4,20},{5,21},{6,22},{7,23},{8,24},{9,... | collective-permute-start | bytes 786440 | tf_op jit(solution)/shard_map/ppermute | solution.py:389
  19.2 19.8 %all-to-all-start.1 = ((bf16[64,64,128]{2,1,0:T(8,128)(2,1)}), bf16[64,64,128]{2,1,0:T(8,128)(2,1)S(1)}, u32[]{:S(2)}, u32[]{:S(2)}) async-start(bf16[64,64,128]{2,1,0:T(8,128)(2,1)} %collect.1), calls=%async_computation.1 | async-start | bytes 2097152 | tf_op jit(solution)/shard_map/all_to_all | solution.py:428
  24.5 0.9 copy-start.1
  29.1 1.0 %copy-start = (f32[64,8,512]{2,1,0:T(8,128)}, f32[64,8,512]{2,1,0:T(8,128)S(1)}, u32[]{:S(2)}) copy-start(f32[64,8,512]{2,1,0:T(8,128)S(1)} %contexts.1.context_ref) | copy-start | bytes 3145732
  52.1 1.4 %collective-permute-start.2 = (f32[224,128]{1,0:T(8,128)S(1)}, f32[224,128]{1,0:T(8,128)S(1)}, u32[]{:S(2)}, u32[]{:S(2)}) collective-permute-start(f32[224,128]{1,0:T(8,128)S(1)} %get-tuple-element.27), channel_id=1, source_target_pairs={{0,1},{1,0},{2,3},{3,2},{4,5},{5,4},{6,7},{7,6},{8,9},{9,8},{10,11... | collective-permute-start | bytes 344072 | tf_op jit(solution)/shard_map/ppermute | solution.py:389
  52.2 2.4 %collective-permute-start.4 = (f32[224,128]{1,0:T(8,128)S(1)}, f32[224,128]{1,0:T(8,128)S(1)}, u32[]{:S(2)}, u32[]{:S(2)}) collective-permute-start(f32[224,128]{1,0:T(8,128)S(1)} %get-tuple-element.29), channel_id=1, source_target_pairs={{0,1},{1,0},{2,3},{3,2},{4,5},{5,4},{6,7},{7,6},{8,9},{9,8},{10,11... | collective-permute-start | bytes 344072 | tf_op jit(solution)/shard_map/ppermute | solution.py:389
  52.7 3.3 %collective-permute-start.6 = (f32[224,128]{1,0:T(8,128)S(1)}, f32[224,128]{1,0:T(8,128)S(1)}, u32[]{:S(2)}, u32[]{:S(2)}) collective-permute-start(f32[224,128]{1,0:T(8,128)S(1)} %get-tuple-element.31), channel_id=1, source_target_pairs={{0,1},{1,0},{2,3},{3,2},{4,5},{5,4},{6,7},{7,6},{8,9},{9,8},{10,11... | collective-permute-start | bytes 344072 | tf_op jit(solution)/shard_map/ppermute | solution.py:389
  52.7 4.5 %collective-permute-start.1 = (f32[224,128]{1,0:T(8,128)S(1)}, f32[224,128]{1,0:T(8,128)S(1)}, u32[]{:S(2)}, u32[]{:S(2)}) collective-permute-start(f32[224,128]{1,0:T(8,128)S(1)} %get-tuple-element.25), channel_id=1, source_target_pairs={{0,1},{1,0},{2,3},{3,2},{4,5},{5,4},{6,7},{7,6},{8,9},{9,8},{10,11... | collective-permute-start | bytes 344072 | tf_op jit(solution)/shard_map/ppermute | solution.py:389
  53.5 7.0 %collective-permute-start.3 = (f32[224,128]{1,0:T(8,128)S(1)}, f32[224,128]{1,0:T(8,128)S(1)}, u32[]{:S(2)}, u32[]{:S(2)}) collective-permute-start(f32[224,128]{1,0:T(8,128)S(1)} %add.28), channel_id=1, source_target_pairs={{0,6},{1,7},{2,4},{3,5},{4,2},{5,3},{6,0},{7,1},{8,14},{9,15},{10,... | collective-permute-start | bytes 344072 | tf_op jit(solution)/shard_map/ppermute | solution.py:389
  54.5 7.0 %collective-permute-start.5 = (f32[224,128]{1,0:T(8,128)S(1)}, f32[224,128]{1,0:T(8,128)S(1)}, u32[]{:S(2)}, u32[]{:S(2)}) collective-permute-start(f32[224,128]{1,0:T(8,128)S(1)} %add.30), channel_id=1, source_target_pairs={{0,2},{1,3},{2,0},{3,1},{4,6},{5,7},{6,4},{7,5},{8,10},{9,11},{10,... | collective-permute-start | bytes 344072 | tf_op jit(solution)/shard_map/ppermute | solution.py:389
  56.0 6.1 %collective-permute-start.7 = (f32[224,128]{1,0:T(8,128)S(1)}, f32[224,128]{1,0:T(8,128)S(1)}, u32[]{:S(2)}, u32[]{:S(2)}) collective-permute-start(f32[224,128]{1,0:T(8,128)S(1)} %add.32), channel_id=1, source_target_pairs={{0,4},{1,5},{2,6},{3,7},{4,0},{5,1},{6,2},{7,3},{8,12},{9,13},{10,... | collective-permute-start | bytes 344072 | tf_op jit(solution)/shard_map/ppermute | solution.py:389
  62.2 4.9 %collective-permute-start.8 = (f32[224,128]{1,0:T(8,128)S(1)}, f32[224,128]{1,0:T(8,128)S(1)}, u32[]{:S(2)}, u32[]{:S(2)}) collective-permute-start(f32[224,128]{1,0:T(8,128)S(1)} %add_add_fusion), channel_id=1, source_target_pairs={{0,8},{1,9},{2,10},{3,11},{4,12},{5,13},{6,14},{7,15},{8,0},{9,1},... | collective-permute-start | bytes 344072 | tf_op jit(solution)/shard_map/ppermute | solution.py:389
  67.0 7.7 %collective-permute-start.9 = (f32[224,128]{1,0:T(8,128)S(1)}, f32[224,128]{1,0:T(8,128)S(1)}, u32[]{:S(2)}, u32[]{:S(2)}) collective-permute-start(f32[224,128]{1,0:T(8,128)S(1)} %add.34), channel_id=1, source_target_pairs={{0,16},{1,17},{2,18},{3,19},{4,20},{5,21},{6,22},{7,23},{8,24},{9,... | collective-permute-start | bytes 344072 | tf_op jit(solution)/shard_map/ppermute | solution.py:389
  74.7 5.3 %collective-permute-start.14 = (f32[224,128]{1,0:T(8,128)S(1)}, f32[224,128]{1,0:T(8,128)S(1)}, u32[]{:S(2)}, u32[]{:S(2)}) collective-permute-start(f32[224,128]{1,0:T(8,128)S(1)} %add.35.rest_7_), channel_id=1, source_target_pairs={{0,4},{1,5},{2,6},{3,7},{4,0},{5,1},{6,2},{7,3},{8,12},{9,13},{10,... | collective-permute-start | bytes 344072 | tf_op jit(solution)/shard_map/ppermute | solution.py:389
  75.5 5.3 %collective-permute-start.12 = (f32[224,128]{1,0:T(8,128)S(1)}, f32[224,128]{1,0:T(8,128)S(1)}, u32[]{:S(2)}, u32[]{:S(2)}) collective-permute-start(f32[224,128]{1,0:T(8,128)S(1)} %add.35.rest_7_), channel_id=1, source_target_pairs={{0,2},{1,3},{2,0},{3,1},{4,6},{5,7},{6,4},{7,5},{8,10},{9,11},{10,... | collective-permute-start | bytes 344072 | tf_op jit(solution)/shard_map/ppermute | solution.py:389
  77.4 5.7 %collective-permute-start.10 = (f32[224,128]{1,0:T(8,128)S(1)}, f32[224,128]{1,0:T(8,128)S(1)}, u32[]{:S(2)}, u32[]{:S(2)}) collective-permute-start(f32[224,128]{1,0:T(8,128)S(1)} %add.35.rest_7_), channel_id=1, source_target_pairs={{0,6},{1,7},{2,4},{3,5},{4,2},{5,3},{6,0},{7,1},{8,14},{9,15},{10,... | collective-permute-start | bytes 344072 | tf_op jit(solution)/shard_map/ppermute | solution.py:389
  78.3 4.8 %collective-permute-start.16 = (f32[224,128]{1,0:T(8,128)S(1)}, f32[224,128]{1,0:T(8,128)S(1)}, u32[]{:S(2)}, u32[]{:S(2)}) collective-permute-start(f32[224,128]{1,0:T(8,128)S(1)} %add.35.rest_7_), channel_id=1, source_target_pairs={{0,1},{1,0},{2,3},{3,2},{4,5},{5,4},{6,7},{7,6},{8,9},{9,8},{10,11... | collective-permute-start | bytes 344072 | tf_op jit(solution)/shard_map/ppermute | solution.py:389
  80.0 3.1 %collective-permute-start.15 = (f32[224,128]{1,0:T(8,128)S(1)}, f32[224,128]{1,0:T(8,128)S(1)}, u32[]{:S(2)}, u32[]{:S(2)}) collective-permute-start(f32[224,128]{1,0:T(8,128)S(1)} %collective-permute-done.14.rest_6_), channel_id=1, source_target_pairs={{0,1},{1,0},{2,3},{3,2},{4,5},{5,4},{6,7},{7,6},{8,9},{9,8},{10,11... | collective-permute-start | bytes 344072 | tf_op jit(solution)/shard_map/ppermute | solution.py:389
  80.8 2.3 %collective-permute-start.13 = (f32[224,128]{1,0:T(8,128)S(1)}, f32[224,128]{1,0:T(8,128)S(1)}, u32[]{:S(2)}, u32[]{:S(2)}) collective-permute-start(f32[224,128]{1,0:T(8,128)S(1)} %collective-permute-done.12.rest_5_), channel_id=1, source_target_pairs={{0,1},{1,0},{2,3},{3,2},{4,5},{5,4},{6,7},{7,6},{8,9},{9,8},{10,11... | collective-permute-start | bytes 344072 | tf_op jit(solution)/shard_map/ppermute | solution.py:389
  83.1 1.3 %collective-permute-start.11 = (f32[224,128]{1,0:T(8,128)S(1)}, f32[224,128]{1,0:T(8,128)S(1)}, u32[]{:S(2)}, u32[]{:S(2)}) collective-permute-start(f32[224,128]{1,0:T(8,128)S(1)} %collective-permute-done.10.rest_4_), channel_id=1, source_target_pairs={{0,1},{1,0},{2,3},{3,2},{4,5},{5,4},{6,7},{7,6},{8,9},{9,8},{10,11... | collective-permute-start | bytes 344072 | tf_op jit(solution)/shard_map/ppermute | solution.py:389

commit v8 on v7

--- a/solution.py
+++ b/solution.py
@@ -163,8 +163,8 @@
     where_ref, count_ref, me_ref, blocks_ref, weights_ref, context_ref, basis_ref, *refs
 ):
     piece_refs, refs = refs[: len(PIECES)], refs[len(PIECES) :]
-    stack_ref, y_ref, square_ref, pack_ref, even_ref, odd_ref = refs[:6]
-    weights_held, context_held, basis_held, weights_sem, context_sem, basis_sem = refs[6:]
+    stack_ref, y_ref, square_ref, pack_ref, product_ref = refs[:5]
+    weights_held, context_held, basis_held, weights_sem, context_sem, basis_sem = refs[5:]
     rank_c, rank_i, users = y_ref.shape
     batches = weights_ref.shape[0] // BATCH
     half = rank_c // 2
@@ -181,18 +181,15 @@
     basis_copy = pltpu.make_async_copy(basis_ref, basis_held, basis_sem)
     basis_copy.start()
 
-    def multiply(batch, place, into_ref):
-        tile = batch * BATCH + place
+    def multiply(tile):
         product = dot(blocks_ref[where_ref[tile]], weights_held[tile])
-        into_ref[place] = product.astype(jnp.bfloat16).astype(jnp.float32)
-
-    def add(batch, part, from_ref):
-        lanes = slice(part // 2 * LANES, (part // 2 + 1) * LANES)
-        ranks = range(part % 2 * half, (part % 2 + 1) * half)
+        return product.astype(jnp.bfloat16).astype(jnp.float32)
+
+    def add(batch, bank, lanes, ranks):
         strips = [slice(i, i + ROWS) for i in range(0, rank_i, ROWS)]
         totals = [[y_ref[r, strip, lanes] for strip in strips] for r in ranks]
         for place in range(BATCH):
-            parts_of = [from_ref[place, strip, lanes] for strip in strips]
+            parts_of = [product_ref[bank, place, strip, lanes] for strip in strips]
             for i, r in enumerate(ranks):
                 values = context_held[batch * BATCH + place, r : r + 1, lanes]
                 values = jnp.broadcast_to(values, (ROWS, LANES))
@@ -203,29 +200,35 @@
                 y_ref[r, strip, lanes] = total
 
     y_ref[...] = jnp.zeros_like(y_ref)
-    parts = 2 * users // LANES
     weights_copy(0).wait()
-    for place in range(BATCH):
-        multiply(0, place, even_ref)
+
+    def first(place, _):
+        product_ref[0, place] = multiply(place)
+        return 0
+
+    lax.fori_loop(0, BATCH, first, 0, unroll=2)
     contexts_copy.wait()
-
-    def turn(batch, from_ref, into_ref):
-        weights_copy(batch + 1).wait()
-        for part in range(max(parts, BATCH)):
-            if part < BATCH:
-                multiply(batch + 1, part, into_ref)
-            if part < parts:
-                add(batch, part, from_ref)
-
-    def pair(index, _):
-        turn(2 * index, even_ref, odd_ref)
-        turn(2 * index + 1, odd_ref, even_ref)
-        return 0
-
-    lax.fori_loop(0, batches // 2 - 1, pair, 0)
-    turn(batches - 2, even_ref, odd_ref)
-    for part in range(parts):
-        add(batches - 1, part, odd_ref)
+    turns = users // LANES
+    share = BATCH // turns
+
+    def turn(index, _):
+        batch, lane = index // turns, lax.rem(index, turns)
+        bank = lax.rem(batch, 2)
+
+        @pl.when(jnp.logical_and(lane == 0, batch + 1 < batches))
+        def _():
+            weights_copy(batch + 1).wait()
+
+        start = jnp.minimum(batch + 1, batches - 1) * BATCH + lane * share
+        products = [multiply(start + i) for i in range(share)]
+        lanes = pl.ds(pl.multiple_of(lane * LANES, LANES), LANES)
+        add(batch, bank, lanes, range(half))
+        add(batch, bank, lanes, range(half, rank_c))
+        for i in range(share):
+            product_ref[1 - bank, lane * share + i] = products[i]
+        return 0
+
+    lax.fori_loop(0, batches * turns, turn, 0)
 
     living = lax.broadcasted_iota(jnp.int32, (rank_i, users), 1) < count_ref[0]
     ranks = rank_c * rank_i
@@ -272,8 +275,7 @@
             pltpu.VMEM((rank_c, rank_i, users), jnp.float32),
             pltpu.VMEM((2 * ranks, ranks), jnp.float32),
             pltpu.VMEM((rows, LANES), jnp.float32),
-            pltpu.VMEM((BATCH, rank_i, users), jnp.float32),
-            pltpu.VMEM((BATCH, rank_i, users), jnp.float32),
+            pltpu.VMEM((2, BATCH, rank_i, users), jnp.float32),
             pltpu.VMEM(weights.shape, weights.dtype),
             pltpu.VMEM(contexts.shape, contexts.dtype),
             pltpu.VMEM(user_basis.shape, user_basis.dtype),
@@ -288,51 +290,60 @@
     return dict(zip(PIECES, out[:-1])), out[-1]
 
 
-def inverse_factor(gram):
-    order = gram.shape[0]
+def inverse_factor(left_ref, right_ref, out_ref):
+    order = left_ref.shape[0]
     panels = order // ROWS
     sub = lax.broadcasted_iota(jnp.int32, (ROWS, order), 0)
     lane = lax.broadcasted_iota(jnp.int32, (ROWS, order), 1)
-    left = [gram[ROWS * i : ROWS * (i + 1)] for i in range(panels)]
-    right = [jnp.where(lane == sub + ROWS * i, 1.0, 0.0) for i in range(panels)]
-    for k in range(panels):
-        columns = {
-            i: [
-                jnp.broadcast_to(left[i][:, ROWS * k + j : ROWS * k + j + 1], (ROWS, order))
-                for j in range(ROWS)
-            ]
-            for i in range(k, panels)
-        }
-        row, tail = left[k], right[k]
-        scale = jnp.zeros((ROWS, order), jnp.float32)
-        rows, tails = [], []
+    for i in range(panels):
+        right_ref[ROWS * i : ROWS * (i + 1)] = jnp.where(lane == sub + ROWS * i, 1.0, 0.0)
+    spread = lambda value, j: jnp.broadcast_to(value[j : j + 1], (ROWS, order))
+
+    def panel(stage, live, step, _):
+        blocks = [slice(ROWS * i, ROWS * (i + 1)) for i in range(live)]
+        row, tail = left_ref[blocks[0]], right_ref[blocks[0]]
+        columns = []
+        for block in blocks:
+            value = left_ref[block]
+            columns.append([jnp.broadcast_to(value[:, j : j + 1], (ROWS, order)) for j in range(ROWS)])
+        scale = jnp.ones((ROWS, order), jnp.float32)
+        rows, tails, facts = [], [], [[] for _ in range(live)]
         for j in range(ROWS):
-            head = columns[k][j]
-            pivot = jnp.broadcast_to(head[j : j + 1], (ROWS, order))
+            head = columns[0][j]
+            pivot = spread(head, j)
             inverse = pl.reciprocal(pivot, approx=True)
             inverse = inverse * (2.0 - pivot * inverse)
             scale = jnp.where(sub == j, pivot, scale)
-            rows.append(jnp.broadcast_to(row[j : j + 1], (ROWS, order)))
-            tails.append(jnp.broadcast_to(tail[j : j + 1], (ROWS, order)))
+            rows.append(spread(row, j))
+            tails.append(spread(tail, j))
             below = jnp.where(sub > j, head, 0.0) * inverse
             row = row - below * rows[j]
             tail = tail - below * tails[j]
-            facts = {k: below}
-            for i in range(k + 1, panels):
-                facts[i] = columns[i][j] * inverse
-            for c in range(j + 1, ROWS):
-                crossing = jnp.broadcast_to(head[c : c + 1], (ROWS, order))
-                for i in range(k, panels):
-                    columns[i][c] = columns[i][c] - facts[i] * crossing
-            for i in range(k + 1, panels):
-                left[i] = left[i] - facts[i] * rows[j]
-                right[i] = right[i] - facts[i] * tails[j]
-        right[k] = tail * lax.rsqrt(scale)
-    return jnp.concatenate(right, axis=0)
+            crossings = {c: spread(head, c) for c in range(j + 1, ROWS)}
+            for i in range(live):
+                facts[i].append(columns[i][j] * inverse if i else below)
+                for c in range(j + 1, ROWS):
+                    columns[i][c] = columns[i][c] - facts[i][j] * crossings[c]
+        out_ref[pl.ds(pl.multiple_of((stage + step) * ROWS, ROWS), ROWS)] = tail * lax.rsqrt(scale)
+        for i in range(1, live):
+            left, right = left_ref[blocks[i]], right_ref[blocks[i]]
+            for j in range(ROWS):
+                left = left - facts[i][j] * rows[j]
+                right = right - facts[i][j] * tails[j]
+            left_ref[blocks[i - 1]] = pltpu.roll(left, order - ROWS, 1)
+            right_ref[blocks[i - 1]] = right
+        left_ref[blocks[-1]] = jnp.zeros((ROWS, order), jnp.float32)
+        right_ref[blocks[-1]] = jnp.zeros((ROWS, order), jnp.float32)
+        return 0
+
+    steps = 4
+    for stage in range(0, panels, steps):
+        lax.fori_loop(0, steps, functools.partial(panel, stage, panels - stage), 0)
 
 
 def finish_kernel(total_users, me_ref, stack_ref, *rest):
-    piece_refs, (basis_ref, core_out_ref, pack_ref, full_ref) = rest[: len(PIECES)], rest[len(PIECES) :]
+    piece_refs, rest = rest[: len(PIECES)], rest[len(PIECES) :]
+    basis_ref, core_out_ref, pack_ref, full_ref, left_ref, right_ref, inverse_ref = rest
     chunk = piece_refs[0].shape[0]
     places = pack_places(me_ref[0])
     for piece, ref in zip(PIECES, piece_refs):
@@ -356,9 +367,10 @@
         [projection[i * LANES : (i + 1) * LANES].T for i in range(groups)], axis=1
     )
     turned_stack = jnp.concatenate(split(turned), axis=0)
-    gram = quarters(dot(turned_stack, jnp.concatenate([crossed_high, crossed_low], axis=1)))
+    left_ref[...] = quarters(dot(turned_stack, jnp.concatenate([crossed_high, crossed_low], axis=1)))
     projected_high, projected_low = split(thrice(turned_stack, stack_ref[:ranks], stack_ref[ranks:], dot))
-    inverse_stack = jnp.concatenate(split(inverse_factor(gram)), axis=0)
+    inverse_factor(left_ref, right_ref, inverse_ref)
+    inverse_stack = jnp.concatenate(split(inverse_ref[...]), axis=0)
     root = total_users ** 0.5
     scaled = thrice(inverse_stack, projected_high, projected_low, dot) * root
     for i in range(scaled.shape[1] // LANES):
@@ -379,7 +391,8 @@
         scratch_shapes=[
             pltpu.VMEM((pack_rows(ranks), LANES), jnp.float32),
             pltpu.VMEM((2 * ranks, ranks), jnp.bfloat16),
-        ],
+        ]
+        + [pltpu.VMEM((LANES, LANES), jnp.float32)] * 3,
         compiler_params=limit(16),
         name="finish",
     )(me, stack, *[pieces[piece] for piece in PIECES])

time: 91.2 us -> 92.9 us (1.019)
  Pallas kernels: 27.2 us -> 28.9 us
    pallas_call x1, Pallas kernels: 6.42 us -> 7.48 us  [finish(): pl.pallas_call(functools.partial(finish_kernel, users * devices), out_sha...]
  transfers between devices with their start and end apart: 18 -> 18, of which waited for: 11 -> 11; matrix products, arithmetic and copies ran while one was open for 1% -> 1% of each run, Pallas kernels for 7% -> 6%
where the time goes in v8:
time: 92.9 us; the launch traced here: 92.6 us
  Pallas kernels  28.9 us (31%)
  waiting for transfers between devices  28.7 us (31%)
  starting transfers between devices  20.1 us (22%)
  blocking collectives  10.5 us (11%)
  local copies, waits for them, and re-layouts  2.89 us (3%)
  between operations  1.39 us (1%)
    ppermute x17, waiting for transfers between devices, swap(): return lax.ppermute(value, 'users', [(i, i ^ mask) for i in range(devices)])  19.8 us
    ppermute x17, starting transfers between devices, swap(): return lax.ppermute(value, 'users', [(i, i ^ mask) for i in range(devices)])  16.5 us
    pallas_call x1, Pallas kernels, tile_sums(): pl.pallas_call(tiles_kernel, out_shape=out_shape, in_specs=[SMEM] * 3 + [...  13.8 us
    all_to_all x1, blocking collectives, body(): lax.all_to_all(requests, 'users', 0, 0, axis_index_groups=sides, tiled=True)  10.5 us
    all_to_all x1, waiting for transfers between devices, body(): lax.all_to_all(found, 'users', 0, 0, axis_index_groups=sides, tiled=True)  8.84 us
    pallas_call x1, Pallas kernels, finish(): pl.pallas_call(functools.partial(finish_kernel, users * devices), out_sha...  7.48 us
    pallas_call x1, Pallas kernels, context_values(): pl.pallas_call(context_kernel, out_shape=jax.ShapeDtypeStruct((tiles, ROW...  3.72 us
    all_to_all x1, starting transfers between devices, body(): lax.all_to_all(found, 'users', 0, 0, axis_index_groups=sides, tiled=True)  3.65 us
  transfers between devices with their start and end apart: 18, of which 11 were waited for; matrix products, arithmetic and copies ran while one was open for 1% of the time, Pallas kernels for 6%

profile of v8, /device:TPU:0, one launch (start us, length us, event | category | flops | bytes accessed | tf_op | source)
XLA Modules:
  0.0 92.6 jit_solution(213151025007497536)
XLA Ops:
  0.6 4.1 %collective-permute-start = (bf16[16,64,128]{2,1,0:T(8,128)(2,1)}, bf16[16,64,128]{2,1,0:T(8,128)(2,1)S(1)}, u32[]{:S(2)}, u32[]{:S(2)}) collective-permute-start(bf16[16,64,128]{2,1,0:T(8,128)(2,1)} %own_ref.1), channel_id=1, source_target_pairs={{0,16},{1,17},{2,18},{3,19},{4,20},{5,21},{6,22},{7,23},{8,24},{9,... | collective-permute-start | bytes 786440 | tf_op jit(solution)/shard_map/ppermute | solution.py:402
  4.7 2.2 %route.1 = (s32[16,1,128]{2,1,0:T(1,128)S(1)}, s32[64]{0:T(128)S(1)}, bf16[16,64,128]{2,1,0:T(8,128)(2,1)S(1)}) custom-call(s32[1]{0:T(128)} %bitcast.me_ref, s32[64]{0:T(128)} %bitcast.6, s32[64]{0:T(128)} %slot_ref.1, bf16[16,64,128]{2,1,0:T(8,128)(2,1)} %own_ref.1), custom_call_target="tpu_custom_call" | custom-call | tf_op jit(solution)/shard_map/route/pallas_call | solution.py:84
  7.0 10.5 %all_to_all.10.asked_ref = s32[16,1,128]{2,1,0:T(1,128)S(1)} all-to-all(s32[16,1,128]{2,1,0:T(1,128)S(1)} %get-tuple-element.18), channel_id=1, replica_groups={{0,1,2,3,4,5,6,7,8,9,10,11,12,13,14,15},{16,17,18,19,20,21,22,23,24,25,..., dimensions={0} | all-to-all | bytes 16384 | tf_op jit(solution)/shard_map/all_to_all | solution.py:438
  17.4 1.7 %collect.1 = bf16[64,64,128]{2,1,0:T(8,128)(2,1)} custom-call(s32[16,1,128]{2,1,0:T(1,128)S(1)} %all_to_all.10.asked_ref, bf16[16,64,128]{2,1,0:T(8,128)(2,1)S(1)} %get-tuple-element.19.own_ref, bf16[16,64,128]{2,1,0:T(8,128)(2,1)S(1)} %collective-permute-done.mirror_ref), custom_call_target="tpu_custom_call" | custom-call | tf_op jit(solution)/shard_map/collect/pallas_call | solution.py:107
  19.2 3.7 %all-to-all-start.1 = ((bf16[64,64,128]{2,1,0:T(8,128)(2,1)}), bf16[64,64,128]{2,1,0:T(8,128)(2,1)S(1)}, u32[]{:S(2)}, u32[]{:S(2)}) async-start(bf16[64,64,128]{2,1,0:T(8,128)(2,1)} %collect.1), calls=%async_computation.1 | async-start | bytes 2097152 | tf_op jit(solution)/shard_map/all_to_all | solution.py:441
  23.5 0.9 reshape.13
  24.5 0.9 copy-done.1
  25.4 3.7 %contexts.1.context_ref = f32[64,8,512]{2,1,0:T(8,128)S(1)} custom-call(s32[64]{0:T(128)} %cblock_ref, f32[64,8,8]{2,1,0:T(8,128)S(1)} %bitcast.5, s32[64,512]{1,0:T(8,128)S(1)} %copy-done.1), custom_call_target="tpu_custom_call" | custom-call | flops 10000000 | bytes 20000000 | tf_op jit(solution)/shard_map/contexts/pallas_call | solution.py:135
  29.2 1.0 %copy-done = f32[64,8,512]{2,1,0:T(8,128)} copy-done((f32[64,8,512]{2,1,0:T(8,128)}, f32[64,8,512]{2,1,0:T(8,128)S(1)}, u32[]{:S(2)}) %copy-start) | copy-done | bytes 1048600
  30.1 8.8 %all-to-all-done.1.blocks_ref = bf16[64,64,128]{2,1,0:T(8,128)(2,1)S(1)} async-done(((bf16[64,64,128]{2,1,0:T(8,128)(2,1)}), bf16[64,64,128]{2,1,0:T(8,128)(2,1)S(1)}, u32[]{:S(2)}, u32[]{:S(2)}) %all-to-all-start.1) | async-done | bytes 1048608 | tf_op jit(solution)/shard_map/all_to_all | solution.py:441
  39.0 13.8 %tile_sums.1 = (f32[224,128]{1,0:T(8,128)S(1)}, f32[224,128]{1,0:T(8,128)S(1)}, f32[224,128]{1,0:T(8,128)S(1)}, f32[224,128]{1,0:T(8,128)S(1)}, f32[224,128]{1,0...) custom-call(s32[64]{0:T(128)S(1)} %get-tuple-element.17.where_ref, ...), custom_call_target="tpu_custom_call" | custom-call | flops 2000000000 | bytes 12000000 | tf_op jit(solution)/shard_map/tile_sums/pallas_call | solution.py:269
  52.8 0.5 collective-permute-start.4
  53.4 0.4 collective-permute-start.1
  53.8 0.3 collective-permute-done.2
  54.1 1.0 %collective-permute-start.3 = (f32[224,128]{1,0:T(8,128)S(1)}, f32[224,128]{1,0:T(8,128)S(1)}, u32[]{:S(2)}, u32[]{:S(2)}) collective-permute-start(f32[224,128]{1,0:T(8,128)S(1)} %add.28), channel_id=1, source_target_pairs={{0,6},{1,7},{2,4},{3,5},{4,2},{5,3},{6,0},{7,1},{8,14},{9,15},{10,... | collective-permute-start | bytes 344072 | tf_op jit(solution)/shard_map/ppermute | solution.py:402
  55.2 1.4 %collective-permute-start.5 = (f32[224,128]{1,0:T(8,128)S(1)}, f32[224,128]{1,0:T(8,128)S(1)}, u32[]{:S(2)}, u32[]{:S(2)}) collective-permute-start(f32[224,128]{1,0:T(8,128)S(1)} %add.30), channel_id=1, source_target_pairs={{0,2},{1,3},{2,0},{3,1},{4,6},{5,7},{6,4},{7,5},{8,10},{9,11},{10,... | collective-permute-start | bytes 344072 | tf_op jit(solution)/shard_map/ppermute | solution.py:402
  56.6 1.2 %collective-permute-start.7 = (f32[224,128]{1,0:T(8,128)S(1)}, f32[224,128]{1,0:T(8,128)S(1)}, u32[]{:S(2)}, u32[]{:S(2)}) collective-permute-start(f32[224,128]{1,0:T(8,128)S(1)} %add.32), channel_id=1, source_target_pairs={{0,4},{1,5},{2,6},{3,7},{4,0},{5,1},{6,2},{7,3},{8,12},{9,13},{10,... | collective-permute-start | bytes 344072 | tf_op jit(solution)/shard_map/ppermute | solution.py:402
  57.9 3.2 %collective-permute-done.3 = f32[224,128]{1,0:T(8,128)S(1)} collective-permute-done((f32[224,128]{1,0:T(8,128)S(1)}, f32[224,128]{1,0:T(8,128)S(1)}, u32[]{:S(2)}, u32[]{:S(2)}) %collective-permute-start.3) | collective-permute-done | bytes 114720 | tf_op jit(solution)/shard_map/ppermute | solution.py:402
  61.1 1.1 %collective-permute-done.5 = f32[224,128]{1,0:T(8,128)S(1)} collective-permute-done((f32[224,128]{1,0:T(8,128)S(1)}, f32[224,128]{1,0:T(8,128)S(1)}, u32[]{:S(2)}, u32[]{:S(2)}) %collective-permute-start.5) | collective-permute-done | bytes 114720 | tf_op jit(solution)/shard_map/ppermute | solution.py:402
  62.1 0.6 collective-permute-done.7
  62.8 0.7 collective-permute-start.8
  63.5 4.2 %collective-permute-done.8 = f32[224,128]{1,0:T(8,128)S(1)} collective-permute-done((f32[224,128]{1,0:T(8,128)S(1)}, f32[224,128]{1,0:T(8,128)S(1)}, u32[]{:S(2)}, u32[]{:S(2)}) %collective-permute-start.8) | collective-permute-done | bytes 114720 | tf_op jit(solution)/shard_map/ppermute | solution.py:402
  67.7 3.4 %collective-permute-start.9 = (f32[224,128]{1,0:T(8,128)S(1)}, f32[224,128]{1,0:T(8,128)S(1)}, u32[]{:S(2)}, u32[]{:S(2)}) collective-permute-start(f32[224,128]{1,0:T(8,128)S(1)} %add.34), channel_id=1, source_target_pairs={{0,16},{1,17},{2,18},{3,19},{4,20},{5,21},{6,22},{7,23},{8,24},{9,... | collective-permute-start | bytes 344072 | tf_op jit(solution)/shard_map/ppermute | solution.py:402
  71.0 4.3 %collective-permute-done.9 = f32[224,128]{1,0:T(8,128)S(1)} collective-permute-done((f32[224,128]{1,0:T(8,128)S(1)}, f32[224,128]{1,0:T(8,128)S(1)}, u32[]{:S(2)}, u32[]{:S(2)}) %collective-permute-start.9) | collective-permute-done | bytes 114720 | tf_op jit(solution)/shard_map/ppermute | solution.py:402
  75.4 0.8 collective-permute-start.14
  76.2 1.9 %collective-permute-start.12 = (f32[224,128]{1,0:T(8,128)S(1)}, f32[224,128]{1,0:T(8,128)S(1)}, u32[]{:S(2)}, u32[]{:S(2)}) collective-permute-start(f32[224,128]{1,0:T(8,128)S(1)} %add.35.rest_7_), channel_id=1, source_target_pairs={{0,2},{1,3},{2,0},{3,1},{4,6},{5,7},{6,4},{7,5},{8,10},{9,11},{10,... | collective-permute-start | bytes 344072 | tf_op jit(solution)/shard_map/ppermute | solution.py:402
  78.0 0.9 collective-permute-start.10
  78.9 1.7 %collective-permute-done.14.rest_6_ = f32[224,128]{1,0:T(8,128)S(1)} collective-permute-done((f32[224,128]{1,0:T(8,128)S(1)}, f32[224,128]{1,0:T(8,128)S(1)}, u32[]{:S(2)}, u32[]{:S(2)}) %collective-permute-start.14) | collective-permute-done | bytes 114720 | tf_op jit(solution)/shard_map/ppermute | solution.py:402
  80.6 0.8 collective-permute-done.12.rest_5_
  81.4 2.3 %collective-permute-done.10.rest_4_ = f32[224,128]{1,0:T(8,128)S(1)} collective-permute-done((f32[224,128]{1,0:T(8,128)S(1)}, f32[224,128]{1,0:T(8,128)S(1)}, u32[]{:S(2)}, u32[]{:S(2)}) %collective-permute-start.10) | collective-permute-done | bytes 114720 | tf_op jit(solution)/shard_map/ppermute | solution.py:402
  83.8 1.3 %collective-permute-done.11.rest_0_ = f32[224,128]{1,0:T(8,128)S(1)} collective-permute-done((f32[224,128]{1,0:T(8,128)S(1)}, f32[224,128]{1,0:T(8,128)S(1)}, u32[]{:S(2)}, u32[]{:S(2)}) %collective-permute-start.11) | collective-permute-done | bytes 114720 | tf_op jit(solution)/shard_map/ppermute | solution.py:402
  85.1 7.5 %finish.1 = (f32[512,128]{1,0:T(8,128)}, f32[128,512]{1,0:T(8,128)}) custom-call(s32[1]{0:T(128)} %bitcast.me_ref, bf16[1024,512]{1,0:T(8,128)(2,1)S(1)} %get-tuple-element.23.stack_ref, f32[224,128]{1,0:T(8,128)S(1)} %collective-permute-done.11.rest_0_, f32[224,128]{1,0:T(8,128)S(1)} %collective-permute-done.13.rest_1_, ...), custom_call_target="tpu_custom_call" | custom-call | tf_op jit(solution)/shard_map/finish/pallas_call | solution.py:383
  (22 shorter events, 0.5 us)
Async XLA Ops:
  0.6 16.8 %collective-permute-start = (bf16[16,64,128]{2,1,0:T(8,128)(2,1)}, bf16[16,64,128]{2,1,0:T(8,128)(2,1)S(1)}, u32[]{:S(2)}, u32[]{:S(2)}) collective-permute-start(bf16[16,64,128]{2,1,0:T(8,128)(2,1)} %own_ref.1), channel_id=1, source_target_pairs={{0,16},{1,17},{2,18},{3,19},{4,20},{5,21},{6,22},{7,23},{8,24},{9,... | collective-permute-start | bytes 786440 | tf_op jit(solution)/shard_map/ppermute | solution.py:402
  19.2 19.8 %all-to-all-start.1 = ((bf16[64,64,128]{2,1,0:T(8,128)(2,1)}), bf16[64,64,128]{2,1,0:T(8,128)(2,1)S(1)}, u32[]{:S(2)}, u32[]{:S(2)}) async-start(bf16[64,64,128]{2,1,0:T(8,128)(2,1)} %collect.1), calls=%async_computation.1 | async-start | bytes 2097152 | tf_op jit(solution)/shard_map/all_to_all | solution.py:441
  24.5 0.9 copy-start.1
  29.2 1.0 %copy-start = (f32[64,8,512]{2,1,0:T(8,128)}, f32[64,8,512]{2,1,0:T(8,128)S(1)}, u32[]{:S(2)}) copy-start(f32[64,8,512]{2,1,0:T(8,128)S(1)} %contexts.1.context_ref) | copy-start | bytes 3145732
  52.7 1.4 %collective-permute-start.2 = (f32[224,128]{1,0:T(8,128)S(1)}, f32[224,128]{1,0:T(8,128)S(1)}, u32[]{:S(2)}, u32[]{:S(2)}) collective-permute-start(f32[224,128]{1,0:T(8,128)S(1)} %get-tuple-element.27), channel_id=1, source_target_pairs={{0,1},{1,0},{2,3},{3,2},{4,5},{5,4},{6,7},{7,6},{8,9},{9,8},{10,11... | collective-permute-start | bytes 344072 | tf_op jit(solution)/shard_map/ppermute | solution.py:402
  52.8 2.3 %collective-permute-start.4 = (f32[224,128]{1,0:T(8,128)S(1)}, f32[224,128]{1,0:T(8,128)S(1)}, u32[]{:S(2)}, u32[]{:S(2)}) collective-permute-start(f32[224,128]{1,0:T(8,128)S(1)} %get-tuple-element.29), channel_id=1, source_target_pairs={{0,1},{1,0},{2,3},{3,2},{4,5},{5,4},{6,7},{7,6},{8,9},{9,8},{10,11... | collective-permute-start | bytes 344072 | tf_op jit(solution)/shard_map/ppermute | solution.py:402
  53.3 3.3 %collective-permute-start.6 = (f32[224,128]{1,0:T(8,128)S(1)}, f32[224,128]{1,0:T(8,128)S(1)}, u32[]{:S(2)}, u32[]{:S(2)}) collective-permute-start(f32[224,128]{1,0:T(8,128)S(1)} %get-tuple-element.31), channel_id=1, source_target_pairs={{0,1},{1,0},{2,3},{3,2},{4,5},{5,4},{6,7},{7,6},{8,9},{9,8},{10,11... | collective-permute-start | bytes 344072 | tf_op jit(solution)/shard_map/ppermute | solution.py:402
  53.4 4.5 %collective-permute-start.1 = (f32[224,128]{1,0:T(8,128)S(1)}, f32[224,128]{1,0:T(8,128)S(1)}, u32[]{:S(2)}, u32[]{:S(2)}) collective-permute-start(f32[224,128]{1,0:T(8,128)S(1)} %get-tuple-element.25), channel_id=1, source_target_pairs={{0,1},{1,0},{2,3},{3,2},{4,5},{5,4},{6,7},{7,6},{8,9},{9,8},{10,11... | collective-permute-start | bytes 344072 | tf_op jit(solution)/shard_map/ppermute | solution.py:402
  54.1 7.0 %collective-permute-start.3 = (f32[224,128]{1,0:T(8,128)S(1)}, f32[224,128]{1,0:T(8,128)S(1)}, u32[]{:S(2)}, u32[]{:S(2)}) collective-permute-start(f32[224,128]{1,0:T(8,128)S(1)} %add.28), channel_id=1, source_target_pairs={{0,6},{1,7},{2,4},{3,5},{4,2},{5,3},{6,0},{7,1},{8,14},{9,15},{10,... | collective-permute-start | bytes 344072 | tf_op jit(solution)/shard_map/ppermute | solution.py:402
  55.2 7.0 %collective-permute-start.5 = (f32[224,128]{1,0:T(8,128)S(1)}, f32[224,128]{1,0:T(8,128)S(1)}, u32[]{:S(2)}, u32[]{:S(2)}) collective-permute-start(f32[224,128]{1,0:T(8,128)S(1)} %add.30), channel_id=1, source_target_pairs={{0,2},{1,3},{2,0},{3,1},{4,6},{5,7},{6,4},{7,5},{8,10},{9,11},{10,... | collective-permute-start | bytes 344072 | tf_op jit(solution)/shard_map/ppermute | solution.py:402
  56.6 6.1 %collective-permute-start.7 = (f32[224,128]{1,0:T(8,128)S(1)}, f32[224,128]{1,0:T(8,128)S(1)}, u32[]{:S(2)}, u32[]{:S(2)}) collective-permute-start(f32[224,128]{1,0:T(8,128)S(1)} %add.32), channel_id=1, source_target_pairs={{0,4},{1,5},{2,6},{3,7},{4,0},{5,1},{6,2},{7,3},{8,12},{9,13},{10,... | collective-permute-start | bytes 344072 | tf_op jit(solution)/shard_map/ppermute | solution.py:402
  62.8 4.9 %collective-permute-start.8 = (f32[224,128]{1,0:T(8,128)S(1)}, f32[224,128]{1,0:T(8,128)S(1)}, u32[]{:S(2)}, u32[]{:S(2)}) collective-permute-start(f32[224,128]{1,0:T(8,128)S(1)} %add_add_fusion), channel_id=1, source_target_pairs={{0,8},{1,9},{2,10},{3,11},{4,12},{5,13},{6,14},{7,15},{8,0},{9,1},... | collective-permute-start | bytes 344072 | tf_op jit(solution)/shard_map/ppermute | solution.py:402
  67.7 7.7 %collective-permute-start.9 = (f32[224,128]{1,0:T(8,128)S(1)}, f32[224,128]{1,0:T(8,128)S(1)}, u32[]{:S(2)}, u32[]{:S(2)}) collective-permute-start(f32[224,128]{1,0:T(8,128)S(1)} %add.34), channel_id=1, source_target_pairs={{0,16},{1,17},{2,18},{3,19},{4,20},{5,21},{6,22},{7,23},{8,24},{9,... | collective-permute-start | bytes 344072 | tf_op jit(solution)/shard_map/ppermute | solution.py:402
  75.4 5.3 %collective-permute-start.14 = (f32[224,128]{1,0:T(8,128)S(1)}, f32[224,128]{1,0:T(8,128)S(1)}, u32[]{:S(2)}, u32[]{:S(2)}) collective-permute-start(f32[224,128]{1,0:T(8,128)S(1)} %add.35.rest_7_), channel_id=1, source_target_pairs={{0,4},{1,5},{2,6},{3,7},{4,0},{5,1},{6,2},{7,3},{8,12},{9,13},{10,... | collective-permute-start | bytes 344072 | tf_op jit(solution)/shard_map/ppermute | solution.py:402
  76.2 5.3 %collective-permute-start.12 = (f32[224,128]{1,0:T(8,128)S(1)}, f32[224,128]{1,0:T(8,128)S(1)}, u32[]{:S(2)}, u32[]{:S(2)}) collective-permute-start(f32[224,128]{1,0:T(8,128)S(1)} %add.35.rest_7_), channel_id=1, source_target_pairs={{0,2},{1,3},{2,0},{3,1},{4,6},{5,7},{6,4},{7,5},{8,10},{9,11},{10,... | collective-permute-start | bytes 344072 | tf_op jit(solution)/shard_map/ppermute | solution.py:402
  78.0 5.7 %collective-permute-start.10 = (f32[224,128]{1,0:T(8,128)S(1)}, f32[224,128]{1,0:T(8,128)S(1)}, u32[]{:S(2)}, u32[]{:S(2)}) collective-permute-start(f32[224,128]{1,0:T(8,128)S(1)} %add.35.rest_7_), channel_id=1, source_target_pairs={{0,6},{1,7},{2,4},{3,5},{4,2},{5,3},{6,0},{7,1},{8,14},{9,15},{10,... | collective-permute-start | bytes 344072 | tf_op jit(solution)/shard_map/ppermute | solution.py:402
  78.9 4.8 %collective-permute-start.16 = (f32[224,128]{1,0:T(8,128)S(1)}, f32[224,128]{1,0:T(8,128)S(1)}, u32[]{:S(2)}, u32[]{:S(2)}) collective-permute-start(f32[224,128]{1,0:T(8,128)S(1)} %add.35.rest_7_), channel_id=1, source_target_pairs={{0,1},{1,0},{2,3},{3,2},{4,5},{5,4},{6,7},{7,6},{8,9},{9,8},{10,11... | collective-permute-start | bytes 344072 | tf_op jit(solution)/shard_map/ppermute | solution.py:402
  80.6 3.1 %collective-permute-start.15 = (f32[224,128]{1,0:T(8,128)S(1)}, f32[224,128]{1,0:T(8,128)S(1)}, u32[]{:S(2)}, u32[]{:S(2)}) collective-permute-start(f32[224,128]{1,0:T(8,128)S(1)} %collective-permute-done.14.rest_6_), channel_id=1, source_target_pairs={{0,1},{1,0},{2,3},{3,2},{4,5},{5,4},{6,7},{7,6},{8,9},{9,8},{10,11... | collective-permute-start | bytes 344072 | tf_op jit(solution)/shard_map/ppermute | solution.py:402
  81.4 2.3 %collective-permute-start.13 = (f32[224,128]{1,0:T(8,128)S(1)}, f32[224,128]{1,0:T(8,128)S(1)}, u32[]{:S(2)}, u32[]{:S(2)}) collective-permute-start(f32[224,128]{1,0:T(8,128)S(1)} %collective-permute-done.12.rest_5_), channel_id=1, source_target_pairs={{0,1},{1,0},{2,3},{3,2},{4,5},{5,4},{6,7},{7,6},{8,9},{9,8},{10,11... | collective-permute-start | bytes 344072 | tf_op jit(solution)/shard_map/ppermute | solution.py:402
  83.8 1.3 %collective-permute-start.11 = (f32[224,128]{1,0:T(8,128)S(1)}, f32[224,128]{1,0:T(8,128)S(1)}, u32[]{:S(2)}, u32[]{:S(2)}) collective-permute-start(f32[224,128]{1,0:T(8,128)S(1)} %collective-permute-done.10.rest_4_), channel_id=1, source_target_pairs={{0,1},{1,0},{2,3},{3,2},{4,5},{5,4},{6,7},{7,6},{8,9},{9,8},{10,11... | collective-permute-start | bytes 344072 | tf_op jit(solution)/shard_map/ppermute | solution.py:402

commit v9 on v7

--- a/solution.py
+++ b/solution.py
@@ -9,7 +9,6 @@
 
 CB = 8
 SLOTS = 2
-PLACES = 2 * SLOTS
 LANES = 128
 ROWS = 8
 BATCH = 8
@@ -53,7 +52,7 @@
     return first[:rows] + (first[rows:] + product(stack[:rows], low))
 
 
-def route_kernel(half, me_ref, owner_ref, slot_ref, own_ref, request_ref, where_ref, held_ref, used_ref, sem_ref):
+def route_kernel(half, me_ref, owner_ref, slot_ref, own_ref, request_ref, tile_ref, held_ref, used_ref, sem_ref):
     copy = pltpu.make_async_copy(own_ref, held_ref, sem_ref)
     copy.start()
     side = me_ref[0] // half
@@ -61,6 +60,8 @@
 
     def clear(place, _):
         used_ref[place] = 0
+        for slot in range(SLOTS):
+            tile_ref[place * SLOTS + slot] = -1
         return 0
 
     lax.fori_loop(0, 2 * half, clear, 0, unroll=8)
@@ -71,9 +72,9 @@
         taken = used_ref[owner]
         used_ref[owner] = taken + 1
         low = lax.rem(owner, half)
-        place = jnp.where(owner // half == side, 0, SLOTS) + taken
-        request_ref[low] = jnp.where(lane == place, slot_ref[tile], request_ref[low])
-        where_ref[tile] = low * PLACES + place
+        mirrored = jnp.where(owner // half == side, 0, 1)
+        request_ref[low] = jnp.where(lane == mirrored * SLOTS + taken, slot_ref[tile], request_ref[low])
+        tile_ref[(mirrored * half + low) * SLOTS + taken] = tile
         return 0
 
     lax.fori_loop(0, owner_ref.shape[0], assign, 0, unroll=4)
@@ -85,7 +86,7 @@
         functools.partial(route_kernel, half),
         out_shape=(
             jax.ShapeDtypeStruct((half, 1, LANES), jnp.int32),
-            jax.ShapeDtypeStruct(owners.shape, jnp.int32),
+            jax.ShapeDtypeStruct((2 * half * SLOTS,), jnp.int32),
             jax.ShapeDtypeStruct(own.shape, own.dtype),
         ),
         in_specs=[SMEM, SMEM, SMEM, ANY],
@@ -96,51 +97,50 @@
     )(me, in_hbm(owners), in_hbm(slots), in_hbm(own))
 
 
-def collect_kernel(asked_ref, own_ref, mirror_ref, out_ref):
+def collect_kernel(lane, asked_ref, source_ref, out_ref):
     for peer in range(asked_ref.shape[0]):
-        for place in range(PLACES):
-            source = own_ref if place < SLOTS else mirror_ref
-            out_ref[peer * PLACES + place] = source[asked_ref[peer, 0, place]]
-
-
-def collect(asked, own, mirror):
+        for slot in range(SLOTS):
+            out_ref[peer * SLOTS + slot] = source_ref[asked_ref[peer, 0, lane + slot]]
+
+
+def collect(lane, asked, source):
     return pl.pallas_call(
-        collect_kernel,
-        out_shape=jax.ShapeDtypeStruct((asked.shape[0] * PLACES,) + own.shape[1:], own.dtype),
-        in_specs=[SMEM, VMEM, VMEM],
+        functools.partial(collect_kernel, lane),
+        out_shape=jax.ShapeDtypeStruct((asked.shape[0] * SLOTS,) + source.shape[1:], source.dtype),
+        in_specs=[SMEM, VMEM],
         out_specs=VMEM,
         compiler_params=limit(4),
         name="collect",
-    )(asked, own, mirror)
-
-
-def context_kernel(cblock_ref, table_ref, marks_ref, context_ref):
-    tiles, users = marks_ref.shape
-
-    def one(tile, _):
-        table = table_ref[cblock_ref[tile]]
+    )(asked, source)
+
+
+def context_kernel(tile_ref, cblock_ref, table_ref, marks_ref, context_ref):
+    users = marks_ref.shape[1]
+
+    def one(slot, _):
+        tile = jnp.maximum(tile_ref[slot], 0)
+        table = jnp.where(tile_ref[slot] >= 0, table_ref[cblock_ref[tile]], 0.0)
         marks = jnp.broadcast_to(marks_ref[pl.ds(tile, 1), :], (ROWS, users))
         total = jnp.zeros((ROWS, users), jnp.float32)
         for k in range(CB):
             column = jnp.broadcast_to(table[:, k : k + 1], (ROWS, users))
             total = jnp.where(marks == k, column, total)
-        context_ref[tile] = total
+        context_ref[slot] = total
         return 0
 
-    lax.fori_loop(0, tiles, one, 0, unroll=2)
-
-
-def context_values(cblock, table, marks):
-    tiles, users = marks.shape
+    lax.fori_loop(0, tile_ref.shape[0], one, 0, unroll=2)
+
+
+def context_values(tile_of, cblock, table, marks):
     return pl.pallas_call(
         context_kernel,
-        out_shape=jax.ShapeDtypeStruct((tiles, ROWS, users), jnp.float32),
-        in_specs=[SMEM, VMEM, VMEM],
+        out_shape=jax.ShapeDtypeStruct((tile_of.shape[0], ROWS, marks.shape[1]), jnp.float32),
+        in_specs=[SMEM, SMEM, VMEM, VMEM],
         out_specs=VMEM,
-        compiler_params=limit(4),
+        compiler_params=limit(8),
         cost_estimate=pl.CostEstimate(flops=10**7, bytes_accessed=2 * 10**7, transcendentals=0),
         name="contexts",
-    )(in_hbm(cblock), table, marks)
+    )(tile_of, in_hbm(cblock), table, marks)
 
 
 def pack_places(me):
@@ -159,31 +159,38 @@
     return (groups * (groups + 1) // 2 + groups) * LANES
 
 
-def tiles_kernel(
-    where_ref, count_ref, me_ref, blocks_ref, weights_ref, context_ref, basis_ref, *refs
-):
-    piece_refs, refs = refs[: len(PIECES)], refs[len(PIECES) :]
-    stack_ref, y_ref, square_ref, pack_ref, even_ref, odd_ref = refs[:6]
-    weights_held, context_held, basis_held, weights_sem, context_sem, basis_sem = refs[6:]
+def tiles_kernel(side, tile_ref, count_ref, me_ref, blocks_ref, weights_ref, context_ref, basis_ref, *refs):
+    if side:
+        before_ref, refs = refs[0], refs[1:]
+        piece_refs, refs = refs[: len(PIECES)], refs[len(PIECES) :]
+        stack_ref, square_ref, pack_ref, basis_held, basis_sem, *refs = refs
+    y_ref, even_ref, odd_ref, weights_held, context_held, weights_sem, context_sem = refs
     rank_c, rank_i, users = y_ref.shape
-    batches = weights_ref.shape[0] // BATCH
+    places = blocks_ref.shape[0]
+    batches = places // BATCH
     half = rank_c // 2
 
-    def weights_copy(batch):
-        rows = pl.ds(batch * BATCH, BATCH)
-        return pltpu.make_async_copy(weights_ref.at[rows], weights_held.at[rows], weights_sem.at[batch])
-
-    weights_copy(0).start()
-    contexts_copy = pltpu.make_async_copy(context_ref, context_held, context_sem)
+    def weights_copy(place):
+        tile = jnp.maximum(tile_ref[side * places + place], 0)
+        return pltpu.make_async_copy(weights_ref.at[tile], weights_held.at[place], weights_sem.at[place])
+
+    def start(place, _):
+        weights_copy(place).start()
+        return 0
+
+    lax.fori_loop(0, BATCH, start, 0)
+    contexts_copy = pltpu.make_async_copy(
+        context_ref.at[pl.ds(side * places, places)], context_held, context_sem
+    )
     contexts_copy.start()
-    for batch in range(1, batches):
-        weights_copy(batch).start()
-    basis_copy = pltpu.make_async_copy(basis_ref, basis_held, basis_sem)
-    basis_copy.start()
+    lax.fori_loop(BATCH, places, start, 0)
+    if side:
+        basis_copy = pltpu.make_async_copy(basis_ref, basis_held, basis_sem)
+        basis_copy.start()
 
     def multiply(batch, place, into_ref):
         tile = batch * BATCH + place
-        product = dot(blocks_ref[where_ref[tile]], weights_held[tile])
+        product = dot(blocks_ref[tile], weights_held[tile])
         into_ref[place] = product.astype(jnp.bfloat16).astype(jnp.float32)
 
     def add(batch, part, from_ref):
@@ -202,15 +209,17 @@
             for strip, total in zip(strips, totals[i]):
                 y_ref[r, strip, lanes] = total
 
-    y_ref[...] = jnp.zeros_like(y_ref)
+    y_ref[...] = before_ref[...] if side else jnp.zeros_like(y_ref)
     parts = 2 * users // LANES
-    weights_copy(0).wait()
+    for place in range(BATCH):
+        weights_copy(place).wait()
     for place in range(BATCH):
         multiply(0, place, even_ref)
     contexts_copy.wait()
 
     def turn(batch, from_ref, into_ref):
-        weights_copy(batch + 1).wait()
+        for place in range(BATCH):
+            weights_copy((batch + 1) * BATCH + place).wait()
         for part in range(max(parts, BATCH)):
             if part < BATCH:
                 multiply(batch + 1, part, into_ref)
@@ -226,6 +235,8 @@
     turn(batches - 2, even_ref, odd_ref)
     for part in range(parts):
         add(batches - 1, part, odd_ref)
+    if not side:
+        return
 
     living = lax.broadcasted_iota(jnp.int32, (rank_i, users), 1) < count_ref[0]
     ranks = rank_c * rank_i
@@ -254,38 +265,48 @@
         ref[...] = pack_ref[pl.ds(pl.multiple_of(places[piece] * chunk, ROWS), chunk)]
 
 
-def tile_sums(where, count, me, blocks, weights, contexts, user_basis):
-    tiles, _, users = weights.shape
-    rank_i = blocks.shape[1]
+def tile_sums(side, tile_of, count, me, blocks, weights, contexts, user_basis, before=None):
+    _, block_len, users = weights.shape
+    places, rank_i = blocks.shape[:2]
     rank_c = contexts.shape[1]
     ranks = rank_c * rank_i
     rows = pack_rows(ranks)
-    out_shape = (jax.ShapeDtypeStruct((rows // CHUNKS, LANES), jnp.float32),) * len(PIECES)
-    out_shape += (jax.ShapeDtypeStruct((2 * ranks, users), jnp.bfloat16),)
-    held = 3 * weights.size * 2 // (2 * MIB)
-    out = pl.pallas_call(
-        tiles_kernel,
-        out_shape=out_shape,
-        in_specs=[SMEM] * 3 + [VMEM] + [ANY] * 3,
-        out_specs=(VMEM,) * len(out_shape),
-        scratch_shapes=[
-            pltpu.VMEM((rank_c, rank_i, users), jnp.float32),
+    y = jax.ShapeDtypeStruct((rank_c, rank_i, users), jnp.float32)
+    scratch = [
+        pltpu.VMEM((BATCH, rank_i, users), jnp.float32),
+        pltpu.VMEM((BATCH, rank_i, users), jnp.float32),
+        pltpu.VMEM((places, block_len, users), weights.dtype),
+        pltpu.VMEM((places,) + contexts.shape[1:], contexts.dtype),
+        pltpu.SemaphoreType.DMA((places,)),
+        pltpu.SemaphoreType.DMA,
+    ]
+    out_shape = (y,)
+    operands = [tile_of, count, me, blocks, in_hbm(weights), in_hbm(contexts), in_hbm(user_basis)]
+    in_specs = [SMEM] * 3 + [VMEM] + [ANY] * 3
+    if side:
+        operands.append(before)
+        in_specs.append(VMEM)
+        out_shape = (jax.ShapeDtypeStruct((rows // CHUNKS, LANES), jnp.float32),) * len(PIECES)
+        out_shape += (jax.ShapeDtypeStruct((2 * ranks, users), jnp.bfloat16),)
+        scratch = [
             pltpu.VMEM((2 * ranks, ranks), jnp.float32),
             pltpu.VMEM((rows, LANES), jnp.float32),
-            pltpu.VMEM((BATCH, rank_i, users), jnp.float32),
-            pltpu.VMEM((BATCH, rank_i, users), jnp.float32),
-            pltpu.VMEM(weights.shape, weights.dtype),
-            pltpu.VMEM(contexts.shape, contexts.dtype),
             pltpu.VMEM(user_basis.shape, user_basis.dtype),
-            pltpu.SemaphoreType.DMA((tiles // BATCH,)),
             pltpu.SemaphoreType.DMA,
-            pltpu.SemaphoreType.DMA,
-        ],
+            pltpu.VMEM(y.shape, y.dtype),
+        ] + scratch
+    held = 3 * places * block_len * users // MIB
+    out = pl.pallas_call(
+        functools.partial(tiles_kernel, side),
+        out_shape=out_shape,
+        in_specs=in_specs,
+        out_specs=(VMEM,) * len(out_shape),
+        scratch_shapes=scratch,
         compiler_params=limit(12 + held),
-        cost_estimate=pl.CostEstimate(flops=2 * 10**9, bytes_accessed=12 * 10**6, transcendentals=0),
+        cost_estimate=pl.CostEstimate(flops=10**9, bytes_accessed=6 * 10**6, transcendentals=0),
         name="tile_sums",
-    )(where, count, me, blocks, in_hbm(weights), in_hbm(contexts), in_hbm(user_basis))
-    return dict(zip(PIECES, out[:-1])), out[-1]
+    )(*operands)
+    return (dict(zip(PIECES, out[:-1])), out[-1]) if side else out[0]
 
 
 def inverse_factor(gram):
@@ -420,18 +441,23 @@
     me = lax.axis_index("users").astype(jnp.int32).reshape(1)
 
     mirror = swap(item_factors, half, devices)
-    requests, where, own = route(me, tile_owner[:, 0], tile_slot, item_factors, half)
+    requests, tile_of, own = route(me, tile_owner[:, 0], tile_slot, item_factors, half)
     sides = [list(range(half)), list(range(half, devices))]
-    asked = lax.all_to_all(requests, "users", 0, 0, axis_index_groups=sides, tiled=True)
-    found = collect(asked, own, mirror)
+
+    def exchange(value):
+        return lax.all_to_all(value, "users", 0, 0, axis_index_groups=sides, tiled=True)
+
+    asked = exchange(requests)
+    found = collect(0, asked, own)
     found, cblock, factors = lax.optimization_barrier((found, tile_cblock, context_factors))
-    blocks = lax.all_to_all(found, "users", 0, 0, axis_index_groups=sides, tiled=True)
+    near = exchange(found)
+    far = exchange(collect(SLOTS, asked, mirror))
 
     table = factors.astype(jnp.float32).reshape(rank_c, -1, CB).transpose(1, 0, 2)
-    contexts = context_values(cblock, table, tile_context)
-    pieces, stack = tile_sums(
-        where, user_counts, me, blocks, tile_weights, contexts, user_basis
-    )
+    contexts = context_values(tile_of, cblock, table, tile_context)
+    shared = (tile_of, user_counts, me)
+    before = tile_sums(0, *shared, near, tile_weights, contexts, user_basis)
+    pieces, stack = tile_sums(1, *shared, far, tile_weights, contexts, user_basis, before)
     pieces = spread_pieces(reduce_pieces(pieces, devices), devices)
     return finish(me, stack, pieces, devices)
 

time: 91.2 us -> 102 us (1.12)
  starting transfers between devices: 20.1 us -> 24.8 us
  waiting for transfers between devices: 28.7 us -> 31.9 us
  Pallas kernels: 27.2 us -> 28.5 us
  blocking collectives: 10.5 us -> 11.6 us
    ppermute x17, waiting for transfers between devices: 19.8 us -> 29.5 us  [swap(): return lax.ppermute(value, 'users', [(i, i ^ mask) for i in range(devices)])]
    all_to_all x1 -> x2, waiting for transfers between devices: 8.84 us -> 2.36 us  [exchange(): lax.all_to_all(value, 'users', 0, 0, axis_index_groups=sides, tiled=True)]
    all_to_all x1 -> x2, starting transfers between devices: 3.65 us -> 9.04 us  [exchange(): lax.all_to_all(value, 'users', 0, 0, axis_index_groups=sides, tiled=True)]
    pallas_call x3 -> x5, Pallas kernels: 18.6 us -> 19.9 us  [the longest x2 13.1 us: tile_sums(): pl.pallas_call(functools.partial(tiles_kernel, side), out_shape=out_shape...]
    all_to_all x1, blocking collectives: 10.5 us -> 11.6 us  [exchange(): lax.all_to_all(value, 'users', 0, 0, axis_index_groups=sides, tiled=True)]
  transfers between devices with their start and end apart: 18 -> 19, of which waited for: 11 -> 11; matrix products, arithmetic and copies ran while one was open for 1% -> 1% of each run, Pallas kernels for 7% -> 11%
where the time goes in v9:
time: 102 us; the launch traced here: 101 us
  waiting for transfers between devices  31.9 us (31%)
  Pallas kernels  28.5 us (28%)
  starting transfers between devices  24.8 us (24%)
  blocking collectives  11.6 us (11%)
  local copies, waits for them, and re-layouts  2.91 us (3%)
  between operations  1.42 us (1%)
    ppermute x17, waiting for transfers between devices, swap(): return lax.ppermute(value, 'users', [(i, i ^ mask) for i in range(devices)])  29.5 us
    ppermute x17, starting transfers between devices, swap(): return lax.ppermute(value, 'users', [(i, i ^ mask) for i in range(devices)])  15.7 us
    pallas_call x2, Pallas kernels, tile_sums(): pl.pallas_call(functools.partial(tiles_kernel, side), out_shape=out_shape...  13.1 us
    all_to_all x1, blocking collectives, exchange(): lax.all_to_all(value, 'users', 0, 0, axis_index_groups=sides, tiled=True)  11.6 us
    all_to_all x2, starting transfers between devices, exchange(): lax.all_to_all(value, 'users', 0, 0, axis_index_groups=sides, tiled=True)  9.04 us
    pallas_call x1, Pallas kernels, finish(): pl.pallas_call(functools.partial(finish_kernel, users * devices), out_sha...  6.41 us
    pallas_call x1, Pallas kernels, context_values(): pl.pallas_call(context_kernel, out_shape=jax.ShapeDtypeStruct((tile_of.sh...  3.72 us
    pallas_call x2, Pallas kernels, collect(): pl.pallas_call(functools.partial(collect_kernel, lane), out_shape=jax.Sha...  3.01 us
  transfers between devices with their start and end apart: 19, of which 11 were waited for; matrix products, arithmetic and copies ran while one was open for 1% of the time, Pallas kernels for 11%

profile of v9, /device:TPU:0, one launch (start us, length us, event | category | flops | bytes accessed | tf_op | source)
XLA Modules:
  0.0 101.1 jit_solution(4760946927736608784)
XLA Ops:
  0.6 2.2 %route.1 = (s32[16,1,128]{2,1,0:T(1,128)S(1)}, s32[64]{0:T(128)S(1)}, bf16[16,64,128]{2,1,0:T(8,128)(2,1)S(1)}) custom-call(s32[1]{0:T(128)} %bitcast.me_ref, s32[64]{0:T(128)} %bitcast.6, s32[64]{0:T(128)} %slot_ref.1, bf16[16,64,128]{2,1,0:T(8,128)(2,1)} %own_ref.1), custom_call_target="tpu_custom_call" | custom-call | tf_op jit(solution)/shard_map/route/pallas_call | solution.py:85
  2.9 11.6 %all_to_all.15.asked_ref = s32[16,1,128]{2,1,0:T(1,128)S(1)} all-to-all(s32[16,1,128]{2,1,0:T(1,128)S(1)} %get-tuple-element.18), channel_id=1, replica_groups={{0,1,2,3,4,5,6,7,8,9,10,11,12,13,14,15},{16,17,18,19,20,21,22,23,24,25,..., dimensions={0} | all-to-all | bytes 16384 | tf_op jit(solution)/shard_map/all_to_all | solution.py:448
  14.4 1.5 %collect.3 = bf16[32,64,128]{2,1,0:T(8,128)(2,1)} custom-call(s32[16,1,128]{2,1,0:T(1,128)S(1)} %all_to_all.15.asked_ref, bf16[16,64,128]{2,1,0:T(8,128)(2,1)S(1)} %get-tuple-element.19.source_ref), custom_call_target="tpu_custom_call" | custom-call | tf_op jit(solution)/shard_map/collect/pallas_call | solution.py:107
  16.0 3.6 %all-to-all-start.2 = ((bf16[32,64,128]{2,1,0:T(8,128)(2,1)}), bf16[32,64,128]{2,1,0:T(8,128)(2,1)S(1)}, u32[]{:S(2)}, u32[]{:S(2)}) async-start(bf16[32,64,128]{2,1,0:T(8,128)(2,1)} %collect.3), calls=%async_computation.2 | async-start | bytes 1048576 | tf_op jit(solution)/shard_map/all_to_all | solution.py:448
  19.5 2.7 %collective-permute-start = (bf16[16,64,128]{2,1,0:T(8,128)(2,1)}, bf16[16,64,128]{2,1,0:T(8,128)(2,1)S(1)}, u32[]{:S(2)}, u32[]{:S(2)}) collective-permute-start(bf16[16,64,128]{2,1,0:T(8,128)(2,1)} %own_ref.1), channel_id=1, source_target_pairs={{0,16},{1,17},{2,18},{3,19},{4,20},{5,21},{6,22},{7,23},{8,24},{9,... | collective-permute-start | bytes 786440 | tf_op jit(solution)/shard_map/ppermute | solution.py:410
  22.2 9.6 %collective-permute-done.source_ref = bf16[16,64,128]{2,1,0:T(8,128)(2,1)S(1)} collective-permute-done((bf16[16,64,128]{2,1,0:T(8,128)(2,1)}, bf16[16,64,128]{2,1,0:T(8,128)(2,1)S(1)}, u32[]{:S(2)}, u32[]{:S(2)}) %collective-permute-start) | collective-permute-done | bytes 262176 | tf_op jit(solution)/shard_map/ppermute | solution.py:410
  31.8 1.5 %collect.2 = bf16[32,64,128]{2,1,0:T(8,128)(2,1)} custom-call(s32[16,1,128]{2,1,0:T(1,128)S(1)} %all_to_all.15.asked_ref, bf16[16,64,128]{2,1,0:T(8,128)(2,1)S(1)} %collective-permute-done.source_ref), custom_call_target="tpu_custom_call" | custom-call | tf_op jit(solution)/shard_map/collect/pallas_call | solution.py:107
  33.3 2.4 %all-to-all-done.2.blocks_ref = bf16[32,64,128]{2,1,0:T(8,128)(2,1)S(1)} async-done(((bf16[32,64,128]{2,1,0:T(8,128)(2,1)}), bf16[32,64,128]{2,1,0:T(8,128)(2,1)S(1)}, u32[]{:S(2)}, u32[]{:S(2)}) %all-to-all-start.2) | async-done | bytes 524320 | tf_op jit(solution)/shard_map/all_to_all | solution.py:448
  35.7 5.5 %all-to-all-start.1 = ((bf16[32,64,128]{2,1,0:T(8,128)(2,1)}), bf16[32,64,128]{2,1,0:T(8,128)(2,1)S(1)}, u32[]{:S(2)}, u32[]{:S(2)}) async-start(bf16[32,64,128]{2,1,0:T(8,128)(2,1)} %collect.2), calls=%async_computation.1 | async-start | bytes 1048576 | tf_op jit(solution)/shard_map/all_to_all | solution.py:448
  41.8 0.9 reshape.13
  42.8 0.9 copy-done.1
  43.7 3.7 %contexts.1.context_ref = f32[64,8,512]{2,1,0:T(8,128)S(1)} custom-call(s32[64]{0:T(128)S(1)} %get-tuple-element.17.tile_ref, s32[64]{0:T(128)} %cblock_ref, f32[64,8,8]{2,1,0:T(8,128)S(1)} %bitcast.5, s32[64,512]{1,0:T(8,128)S(1)} %copy-done.1), custom_call_target="tpu_custom_call" | custom-call | flops 10000000 | bytes 20000000 | tf_op jit(solution)/shard_map/contexts/pallas_call | solution.py:135
  47.5 1.0 copy-done
  48.4 5.7 %tile_sums.2.refs_0_ = f32[8,64,512]{2,1,0:T(8,128)S(1)} custom-call(s32[64]{0:T(128)S(1)} %get-tuple-element.17.tile_ref, s32[1]{0:T(128)S(6)} %copy.14.count_ref, s32[1]{0:T(128)} %bitcast.me_ref, bf16[32,64,128]{2,1,0:T(8,128)(2,1)S(1)} %all-to-all-done.2.blocks_ref, bf16[64,128,512]{2,1,0:T(8,128)(2,1)} %weights_ref.3, f32[64,8,512]{2,1,0:T(8,128)} %copy-done, ...), custom_call_target="tpu_custom_call" | custom-call | flops 1000000000 | bytes 6000000 | tf_op jit(solution)/shard_map/tile_sums/pallas_call | solution.py:299
  54.2 7.4 %tile_sums.3 = (f32[224,128]{1,0:T(8,128)S(1)}, f32[224,128]{1,0:T(8,128)S(1)}, f32[224,128]{1,0:T(8,128)S(1)}, f32[224,128]{1,0:T(8,128)S(1)}, f32[224,128]{1,0...) custom-call(s32[64]{0:T(128)S(1)} %get-tuple-element.17.tile_ref, ...), custom_call_target="tpu_custom_call" | custom-call | flops 1000000000 | bytes 6000000 | tf_op jit(solution)/shard_map/tile_sums/pallas_call | solution.py:299
  61.6 0.5 collective-permute-start.2
  62.2 0.4 collective-permute-start.6
  63.1 2.9 %collective-permute-start.3 = (f32[224,128]{1,0:T(8,128)S(1)}, f32[224,128]{1,0:T(8,128)S(1)}, u32[]{:S(2)}, u32[]{:S(2)}) collective-permute-start(f32[224,128]{1,0:T(8,128)S(1)} %add.28), channel_id=1, source_target_pairs={{0,6},{1,7},{2,4},{3,5},{4,2},{5,3},{6,0},{7,1},{8,14},{9,15},{10,... | collective-permute-start | bytes 344072 | tf_op jit(solution)/shard_map/ppermute | solution.py:410
  65.9 0.6 collective-permute-start.5
  66.8 3.2 %collective-permute-done.3 = f32[224,128]{1,0:T(8,128)S(1)} collective-permute-done((f32[224,128]{1,0:T(8,128)S(1)}, f32[224,128]{1,0:T(8,128)S(1)}, u32[]{:S(2)}, u32[]{:S(2)}) %collective-permute-start.3) | collective-permute-done | bytes 114720 | tf_op jit(solution)/shard_map/ppermute | solution.py:410
  70.0 2.1 %collective-permute-done.5 = f32[224,128]{1,0:T(8,128)S(1)} collective-permute-done((f32[224,128]{1,0:T(8,128)S(1)}, f32[224,128]{1,0:T(8,128)S(1)}, u32[]{:S(2)}, u32[]{:S(2)}) %collective-permute-start.5) | collective-permute-done | bytes 114720 | tf_op jit(solution)/shard_map/ppermute | solution.py:410
  72.2 1.5 %collective-permute-start.8 = (f32[224,128]{1,0:T(8,128)S(1)}, f32[224,128]{1,0:T(8,128)S(1)}, u32[]{:S(2)}, u32[]{:S(2)}) collective-permute-start(f32[224,128]{1,0:T(8,128)S(1)} %add_add_fusion), channel_id=1, source_target_pairs={{0,8},{1,9},{2,10},{3,11},{4,12},{5,13},{6,14},{7,15},{8,0},{9,1},... | collective-permute-start | bytes 344072 | tf_op jit(solution)/shard_map/ppermute | solution.py:410
  73.7 3.3 %collective-permute-done.8 = f32[224,128]{1,0:T(8,128)S(1)} collective-permute-done((f32[224,128]{1,0:T(8,128)S(1)}, f32[224,128]{1,0:T(8,128)S(1)}, u32[]{:S(2)}, u32[]{:S(2)}) %collective-permute-start.8) | collective-permute-done | bytes 114720 | tf_op jit(solution)/shard_map/ppermute | solution.py:410
  77.0 2.7 %collective-permute-start.9 = (f32[224,128]{1,0:T(8,128)S(1)}, f32[224,128]{1,0:T(8,128)S(1)}, u32[]{:S(2)}, u32[]{:S(2)}) collective-permute-start(f32[224,128]{1,0:T(8,128)S(1)} %add.34), channel_id=1, source_target_pairs={{0,16},{1,17},{2,18},{3,19},{4,20},{5,21},{6,22},{7,23},{8,24},{9,... | collective-permute-start | bytes 344072 | tf_op jit(solution)/shard_map/ppermute | solution.py:410
  79.8 4.2 %collective-permute-done.9 = f32[224,128]{1,0:T(8,128)S(1)} collective-permute-done((f32[224,128]{1,0:T(8,128)S(1)}, f32[224,128]{1,0:T(8,128)S(1)}, u32[]{:S(2)}, u32[]{:S(2)}) %collective-permute-start.9) | collective-permute-done | bytes 114720 | tf_op jit(solution)/shard_map/ppermute | solution.py:410
  84.0 2.5 %collective-permute-start.14 = (f32[224,128]{1,0:T(8,128)S(1)}, f32[224,128]{1,0:T(8,128)S(1)}, u32[]{:S(2)}, u32[]{:S(2)}) collective-permute-start(f32[224,128]{1,0:T(8,128)S(1)} %add.35.rest_7_), channel_id=1, source_target_pairs={{0,4},{1,5},{2,6},{3,7},{4,0},{5,1},{6,2},{7,3},{8,12},{9,13},{10,... | collective-permute-start | bytes 344072 | tf_op jit(solution)/shard_map/ppermute | solution.py:410
  86.5 1.2 %collective-permute-start.12 = (f32[224,128]{1,0:T(8,128)S(1)}, f32[224,128]{1,0:T(8,128)S(1)}, u32[]{:S(2)}, u32[]{:S(2)}) collective-permute-start(f32[224,128]{1,0:T(8,128)S(1)} %add.35.rest_7_), channel_id=1, source_target_pairs={{0,2},{1,3},{2,0},{3,1},{4,6},{5,7},{6,4},{7,5},{8,10},{9,11},{10,... | collective-permute-start | bytes 344072 | tf_op jit(solution)/shard_map/ppermute | solution.py:410
  88.1 1.8 %collective-permute-done.14.rest_6_ = f32[224,128]{1,0:T(8,128)S(1)} collective-permute-done((f32[224,128]{1,0:T(8,128)S(1)}, f32[224,128]{1,0:T(8,128)S(1)}, u32[]{:S(2)}, u32[]{:S(2)}) %collective-permute-start.14) | collective-permute-done | bytes 114720 | tf_op jit(solution)/shard_map/ppermute | solution.py:410
  89.9 2.0 %collective-permute-done.12.rest_5_ = f32[224,128]{1,0:T(8,128)S(1)} collective-permute-done((f32[224,128]{1,0:T(8,128)S(1)}, f32[224,128]{1,0:T(8,128)S(1)}, u32[]{:S(2)}, u32[]{:S(2)}) %collective-permute-start.12) | collective-permute-done | bytes 114720 | tf_op jit(solution)/shard_map/ppermute | solution.py:410
  91.9 1.5 %collective-permute-done.10.rest_4_ = f32[224,128]{1,0:T(8,128)S(1)} collective-permute-done((f32[224,128]{1,0:T(8,128)S(1)}, f32[224,128]{1,0:T(8,128)S(1)}, u32[]{:S(2)}, u32[]{:S(2)}) %collective-permute-start.10) | collective-permute-done | bytes 114720 | tf_op jit(solution)/shard_map/ppermute | solution.py:410
  93.4 1.3 %collective-permute-done.11.rest_0_ = f32[224,128]{1,0:T(8,128)S(1)} collective-permute-done((f32[224,128]{1,0:T(8,128)S(1)}, f32[224,128]{1,0:T(8,128)S(1)}, u32[]{:S(2)}, u32[]{:S(2)}) %collective-permute-start.11) | collective-permute-done | bytes 114720 | tf_op jit(solution)/shard_map/ppermute | solution.py:410
  94.7 6.4 %finish.1 = (f32[512,128]{1,0:T(8,128)}, f32[128,512]{1,0:T(8,128)}) custom-call(s32[1]{0:T(128)} %bitcast.me_ref, bf16[1024,512]{1,0:T(8,128)(2,1)S(1)} %get-tuple-element.23.stack_ref, f32[224,128]{1,0:T(8,128)S(1)} %collective-permute-done.11.rest_0_, f32[224,128]{1,0:T(8,128)S(1)} %collective-permute-done.13.rest_1_, ...), custom_call_target="tpu_custom_call" | custom-call | tf_op jit(solution)/shard_map/finish/pallas_call | solution.py:392
  (26 shorter events, 1.4 us)
Async XLA Ops:
  16.0 19.7 %all-to-all-start.2 = ((bf16[32,64,128]{2,1,0:T(8,128)(2,1)}), bf16[32,64,128]{2,1,0:T(8,128)(2,1)S(1)}, u32[]{:S(2)}, u32[]{:S(2)}) async-start(bf16[32,64,128]{2,1,0:T(8,128)(2,1)} %collect.3), calls=%async_computation.2 | async-start | bytes 1048576 | tf_op jit(solution)/shard_map/all_to_all | solution.py:448
  19.5 12.3 %collective-permute-start = (bf16[16,64,128]{2,1,0:T(8,128)(2,1)}, bf16[16,64,128]{2,1,0:T(8,128)(2,1)S(1)}, u32[]{:S(2)}, u32[]{:S(2)}) collective-permute-start(bf16[16,64,128]{2,1,0:T(8,128)(2,1)} %own_ref.1), channel_id=1, source_target_pairs={{0,16},{1,17},{2,18},{3,19},{4,20},{5,21},{6,22},{7,23},{8,24},{9,... | collective-permute-start | bytes 786440 | tf_op jit(solution)/shard_map/ppermute | solution.py:410
  35.7 18.5 %all-to-all-start.1 = ((bf16[32,64,128]{2,1,0:T(8,128)(2,1)}), bf16[32,64,128]{2,1,0:T(8,128)(2,1)S(1)}, u32[]{:S(2)}, u32[]{:S(2)}) async-start(bf16[32,64,128]{2,1,0:T(8,128)(2,1)} %collect.2), calls=%async_computation.1 | async-start | bytes 1048576 | tf_op jit(solution)/shard_map/all_to_all | solution.py:448
  42.8 0.9 copy-start.1
  47.5 1.0 copy-start
  61.6 1.4 %collective-permute-start.2 = (f32[224,128]{1,0:T(8,128)S(1)}, f32[224,128]{1,0:T(8,128)S(1)}, u32[]{:S(2)}, u32[]{:S(2)}) collective-permute-start(f32[224,128]{1,0:T(8,128)S(1)} %get-tuple-element.27), channel_id=1, source_target_pairs={{0,1},{1,0},{2,3},{3,2},{4,5},{5,4},{6,7},{7,6},{8,9},{9,8},{10,11... | collective-permute-start | bytes 344072 | tf_op jit(solution)/shard_map/ppermute | solution.py:410
  62.1 3.9 %collective-permute-start.4 = (f32[224,128]{1,0:T(8,128)S(1)}, f32[224,128]{1,0:T(8,128)S(1)}, u32[]{:S(2)}, u32[]{:S(2)}) collective-permute-start(f32[224,128]{1,0:T(8,128)S(1)} %get-tuple-element.29), channel_id=1, source_target_pairs={{0,1},{1,0},{2,3},{3,2},{4,5},{5,4},{6,7},{7,6},{8,9},{9,8},{10,11... | collective-permute-start | bytes 344072 | tf_op jit(solution)/shard_map/ppermute | solution.py:410
  62.2 4.4 %collective-permute-start.6 = (f32[224,128]{1,0:T(8,128)S(1)}, f32[224,128]{1,0:T(8,128)S(1)}, u32[]{:S(2)}, u32[]{:S(2)}) collective-permute-start(f32[224,128]{1,0:T(8,128)S(1)} %get-tuple-element.31), channel_id=1, source_target_pairs={{0,1},{1,0},{2,3},{3,2},{4,5},{5,4},{6,7},{7,6},{8,9},{9,8},{10,11... | collective-permute-start | bytes 344072 | tf_op jit(solution)/shard_map/ppermute | solution.py:410
  62.6 4.2 %collective-permute-start.1 = (f32[224,128]{1,0:T(8,128)S(1)}, f32[224,128]{1,0:T(8,128)S(1)}, u32[]{:S(2)}, u32[]{:S(2)}) collective-permute-start(f32[224,128]{1,0:T(8,128)S(1)} %get-tuple-element.25), channel_id=1, source_target_pairs={{0,1},{1,0},{2,3},{3,2},{4,5},{5,4},{6,7},{7,6},{8,9},{9,8},{10,11... | collective-permute-start | bytes 344072 | tf_op jit(solution)/shard_map/ppermute | solution.py:410
  63.1 6.9 %collective-permute-start.3 = (f32[224,128]{1,0:T(8,128)S(1)}, f32[224,128]{1,0:T(8,128)S(1)}, u32[]{:S(2)}, u32[]{:S(2)}) collective-permute-start(f32[224,128]{1,0:T(8,128)S(1)} %add.28), channel_id=1, source_target_pairs={{0,6},{1,7},{2,4},{3,5},{4,2},{5,3},{6,0},{7,1},{8,14},{9,15},{10,... | collective-permute-start | bytes 344072 | tf_op jit(solution)/shard_map/ppermute | solution.py:410
  65.9 6.2 %collective-permute-start.5 = (f32[224,128]{1,0:T(8,128)S(1)}, f32[224,128]{1,0:T(8,128)S(1)}, u32[]{:S(2)}, u32[]{:S(2)}) collective-permute-start(f32[224,128]{1,0:T(8,128)S(1)} %add.30), channel_id=1, source_target_pairs={{0,2},{1,3},{2,0},{3,1},{4,6},{5,7},{6,4},{7,5},{8,10},{9,11},{10,... | collective-permute-start | bytes 344072 | tf_op jit(solution)/shard_map/ppermute | solution.py:410
  66.6 5.5 %collective-permute-start.7 = (f32[224,128]{1,0:T(8,128)S(1)}, f32[224,128]{1,0:T(8,128)S(1)}, u32[]{:S(2)}, u32[]{:S(2)}) collective-permute-start(f32[224,128]{1,0:T(8,128)S(1)} %add.32), channel_id=1, source_target_pairs={{0,4},{1,5},{2,6},{3,7},{4,0},{5,1},{6,2},{7,3},{8,12},{9,13},{10,... | collective-permute-start | bytes 344072 | tf_op jit(solution)/shard_map/ppermute | solution.py:410
  72.2 4.9 %collective-permute-start.8 = (f32[224,128]{1,0:T(8,128)S(1)}, f32[224,128]{1,0:T(8,128)S(1)}, u32[]{:S(2)}, u32[]{:S(2)}) collective-permute-start(f32[224,128]{1,0:T(8,128)S(1)} %add_add_fusion), channel_id=1, source_target_pairs={{0,8},{1,9},{2,10},{3,11},{4,12},{5,13},{6,14},{7,15},{8,0},{9,1},... | collective-permute-start | bytes 344072 | tf_op jit(solution)/shard_map/ppermute | solution.py:410
  77.0 7.0 %collective-permute-start.9 = (f32[224,128]{1,0:T(8,128)S(1)}, f32[224,128]{1,0:T(8,128)S(1)}, u32[]{:S(2)}, u32[]{:S(2)}) collective-permute-start(f32[224,128]{1,0:T(8,128)S(1)} %add.34), channel_id=1, source_target_pairs={{0,16},{1,17},{2,18},{3,19},{4,20},{5,21},{6,22},{7,23},{8,24},{9,... | collective-permute-start | bytes 344072 | tf_op jit(solution)/shard_map/ppermute | solution.py:410
  84.0 5.9 %collective-permute-start.14 = (f32[224,128]{1,0:T(8,128)S(1)}, f32[224,128]{1,0:T(8,128)S(1)}, u32[]{:S(2)}, u32[]{:S(2)}) collective-permute-start(f32[224,128]{1,0:T(8,128)S(1)} %add.35.rest_7_), channel_id=1, source_target_pairs={{0,4},{1,5},{2,6},{3,7},{4,0},{5,1},{6,2},{7,3},{8,12},{9,13},{10,... | collective-permute-start | bytes 344072 | tf_op jit(solution)/shard_map/ppermute | solution.py:410
  86.5 5.3 %collective-permute-start.12 = (f32[224,128]{1,0:T(8,128)S(1)}, f32[224,128]{1,0:T(8,128)S(1)}, u32[]{:S(2)}, u32[]{:S(2)}) collective-permute-start(f32[224,128]{1,0:T(8,128)S(1)} %add.35.rest_7_), channel_id=1, source_target_pairs={{0,2},{1,3},{2,0},{3,1},{4,6},{5,7},{6,4},{7,5},{8,10},{9,11},{10,... | collective-permute-start | bytes 344072 | tf_op jit(solution)/shard_map/ppermute | solution.py:410
  87.7 5.7 %collective-permute-start.10 = (f32[224,128]{1,0:T(8,128)S(1)}, f32[224,128]{1,0:T(8,128)S(1)}, u32[]{:S(2)}, u32[]{:S(2)}) collective-permute-start(f32[224,128]{1,0:T(8,128)S(1)} %add.35.rest_7_), channel_id=1, source_target_pairs={{0,6},{1,7},{2,4},{3,5},{4,2},{5,3},{6,0},{7,1},{8,14},{9,15},{10,... | collective-permute-start | bytes 344072 | tf_op jit(solution)/shard_map/ppermute | solution.py:410
  88.1 5.3 %collective-permute-start.16 = (f32[224,128]{1,0:T(8,128)S(1)}, f32[224,128]{1,0:T(8,128)S(1)}, u32[]{:S(2)}, u32[]{:S(2)}) collective-permute-start(f32[224,128]{1,0:T(8,128)S(1)} %add.35.rest_7_), channel_id=1, source_target_pairs={{0,1},{1,0},{2,3},{3,2},{4,5},{5,4},{6,7},{7,6},{8,9},{9,8},{10,11... | collective-permute-start | bytes 344072 | tf_op jit(solution)/shard_map/ppermute | solution.py:410
  89.9 3.5 %collective-permute-start.15 = (f32[224,128]{1,0:T(8,128)S(1)}, f32[224,128]{1,0:T(8,128)S(1)}, u32[]{:S(2)}, u32[]{:S(2)}) collective-permute-start(f32[224,128]{1,0:T(8,128)S(1)} %collective-permute-done.14.rest_6_), channel_id=1, source_target_pairs={{0,1},{1,0},{2,3},{3,2},{4,5},{5,4},{6,7},{7,6},{8,9},{9,8},{10,11... | collective-permute-start | bytes 344072 | tf_op jit(solution)/shard_map/ppermute | solution.py:410
  91.9 1.6 %collective-permute-start.13 = (f32[224,128]{1,0:T(8,128)S(1)}, f32[224,128]{1,0:T(8,128)S(1)}, u32[]{:S(2)}, u32[]{:S(2)}) collective-permute-start(f32[224,128]{1,0:T(8,128)S(1)} %collective-permute-done.12.rest_5_), channel_id=1, source_target_pairs={{0,1},{1,0},{2,3},{3,2},{4,5},{5,4},{6,7},{7,6},{8,9},{9,8},{10,11... | collective-permute-start | bytes 344072 | tf_op jit(solution)/shard_map/ppermute | solution.py:410
  93.4 1.3 %collective-permute-start.11 = (f32[224,128]{1,0:T(8,128)S(1)}, f32[224,128]{1,0:T(8,128)S(1)}, u32[]{:S(2)}, u32[]{:S(2)}) collective-permute-start(f32[224,128]{1,0:T(8,128)S(1)} %collective-permute-done.10.rest_4_), channel_id=1, source_target_pairs={{0,1},{1,0},{2,3},{3,2},{4,5},{5,4},{6,7},{7,6},{8,9},{9,8},{10,11... | collective-permute-start | bytes 344072 | tf_op jit(solution)/shard_map/ppermute | solution.py:410

commit v10 on v9

--- a/solution.py
+++ b/solution.py
@@ -97,50 +97,72 @@
     )(me, in_hbm(owners), in_hbm(slots), in_hbm(own))
 
 
-def collect_kernel(lane, asked_ref, source_ref, out_ref):
+def collect_kernel(asked_ref, own_ref, mirror_ref, near_ref, far_ref):
     for peer in range(asked_ref.shape[0]):
         for slot in range(SLOTS):
-            out_ref[peer * SLOTS + slot] = source_ref[asked_ref[peer, 0, lane + slot]]
-
-
-def collect(lane, asked, source):
+            near_ref[peer * SLOTS + slot] = own_ref[asked_ref[peer, 0, slot]]
+            far_ref[peer * SLOTS + slot] = mirror_ref[asked_ref[peer, 0, SLOTS + slot]]
+
+
+def collect(asked, own, mirror):
     return pl.pallas_call(
-        functools.partial(collect_kernel, lane),
-        out_shape=jax.ShapeDtypeStruct((asked.shape[0] * SLOTS,) + source.shape[1:], source.dtype),
-        in_specs=[SMEM, VMEM],
-        out_specs=VMEM,
+        collect_kernel,
+        out_shape=(jax.ShapeDtypeStruct((asked.shape[0] * SLOTS,) + own.shape[1:], own.dtype),) * 2,
+        in_specs=[SMEM, VMEM, VMEM],
+        out_specs=(VMEM, VMEM),
         compiler_params=limit(4),
         name="collect",
-    )(asked, source)
-
-
-def context_kernel(tile_ref, cblock_ref, table_ref, marks_ref, context_ref):
-    users = marks_ref.shape[1]
-
-    def one(slot, _):
-        tile = jnp.maximum(tile_ref[slot], 0)
-        table = jnp.where(tile_ref[slot] >= 0, table_ref[cblock_ref[tile]], 0.0)
-        marks = jnp.broadcast_to(marks_ref[pl.ds(tile, 1), :], (ROWS, users))
-        total = jnp.zeros((ROWS, users), jnp.float32)
-        for k in range(CB):
-            column = jnp.broadcast_to(table[:, k : k + 1], (ROWS, users))
-            total = jnp.where(marks == k, column, total)
-        context_ref[slot] = total
+    )(asked, own, mirror)
+
+
+def context_kernel(tile_ref, cblock_ref, factors_ref, marks_ref, context_ref, wide_ref, held_ref, sem_ref):
+    copy = pltpu.make_async_copy(marks_ref, held_ref, sem_ref)
+    copy.start()
+    users = held_ref.shape[1]
+    per = LANES // CB
+    wide_ref[...] = factors_ref[...].astype(jnp.float32)
+    lane = lax.broadcasted_iota(jnp.int32, (ROWS, LANES), 1)
+    sub = lax.broadcasted_iota(jnp.int32, (CB, users), 0)
+    copy.wait()
+
+    def some(first, _):
+        factors, hits = [], []
+        for i in range(per):
+            named = tile_ref[first * per + i]
+            tile = jnp.maximum(named, 0)
+            cblock = cblock_ref[tile]
+            start = pl.multiple_of(cblock // per * LANES, LANES)
+            shift = lax.rem(LANES + (i - lax.rem(cblock, per)) * CB, LANES)
+            turned = pltpu.roll(wide_ref[:, pl.ds(start, LANES)], shift, 1)
+            here = jnp.logical_and(lane // CB == i, named >= 0)
+            factors.append(jnp.where(here, turned, 0.0))
+            marks = jnp.broadcast_to(held_ref[pl.ds(tile, 1), :], (CB, users))
+            hits.append(jnp.where(marks == sub, 1.0, 0.0))
+        factors = jnp.concatenate(factors, axis=0).astype(jnp.bfloat16)
+        hits = jnp.concatenate(hits, axis=0).astype(jnp.bfloat16)
+        rows = pl.ds(pl.multiple_of(first * per, per), per)
+        context_ref[rows] = dot(factors, hits).reshape(per, ROWS, users)
         return 0
 
-    lax.fori_loop(0, tile_ref.shape[0], one, 0, unroll=2)
-
-
-def context_values(tile_of, cblock, table, marks):
+    lax.fori_loop(0, tile_ref.shape[0] // per, some, 0)
+
+
+def context_values(tile_of, cblock, factors, marks):
+    places, users = tile_of.shape[0], marks.shape[1]
     return pl.pallas_call(
         context_kernel,
-        out_shape=jax.ShapeDtypeStruct((tile_of.shape[0], ROWS, marks.shape[1]), jnp.float32),
-        in_specs=[SMEM, SMEM, VMEM, VMEM],
+        out_shape=jax.ShapeDtypeStruct((places, ROWS, users), jnp.float32),
+        in_specs=[SMEM, SMEM, VMEM, ANY],
         out_specs=VMEM,
+        scratch_shapes=[
+            pltpu.VMEM(factors.shape, jnp.float32),
+            pltpu.VMEM(marks.shape, marks.dtype),
+            pltpu.SemaphoreType.DMA,
+        ],
         compiler_params=limit(8),
         cost_estimate=pl.CostEstimate(flops=10**7, bytes_accessed=2 * 10**7, transcendentals=0),
         name="contexts",
-    )(tile_of, in_hbm(cblock), table, marks)
+    )(tile_of, in_hbm(cblock), factors, in_hbm(marks))
 
 
 def pack_places(me):
@@ -281,7 +303,7 @@
         pltpu.SemaphoreType.DMA,
     ]
     out_shape = (y,)
-    operands = [tile_of, count, me, blocks, in_hbm(weights), in_hbm(contexts), in_hbm(user_basis)]
+    operands = [tile_of, count, me, blocks, in_hbm(weights), contexts, in_hbm(user_basis)]
     in_specs = [SMEM] * 3 + [VMEM] + [ANY] * 3
     if side:
         operands.append(before)
@@ -437,7 +459,6 @@
 ):
     devices = lax.axis_size("users")
     half = devices // 2
-    rank_c = context_factors.shape[0]
     me = lax.axis_index("users").astype(jnp.int32).reshape(1)
 
     mirror = swap(item_factors, half, devices)
@@ -447,14 +468,11 @@
     def exchange(value):
         return lax.all_to_all(value, "users", 0, 0, axis_index_groups=sides, tiled=True)
 
-    asked = exchange(requests)
-    found = collect(0, asked, own)
-    found, cblock, factors = lax.optimization_barrier((found, tile_cblock, context_factors))
-    near = exchange(found)
-    far = exchange(collect(SLOTS, asked, mirror))
-
-    table = factors.astype(jnp.float32).reshape(rank_c, -1, CB).transpose(1, 0, 2)
-    contexts = context_values(tile_of, cblock, table, tile_context)
+    asked, mirror = lax.optimization_barrier((exchange(requests), mirror))
+    near, far = collect(asked, own, mirror)
+    near, far, cblock = lax.optimization_barrier((near, far, tile_cblock))
+    near, far = exchange(near), exchange(far)
+    contexts = context_values(tile_of, cblock, context_factors, tile_context)
     shared = (tile_of, user_counts, me)
     before = tile_sums(0, *shared, near, tile_weights, contexts, user_basis)
     pieces, stack = tile_sums(1, *shared, far, tile_weights, contexts, user_basis, before)

time: 102 us -> 94.1 us (0.923)
  blocking collectives: 11.6 us -> 24.4 us
  waiting for transfers between devices: 31.9 us -> 20.5 us
  starting transfers between devices: 24.8 us -> 20.8 us
  Pallas kernels: 28.5 us -> 25.9 us
  local copies, waits for them, and re-layouts: 2.91 us -> 0.69 us
    all_to_all x1 -> x2, blocking collectives: 11.6 us -> 24.4 us  [exchange(): lax.all_to_all(value, 'users', 0, 0, axis_index_groups=sides, tiled=True)]
    ppermute x17, waiting for transfers between devices: 29.5 us -> 19.8 us  [swap(): return lax.ppermute(value, 'users', [(i, i ^ mask) for i in range(devices)])]
    all_to_all x2 -> x1, starting transfers between devices: 9.04 us -> 3.57 us  [exchange(): lax.all_to_all(value, 'users', 0, 0, axis_index_groups=sides, tiled=True)]
    pallas_call x3 -> x2, Pallas kernels: 6.73 us -> 4.44 us  [the longest x1 2.9 us: context_values(): pl.pallas_call(context_kernel, out_shape=jax.ShapeDtypeStruct((places, RO...]
    all_to_all x2 -> x1, waiting for transfers between devices: 2.36 us -> 0.69 us  [exchange(): lax.all_to_all(value, 'users', 0, 0, axis_index_groups=sides, tiled=True)]
    ppermute x17, starting transfers between devices: 15.7 us -> 17.2 us  [swap(): return lax.ppermute(value, 'users', [(i, i ^ mask) for i in range(devices)])]
    unnamed x4 -> x2, local copies, waits for them, and re-layouts: 1.88 us -> 0.69 us
    transpose x2 -> x0, local copies, waits for them, and re-layouts: 1.02 us -> none  [body(): factors.astype(jnp.float32).reshape(rank_c, -1, CB).transpose(1, 0, 2)]
  transfers between devices with their start and end apart: 19 -> 18, of which waited for: 11 -> 11; matrix products, arithmetic and copies ran while one was open for 1% -> 0% of each run, Pallas kernels for 11% -> 11%
where the time goes in v10:
time: 94.1 us; the launch traced here: 93.7 us
  Pallas kernels  25.9 us (28%)
  blocking collectives  24.4 us (26%)
  starting transfers between devices  20.8 us (22%)
  waiting for transfers between devices  20.5 us (22%)
  between operations  1.39 us (1%)
    all_to_all x2, blocking collectives, exchange(): lax.all_to_all(value, 'users', 0, 0, axis_index_groups=sides, tiled=True)  24.4 us
    ppermute x17, waiting for transfers between devices, swap(): return lax.ppermute(value, 'users', [(i, i ^ mask) for i in range(devices)])  19.8 us
    ppermute x17, starting transfers between devices, swap(): return lax.ppermute(value, 'users', [(i, i ^ mask) for i in range(devices)])  17.2 us
    pallas_call x2, Pallas kernels, tile_sums(): pl.pallas_call(functools.partial(tiles_kernel, side), out_shape=out_shape...  12.8 us
    pallas_call x1, Pallas kernels, finish(): pl.pallas_call(functools.partial(finish_kernel, users * devices), out_sha...  6.41 us
    all_to_all x1, starting transfers between devices, exchange(): lax.all_to_all(value, 'users', 0, 0, axis_index_groups=sides, tiled=True)  3.57 us
    pallas_call x1, Pallas kernels, context_values(): pl.pallas_call(context_kernel, out_shape=jax.ShapeDtypeStruct((places, RO...  2.9 us
    pallas_call x1, Pallas kernels, route(): pl.pallas_call(functools.partial(route_kernel, half), out_shape=(jax.Shap...  2.22 us
  transfers between devices with their start and end apart: 18, of which 11 were waited for; matrix products, arithmetic and copies ran while one was open for 0% of the time, Pallas kernels for 11%

profile of v10, /device:TPU:0, one launch (start us, length us, event | category | flops | bytes accessed | tf_op | source)
XLA Modules:
  0.0 93.7 jit_solution(76779014016503556)
XLA Ops:
  0.6 4.1 %collective-permute-start = (bf16[16,64,128]{2,1,0:T(8,128)(2,1)}, bf16[16,64,128]{2,1,0:T(8,128)(2,1)S(1)}, u32[]{:S(2)}, u32[]{:S(2)}) collective-permute-start(bf16[16,64,128]{2,1,0:T(8,128)(2,1)} %own_ref.1), channel_id=1, source_target_pairs={{0,16},{1,17},{2,18},{3,19},{4,20},{5,21},{6,22},{7,23},{8,24},{9,... | collective-permute-start | bytes 786440 | tf_op jit(solution)/shard_map/ppermute | solution.py:432
  4.7 2.2 %route.1 = (s32[16,1,128]{2,1,0:T(1,128)S(1)}, s32[64]{0:T(128)S(1)}, bf16[16,64,128]{2,1,0:T(8,128)(2,1)S(1)}) custom-call(s32[1]{0:T(128)} %bitcast.me_ref, s32[64]{0:T(128)} %bitcast.2, s32[64]{0:T(128)} %slot_ref.1, bf16[16,64,128]{2,1,0:T(8,128)(2,1)} %own_ref.1), custom_call_target="tpu_custom_call" | custom-call | tf_op jit(solution)/shard_map/route/pallas_call | solution.py:85
  7.0 10.5 %all_to_all.15.asked_ref = s32[16,1,128]{2,1,0:T(1,128)S(1)} all-to-all(s32[16,1,128]{2,1,0:T(1,128)S(1)} %get-tuple-element.22), channel_id=1, replica_groups={{0,1,2,3,4,5,6,7,8,9,10,11,12,13,14,15},{16,17,18,19,20,21,22,23,24,25,..., dimensions={0} | all-to-all | bytes 16384 | tf_op jit(solution)/shard_map/all_to_all | solution.py:469
  17.4 1.5 %collect.1 = (bf16[32,64,128]{2,1,0:T(8,128)(2,1)S(1)}, bf16[32,64,128]{2,1,0:T(8,128)(2,1)}) custom-call(s32[16,1,128]{2,1,0:T(1,128)S(1)} %all_to_all.15.asked_ref, bf16[16,64,128]{2,1,0:T(8,128)(2,1)S(1)} %get-tuple-element.24.own_ref, bf16[16,64,128]{2,1,0:T(8,128)(2,1)S(1)} %collective-permute-done.mirror_ref), custom_call_target="tpu_custom_call" | custom-call | tf_op jit(solution)/shard_map/collect/pallas_call | solution.py:108
  19.0 13.9 %all_to_all.16.blocks_ref = bf16[32,64,128]{2,1,0:T(8,128)(2,1)S(1)} all-to-all(bf16[32,64,128]{2,1,0:T(8,128)(2,1)S(1)} %get-tuple-element.30), channel_id=1, replica_groups={{0,1,2,3,4,5,6,7,8,9,10,11,12,13,14,15},{16,17,18,19,20,21,22,23,24,25,..., dimensions={0} | all-to-all | bytes 1048576 | tf_op jit(solution)/shard_map/all_to_all | solution.py:469
  32.9 3.6 %all-to-all-start.1 = ((bf16[32,64,128]{2,1,0:T(8,128)(2,1)}), bf16[32,64,128]{2,1,0:T(8,128)(2,1)S(1)}, u32[]{:S(2)}, u32[]{:S(2)}) async-start(bf16[32,64,128]{2,1,0:T(8,128)(2,1)} %get-tuple-element.28), calls=%async_computation.1 | async-start | bytes 1048576 | tf_op jit(solution)/shard_map/all_to_all | solution.py:469
  37.1 0.7 copy-done
  37.8 2.9 %contexts.1.context_ref = f32[64,8,512]{2,1,0:T(8,128)S(1)} custom-call(s32[64]{0:T(128)S(1)} %get-tuple-element.21.tile_ref, s32[64]{0:T(128)} %cblock_ref, bf16[8,512]{1,0:T(8,128)(2,1)S(1)} %copy-done, s32[64,512]{1,0:T(8,128)} %marks_ref.1), custom_call_target="tpu_custom_call" | custom-call | flops 10000000 | bytes 20000000 | tf_op jit(solution)/shard_map/contexts/pallas_call | solution.py:152
  40.7 5.6 %tile_sums.2.refs_0_ = f32[8,64,512]{2,1,0:T(8,128)S(1)} custom-call(s32[64]{0:T(128)S(1)} %get-tuple-element.21.tile_ref, s32[1]{0:T(128)S(6)} %copy.11.count_ref, s32[1]{0:T(128)} %bitcast.me_ref, bf16[32,64,128]{2,1,0:T(8,128)(2,1)S(1)} %all_to_all.16.blocks_ref, bf16[64,128,512]{2,1,0:T(8,128)(2,1)} %weights_ref.3, ...), custom_call_target="tpu_custom_call" | custom-call | flops 1000000000 | bytes 6000000 | tf_op jit(solution)/shard_map/tile_sums/pallas_call | solution.py:321
  46.3 0.7 all-to-all-done.1.blocks_ref
  47.0 7.3 %tile_sums.3 = (f32[224,128]{1,0:T(8,128)S(1)}, f32[224,128]{1,0:T(8,128)S(1)}, f32[224,128]{1,0:T(8,128)S(1)}, f32[224,128]{1,0:T(8,128)S(1)}, f32[224,128]{1,0...) custom-call(s32[64]{0:T(128)S(1)} %get-tuple-element.21.tile_ref, ...), custom_call_target="tpu_custom_call" | custom-call | flops 1000000000 | bytes 6000000 | tf_op jit(solution)/shard_map/tile_sums/pallas_call | solution.py:321
  54.3 0.5 collective-permute-start.4
  54.8 0.1 collective-permute-start.6
  54.9 0.4 collective-permute-start.1
  55.3 0.3 collective-permute-done.2
  55.6 2.2 %collective-permute-start.3 = (f32[224,128]{1,0:T(8,128)S(1)}, f32[224,128]{1,0:T(8,128)S(1)}, u32[]{:S(2)}, u32[]{:S(2)}) collective-permute-start(f32[224,128]{1,0:T(8,128)S(1)} %add.28), channel_id=1, source_target_pairs={{0,6},{1,7},{2,4},{3,5},{4,2},{5,3},{6,0},{7,1},{8,14},{9,15},{10,... | collective-permute-start | bytes 344072 | tf_op jit(solution)/shard_map/ppermute | solution.py:432
  57.8 0.6 collective-permute-start.5
  58.4 0.9 collective-permute-start.7
  59.4 3.2 %collective-permute-done.3 = f32[224,128]{1,0:T(8,128)S(1)} collective-permute-done((f32[224,128]{1,0:T(8,128)S(1)}, f32[224,128]{1,0:T(8,128)S(1)}, u32[]{:S(2)}, u32[]{:S(2)}) %collective-permute-start.3) | collective-permute-done | bytes 114720 | tf_op jit(solution)/shard_map/ppermute | solution.py:432
  62.6 1.4 %collective-permute-done.5 = f32[224,128]{1,0:T(8,128)S(1)} collective-permute-done((f32[224,128]{1,0:T(8,128)S(1)}, f32[224,128]{1,0:T(8,128)S(1)}, u32[]{:S(2)}, u32[]{:S(2)}) %collective-permute-start.5) | collective-permute-done | bytes 114720 | tf_op jit(solution)/shard_map/ppermute | solution.py:432
  64.0 0.3 collective-permute-done.7
  64.3 1.3 %collective-permute-start.8 = (f32[224,128]{1,0:T(8,128)S(1)}, f32[224,128]{1,0:T(8,128)S(1)}, u32[]{:S(2)}, u32[]{:S(2)}) collective-permute-start(f32[224,128]{1,0:T(8,128)S(1)} %add_add_fusion), channel_id=1, source_target_pairs={{0,8},{1,9},{2,10},{3,11},{4,12},{5,13},{6,14},{7,15},{8,0},{9,1},... | collective-permute-start | bytes 344072 | tf_op jit(solution)/shard_map/ppermute | solution.py:432
  65.6 3.6 %collective-permute-done.8 = f32[224,128]{1,0:T(8,128)S(1)} collective-permute-done((f32[224,128]{1,0:T(8,128)S(1)}, f32[224,128]{1,0:T(8,128)S(1)}, u32[]{:S(2)}, u32[]{:S(2)}) %collective-permute-start.8) | collective-permute-done | bytes 114720 | tf_op jit(solution)/shard_map/ppermute | solution.py:432
  69.2 3.4 %collective-permute-start.9 = (f32[224,128]{1,0:T(8,128)S(1)}, f32[224,128]{1,0:T(8,128)S(1)}, u32[]{:S(2)}, u32[]{:S(2)}) collective-permute-start(f32[224,128]{1,0:T(8,128)S(1)} %add.34), channel_id=1, source_target_pairs={{0,16},{1,17},{2,18},{3,19},{4,20},{5,21},{6,22},{7,23},{8,24},{9,... | collective-permute-start | bytes 344072 | tf_op jit(solution)/shard_map/ppermute | solution.py:432
  72.6 4.2 %collective-permute-done.9 = f32[224,128]{1,0:T(8,128)S(1)} collective-permute-done((f32[224,128]{1,0:T(8,128)S(1)}, f32[224,128]{1,0:T(8,128)S(1)}, u32[]{:S(2)}, u32[]{:S(2)}) %collective-permute-start.9) | collective-permute-done | bytes 114720 | tf_op jit(solution)/shard_map/ppermute | solution.py:432
  76.8 1.8 %collective-permute-start.14 = (f32[224,128]{1,0:T(8,128)S(1)}, f32[224,128]{1,0:T(8,128)S(1)}, u32[]{:S(2)}, u32[]{:S(2)}) collective-permute-start(f32[224,128]{1,0:T(8,128)S(1)} %add.35.rest_7_), channel_id=1, source_target_pairs={{0,4},{1,5},{2,6},{3,7},{4,0},{5,1},{6,2},{7,3},{8,12},{9,13},{10,... | collective-permute-start | bytes 344072 | tf_op jit(solution)/shard_map/ppermute | solution.py:432
  78.5 1.8 %collective-permute-start.12 = (f32[224,128]{1,0:T(8,128)S(1)}, f32[224,128]{1,0:T(8,128)S(1)}, u32[]{:S(2)}, u32[]{:S(2)}) collective-permute-start(f32[224,128]{1,0:T(8,128)S(1)} %add.35.rest_7_), channel_id=1, source_target_pairs={{0,2},{1,3},{2,0},{3,1},{4,6},{5,7},{6,4},{7,5},{8,10},{9,11},{10,... | collective-permute-start | bytes 344072 | tf_op jit(solution)/shard_map/ppermute | solution.py:432
  80.3 2.5 %collective-permute-done.14.rest_6_ = f32[224,128]{1,0:T(8,128)S(1)} collective-permute-done((f32[224,128]{1,0:T(8,128)S(1)}, f32[224,128]{1,0:T(8,128)S(1)}, u32[]{:S(2)}, u32[]{:S(2)}) %collective-permute-start.14) | collective-permute-done | bytes 114720 | tf_op jit(solution)/shard_map/ppermute | solution.py:432
  82.8 0.5 collective-permute-done.12.rest_5_
  83.4 2.6 %collective-permute-done.10.rest_4_ = f32[224,128]{1,0:T(8,128)S(1)} collective-permute-done((f32[224,128]{1,0:T(8,128)S(1)}, f32[224,128]{1,0:T(8,128)S(1)}, u32[]{:S(2)}, u32[]{:S(2)}) %collective-permute-start.10) | collective-permute-done | bytes 114720 | tf_op jit(solution)/shard_map/ppermute | solution.py:432
  86.0 1.3 %collective-permute-done.11.rest_0_ = f32[224,128]{1,0:T(8,128)S(1)} collective-permute-done((f32[224,128]{1,0:T(8,128)S(1)}, f32[224,128]{1,0:T(8,128)S(1)}, u32[]{:S(2)}, u32[]{:S(2)}) %collective-permute-start.11) | collective-permute-done | bytes 114720 | tf_op jit(solution)/shard_map/ppermute | solution.py:432
  87.3 6.4 %finish.1 = (f32[512,128]{1,0:T(8,128)}, f32[128,512]{1,0:T(8,128)}) custom-call(s32[1]{0:T(128)} %bitcast.me_ref, bf16[1024,512]{1,0:T(8,128)(2,1)S(1)} %get-tuple-element.31.stack_ref, f32[224,128]{1,0:T(8,128)S(1)} %collective-permute-done.11.rest_0_, f32[224,128]{1,0:T(8,128)S(1)} %collective-permute-done.13.rest_1_, ...), custom_call_target="tpu_custom_call" | custom-call | tf_op jit(solution)/shard_map/finish/pallas_call | solution.py:414
  (20 shorter events, 0.3 us)
Async XLA Ops:
  0.6 16.8 %collective-permute-start = (bf16[16,64,128]{2,1,0:T(8,128)(2,1)}, bf16[16,64,128]{2,1,0:T(8,128)(2,1)S(1)}, u32[]{:S(2)}, u32[]{:S(2)}) collective-permute-start(bf16[16,64,128]{2,1,0:T(8,128)(2,1)} %own_ref.1), channel_id=1, source_target_pairs={{0,16},{1,17},{2,18},{3,19},{4,20},{5,21},{6,22},{7,23},{8,24},{9,... | collective-permute-start | bytes 786440 | tf_op jit(solution)/shard_map/ppermute | solution.py:432
  32.9 14.1 %all-to-all-start.1 = ((bf16[32,64,128]{2,1,0:T(8,128)(2,1)}), bf16[32,64,128]{2,1,0:T(8,128)(2,1)S(1)}, u32[]{:S(2)}, u32[]{:S(2)}) async-start(bf16[32,64,128]{2,1,0:T(8,128)(2,1)} %get-tuple-element.28), calls=%async_computation.1 | async-start | bytes 1048576 | tf_op jit(solution)/shard_map/all_to_all | solution.py:469
  37.1 0.7 copy-start
  54.2 1.4 %collective-permute-start.2 = (f32[224,128]{1,0:T(8,128)S(1)}, f32[224,128]{1,0:T(8,128)S(1)}, u32[]{:S(2)}, u32[]{:S(2)}) collective-permute-start(f32[224,128]{1,0:T(8,128)S(1)} %get-tuple-element.35), channel_id=1, source_target_pairs={{0,1},{1,0},{2,3},{3,2},{4,5},{5,4},{6,7},{7,6},{8,9},{9,8},{10,11... | collective-permute-start | bytes 344072 | tf_op jit(solution)/shard_map/ppermute | solution.py:432
  54.3 3.5 %collective-permute-start.4 = (f32[224,128]{1,0:T(8,128)S(1)}, f32[224,128]{1,0:T(8,128)S(1)}, u32[]{:S(2)}, u32[]{:S(2)}) collective-permute-start(f32[224,128]{1,0:T(8,128)S(1)} %get-tuple-element.37), channel_id=1, source_target_pairs={{0,1},{1,0},{2,3},{3,2},{4,5},{5,4},{6,7},{7,6},{8,9},{9,8},{10,11... | collective-permute-start | bytes 344072 | tf_op jit(solution)/shard_map/ppermute | solution.py:432
  54.8 3.6 %collective-permute-start.6 = (f32[224,128]{1,0:T(8,128)S(1)}, f32[224,128]{1,0:T(8,128)S(1)}, u32[]{:S(2)}, u32[]{:S(2)}) collective-permute-start(f32[224,128]{1,0:T(8,128)S(1)} %get-tuple-element.39), channel_id=1, source_target_pairs={{0,1},{1,0},{2,3},{3,2},{4,5},{5,4},{6,7},{7,6},{8,9},{9,8},{10,11... | collective-permute-start | bytes 344072 | tf_op jit(solution)/shard_map/ppermute | solution.py:432
  54.9 4.5 %collective-permute-start.1 = (f32[224,128]{1,0:T(8,128)S(1)}, f32[224,128]{1,0:T(8,128)S(1)}, u32[]{:S(2)}, u32[]{:S(2)}) collective-permute-start(f32[224,128]{1,0:T(8,128)S(1)} %get-tuple-element.33), channel_id=1, source_target_pairs={{0,1},{1,0},{2,3},{3,2},{4,5},{5,4},{6,7},{7,6},{8,9},{9,8},{10,11... | collective-permute-start | bytes 344072 | tf_op jit(solution)/shard_map/ppermute | solution.py:432
  55.6 7.0 %collective-permute-start.3 = (f32[224,128]{1,0:T(8,128)S(1)}, f32[224,128]{1,0:T(8,128)S(1)}, u32[]{:S(2)}, u32[]{:S(2)}) collective-permute-start(f32[224,128]{1,0:T(8,128)S(1)} %add.28), channel_id=1, source_target_pairs={{0,6},{1,7},{2,4},{3,5},{4,2},{5,3},{6,0},{7,1},{8,14},{9,15},{10,... | collective-permute-start | bytes 344072 | tf_op jit(solution)/shard_map/ppermute | solution.py:432
  57.8 6.2 %collective-permute-start.5 = (f32[224,128]{1,0:T(8,128)S(1)}, f32[224,128]{1,0:T(8,128)S(1)}, u32[]{:S(2)}, u32[]{:S(2)}) collective-permute-start(f32[224,128]{1,0:T(8,128)S(1)} %add.30), channel_id=1, source_target_pairs={{0,2},{1,3},{2,0},{3,1},{4,6},{5,7},{6,4},{7,5},{8,10},{9,11},{10,... | collective-permute-start | bytes 344072 | tf_op jit(solution)/shard_map/ppermute | solution.py:432
  58.4 5.8 %collective-permute-start.7 = (f32[224,128]{1,0:T(8,128)S(1)}, f32[224,128]{1,0:T(8,128)S(1)}, u32[]{:S(2)}, u32[]{:S(2)}) collective-permute-start(f32[224,128]{1,0:T(8,128)S(1)} %add.32), channel_id=1, source_target_pairs={{0,4},{1,5},{2,6},{3,7},{4,0},{5,1},{6,2},{7,3},{8,12},{9,13},{10,... | collective-permute-start | bytes 344072 | tf_op jit(solution)/shard_map/ppermute | solution.py:432
  64.3 4.9 %collective-permute-start.8 = (f32[224,128]{1,0:T(8,128)S(1)}, f32[224,128]{1,0:T(8,128)S(1)}, u32[]{:S(2)}, u32[]{:S(2)}) collective-permute-start(f32[224,128]{1,0:T(8,128)S(1)} %add_add_fusion), channel_id=1, source_target_pairs={{0,8},{1,9},{2,10},{3,11},{4,12},{5,13},{6,14},{7,15},{8,0},{9,1},... | collective-permute-start | bytes 344072 | tf_op jit(solution)/shard_map/ppermute | solution.py:432
  69.2 7.6 %collective-permute-start.9 = (f32[224,128]{1,0:T(8,128)S(1)}, f32[224,128]{1,0:T(8,128)S(1)}, u32[]{:S(2)}, u32[]{:S(2)}) collective-permute-start(f32[224,128]{1,0:T(8,128)S(1)} %add.34), channel_id=1, source_target_pairs={{0,16},{1,17},{2,18},{3,19},{4,20},{5,21},{6,22},{7,23},{8,24},{9,... | collective-permute-start | bytes 344072 | tf_op jit(solution)/shard_map/ppermute | solution.py:432
  76.8 6.1 %collective-permute-start.14 = (f32[224,128]{1,0:T(8,128)S(1)}, f32[224,128]{1,0:T(8,128)S(1)}, u32[]{:S(2)}, u32[]{:S(2)}) collective-permute-start(f32[224,128]{1,0:T(8,128)S(1)} %add.35.rest_7_), channel_id=1, source_target_pairs={{0,4},{1,5},{2,6},{3,7},{4,0},{5,1},{6,2},{7,3},{8,12},{9,13},{10,... | collective-permute-start | bytes 344072 | tf_op jit(solution)/shard_map/ppermute | solution.py:432
  78.5 4.8 %collective-permute-start.12 = (f32[224,128]{1,0:T(8,128)S(1)}, f32[224,128]{1,0:T(8,128)S(1)}, u32[]{:S(2)}, u32[]{:S(2)}) collective-permute-start(f32[224,128]{1,0:T(8,128)S(1)} %add.35.rest_7_), channel_id=1, source_target_pairs={{0,2},{1,3},{2,0},{3,1},{4,6},{5,7},{6,4},{7,5},{8,10},{9,11},{10,... | collective-permute-start | bytes 344072 | tf_op jit(solution)/shard_map/ppermute | solution.py:432
  80.3 5.7 %collective-permute-start.10 = (f32[224,128]{1,0:T(8,128)S(1)}, f32[224,128]{1,0:T(8,128)S(1)}, u32[]{:S(2)}, u32[]{:S(2)}) collective-permute-start(f32[224,128]{1,0:T(8,128)S(1)} %add.35.rest_7_), channel_id=1, source_target_pairs={{0,6},{1,7},{2,4},{3,5},{4,2},{5,3},{6,0},{7,1},{8,14},{9,15},{10,... | collective-permute-start | bytes 344072 | tf_op jit(solution)/shard_map/ppermute | solution.py:432
  80.3 5.7 %collective-permute-start.16 = (f32[224,128]{1,0:T(8,128)S(1)}, f32[224,128]{1,0:T(8,128)S(1)}, u32[]{:S(2)}, u32[]{:S(2)}) collective-permute-start(f32[224,128]{1,0:T(8,128)S(1)} %add.35.rest_7_), channel_id=1, source_target_pairs={{0,1},{1,0},{2,3},{3,2},{4,5},{5,4},{6,7},{7,6},{8,9},{9,8},{10,11... | collective-permute-start | bytes 344072 | tf_op jit(solution)/shard_map/ppermute | solution.py:432
  82.8 3.1 %collective-permute-start.15 = (f32[224,128]{1,0:T(8,128)S(1)}, f32[224,128]{1,0:T(8,128)S(1)}, u32[]{:S(2)}, u32[]{:S(2)}) collective-permute-start(f32[224,128]{1,0:T(8,128)S(1)} %collective-permute-done.14.rest_6_), channel_id=1, source_target_pairs={{0,1},{1,0},{2,3},{3,2},{4,5},{5,4},{6,7},{7,6},{8,9},{9,8},{10,11... | collective-permute-start | bytes 344072 | tf_op jit(solution)/shard_map/ppermute | solution.py:432
  83.3 2.7 %collective-permute-start.13 = (f32[224,128]{1,0:T(8,128)S(1)}, f32[224,128]{1,0:T(8,128)S(1)}, u32[]{:S(2)}, u32[]{:S(2)}) collective-permute-start(f32[224,128]{1,0:T(8,128)S(1)} %collective-permute-done.12.rest_5_), channel_id=1, source_target_pairs={{0,1},{1,0},{2,3},{3,2},{4,5},{5,4},{6,7},{7,6},{8,9},{9,8},{10,11... | collective-permute-start | bytes 344072 | tf_op jit(solution)/shard_map/ppermute | solution.py:432
  86.0 1.3 %collective-permute-start.11 = (f32[224,128]{1,0:T(8,128)S(1)}, f32[224,128]{1,0:T(8,128)S(1)}, u32[]{:S(2)}, u32[]{:S(2)}) collective-permute-start(f32[224,128]{1,0:T(8,128)S(1)} %collective-permute-done.10.rest_4_), channel_id=1, source_target_pairs={{0,1},{1,0},{2,3},{3,2},{4,5},{5,4},{6,7},{7,6},{8,9},{9,8},{10,11... | collective-permute-start | bytes 344072 | tf_op jit(solution)/shard_map/ppermute | solution.py:432

commit v11 on v7

--- a/solution.py
+++ b/solution.py
@@ -14,6 +14,7 @@
 ROWS = 8
 BATCH = 8
 CHUNKS = 8
+GROUP = 32
 MIB = 2**20
 
 SMEM = pl.BlockSpec(memory_space=pltpu.SMEM)
@@ -389,25 +390,47 @@
     return lax.ppermute(value, "users", [(i, i ^ mask) for i in range(devices)])
 
 
+def encode(value):
+    rows, lanes = value.shape
+    groups = rows // GROUP
+    parts = value.reshape(groups, GROUP, lanes)
+    most = jnp.max(jnp.abs(parts), axis=1, keepdims=True)
+    exponent = jnp.clip(jnp.floor(jnp.log2(most)) + 1.0, -110.0, 128.0)
+    coded = jnp.clip(jnp.round(parts * jnp.exp2(14.0 - exponent)), -32767.0, 32767.0)
+    extra = jnp.pad(exponent.reshape(groups, lanes), ((0, -groups % 16), (0, 0)))
+    return jnp.concatenate([coded.reshape(rows, lanes), extra], axis=0).astype(jnp.int16)
+
+
+def decode(coded, rows):
+    lanes = coded.shape[1]
+    groups = rows // GROUP
+    scale = jnp.exp2(coded[rows : rows + groups].astype(jnp.float32) - 14.0)
+    parts = coded[:rows].astype(jnp.float32).reshape(groups, GROUP, lanes)
+    return (parts * scale.reshape(groups, 1, lanes)).reshape(rows, lanes)
+
+
 def reduce_pieces(pieces, devices):
+    rows = pieces[0, 0].shape[0]
     got = {plane: swap(pieces[1, plane], 1, devices) for plane in (3, 1, 2, 0)}
     total = pieces[0, 0] + got[0]
     for plane in (3, 1, 2):
-        total = total + swap(pieces[0, plane] + got[plane], 2 * plane, devices)
+        coded = encode(pieces[0, plane] + got[plane])
+        total = total + decode(swap(coded, 2 * plane, devices), rows)
     mask = CHUNKS
     while mask < devices:
-        total = total + swap(total, mask, devices)
+        coded = encode(total)
+        total = decode(coded, rows) + decode(swap(coded, mask, devices), rows)
         mask *= 2
-    return total
-
-
-def spread_pieces(total, devices):
-    pieces = {(0, 0): total}
+    return encode(total)
+
+
+def spread_pieces(total, devices, rows):
+    coded = {(0, 0): total}
     for plane in (3, 1, 2):
-        pieces[0, plane] = swap(total, 2 * plane, devices)
+        coded[0, plane] = swap(total, 2 * plane, devices)
     for plane in (0, 3, 1, 2):
-        pieces[1, plane] = swap(pieces[0, plane], 1, devices)
-    return pieces
+        coded[1, plane] = swap(coded[0, plane], 1, devices)
+    return {piece: decode(value, rows) for piece, value in coded.items()}
 
 
 def body(
@@ -432,7 +455,8 @@
     pieces, stack = tile_sums(
         where, user_counts, me, blocks, tile_weights, contexts, user_basis
     )
-    pieces = spread_pieces(reduce_pieces(pieces, devices), devices)
+    rows = pieces[0, 0].shape[0]
+    pieces = spread_pieces(reduce_pieces(pieces, devices), devices, rows)
     return finish(me, stack, pieces, devices)
 
 

time: 91.2 us -> 87.3 us (0.957)
  waiting for transfers between devices: 28.7 us -> 23.2 us
  other arithmetic: 0.11 us -> 1.07 us
    ppermute x17, waiting for transfers between devices: 19.8 us -> 14.4 us  [swap(): return lax.ppermute(value, 'users', [(i, i ^ mask) for i in range(devices)])]
  transfers between devices with their start and end apart: 18 -> 18, of which waited for: 11 -> 10; matrix products, arithmetic and copies ran while one was open for 1% -> 2% of each run, Pallas kernels for 7% -> 7%
where the time goes in v11:
time: 87.3 us; the launch traced here: 87 us
  Pallas kernels  27.4 us (31%)
  waiting for transfers between devices  23.2 us (27%)
  starting transfers between devices  20.3 us (23%)
  blocking collectives  10.5 us (12%)
  local copies, waits for them, and re-layouts  2.9 us (3%)
  between operations  1.62 us (2%)
  other arithmetic  1.07 us (1%)
    ppermute x17, starting transfers between devices, swap(): return lax.ppermute(value, 'users', [(i, i ^ mask) for i in range(devices)])  16.7 us
    ppermute x17, waiting for transfers between devices, swap(): return lax.ppermute(value, 'users', [(i, i ^ mask) for i in range(devices)])  14.4 us
    pallas_call x1, Pallas kernels, tile_sums(): pl.pallas_call(tiles_kernel, out_shape=out_shape, in_specs=[SMEM] * 3 + [...  13.3 us
    all_to_all x1, blocking collectives, body(): lax.all_to_all(requests, 'users', 0, 0, axis_index_groups=sides, tiled=True)  10.5 us
    all_to_all x1, waiting for transfers between devices, body(): lax.all_to_all(found, 'users', 0, 0, axis_index_groups=sides, tiled=True)  8.83 us
    pallas_call x1, Pallas kernels, finish(): pl.pallas_call(functools.partial(finish_kernel, users * devices), out_sha...  6.41 us
    pallas_call x1, Pallas kernels, context_values(): pl.pallas_call(context_kernel, out_shape=jax.ShapeDtypeStruct((tiles, ROW...  3.71 us
    all_to_all x1, starting transfers between devices, body(): lax.all_to_all(found, 'users', 0, 0, axis_index_groups=sides, tiled=True)  3.65 us
  transfers between devices with their start and end apart: 18, of which 10 were waited for; matrix products, arithmetic and copies ran while one was open for 2% of the time, Pallas kernels for 7%

profile of v11, /device:TPU:0, one launch (start us, length us, event | category | flops | bytes accessed | tf_op | source)
XLA Modules:
  0.0 87.0 jit_solution(15182363155112095381)
XLA Ops:
  0.6 4.1 %collective-permute-start = (bf16[16,64,128]{2,1,0:T(8,128)(2,1)}, bf16[16,64,128]{2,1,0:T(8,128)(2,1)S(1)}, u32[]{:S(2)}, u32[]{:S(2)}) collective-permute-start(bf16[16,64,128]{2,1,0:T(8,128)(2,1)} %own_ref.1), channel_id=1, source_target_pairs={{0,16},{1,17},{2,18},{3,19},{4,20},{5,21},{6,22},{7,23},{8,24},{9,... | collective-permute-start | bytes 786440 | tf_op jit(solution)/shard_map/ppermute | solution.py:390
  4.7 2.2 %route.1 = (s32[16,1,128]{2,1,0:T(1,128)S(1)}, s32[64]{0:T(128)S(1)}, bf16[16,64,128]{2,1,0:T(8,128)(2,1)S(1)}) custom-call(s32[1]{0:T(128)} %bitcast.me_ref, s32[64]{0:T(128)} %bitcast.136, s32[64]{0:T(128)} %slot_ref.1, bf16[16,64,128]{2,1,0:T(8,128)(2,1)} %own_ref.1), custom_call_target="tpu_custom_call" | custom-call | tf_op jit(solution)/shard_map/route/pallas_call | solution.py:85
  7.0 10.5 %all_to_all.10.asked_ref = s32[16,1,128]{2,1,0:T(1,128)S(1)} all-to-all(s32[16,1,128]{2,1,0:T(1,128)S(1)} %get-tuple-element.18), channel_id=1, replica_groups={{0,1,2,3,4,5,6,7,8,9,10,11,12,13,14,15},{16,17,18,19,20,21,22,23,24,25,..., dimensions={0} | all-to-all | bytes 16384 | tf_op jit(solution)/shard_map/all_to_all | solution.py:448
  17.4 1.7 %collect.1 = bf16[64,64,128]{2,1,0:T(8,128)(2,1)} custom-call(s32[16,1,128]{2,1,0:T(1,128)S(1)} %all_to_all.10.asked_ref, bf16[16,64,128]{2,1,0:T(8,128)(2,1)S(1)} %get-tuple-element.19.own_ref, bf16[16,64,128]{2,1,0:T(8,128)(2,1)S(1)} %collective-permute-done.mirror_ref), custom_call_target="tpu_custom_call" | custom-call | tf_op jit(solution)/shard_map/collect/pallas_call | solution.py:108
  19.1 3.7 %all-to-all-start.1 = ((bf16[64,64,128]{2,1,0:T(8,128)(2,1)}), bf16[64,64,128]{2,1,0:T(8,128)(2,1)S(1)}, u32[]{:S(2)}, u32[]{:S(2)}) async-start(bf16[64,64,128]{2,1,0:T(8,128)(2,1)} %collect.1), calls=%async_computation.1 | async-start | bytes 2097152 | tf_op jit(solution)/shard_map/all_to_all | solution.py:451
  23.5 0.9 reshape.232
  24.3 0.2 copy.13
  24.5 0.9 %copy-done.1 = s32[64,512]{1,0:T(8,128)S(1)} copy-done((s32[64,512]{1,0:T(8,128)S(1)}, s32[64,512]{1,0:T(8,128)}, u32[]{:S(2)}) %copy-start.1) | copy-done | bytes 131096
  25.4 3.7 %contexts.1.context_ref = f32[64,8,512]{2,1,0:T(8,128)S(1)} custom-call(s32[64]{0:T(128)} %cblock_ref, f32[64,8,8]{2,1,0:T(8,128)S(1)} %bitcast.129, s32[64,512]{1,0:T(8,128)S(1)} %copy-done.1), custom_call_target="tpu_custom_call" | custom-call | flops 10000000 | bytes 20000000 | tf_op jit(solution)/shard_map/contexts/pallas_call | solution.py:136
  29.1 1.0 %copy-done = f32[64,8,512]{2,1,0:T(8,128)} copy-done((f32[64,8,512]{2,1,0:T(8,128)}, f32[64,8,512]{2,1,0:T(8,128)S(1)}, u32[]{:S(2)}) %copy-start) | copy-done | bytes 1048600
  30.1 8.8 %all-to-all-done.1.blocks_ref = bf16[64,64,128]{2,1,0:T(8,128)(2,1)S(1)} async-done(((bf16[64,64,128]{2,1,0:T(8,128)(2,1)}), bf16[64,64,128]{2,1,0:T(8,128)(2,1)S(1)}, u32[]{:S(2)}, u32[]{:S(2)}) %all-to-all-start.1) | async-done | bytes 1048608 | tf_op jit(solution)/shard_map/all_to_all | solution.py:451
  38.9 13.3 %tile_sums.1 = (f32[224,128]{1,0:T(8,128)S(1)}, f32[224,128]{1,0:T(8,128)S(1)}, f32[224,128]{1,0:T(8,128)S(1)}, f32[224,128]{1,0:T(8,128)S(1)}, f32[224,128]{1,0...) custom-call(s32[64]{0:T(128)S(1)} %get-tuple-element.17.where_ref, ...), custom_call_target="tpu_custom_call" | custom-call | flops 2000000000 | bytes 12000000 | tf_op jit(solution)/shard_map/tile_sums/pallas_call | solution.py:267
  52.3 0.5 collective-permute-start.1
  52.9 0.4 collective-permute-start.6
  53.3 0.3 collective-permute-done.2
  53.8 1.0 %collective-permute-start.3 = (s16[240,128]{1,0:T(8,128)(2,1)S(1)}, s16[240,128]{1,0:T(8,128)(2,1)S(1)}, u32[]{:S(2)}, u32[]{:S(2)}) collective-permute-start(s16[240,128]{1,0:T(8,128)(2,1)S(1)} %pad_add_fusion.5), channel_id=1, source_target_pairs={{0,6},{1,7},{2,4},{3,5},{4,2},{5,3},{6,0},{7,1},{8,14},{9,15},{10,... | collective-permute-start | bytes 184328 | tf_op jit(solution)/shard_map/ppermute | solution.py:390
  54.9 1.4 %collective-permute-start.5 = (s16[240,128]{1,0:T(8,128)(2,1)S(1)}, s16[240,128]{1,0:T(8,128)(2,1)S(1)}, u32[]{:S(2)}, u32[]{:S(2)}) collective-permute-start(s16[240,128]{1,0:T(8,128)(2,1)S(1)} %pad_add_fusion.4), channel_id=1, source_target_pairs={{0,2},{1,3},{2,0},{3,1},{4,6},{5,7},{6,4},{7,5},{8,10},{9,11},{10,... | collective-permute-start | bytes 184328 | tf_op jit(solution)/shard_map/ppermute | solution.py:390
  56.4 1.2 %collective-permute-start.7 = (s16[240,128]{1,0:T(8,128)(2,1)S(1)}, s16[240,128]{1,0:T(8,128)(2,1)S(1)}, u32[]{:S(2)}, u32[]{:S(2)}) collective-permute-start(s16[240,128]{1,0:T(8,128)(2,1)S(1)} %pad_add_fusion.3), channel_id=1, source_target_pairs={{0,4},{1,5},{2,6},{3,7},{4,0},{5,1},{6,2},{7,3},{8,12},{9,13},{10,... | collective-permute-start | bytes 184328 | tf_op jit(solution)/shard_map/ppermute | solution.py:390
  57.7 1.9 %collective-permute-done.3 = s16[240,128]{1,0:T(8,128)(2,1)S(1)} collective-permute-done((s16[240,128]{1,0:T(8,128)(2,1)S(1)}, s16[240,128]{1,0:T(8,128)(2,1)S(1)}, u32[]{:S(2)}, u32[]{:S(2)}) %collective-permute-start.3) | collective-permute-done | bytes 61472 | tf_op jit(solution)/shard_map/ppermute | solution.py:390
  59.6 1.1 %collective-permute-done.7 = s16[240,128]{1,0:T(8,128)(2,1)S(1)} collective-permute-done((s16[240,128]{1,0:T(8,128)(2,1)S(1)}, s16[240,128]{1,0:T(8,128)(2,1)S(1)}, u32[]{:S(2)}, u32[]{:S(2)}) %collective-permute-start.7) | collective-permute-done | bytes 61472 | tf_op jit(solution)/shard_map/ppermute | solution.py:390
  60.7 0.1 fusion.35
  60.9 0.6 collective-permute-start.8
  61.5 3.7 %collective-permute-done.8 = s16[240,128]{1,0:T(8,128)(2,1)S(1)} collective-permute-done((s16[240,128]{1,0:T(8,128)(2,1)S(1)}, s16[240,128]{1,0:T(8,128)(2,1)S(1)}, u32[]{:S(2)}, u32[]{:S(2)}) %collective-permute-start.8) | collective-permute-done | bytes 61472 | tf_op jit(solution)/shard_map/ppermute | solution.py:390
  65.4 3.6 %collective-permute-start.9 = (s16[240,128]{1,0:T(8,128)(2,1)S(1)}, s16[240,128]{1,0:T(8,128)(2,1)S(1)}, u32[]{:S(2)}, u32[]{:S(2)}) collective-permute-start(s16[240,128]{1,0:T(8,128)(2,1)S(1)} %pad_add_fusion.1), channel_id=1, source_target_pairs={{0,16},{1,17},{2,18},{3,19},{4,20},{5,21},{6,22},{7,23},{8,24},{9,... | collective-permute-start | bytes 184328 | tf_op jit(solution)/shard_map/ppermute | solution.py:390
  69.1 2.7 %collective-permute-done.9 = s16[240,128]{1,0:T(8,128)(2,1)S(1)} collective-permute-done((s16[240,128]{1,0:T(8,128)(2,1)S(1)}, s16[240,128]{1,0:T(8,128)(2,1)S(1)}, u32[]{:S(2)}, u32[]{:S(2)}) %collective-permute-start.9) | collective-permute-done | bytes 61472 | tf_op jit(solution)/shard_map/ppermute | solution.py:390
  72.0 1.2 %collective-permute-start.14 = (s16[240,128]{1,0:T(8,128)(2,1)S(1)}, s16[240,128]{1,0:T(8,128)(2,1)S(1)}, u32[]{:S(2)}, u32[]{:S(2)}) collective-permute-start(s16[240,128]{1,0:T(8,128)(2,1)S(1)} %pad_add_fusion), channel_id=1, source_target_pairs={{0,4},{1,5},{2,6},{3,7},{4,0},{5,1},{6,2},{7,3},{8,12},{9,13},{10,... | collective-permute-start | bytes 184328 | tf_op jit(solution)/shard_map/ppermute | solution.py:390
  73.2 2.3 %collective-permute-start.10 = (s16[240,128]{1,0:T(8,128)(2,1)S(1)}, s16[240,128]{1,0:T(8,128)(2,1)S(1)}, u32[]{:S(2)}, u32[]{:S(2)}) collective-permute-start(s16[240,128]{1,0:T(8,128)(2,1)S(1)} %pad_add_fusion), channel_id=1, source_target_pairs={{0,6},{1,7},{2,4},{3,5},{4,2},{5,3},{6,0},{7,1},{8,14},{9,15},{10,... | collective-permute-start | bytes 184328 | tf_op jit(solution)/shard_map/ppermute | solution.py:390
  75.5 0.7 collective-permute-done.14
  76.3 1.7 %collective-permute-done.12 = s16[240,128]{1,0:T(8,128)(2,1)S(1)} collective-permute-done((s16[240,128]{1,0:T(8,128)(2,1)S(1)}, s16[240,128]{1,0:T(8,128)(2,1)S(1)}, u32[]{:S(2)}, u32[]{:S(2)}) %collective-permute-start.12) | collective-permute-done | bytes 61472 | tf_op jit(solution)/shard_map/ppermute | solution.py:390
  78.0 1.2 %collective-permute-done.10 = s16[240,128]{1,0:T(8,128)(2,1)S(1)} collective-permute-done((s16[240,128]{1,0:T(8,128)(2,1)S(1)}, s16[240,128]{1,0:T(8,128)(2,1)S(1)}, u32[]{:S(2)}, u32[]{:S(2)}) %collective-permute-start.10) | collective-permute-done | bytes 61472 | tf_op jit(solution)/shard_map/ppermute | solution.py:390
  79.5 1.0 %collective-permute-done.11 = s16[240,128]{1,0:T(8,128)(2,1)S(1)} collective-permute-done((s16[240,128]{1,0:T(8,128)(2,1)S(1)}, s16[240,128]{1,0:T(8,128)(2,1)S(1)}, u32[]{:S(2)}, u32[]{:S(2)}) %collective-permute-start.11) | collective-permute-done | bytes 61472 | tf_op jit(solution)/shard_map/ppermute | solution.py:390
  80.5 6.4 %finish.1 = (f32[512,128]{1,0:T(8,128)}, f32[128,512]{1,0:T(8,128)}) custom-call(s32[1]{0:T(128)} %bitcast.me_ref, bf16[1024,512]{1,0:T(8,128)(2,1)S(1)} %get-tuple-element.23.stack_ref, f32[224,128]{1,0:T(8,128)S(1)} %bitcast_multiply_fusion.7.rest_0_, f32[224,128]{1,0:T(8,128)S(1)} %bitcast_multiply_fusion.6.rest_1_, ...), custom_call_target="tpu_custom_call" | custom-call | tf_op jit(solution)/shard_map/finish/pallas_call | solution.py:372
  (65 shorter events, 1.2 us)
Async XLA Ops:
  0.6 16.8 %collective-permute-start = (bf16[16,64,128]{2,1,0:T(8,128)(2,1)}, bf16[16,64,128]{2,1,0:T(8,128)(2,1)S(1)}, u32[]{:S(2)}, u32[]{:S(2)}) collective-permute-start(bf16[16,64,128]{2,1,0:T(8,128)(2,1)} %own_ref.1), channel_id=1, source_target_pairs={{0,16},{1,17},{2,18},{3,19},{4,20},{5,21},{6,22},{7,23},{8,24},{9,... | collective-permute-start | bytes 786440 | tf_op jit(solution)/shard_map/ppermute | solution.py:390
  19.1 19.8 %all-to-all-start.1 = ((bf16[64,64,128]{2,1,0:T(8,128)(2,1)}), bf16[64,64,128]{2,1,0:T(8,128)(2,1)S(1)}, u32[]{:S(2)}, u32[]{:S(2)}) async-start(bf16[64,64,128]{2,1,0:T(8,128)(2,1)} %collect.1), calls=%async_computation.1 | async-start | bytes 2097152 | tf_op jit(solution)/shard_map/all_to_all | solution.py:451
  24.5 0.9 %copy-start.1 = (s32[64,512]{1,0:T(8,128)S(1)}, s32[64,512]{1,0:T(8,128)}, u32[]{:S(2)}) copy-start(s32[64,512]{1,0:T(8,128)} %marks_ref.1) | copy-start | bytes 393220
  29.1 1.0 %copy-start = (f32[64,8,512]{2,1,0:T(8,128)}, f32[64,8,512]{2,1,0:T(8,128)S(1)}, u32[]{:S(2)}) copy-start(f32[64,8,512]{2,1,0:T(8,128)S(1)} %contexts.1.context_ref) | copy-start | bytes 3145732
  52.2 1.4 %collective-permute-start.2 = (f32[224,128]{1,0:T(8,128)S(1)}, f32[224,128]{1,0:T(8,128)S(1)}, u32[]{:S(2)}, u32[]{:S(2)}) collective-permute-start(f32[224,128]{1,0:T(8,128)S(1)} %get-tuple-element.27), channel_id=1, source_target_pairs={{0,1},{1,0},{2,3},{3,2},{4,5},{5,4},{6,7},{7,6},{8,9},{9,8},{10,11... | collective-permute-start | bytes 344072 | tf_op jit(solution)/shard_map/ppermute | solution.py:390
  52.3 8.4 %collective-permute-start.1 = (f32[224,128]{1,0:T(8,128)S(1)}, f32[224,128]{1,0:T(8,128)S(1)}, u32[]{:S(2)}, u32[]{:S(2)}) collective-permute-start(f32[224,128]{1,0:T(8,128)S(1)} %get-tuple-element.25), channel_id=1, source_target_pairs={{0,1},{1,0},{2,3},{3,2},{4,5},{5,4},{6,7},{7,6},{8,9},{9,8},{10,11... | collective-permute-start | bytes 344072 | tf_op jit(solution)/shard_map/ppermute | solution.py:390
  52.8 1.9 %collective-permute-start.4 = (f32[224,128]{1,0:T(8,128)S(1)}, f32[224,128]{1,0:T(8,128)S(1)}, u32[]{:S(2)}, u32[]{:S(2)}) collective-permute-start(f32[224,128]{1,0:T(8,128)S(1)} %get-tuple-element.29), channel_id=1, source_target_pairs={{0,1},{1,0},{2,3},{3,2},{4,5},{5,4},{6,7},{7,6},{8,9},{9,8},{10,11... | collective-permute-start | bytes 344072 | tf_op jit(solution)/shard_map/ppermute | solution.py:390
  52.9 3.4 %collective-permute-start.6 = (f32[224,128]{1,0:T(8,128)S(1)}, f32[224,128]{1,0:T(8,128)S(1)}, u32[]{:S(2)}, u32[]{:S(2)}) collective-permute-start(f32[224,128]{1,0:T(8,128)S(1)} %get-tuple-element.31), channel_id=1, source_target_pairs={{0,1},{1,0},{2,3},{3,2},{4,5},{5,4},{6,7},{7,6},{8,9},{9,8},{10,11... | collective-permute-start | bytes 344072 | tf_op jit(solution)/shard_map/ppermute | solution.py:390
  53.8 5.8 %collective-permute-start.3 = (s16[240,128]{1,0:T(8,128)(2,1)S(1)}, s16[240,128]{1,0:T(8,128)(2,1)S(1)}, u32[]{:S(2)}, u32[]{:S(2)}) collective-permute-start(s16[240,128]{1,0:T(8,128)(2,1)S(1)} %pad_add_fusion.5), channel_id=1, source_target_pairs={{0,6},{1,7},{2,4},{3,5},{4,2},{5,3},{6,0},{7,1},{8,14},{9,15},{10,... | collective-permute-start | bytes 184328 | tf_op jit(solution)/shard_map/ppermute | solution.py:390
  54.9 4.7 %collective-permute-start.5 = (s16[240,128]{1,0:T(8,128)(2,1)S(1)}, s16[240,128]{1,0:T(8,128)(2,1)S(1)}, u32[]{:S(2)}, u32[]{:S(2)}) collective-permute-start(s16[240,128]{1,0:T(8,128)(2,1)S(1)} %pad_add_fusion.4), channel_id=1, source_target_pairs={{0,2},{1,3},{2,0},{3,1},{4,6},{5,7},{6,4},{7,5},{8,10},{9,11},{10,... | collective-permute-start | bytes 184328 | tf_op jit(solution)/shard_map/ppermute | solution.py:390
  56.4 4.3 %collective-permute-start.7 = (s16[240,128]{1,0:T(8,128)(2,1)S(1)}, s16[240,128]{1,0:T(8,128)(2,1)S(1)}, u32[]{:S(2)}, u32[]{:S(2)}) collective-permute-start(s16[240,128]{1,0:T(8,128)(2,1)S(1)} %pad_add_fusion.3), channel_id=1, source_target_pairs={{0,4},{1,5},{2,6},{3,7},{4,0},{5,1},{6,2},{7,3},{8,12},{9,13},{10,... | collective-permute-start | bytes 184328 | tf_op jit(solution)/shard_map/ppermute | solution.py:390
  60.9 4.3 %collective-permute-start.8 = (s16[240,128]{1,0:T(8,128)(2,1)S(1)}, s16[240,128]{1,0:T(8,128)(2,1)S(1)}, u32[]{:S(2)}, u32[]{:S(2)}) collective-permute-start(s16[240,128]{1,0:T(8,128)(2,1)S(1)} %pad_add_fusion.2), channel_id=1, source_target_pairs={{0,8},{1,9},{2,10},{3,11},{4,12},{5,13},{6,14},{7,15},{8,0},{9,1},... | collective-permute-start | bytes 184328 | tf_op jit(solution)/shard_map/ppermute | solution.py:390
  65.4 6.3 %collective-permute-start.9 = (s16[240,128]{1,0:T(8,128)(2,1)S(1)}, s16[240,128]{1,0:T(8,128)(2,1)S(1)}, u32[]{:S(2)}, u32[]{:S(2)}) collective-permute-start(s16[240,128]{1,0:T(8,128)(2,1)S(1)} %pad_add_fusion.1), channel_id=1, source_target_pairs={{0,16},{1,17},{2,18},{3,19},{4,20},{5,21},{6,22},{7,23},{8,24},{9,... | collective-permute-start | bytes 184328 | tf_op jit(solution)/shard_map/ppermute | solution.py:390
  72.0 4.3 %collective-permute-start.14 = (s16[240,128]{1,0:T(8,128)(2,1)S(1)}, s16[240,128]{1,0:T(8,128)(2,1)S(1)}, u32[]{:S(2)}, u32[]{:S(2)}) collective-permute-start(s16[240,128]{1,0:T(8,128)(2,1)S(1)} %pad_add_fusion), channel_id=1, source_target_pairs={{0,4},{1,5},{2,6},{3,7},{4,0},{5,1},{6,2},{7,3},{8,12},{9,13},{10,... | collective-permute-start | bytes 184328 | tf_op jit(solution)/shard_map/ppermute | solution.py:390
  73.2 6.1 %collective-permute-start.16 = (s16[240,128]{1,0:T(8,128)(2,1)S(1)}, s16[240,128]{1,0:T(8,128)(2,1)S(1)}, u32[]{:S(2)}, u32[]{:S(2)}) collective-permute-start(s16[240,128]{1,0:T(8,128)(2,1)S(1)} %pad_add_fusion), channel_id=1, source_target_pairs={{0,1},{1,0},{2,3},{3,2},{4,5},{5,4},{6,7},{7,6},{8,9},{9,8},{10,11... | collective-permute-start | bytes 184328 | tf_op jit(solution)/shard_map/ppermute | solution.py:390
  73.2 4.8 %collective-permute-start.12 = (s16[240,128]{1,0:T(8,128)(2,1)S(1)}, s16[240,128]{1,0:T(8,128)(2,1)S(1)}, u32[]{:S(2)}, u32[]{:S(2)}) collective-permute-start(s16[240,128]{1,0:T(8,128)(2,1)S(1)} %pad_add_fusion), channel_id=1, source_target_pairs={{0,2},{1,3},{2,0},{3,1},{4,6},{5,7},{6,4},{7,5},{8,10},{9,11},{10,... | collective-permute-start | bytes 184328 | tf_op jit(solution)/shard_map/ppermute | solution.py:390
  73.2 6.0 %collective-permute-start.10 = (s16[240,128]{1,0:T(8,128)(2,1)S(1)}, s16[240,128]{1,0:T(8,128)(2,1)S(1)}, u32[]{:S(2)}, u32[]{:S(2)}) collective-permute-start(s16[240,128]{1,0:T(8,128)(2,1)S(1)} %pad_add_fusion), channel_id=1, source_target_pairs={{0,6},{1,7},{2,4},{3,5},{4,2},{5,3},{6,0},{7,1},{8,14},{9,15},{10,... | collective-permute-start | bytes 184328 | tf_op jit(solution)/shard_map/ppermute | solution.py:390
  76.3 3.1 %collective-permute-start.15 = (s16[240,128]{1,0:T(8,128)(2,1)S(1)}, s16[240,128]{1,0:T(8,128)(2,1)S(1)}, u32[]{:S(2)}, u32[]{:S(2)}) collective-permute-start(s16[240,128]{1,0:T(8,128)(2,1)S(1)} %collective-permute-done.14), channel_id=1, source_target_pairs={{0,1},{1,0},{2,3},{3,2},{4,5},{5,4},{6,7},{7,6},{8,9},{9,8},{10,11... | collective-permute-start | bytes 184328 | tf_op jit(solution)/shard_map/ppermute | solution.py:390
  78.0 1.4 %collective-permute-start.13 = (s16[240,128]{1,0:T(8,128)(2,1)S(1)}, s16[240,128]{1,0:T(8,128)(2,1)S(1)}, u32[]{:S(2)}, u32[]{:S(2)}) collective-permute-start(s16[240,128]{1,0:T(8,128)(2,1)S(1)} %collective-permute-done.12), channel_id=1, source_target_pairs={{0,1},{1,0},{2,3},{3,2},{4,5},{5,4},{6,7},{7,6},{8,9},{9,8},{10,11... | collective-permute-start | bytes 184328 | tf_op jit(solution)/shard_map/ppermute | solution.py:390
  79.2 1.3 %collective-permute-start.11 = (s16[240,128]{1,0:T(8,128)(2,1)S(1)}, s16[240,128]{1,0:T(8,128)(2,1)S(1)}, u32[]{:S(2)}, u32[]{:S(2)}) collective-permute-start(s16[240,128]{1,0:T(8,128)(2,1)S(1)} %collective-permute-done.10), channel_id=1, source_target_pairs={{0,1},{1,0},{2,3},{3,2},{4,5},{5,4},{6,7},{7,6},{8,9},{9,8},{10,11... | collective-permute-start | bytes 184328 | tf_op jit(solution)/shard_map/ppermute | solution.py:390

commit v12 on v11

--- a/solution.py
+++ b/solution.py
@@ -164,9 +164,10 @@
     where_ref, count_ref, me_ref, blocks_ref, weights_ref, context_ref, basis_ref, *refs
 ):
     piece_refs, refs = refs[: len(PIECES)], refs[len(PIECES) :]
-    stack_ref, y_ref, square_ref, pack_ref, even_ref, odd_ref = refs[:6]
-    weights_held, context_held, basis_held, weights_sem, context_sem, basis_sem = refs[6:]
+    stack_ref, y_ref, square_ref, pack_ref, even_ref, odd_ref, paired_ref = refs[:7]
+    weights_held, context_held, basis_held, weights_sem, context_sem, basis_sem = refs[7:]
     rank_c, rank_i, users = y_ref.shape
+    block_len = weights_ref.shape[1]
     batches = weights_ref.shape[0] // BATCH
     half = rank_c // 2
 
@@ -182,10 +183,20 @@
     basis_copy = pltpu.make_async_copy(basis_ref, basis_held, basis_sem)
     basis_copy.start()
 
+    def set_pair(pair, _):
+        paired_ref[pair] = jnp.zeros(paired_ref.shape[1:], paired_ref.dtype)
+        for i in range(2):
+            block = blocks_ref[where_ref[2 * pair + i]]
+            paired_ref[pair, i * rank_i : (i + 1) * rank_i, i * block_len : (i + 1) * block_len] = block
+        return 0
+
+    lax.fori_loop(0, paired_ref.shape[0], set_pair, 0, unroll=2)
+
     def multiply(batch, place, into_ref):
-        tile = batch * BATCH + place
-        product = dot(blocks_ref[where_ref[tile]], weights_held[tile])
-        into_ref[place] = product.astype(jnp.bfloat16).astype(jnp.float32)
+        pair = (batch * BATCH + place) // 2
+        weights = weights_held[pl.ds(2 * pair, 2)].reshape(2 * block_len, users)
+        product = dot(paired_ref[pair], weights).astype(jnp.bfloat16).astype(jnp.float32)
+        into_ref[place : place + 2] = product.reshape(2, rank_i, users)
 
     def add(batch, part, from_ref):
         lanes = slice(part // 2 * LANES, (part // 2 + 1) * LANES)
@@ -206,14 +217,14 @@
     y_ref[...] = jnp.zeros_like(y_ref)
     parts = 2 * users // LANES
     weights_copy(0).wait()
-    for place in range(BATCH):
+    for place in range(0, BATCH, 2):
         multiply(0, place, even_ref)
     contexts_copy.wait()
 
     def turn(batch, from_ref, into_ref):
         weights_copy(batch + 1).wait()
         for part in range(max(parts, BATCH)):
-            if part < BATCH:
+            if part < BATCH and part % 2 == 0:
                 multiply(batch + 1, part, into_ref)
             if part < parts:
                 add(batch, part, from_ref)
@@ -256,7 +267,7 @@
 
 
 def tile_sums(where, count, me, blocks, weights, contexts, user_basis):
-    tiles, _, users = weights.shape
+    tiles, block_len, users = weights.shape
     rank_i = blocks.shape[1]
     rank_c = contexts.shape[1]
     ranks = rank_c * rank_i
@@ -275,6 +286,7 @@
             pltpu.VMEM((rows, LANES), jnp.float32),
             pltpu.VMEM((BATCH, rank_i, users), jnp.float32),
             pltpu.VMEM((BATCH, rank_i, users), jnp.float32),
+            pltpu.VMEM((tiles // 2, 2 * rank_i, 2 * block_len), blocks.dtype),
             pltpu.VMEM(weights.shape, weights.dtype),
             pltpu.VMEM(contexts.shape, contexts.dtype),
             pltpu.VMEM(user_basis.shape, user_basis.dtype),
@@ -282,7 +294,7 @@
             pltpu.SemaphoreType.DMA,
             pltpu.SemaphoreType.DMA,
         ],
-        compiler_params=limit(12 + held),
+        compiler_params=limit(14 + held),
         cost_estimate=pl.CostEstimate(flops=2 * 10**9, bytes_accessed=12 * 10**6, transcendentals=0),
         name="tile_sums",
     )(where, count, me, blocks, in_hbm(weights), in_hbm(contexts), in_hbm(user_basis))
@@ -296,6 +308,12 @@
     lane = lax.broadcasted_iota(jnp.int32, (ROWS, order), 1)
     left = [gram[ROWS * i : ROWS * (i + 1)] for i in range(panels)]
     right = [jnp.where(lane == sub + ROWS * i, 1.0, 0.0) for i in range(panels)]
+    spread = lambda value, j: jnp.broadcast_to(value[j : j + 1], (ROWS, order))
+
+    def invert(value):
+        guess = pl.reciprocal(value, approx=True)
+        return guess * (2.0 - value * guess)
+
     for k in range(panels):
         columns = {
             i: [
@@ -305,29 +323,32 @@
             for i in range(k, panels)
         }
         row, tail = left[k], right[k]
-        scale = jnp.zeros((ROWS, order), jnp.float32)
-        rows, tails = [], []
-        for j in range(ROWS):
-            head = columns[k][j]
-            pivot = jnp.broadcast_to(head[j : j + 1], (ROWS, order))
-            inverse = pl.reciprocal(pivot, approx=True)
-            inverse = inverse * (2.0 - pivot * inverse)
-            scale = jnp.where(sub == j, pivot, scale)
-            rows.append(jnp.broadcast_to(row[j : j + 1], (ROWS, order)))
-            tails.append(jnp.broadcast_to(tail[j : j + 1], (ROWS, order)))
-            below = jnp.where(sub > j, head, 0.0) * inverse
-            row = row - below * rows[j]
-            tail = tail - below * tails[j]
-            facts = {k: below}
+        scale = jnp.ones((ROWS, order), jnp.float32)
+        for j in range(0, ROWS, 2):
+            first, second = columns[k][j], columns[k][j + 1]
+            a, b, d = spread(first, j), spread(first, j + 1), spread(second, j + 1)
+            minor = a * d - b * b
+            inverse = invert(minor)
+            along_a, along_b, along_d = a * inverse, b * inverse, d * inverse
+            rows = spread(row, j), spread(row, j + 1)
+            tails = spread(tail, j), spread(tail, j + 1)
+            lower = invert(a)
+            scale = jnp.where(sub == j, a, jnp.where(sub == j + 1, minor * lower, scale))
+            facts = {}
+            for i in range(k, panels):
+                x, y = columns[i][j], columns[i][j + 1]
+                facts[i] = x * along_d - y * along_b, y * along_a - x * along_b
+            facts[k] = tuple(jnp.where(sub > j + 1, fact, 0.0) for fact in facts[k])
+            for c in range(j + 2, ROWS):
+                crossings = spread(first, c), spread(second, c)
+                for i in range(k, panels):
+                    columns[i][c] = columns[i][c] - (facts[i][0] * crossings[0] + facts[i][1] * crossings[1])
+            row = row - (facts[k][0] * rows[0] + facts[k][1] * rows[1])
+            tail = tail - (facts[k][0] * tails[0] + facts[k][1] * tails[1])
+            tail = tail - jnp.where(sub == j + 1, b * lower, 0.0) * tails[0]
             for i in range(k + 1, panels):
-                facts[i] = columns[i][j] * inverse
-            for c in range(j + 1, ROWS):
-                crossing = jnp.broadcast_to(head[c : c + 1], (ROWS, order))
-                for i in range(k, panels):
-                    columns[i][c] = columns[i][c] - facts[i] * crossing
-            for i in range(k + 1, panels):
-                left[i] = left[i] - facts[i] * rows[j]
-                right[i] = right[i] - facts[i] * tails[j]
+                left[i] = left[i] - (facts[i][0] * rows[0] + facts[i][1] * rows[1])
+                right[i] = right[i] - (facts[i][0] * tails[0] + facts[i][1] * tails[1])
         right[k] = tail * lax.rsqrt(scale)
     return jnp.concatenate(right, axis=0)
 
@@ -359,7 +380,9 @@
     turned_stack = jnp.concatenate(split(turned), axis=0)
     gram = quarters(dot(turned_stack, jnp.concatenate([crossed_high, crossed_low], axis=1)))
     projected_high, projected_low = split(thrice(turned_stack, stack_ref[:ranks], stack_ref[ranks:], dot))
-    inverse_stack = jnp.concatenate(split(inverse_factor(gram)), axis=0)
+    most = jnp.max(jnp.max(gram, axis=1, keepdims=True), axis=0, keepdims=True)
+    inverse = inverse_factor(gram * (1.0 / most)) * lax.rsqrt(most)
+    inverse_stack = jnp.concatenate(split(inverse), axis=0)
     root = total_users ** 0.5
     scaled = thrice(inverse_stack, projected_high, projected_low, dot) * root
     for i in range(scaled.shape[1] // LANES):

time: 87.3 us -> 87.2 us (level)
  no operation moved by 1% of the time
where the time goes in v12:
time: 87.2 us; the launch traced here: 86.9 us
  Pallas kernels  27.2 us (31%)
  waiting for transfers between devices  23.2 us (27%)
  starting transfers between devices  20.4 us (23%)
  blocking collectives  10.5 us (12%)
  local copies, waits for them, and re-layouts  2.9 us (3%)
  between operations  1.62 us (2%)
  other arithmetic  1.07 us (1%)
    ppermute x17, starting transfers between devices, swap(): return lax.ppermute(value, 'users', [(i, i ^ mask) for i in range(devices)])  16.7 us
    ppermute x17, waiting for transfers between devices, swap(): return lax.ppermute(value, 'users', [(i, i ^ mask) for i in range(devices)])  14.4 us
    pallas_call x1, Pallas kernels, tile_sums(): pl.pallas_call(tiles_kernel, out_shape=out_shape, in_specs=[SMEM] * 3 + [...  13.1 us
    all_to_all x1, blocking collectives, body(): lax.all_to_all(requests, 'users', 0, 0, axis_index_groups=sides, tiled=True)  10.5 us
    all_to_all x1, waiting for transfers between devices, body(): lax.all_to_all(found, 'users', 0, 0, axis_index_groups=sides, tiled=True)  8.83 us
    pallas_call x1, Pallas kernels, finish(): pl.pallas_call(functools.partial(finish_kernel, users * devices), out_sha...  6.46 us
    pallas_call x1, Pallas kernels, context_values(): pl.pallas_call(context_kernel, out_shape=jax.ShapeDtypeStruct((tiles, ROW...  3.71 us
    all_to_all x1, starting transfers between devices, body(): lax.all_to_all(found, 'users', 0, 0, axis_index_groups=sides, tiled=True)  3.65 us
  transfers between devices with their start and end apart: 18, of which 10 were waited for; matrix products, arithmetic and copies ran while one was open for 2% of the time, Pallas kernels for 7%

profile of v12, /device:TPU:0, one launch (start us, length us, event | category | flops | bytes accessed | tf_op | source)
XLA Modules:
  0.0 86.9 jit_solution(4114243604321693313)
XLA Ops:
  0.6 4.1 %collective-permute-start = (bf16[16,64,128]{2,1,0:T(8,128)(2,1)}, bf16[16,64,128]{2,1,0:T(8,128)(2,1)S(1)}, u32[]{:S(2)}, u32[]{:S(2)}) collective-permute-start(bf16[16,64,128]{2,1,0:T(8,128)(2,1)} %own_ref.1), channel_id=1, source_target_pairs={{0,16},{1,17},{2,18},{3,19},{4,20},{5,21},{6,22},{7,23},{8,24},{9,... | collective-permute-start | bytes 786440 | tf_op jit(solution)/shard_map/ppermute | solution.py:413
  4.7 2.2 %route.1 = (s32[16,1,128]{2,1,0:T(1,128)S(1)}, s32[64]{0:T(128)S(1)}, bf16[16,64,128]{2,1,0:T(8,128)(2,1)S(1)}) custom-call(s32[1]{0:T(128)} %bitcast.me_ref, s32[64]{0:T(128)} %bitcast.136, s32[64]{0:T(128)} %slot_ref.1, bf16[16,64,128]{2,1,0:T(8,128)(2,1)} %own_ref.1), custom_call_target="tpu_custom_call" | custom-call | tf_op jit(solution)/shard_map/route/pallas_call | solution.py:85
  7.0 10.5 %all_to_all.10.asked_ref = s32[16,1,128]{2,1,0:T(1,128)S(1)} all-to-all(s32[16,1,128]{2,1,0:T(1,128)S(1)} %get-tuple-element.18), channel_id=1, replica_groups={{0,1,2,3,4,5,6,7,8,9,10,11,12,13,14,15},{16,17,18,19,20,21,22,23,24,25,..., dimensions={0} | all-to-all | bytes 16384 | tf_op jit(solution)/shard_map/all_to_all | solution.py:471
  17.4 1.7 %collect.1 = bf16[64,64,128]{2,1,0:T(8,128)(2,1)} custom-call(s32[16,1,128]{2,1,0:T(1,128)S(1)} %all_to_all.10.asked_ref, bf16[16,64,128]{2,1,0:T(8,128)(2,1)S(1)} %get-tuple-element.19.own_ref, bf16[16,64,128]{2,1,0:T(8,128)(2,1)S(1)} %collective-permute-done.mirror_ref), custom_call_target="tpu_custom_call" | custom-call | tf_op jit(solution)/shard_map/collect/pallas_call | solution.py:108
  19.1 3.7 %all-to-all-start.1 = ((bf16[64,64,128]{2,1,0:T(8,128)(2,1)}), bf16[64,64,128]{2,1,0:T(8,128)(2,1)S(1)}, u32[]{:S(2)}, u32[]{:S(2)}) async-start(bf16[64,64,128]{2,1,0:T(8,128)(2,1)} %collect.1), calls=%async_computation.1 | async-start | bytes 2097152 | tf_op jit(solution)/shard_map/all_to_all | solution.py:474
  23.5 0.9 reshape.232
  24.3 0.2 copy.13
  24.5 0.9 %copy-done.1 = s32[64,512]{1,0:T(8,128)S(1)} copy-done((s32[64,512]{1,0:T(8,128)S(1)}, s32[64,512]{1,0:T(8,128)}, u32[]{:S(2)}) %copy-start.1) | copy-done | bytes 131096
  25.4 3.7 %contexts.1.context_ref = f32[64,8,512]{2,1,0:T(8,128)S(1)} custom-call(s32[64]{0:T(128)} %cblock_ref, f32[64,8,8]{2,1,0:T(8,128)S(1)} %bitcast.129, s32[64,512]{1,0:T(8,128)S(1)} %copy-done.1), custom_call_target="tpu_custom_call" | custom-call | flops 10000000 | bytes 20000000 | tf_op jit(solution)/shard_map/contexts/pallas_call | solution.py:136
  29.1 1.0 %copy-done = f32[64,8,512]{2,1,0:T(8,128)} copy-done((f32[64,8,512]{2,1,0:T(8,128)}, f32[64,8,512]{2,1,0:T(8,128)S(1)}, u32[]{:S(2)}) %copy-start) | copy-done | bytes 1048600
  30.1 8.8 %all-to-all-done.1.blocks_ref = bf16[64,64,128]{2,1,0:T(8,128)(2,1)S(1)} async-done(((bf16[64,64,128]{2,1,0:T(8,128)(2,1)}), bf16[64,64,128]{2,1,0:T(8,128)(2,1)S(1)}, u32[]{:S(2)}, u32[]{:S(2)}) %all-to-all-start.1) | async-done | bytes 1048608 | tf_op jit(solution)/shard_map/all_to_all | solution.py:474
  38.9 13.1 %tile_sums.1 = (f32[224,128]{1,0:T(8,128)S(1)}, f32[224,128]{1,0:T(8,128)S(1)}, f32[224,128]{1,0:T(8,128)S(1)}, f32[224,128]{1,0:T(8,128)S(1)}, f32[224,128]{1,0...) custom-call(s32[64]{0:T(128)S(1)} %get-tuple-element.17.where_ref, ...), custom_call_target="tpu_custom_call" | custom-call | flops 2000000000 | bytes 12000000 | tf_op jit(solution)/shard_map/tile_sums/pallas_call | solution.py:278
  52.2 0.5 collective-permute-start.1
  52.7 0.4 collective-permute-start.6
  53.2 0.3 collective-permute-done.2
  53.6 1.0 %collective-permute-start.3 = (s16[240,128]{1,0:T(8,128)(2,1)S(1)}, s16[240,128]{1,0:T(8,128)(2,1)S(1)}, u32[]{:S(2)}, u32[]{:S(2)}) collective-permute-start(s16[240,128]{1,0:T(8,128)(2,1)S(1)} %pad_add_fusion.5), channel_id=1, source_target_pairs={{0,6},{1,7},{2,4},{3,5},{4,2},{5,3},{6,0},{7,1},{8,14},{9,15},{10,... | collective-permute-start | bytes 184328 | tf_op jit(solution)/shard_map/ppermute | solution.py:413
  54.7 1.4 %collective-permute-start.5 = (s16[240,128]{1,0:T(8,128)(2,1)S(1)}, s16[240,128]{1,0:T(8,128)(2,1)S(1)}, u32[]{:S(2)}, u32[]{:S(2)}) collective-permute-start(s16[240,128]{1,0:T(8,128)(2,1)S(1)} %pad_add_fusion.4), channel_id=1, source_target_pairs={{0,2},{1,3},{2,0},{3,1},{4,6},{5,7},{6,4},{7,5},{8,10},{9,11},{10,... | collective-permute-start | bytes 184328 | tf_op jit(solution)/shard_map/ppermute | solution.py:413
  56.3 1.2 %collective-permute-start.7 = (s16[240,128]{1,0:T(8,128)(2,1)S(1)}, s16[240,128]{1,0:T(8,128)(2,1)S(1)}, u32[]{:S(2)}, u32[]{:S(2)}) collective-permute-start(s16[240,128]{1,0:T(8,128)(2,1)S(1)} %pad_add_fusion.3), channel_id=1, source_target_pairs={{0,4},{1,5},{2,6},{3,7},{4,0},{5,1},{6,2},{7,3},{8,12},{9,13},{10,... | collective-permute-start | bytes 184328 | tf_op jit(solution)/shard_map/ppermute | solution.py:413
  57.5 1.9 %collective-permute-done.3 = s16[240,128]{1,0:T(8,128)(2,1)S(1)} collective-permute-done((s16[240,128]{1,0:T(8,128)(2,1)S(1)}, s16[240,128]{1,0:T(8,128)(2,1)S(1)}, u32[]{:S(2)}, u32[]{:S(2)}) %collective-permute-start.3) | collective-permute-done | bytes 61472 | tf_op jit(solution)/shard_map/ppermute | solution.py:413
  59.4 1.1 %collective-permute-done.7 = s16[240,128]{1,0:T(8,128)(2,1)S(1)} collective-permute-done((s16[240,128]{1,0:T(8,128)(2,1)S(1)}, s16[240,128]{1,0:T(8,128)(2,1)S(1)}, u32[]{:S(2)}, u32[]{:S(2)}) %collective-permute-start.7) | collective-permute-done | bytes 61472 | tf_op jit(solution)/shard_map/ppermute | solution.py:413
  60.6 0.1 fusion.35
  60.8 0.6 collective-permute-start.8
  61.4 3.7 %collective-permute-done.8 = s16[240,128]{1,0:T(8,128)(2,1)S(1)} collective-permute-done((s16[240,128]{1,0:T(8,128)(2,1)S(1)}, s16[240,128]{1,0:T(8,128)(2,1)S(1)}, u32[]{:S(2)}, u32[]{:S(2)}) %collective-permute-start.8) | collective-permute-done | bytes 61472 | tf_op jit(solution)/shard_map/ppermute | solution.py:413
  65.3 3.7 %collective-permute-start.9 = (s16[240,128]{1,0:T(8,128)(2,1)S(1)}, s16[240,128]{1,0:T(8,128)(2,1)S(1)}, u32[]{:S(2)}, u32[]{:S(2)}) collective-permute-start(s16[240,128]{1,0:T(8,128)(2,1)S(1)} %pad_add_fusion.1), channel_id=1, source_target_pairs={{0,16},{1,17},{2,18},{3,19},{4,20},{5,21},{6,22},{7,23},{8,24},{9,... | collective-permute-start | bytes 184328 | tf_op jit(solution)/shard_map/ppermute | solution.py:413
  68.9 2.7 %collective-permute-done.9 = s16[240,128]{1,0:T(8,128)(2,1)S(1)} collective-permute-done((s16[240,128]{1,0:T(8,128)(2,1)S(1)}, s16[240,128]{1,0:T(8,128)(2,1)S(1)}, u32[]{:S(2)}, u32[]{:S(2)}) %collective-permute-start.9) | collective-permute-done | bytes 61472 | tf_op jit(solution)/shard_map/ppermute | solution.py:413
  71.8 1.2 %collective-permute-start.14 = (s16[240,128]{1,0:T(8,128)(2,1)S(1)}, s16[240,128]{1,0:T(8,128)(2,1)S(1)}, u32[]{:S(2)}, u32[]{:S(2)}) collective-permute-start(s16[240,128]{1,0:T(8,128)(2,1)S(1)} %pad_add_fusion), channel_id=1, source_target_pairs={{0,4},{1,5},{2,6},{3,7},{4,0},{5,1},{6,2},{7,3},{8,12},{9,13},{10,... | collective-permute-start | bytes 184328 | tf_op jit(solution)/shard_map/ppermute | solution.py:413
  73.0 2.4 %collective-permute-start.10 = (s16[240,128]{1,0:T(8,128)(2,1)S(1)}, s16[240,128]{1,0:T(8,128)(2,1)S(1)}, u32[]{:S(2)}, u32[]{:S(2)}) collective-permute-start(s16[240,128]{1,0:T(8,128)(2,1)S(1)} %pad_add_fusion), channel_id=1, source_target_pairs={{0,6},{1,7},{2,4},{3,5},{4,2},{5,3},{6,0},{7,1},{8,14},{9,15},{10,... | collective-permute-start | bytes 184328 | tf_op jit(solution)/shard_map/ppermute | solution.py:413
  75.4 0.7 collective-permute-done.14
  76.1 1.7 %collective-permute-done.12 = s16[240,128]{1,0:T(8,128)(2,1)S(1)} collective-permute-done((s16[240,128]{1,0:T(8,128)(2,1)S(1)}, s16[240,128]{1,0:T(8,128)(2,1)S(1)}, u32[]{:S(2)}, u32[]{:S(2)}) %collective-permute-start.12) | collective-permute-done | bytes 61472 | tf_op jit(solution)/shard_map/ppermute | solution.py:413
  77.8 1.3 %collective-permute-done.10 = s16[240,128]{1,0:T(8,128)(2,1)S(1)} collective-permute-done((s16[240,128]{1,0:T(8,128)(2,1)S(1)}, s16[240,128]{1,0:T(8,128)(2,1)S(1)}, u32[]{:S(2)}, u32[]{:S(2)}) %collective-permute-start.10) | collective-permute-done | bytes 61472 | tf_op jit(solution)/shard_map/ppermute | solution.py:413
  79.4 1.0 %collective-permute-done.11 = s16[240,128]{1,0:T(8,128)(2,1)S(1)} collective-permute-done((s16[240,128]{1,0:T(8,128)(2,1)S(1)}, s16[240,128]{1,0:T(8,128)(2,1)S(1)}, u32[]{:S(2)}, u32[]{:S(2)}) %collective-permute-start.11) | collective-permute-done | bytes 61472 | tf_op jit(solution)/shard_map/ppermute | solution.py:413
  80.4 6.5 %finish.1 = (f32[512,128]{1,0:T(8,128)}, f32[128,512]{1,0:T(8,128)}) custom-call(s32[1]{0:T(128)} %bitcast.me_ref, bf16[1024,512]{1,0:T(8,128)(2,1)S(1)} %get-tuple-element.23.stack_ref, f32[224,128]{1,0:T(8,128)S(1)} %bitcast_multiply_fusion.7.rest_0_, f32[224,128]{1,0:T(8,128)S(1)} %bitcast_multiply_fusion.6.rest_1_, ...), custom_call_target="tpu_custom_call" | custom-call | tf_op jit(solution)/shard_map/finish/pallas_call | solution.py:395
  (65 shorter events, 1.2 us)
Async XLA Ops:
  0.6 16.8 %collective-permute-start = (bf16[16,64,128]{2,1,0:T(8,128)(2,1)}, bf16[16,64,128]{2,1,0:T(8,128)(2,1)S(1)}, u32[]{:S(2)}, u32[]{:S(2)}) collective-permute-start(bf16[16,64,128]{2,1,0:T(8,128)(2,1)} %own_ref.1), channel_id=1, source_target_pairs={{0,16},{1,17},{2,18},{3,19},{4,20},{5,21},{6,22},{7,23},{8,24},{9,... | collective-permute-start | bytes 786440 | tf_op jit(solution)/shard_map/ppermute | solution.py:413
  19.1 19.8 %all-to-all-start.1 = ((bf16[64,64,128]{2,1,0:T(8,128)(2,1)}), bf16[64,64,128]{2,1,0:T(8,128)(2,1)S(1)}, u32[]{:S(2)}, u32[]{:S(2)}) async-start(bf16[64,64,128]{2,1,0:T(8,128)(2,1)} %collect.1), calls=%async_computation.1 | async-start | bytes 2097152 | tf_op jit(solution)/shard_map/all_to_all | solution.py:474
  24.5 0.9 %copy-start.1 = (s32[64,512]{1,0:T(8,128)S(1)}, s32[64,512]{1,0:T(8,128)}, u32[]{:S(2)}) copy-start(s32[64,512]{1,0:T(8,128)} %marks_ref.1) | copy-start | bytes 393220
  29.1 1.0 %copy-start = (f32[64,8,512]{2,1,0:T(8,128)}, f32[64,8,512]{2,1,0:T(8,128)S(1)}, u32[]{:S(2)}) copy-start(f32[64,8,512]{2,1,0:T(8,128)S(1)} %contexts.1.context_ref) | copy-start | bytes 3145732
  52.1 1.4 %collective-permute-start.2 = (f32[224,128]{1,0:T(8,128)S(1)}, f32[224,128]{1,0:T(8,128)S(1)}, u32[]{:S(2)}, u32[]{:S(2)}) collective-permute-start(f32[224,128]{1,0:T(8,128)S(1)} %get-tuple-element.27), channel_id=1, source_target_pairs={{0,1},{1,0},{2,3},{3,2},{4,5},{5,4},{6,7},{7,6},{8,9},{9,8},{10,11... | collective-permute-start | bytes 344072 | tf_op jit(solution)/shard_map/ppermute | solution.py:413
  52.2 8.4 %collective-permute-start.1 = (f32[224,128]{1,0:T(8,128)S(1)}, f32[224,128]{1,0:T(8,128)S(1)}, u32[]{:S(2)}, u32[]{:S(2)}) collective-permute-start(f32[224,128]{1,0:T(8,128)S(1)} %get-tuple-element.25), channel_id=1, source_target_pairs={{0,1},{1,0},{2,3},{3,2},{4,5},{5,4},{6,7},{7,6},{8,9},{9,8},{10,11... | collective-permute-start | bytes 344072 | tf_op jit(solution)/shard_map/ppermute | solution.py:413
  52.7 2.0 %collective-permute-start.4 = (f32[224,128]{1,0:T(8,128)S(1)}, f32[224,128]{1,0:T(8,128)S(1)}, u32[]{:S(2)}, u32[]{:S(2)}) collective-permute-start(f32[224,128]{1,0:T(8,128)S(1)} %get-tuple-element.29), channel_id=1, source_target_pairs={{0,1},{1,0},{2,3},{3,2},{4,5},{5,4},{6,7},{7,6},{8,9},{9,8},{10,11... | collective-permute-start | bytes 344072 | tf_op jit(solution)/shard_map/ppermute | solution.py:413
  52.7 3.4 %collective-permute-start.6 = (f32[224,128]{1,0:T(8,128)S(1)}, f32[224,128]{1,0:T(8,128)S(1)}, u32[]{:S(2)}, u32[]{:S(2)}) collective-permute-start(f32[224,128]{1,0:T(8,128)S(1)} %get-tuple-element.31), channel_id=1, source_target_pairs={{0,1},{1,0},{2,3},{3,2},{4,5},{5,4},{6,7},{7,6},{8,9},{9,8},{10,11... | collective-permute-start | bytes 344072 | tf_op jit(solution)/shard_map/ppermute | solution.py:413
  53.6 5.8 %collective-permute-start.3 = (s16[240,128]{1,0:T(8,128)(2,1)S(1)}, s16[240,128]{1,0:T(8,128)(2,1)S(1)}, u32[]{:S(2)}, u32[]{:S(2)}) collective-permute-start(s16[240,128]{1,0:T(8,128)(2,1)S(1)} %pad_add_fusion.5), channel_id=1, source_target_pairs={{0,6},{1,7},{2,4},{3,5},{4,2},{5,3},{6,0},{7,1},{8,14},{9,15},{10,... | collective-permute-start | bytes 184328 | tf_op jit(solution)/shard_map/ppermute | solution.py:413
  54.7 4.7 %collective-permute-start.5 = (s16[240,128]{1,0:T(8,128)(2,1)S(1)}, s16[240,128]{1,0:T(8,128)(2,1)S(1)}, u32[]{:S(2)}, u32[]{:S(2)}) collective-permute-start(s16[240,128]{1,0:T(8,128)(2,1)S(1)} %pad_add_fusion.4), channel_id=1, source_target_pairs={{0,2},{1,3},{2,0},{3,1},{4,6},{5,7},{6,4},{7,5},{8,10},{9,11},{10,... | collective-permute-start | bytes 184328 | tf_op jit(solution)/shard_map/ppermute | solution.py:413
  56.3 4.3 %collective-permute-start.7 = (s16[240,128]{1,0:T(8,128)(2,1)S(1)}, s16[240,128]{1,0:T(8,128)(2,1)S(1)}, u32[]{:S(2)}, u32[]{:S(2)}) collective-permute-start(s16[240,128]{1,0:T(8,128)(2,1)S(1)} %pad_add_fusion.3), channel_id=1, source_target_pairs={{0,4},{1,5},{2,6},{3,7},{4,0},{5,1},{6,2},{7,3},{8,12},{9,13},{10,... | collective-permute-start | bytes 184328 | tf_op jit(solution)/shard_map/ppermute | solution.py:413
  60.8 4.3 %collective-permute-start.8 = (s16[240,128]{1,0:T(8,128)(2,1)S(1)}, s16[240,128]{1,0:T(8,128)(2,1)S(1)}, u32[]{:S(2)}, u32[]{:S(2)}) collective-permute-start(s16[240,128]{1,0:T(8,128)(2,1)S(1)} %pad_add_fusion.2), channel_id=1, source_target_pairs={{0,8},{1,9},{2,10},{3,11},{4,12},{5,13},{6,14},{7,15},{8,0},{9,1},... | collective-permute-start | bytes 184328 | tf_op jit(solution)/shard_map/ppermute | solution.py:413
  65.3 6.3 %collective-permute-start.9 = (s16[240,128]{1,0:T(8,128)(2,1)S(1)}, s16[240,128]{1,0:T(8,128)(2,1)S(1)}, u32[]{:S(2)}, u32[]{:S(2)}) collective-permute-start(s16[240,128]{1,0:T(8,128)(2,1)S(1)} %pad_add_fusion.1), channel_id=1, source_target_pairs={{0,16},{1,17},{2,18},{3,19},{4,20},{5,21},{6,22},{7,23},{8,24},{9,... | collective-permute-start | bytes 184328 | tf_op jit(solution)/shard_map/ppermute | solution.py:413
  71.8 4.3 %collective-permute-start.14 = (s16[240,128]{1,0:T(8,128)(2,1)S(1)}, s16[240,128]{1,0:T(8,128)(2,1)S(1)}, u32[]{:S(2)}, u32[]{:S(2)}) collective-permute-start(s16[240,128]{1,0:T(8,128)(2,1)S(1)} %pad_add_fusion), channel_id=1, source_target_pairs={{0,4},{1,5},{2,6},{3,7},{4,0},{5,1},{6,2},{7,3},{8,12},{9,13},{10,... | collective-permute-start | bytes 184328 | tf_op jit(solution)/shard_map/ppermute | solution.py:413
  73.0 6.1 %collective-permute-start.16 = (s16[240,128]{1,0:T(8,128)(2,1)S(1)}, s16[240,128]{1,0:T(8,128)(2,1)S(1)}, u32[]{:S(2)}, u32[]{:S(2)}) collective-permute-start(s16[240,128]{1,0:T(8,128)(2,1)S(1)} %pad_add_fusion), channel_id=1, source_target_pairs={{0,1},{1,0},{2,3},{3,2},{4,5},{5,4},{6,7},{7,6},{8,9},{9,8},{10,11... | collective-permute-start | bytes 184328 | tf_op jit(solution)/shard_map/ppermute | solution.py:413
  73.0 4.8 %collective-permute-start.12 = (s16[240,128]{1,0:T(8,128)(2,1)S(1)}, s16[240,128]{1,0:T(8,128)(2,1)S(1)}, u32[]{:S(2)}, u32[]{:S(2)}) collective-permute-start(s16[240,128]{1,0:T(8,128)(2,1)S(1)} %pad_add_fusion), channel_id=1, source_target_pairs={{0,2},{1,3},{2,0},{3,1},{4,6},{5,7},{6,4},{7,5},{8,10},{9,11},{10,... | collective-permute-start | bytes 184328 | tf_op jit(solution)/shard_map/ppermute | solution.py:413
  73.0 6.1 %collective-permute-start.10 = (s16[240,128]{1,0:T(8,128)(2,1)S(1)}, s16[240,128]{1,0:T(8,128)(2,1)S(1)}, u32[]{:S(2)}, u32[]{:S(2)}) collective-permute-start(s16[240,128]{1,0:T(8,128)(2,1)S(1)} %pad_add_fusion), channel_id=1, source_target_pairs={{0,6},{1,7},{2,4},{3,5},{4,2},{5,3},{6,0},{7,1},{8,14},{9,15},{10,... | collective-permute-start | bytes 184328 | tf_op jit(solution)/shard_map/ppermute | solution.py:413
  76.1 3.1 %collective-permute-start.15 = (s16[240,128]{1,0:T(8,128)(2,1)S(1)}, s16[240,128]{1,0:T(8,128)(2,1)S(1)}, u32[]{:S(2)}, u32[]{:S(2)}) collective-permute-start(s16[240,128]{1,0:T(8,128)(2,1)S(1)} %collective-permute-done.14), channel_id=1, source_target_pairs={{0,1},{1,0},{2,3},{3,2},{4,5},{5,4},{6,7},{7,6},{8,9},{9,8},{10,11... | collective-permute-start | bytes 184328 | tf_op jit(solution)/shard_map/ppermute | solution.py:413
  77.8 1.5 %collective-permute-start.13 = (s16[240,128]{1,0:T(8,128)(2,1)S(1)}, s16[240,128]{1,0:T(8,128)(2,1)S(1)}, u32[]{:S(2)}, u32[]{:S(2)}) collective-permute-start(s16[240,128]{1,0:T(8,128)(2,1)S(1)} %collective-permute-done.12), channel_id=1, source_target_pairs={{0,1},{1,0},{2,3},{3,2},{4,5},{5,4},{6,7},{7,6},{8,9},{9,8},{10,11... | collective-permute-start | bytes 184328 | tf_op jit(solution)/shard_map/ppermute | solution.py:413
  79.1 1.3 %collective-permute-start.11 = (s16[240,128]{1,0:T(8,128)(2,1)S(1)}, s16[240,128]{1,0:T(8,128)(2,1)S(1)}, u32[]{:S(2)}, u32[]{:S(2)}) collective-permute-start(s16[240,128]{1,0:T(8,128)(2,1)S(1)} %collective-permute-done.10), channel_id=1, source_target_pairs={{0,1},{1,0},{2,3},{3,2},{4,5},{5,4},{6,7},{7,6},{8,9},{9,8},{10,11... | collective-permute-start | bytes 184328 | tf_op jit(solution)/shard_map/ppermute | solution.py:413

commit v13 on v11

--- a/solution.py
+++ b/solution.py
@@ -170,17 +170,22 @@
     batches = weights_ref.shape[0] // BATCH
     half = rank_c // 2
 
-    def weights_copy(batch):
+    def copies(batch):
         rows = pl.ds(batch * BATCH, BATCH)
-        return pltpu.make_async_copy(weights_ref.at[rows], weights_held.at[rows], weights_sem.at[batch])
-
-    weights_copy(0).start()
-    contexts_copy = pltpu.make_async_copy(context_ref, context_held, context_sem)
-    contexts_copy.start()
-    for batch in range(1, batches):
-        weights_copy(batch).start()
-    basis_copy = pltpu.make_async_copy(basis_ref, basis_held, basis_sem)
-    basis_copy.start()
+        return (
+            pltpu.make_async_copy(weights_ref.at[rows], weights_held.at[rows], weights_sem.at[batch]),
+            pltpu.make_async_copy(context_ref.at[rows], context_held.at[rows], context_sem.at[batch]),
+        )
+
+    def start(batch):
+        for copy in copies(batch):
+            copy.start()
+
+    def wait(batch):
+        for copy in copies(batch):
+            copy.wait()
+
+    start(0)
 
     def multiply(batch, place, into_ref):
         tile = batch * BATCH + place
@@ -205,13 +210,18 @@
 
     y_ref[...] = jnp.zeros_like(y_ref)
     parts = 2 * users // LANES
-    weights_copy(0).wait()
+    wait(0)
+    start(1)
     for place in range(BATCH):
         multiply(0, place, even_ref)
-    contexts_copy.wait()
 
     def turn(batch, from_ref, into_ref):
-        weights_copy(batch + 1).wait()
+        wait(batch + 1)
+
+        @pl.when(batch + 2 < batches)
+        def _():
+            start(batch + 2)
+
         for part in range(max(parts, BATCH)):
             if part < BATCH:
                 multiply(batch + 1, part, into_ref)
@@ -224,6 +234,8 @@
         return 0
 
     lax.fori_loop(0, batches // 2 - 1, pair, 0)
+    basis_copy = pltpu.make_async_copy(basis_ref, basis_held, basis_sem)
+    basis_copy.start()
     turn(batches - 2, even_ref, odd_ref)
     for part in range(parts):
         add(batches - 1, part, odd_ref)
@@ -279,7 +291,7 @@
             pltpu.VMEM(contexts.shape, contexts.dtype),
             pltpu.VMEM(user_basis.shape, user_basis.dtype),
             pltpu.SemaphoreType.DMA((tiles // BATCH,)),
-            pltpu.SemaphoreType.DMA,
+            pltpu.SemaphoreType.DMA((tiles // BATCH,)),
             pltpu.SemaphoreType.DMA,
         ],
         compiler_params=limit(12 + held),
@@ -289,7 +301,7 @@
     return dict(zip(PIECES, out[:-1])), out[-1]
 
 
-def inverse_factor(gram):
+def inverse_factor(gram, between):
     order = gram.shape[0]
     panels = order // ROWS
     sub = lax.broadcasted_iota(jnp.int32, (ROWS, order), 0)
@@ -297,6 +309,7 @@
     left = [gram[ROWS * i : ROWS * (i + 1)] for i in range(panels)]
     right = [jnp.where(lane == sub + ROWS * i, 1.0, 0.0) for i in range(panels)]
     for k in range(panels):
+        between(k)
         columns = {
             i: [
                 jnp.broadcast_to(left[i][:, ROWS * k + j : ROWS * k + j + 1], (ROWS, order))
@@ -333,7 +346,8 @@
 
 
 def finish_kernel(total_users, me_ref, stack_ref, *rest):
-    piece_refs, (basis_ref, core_out_ref, pack_ref, full_ref) = rest[: len(PIECES)], rest[len(PIECES) :]
+    piece_refs, rest = rest[: len(PIECES)], rest[len(PIECES) :]
+    basis_ref, core_out_ref, pack_ref, full_ref, high_ref, low_ref = rest
     chunk = piece_refs[0].shape[0]
     places = pack_places(me_ref[0])
     for piece, ref in zip(PIECES, piece_refs):
@@ -358,10 +372,17 @@
     )
     turned_stack = jnp.concatenate(split(turned), axis=0)
     gram = quarters(dot(turned_stack, jnp.concatenate([crossed_high, crossed_low], axis=1)))
-    projected_high, projected_low = split(thrice(turned_stack, stack_ref[:ranks], stack_ref[ranks:], dot))
-    inverse_stack = jnp.concatenate(split(inverse_factor(gram)), axis=0)
+    strips = basis_ref.shape[0] // LANES
+
+    def project(k):
+        if k % 3 == 0 and k // 3 < strips:
+            lanes = slice(k // 3 * LANES, (k // 3 + 1) * LANES)
+            part = thrice(turned_stack, stack_ref[:ranks, lanes], stack_ref[ranks:, lanes], dot)
+            high_ref[:, lanes], low_ref[:, lanes] = split(part)
+
+    inverse_stack = jnp.concatenate(split(inverse_factor(gram, project)), axis=0)
     root = total_users ** 0.5
-    scaled = thrice(inverse_stack, projected_high, projected_low, dot) * root
+    scaled = thrice(inverse_stack, high_ref[...], low_ref[...], dot) * root
     for i in range(scaled.shape[1] // LANES):
         basis_ref[i * LANES : (i + 1) * LANES] = scaled[:, i * LANES : (i + 1) * LANES].T
     core_out_ref[...] = thrice(inverse_stack, crossed_high, crossed_low, dot_nt) * (1.0 / root)
@@ -380,6 +401,8 @@
         scratch_shapes=[
             pltpu.VMEM((pack_rows(ranks), LANES), jnp.float32),
             pltpu.VMEM((2 * ranks, ranks), jnp.bfloat16),
+            pltpu.VMEM((LANES, users), jnp.bfloat16),
+            pltpu.VMEM((LANES, users), jnp.bfloat16),
         ],
         compiler_params=limit(16),
         name="finish",

time: 87.3 us -> 88.4 us (1.013)
  no operation moved by 1% of the time
where the time goes in v13:
time: 88.4 us; the launch traced here: 87.8 us
  Pallas kernels  28.2 us (32%)
  waiting for transfers between devices  23.2 us (26%)
  starting transfers between devices  20.3 us (23%)
  blocking collectives  10.5 us (12%)
  local copies, waits for them, and re-layouts  2.9 us (3%)
  between operations  1.62 us (2%)
  other arithmetic  1.07 us (1%)
    ppermute x17, starting transfers between devices, swap(): return lax.ppermute(value, 'users', [(i, i ^ mask) for i in range(devices)])  16.7 us
    ppermute x17, waiting for transfers between devices, swap(): return lax.ppermute(value, 'users', [(i, i ^ mask) for i in range(devices)])  14.4 us
    pallas_call x1, Pallas kernels, tile_sums(): pl.pallas_call(tiles_kernel, out_shape=out_shape, in_specs=[SMEM] * 3 + [...  14.1 us
    all_to_all x1, blocking collectives, body(): lax.all_to_all(requests, 'users', 0, 0, axis_index_groups=sides, tiled=True)  10.5 us
    all_to_all x1, waiting for transfers between devices, body(): lax.all_to_all(found, 'users', 0, 0, axis_index_groups=sides, tiled=True)  8.82 us
    pallas_call x1, Pallas kernels, finish(): pl.pallas_call(functools.partial(finish_kernel, users * devices), out_sha...  6.45 us
    pallas_call x1, Pallas kernels, context_values(): pl.pallas_call(context_kernel, out_shape=jax.ShapeDtypeStruct((tiles, ROW...  3.72 us
    all_to_all x1, starting transfers between devices, body(): lax.all_to_all(found, 'users', 0, 0, axis_index_groups=sides, tiled=True)  3.65 us
  transfers between devices with their start and end apart: 18, of which 10 were waited for; matrix products, arithmetic and copies ran while one was open for 2% of the time, Pallas kernels for 7%

profile of v13, /device:TPU:0, one launch (start us, length us, event | category | flops | bytes accessed | tf_op | source)
XLA Modules:
  0.0 87.8 jit_solution(17883029499935221053)
XLA Ops:
  0.6 4.1 %collective-permute-start = (bf16[16,64,128]{2,1,0:T(8,128)(2,1)}, bf16[16,64,128]{2,1,0:T(8,128)(2,1)S(1)}, u32[]{:S(2)}, u32[]{:S(2)}) collective-permute-start(bf16[16,64,128]{2,1,0:T(8,128)(2,1)} %own_ref.1), channel_id=1, source_target_pairs={{0,16},{1,17},{2,18},{3,19},{4,20},{5,21},{6,22},{7,23},{8,24},{9,... | collective-permute-start | bytes 786440 | tf_op jit(solution)/shard_map/ppermute | solution.py:413
  4.7 2.2 %route.1 = (s32[16,1,128]{2,1,0:T(1,128)S(1)}, s32[64]{0:T(128)S(1)}, bf16[16,64,128]{2,1,0:T(8,128)(2,1)S(1)}) custom-call(s32[1]{0:T(128)} %bitcast.me_ref, s32[64]{0:T(128)} %bitcast.136, s32[64]{0:T(128)} %slot_ref.1, bf16[16,64,128]{2,1,0:T(8,128)(2,1)} %own_ref.1), custom_call_target="tpu_custom_call" | custom-call | tf_op jit(solution)/shard_map/route/pallas_call | solution.py:85
  7.0 10.5 %all_to_all.10.asked_ref = s32[16,1,128]{2,1,0:T(1,128)S(1)} all-to-all(s32[16,1,128]{2,1,0:T(1,128)S(1)} %get-tuple-element.18), channel_id=1, replica_groups={{0,1,2,3,4,5,6,7,8,9,10,11,12,13,14,15},{16,17,18,19,20,21,22,23,24,25,..., dimensions={0} | all-to-all | bytes 16384 | tf_op jit(solution)/shard_map/all_to_all | solution.py:471
  17.4 1.7 %collect.1 = bf16[64,64,128]{2,1,0:T(8,128)(2,1)} custom-call(s32[16,1,128]{2,1,0:T(1,128)S(1)} %all_to_all.10.asked_ref, bf16[16,64,128]{2,1,0:T(8,128)(2,1)S(1)} %get-tuple-element.19.own_ref, bf16[16,64,128]{2,1,0:T(8,128)(2,1)S(1)} %collective-permute-done.mirror_ref), custom_call_target="tpu_custom_call" | custom-call | tf_op jit(solution)/shard_map/collect/pallas_call | solution.py:108
  19.1 3.7 %all-to-all-start.1 = ((bf16[64,64,128]{2,1,0:T(8,128)(2,1)}), bf16[64,64,128]{2,1,0:T(8,128)(2,1)S(1)}, u32[]{:S(2)}, u32[]{:S(2)}) async-start(bf16[64,64,128]{2,1,0:T(8,128)(2,1)} %collect.1), calls=%async_computation.1 | async-start | bytes 2097152 | tf_op jit(solution)/shard_map/all_to_all | solution.py:474
  23.5 0.9 reshape.232
  24.3 0.2 copy.13
  24.5 0.9 %copy-done.1 = s32[64,512]{1,0:T(8,128)S(1)} copy-done((s32[64,512]{1,0:T(8,128)S(1)}, s32[64,512]{1,0:T(8,128)}, u32[]{:S(2)}) %copy-start.1) | copy-done | bytes 131096
  25.4 3.7 %contexts.1.context_ref = f32[64,8,512]{2,1,0:T(8,128)S(1)} custom-call(s32[64]{0:T(128)} %cblock_ref, f32[64,8,8]{2,1,0:T(8,128)S(1)} %bitcast.129, s32[64,512]{1,0:T(8,128)S(1)} %copy-done.1), custom_call_target="tpu_custom_call" | custom-call | flops 10000000 | bytes 20000000 | tf_op jit(solution)/shard_map/contexts/pallas_call | solution.py:136
  29.1 1.0 %copy-done = f32[64,8,512]{2,1,0:T(8,128)} copy-done((f32[64,8,512]{2,1,0:T(8,128)}, f32[64,8,512]{2,1,0:T(8,128)S(1)}, u32[]{:S(2)}) %copy-start) | copy-done | bytes 1048600
  30.1 8.8 %all-to-all-done.1.blocks_ref = bf16[64,64,128]{2,1,0:T(8,128)(2,1)S(1)} async-done(((bf16[64,64,128]{2,1,0:T(8,128)(2,1)}), bf16[64,64,128]{2,1,0:T(8,128)(2,1)S(1)}, u32[]{:S(2)}, u32[]{:S(2)}) %all-to-all-start.1) | async-done | bytes 1048608 | tf_op jit(solution)/shard_map/all_to_all | solution.py:474
  38.9 14.1 %tile_sums.1 = (f32[224,128]{1,0:T(8,128)S(1)}, f32[224,128]{1,0:T(8,128)S(1)}, f32[224,128]{1,0:T(8,128)S(1)}, f32[224,128]{1,0:T(8,128)S(1)}, f32[224,128]{1,0...) custom-call(s32[64]{0:T(128)S(1)} %get-tuple-element.17.where_ref, ...), custom_call_target="tpu_custom_call" | custom-call | flops 2000000000 | bytes 12000000 | tf_op jit(solution)/shard_map/tile_sums/pallas_call | solution.py:279
  53.2 0.5 collective-permute-start.1
  53.7 0.4 collective-permute-start.6
  54.2 0.3 collective-permute-done.2
  54.6 1.0 %collective-permute-start.3 = (s16[240,128]{1,0:T(8,128)(2,1)S(1)}, s16[240,128]{1,0:T(8,128)(2,1)S(1)}, u32[]{:S(2)}, u32[]{:S(2)}) collective-permute-start(s16[240,128]{1,0:T(8,128)(2,1)S(1)} %pad_add_fusion.5), channel_id=1, source_target_pairs={{0,6},{1,7},{2,4},{3,5},{4,2},{5,3},{6,0},{7,1},{8,14},{9,15},{10,... | collective-permute-start | bytes 184328 | tf_op jit(solution)/shard_map/ppermute | solution.py:413
  55.7 1.4 %collective-permute-start.5 = (s16[240,128]{1,0:T(8,128)(2,1)S(1)}, s16[240,128]{1,0:T(8,128)(2,1)S(1)}, u32[]{:S(2)}, u32[]{:S(2)}) collective-permute-start(s16[240,128]{1,0:T(8,128)(2,1)S(1)} %pad_add_fusion.4), channel_id=1, source_target_pairs={{0,2},{1,3},{2,0},{3,1},{4,6},{5,7},{6,4},{7,5},{8,10},{9,11},{10,... | collective-permute-start | bytes 184328 | tf_op jit(solution)/shard_map/ppermute | solution.py:413
  57.3 1.2 %collective-permute-start.7 = (s16[240,128]{1,0:T(8,128)(2,1)S(1)}, s16[240,128]{1,0:T(8,128)(2,1)S(1)}, u32[]{:S(2)}, u32[]{:S(2)}) collective-permute-start(s16[240,128]{1,0:T(8,128)(2,1)S(1)} %pad_add_fusion.3), channel_id=1, source_target_pairs={{0,4},{1,5},{2,6},{3,7},{4,0},{5,1},{6,2},{7,3},{8,12},{9,13},{10,... | collective-permute-start | bytes 184328 | tf_op jit(solution)/shard_map/ppermute | solution.py:413
  58.5 1.9 %collective-permute-done.3 = s16[240,128]{1,0:T(8,128)(2,1)S(1)} collective-permute-done((s16[240,128]{1,0:T(8,128)(2,1)S(1)}, s16[240,128]{1,0:T(8,128)(2,1)S(1)}, u32[]{:S(2)}, u32[]{:S(2)}) %collective-permute-start.3) | collective-permute-done | bytes 61472 | tf_op jit(solution)/shard_map/ppermute | solution.py:413
  60.4 1.1 %collective-permute-done.7 = s16[240,128]{1,0:T(8,128)(2,1)S(1)} collective-permute-done((s16[240,128]{1,0:T(8,128)(2,1)S(1)}, s16[240,128]{1,0:T(8,128)(2,1)S(1)}, u32[]{:S(2)}, u32[]{:S(2)}) %collective-permute-start.7) | collective-permute-done | bytes 61472 | tf_op jit(solution)/shard_map/ppermute | solution.py:413
  61.6 0.1 fusion.35
  61.7 0.6 collective-permute-start.8
  62.4 3.7 %collective-permute-done.8 = s16[240,128]{1,0:T(8,128)(2,1)S(1)} collective-permute-done((s16[240,128]{1,0:T(8,128)(2,1)S(1)}, s16[240,128]{1,0:T(8,128)(2,1)S(1)}, u32[]{:S(2)}, u32[]{:S(2)}) %collective-permute-start.8) | collective-permute-done | bytes 61472 | tf_op jit(solution)/shard_map/ppermute | solution.py:413
  66.2 3.6 %collective-permute-start.9 = (s16[240,128]{1,0:T(8,128)(2,1)S(1)}, s16[240,128]{1,0:T(8,128)(2,1)S(1)}, u32[]{:S(2)}, u32[]{:S(2)}) collective-permute-start(s16[240,128]{1,0:T(8,128)(2,1)S(1)} %pad_add_fusion.1), channel_id=1, source_target_pairs={{0,16},{1,17},{2,18},{3,19},{4,20},{5,21},{6,22},{7,23},{8,24},{9,... | collective-permute-start | bytes 184328 | tf_op jit(solution)/shard_map/ppermute | solution.py:413
  69.9 2.7 %collective-permute-done.9 = s16[240,128]{1,0:T(8,128)(2,1)S(1)} collective-permute-done((s16[240,128]{1,0:T(8,128)(2,1)S(1)}, s16[240,128]{1,0:T(8,128)(2,1)S(1)}, u32[]{:S(2)}, u32[]{:S(2)}) %collective-permute-start.9) | collective-permute-done | bytes 61472 | tf_op jit(solution)/shard_map/ppermute | solution.py:413
  72.8 1.2 %collective-permute-start.14 = (s16[240,128]{1,0:T(8,128)(2,1)S(1)}, s16[240,128]{1,0:T(8,128)(2,1)S(1)}, u32[]{:S(2)}, u32[]{:S(2)}) collective-permute-start(s16[240,128]{1,0:T(8,128)(2,1)S(1)} %pad_add_fusion), channel_id=1, source_target_pairs={{0,4},{1,5},{2,6},{3,7},{4,0},{5,1},{6,2},{7,3},{8,12},{9,13},{10,... | collective-permute-start | bytes 184328 | tf_op jit(solution)/shard_map/ppermute | solution.py:413
  74.0 2.3 %collective-permute-start.10 = (s16[240,128]{1,0:T(8,128)(2,1)S(1)}, s16[240,128]{1,0:T(8,128)(2,1)S(1)}, u32[]{:S(2)}, u32[]{:S(2)}) collective-permute-start(s16[240,128]{1,0:T(8,128)(2,1)S(1)} %pad_add_fusion), channel_id=1, source_target_pairs={{0,6},{1,7},{2,4},{3,5},{4,2},{5,3},{6,0},{7,1},{8,14},{9,15},{10,... | collective-permute-start | bytes 184328 | tf_op jit(solution)/shard_map/ppermute | solution.py:413
  76.3 0.7 collective-permute-done.14
  77.1 1.7 %collective-permute-done.12 = s16[240,128]{1,0:T(8,128)(2,1)S(1)} collective-permute-done((s16[240,128]{1,0:T(8,128)(2,1)S(1)}, s16[240,128]{1,0:T(8,128)(2,1)S(1)}, u32[]{:S(2)}, u32[]{:S(2)}) %collective-permute-start.12) | collective-permute-done | bytes 61472 | tf_op jit(solution)/shard_map/ppermute | solution.py:413
  78.8 1.2 %collective-permute-done.10 = s16[240,128]{1,0:T(8,128)(2,1)S(1)} collective-permute-done((s16[240,128]{1,0:T(8,128)(2,1)S(1)}, s16[240,128]{1,0:T(8,128)(2,1)S(1)}, u32[]{:S(2)}, u32[]{:S(2)}) %collective-permute-start.10) | collective-permute-done | bytes 61472 | tf_op jit(solution)/shard_map/ppermute | solution.py:413
  80.3 1.0 %collective-permute-done.11 = s16[240,128]{1,0:T(8,128)(2,1)S(1)} collective-permute-done((s16[240,128]{1,0:T(8,128)(2,1)S(1)}, s16[240,128]{1,0:T(8,128)(2,1)S(1)}, u32[]{:S(2)}, u32[]{:S(2)}) %collective-permute-start.11) | collective-permute-done | bytes 61472 | tf_op jit(solution)/shard_map/ppermute | solution.py:413
  81.4 6.4 %finish.1 = (f32[512,128]{1,0:T(8,128)}, f32[128,512]{1,0:T(8,128)}) custom-call(s32[1]{0:T(128)} %bitcast.me_ref, bf16[1024,512]{1,0:T(8,128)(2,1)S(1)} %get-tuple-element.23.stack_ref, f32[224,128]{1,0:T(8,128)S(1)} %bitcast_multiply_fusion.7.rest_0_, f32[224,128]{1,0:T(8,128)S(1)} %bitcast_multiply_fusion.6.rest_1_, ...), custom_call_target="tpu_custom_call" | custom-call | tf_op jit(solution)/shard_map/finish/pallas_call | solution.py:393
  (65 shorter events, 1.2 us)
Async XLA Ops:
  0.6 16.8 %collective-permute-start = (bf16[16,64,128]{2,1,0:T(8,128)(2,1)}, bf16[16,64,128]{2,1,0:T(8,128)(2,1)S(1)}, u32[]{:S(2)}, u32[]{:S(2)}) collective-permute-start(bf16[16,64,128]{2,1,0:T(8,128)(2,1)} %own_ref.1), channel_id=1, source_target_pairs={{0,16},{1,17},{2,18},{3,19},{4,20},{5,21},{6,22},{7,23},{8,24},{9,... | collective-permute-start | bytes 786440 | tf_op jit(solution)/shard_map/ppermute | solution.py:413
  19.1 19.8 %all-to-all-start.1 = ((bf16[64,64,128]{2,1,0:T(8,128)(2,1)}), bf16[64,64,128]{2,1,0:T(8,128)(2,1)S(1)}, u32[]{:S(2)}, u32[]{:S(2)}) async-start(bf16[64,64,128]{2,1,0:T(8,128)(2,1)} %collect.1), calls=%async_computation.1 | async-start | bytes 2097152 | tf_op jit(solution)/shard_map/all_to_all | solution.py:474
  24.5 0.9 %copy-start.1 = (s32[64,512]{1,0:T(8,128)S(1)}, s32[64,512]{1,0:T(8,128)}, u32[]{:S(2)}) copy-start(s32[64,512]{1,0:T(8,128)} %marks_ref.1) | copy-start | bytes 393220
  29.1 1.0 %copy-start = (f32[64,8,512]{2,1,0:T(8,128)}, f32[64,8,512]{2,1,0:T(8,128)S(1)}, u32[]{:S(2)}) copy-start(f32[64,8,512]{2,1,0:T(8,128)S(1)} %contexts.1.context_ref) | copy-start | bytes 3145732
  53.1 1.4 %collective-permute-start.2 = (f32[224,128]{1,0:T(8,128)S(1)}, f32[224,128]{1,0:T(8,128)S(1)}, u32[]{:S(2)}, u32[]{:S(2)}) collective-permute-start(f32[224,128]{1,0:T(8,128)S(1)} %get-tuple-element.27), channel_id=1, source_target_pairs={{0,1},{1,0},{2,3},{3,2},{4,5},{5,4},{6,7},{7,6},{8,9},{9,8},{10,11... | collective-permute-start | bytes 344072 | tf_op jit(solution)/shard_map/ppermute | solution.py:413
  53.2 8.4 %collective-permute-start.1 = (f32[224,128]{1,0:T(8,128)S(1)}, f32[224,128]{1,0:T(8,128)S(1)}, u32[]{:S(2)}, u32[]{:S(2)}) collective-permute-start(f32[224,128]{1,0:T(8,128)S(1)} %get-tuple-element.25), channel_id=1, source_target_pairs={{0,1},{1,0},{2,3},{3,2},{4,5},{5,4},{6,7},{7,6},{8,9},{9,8},{10,11... | collective-permute-start | bytes 344072 | tf_op jit(solution)/shard_map/ppermute | solution.py:413
  53.7 1.9 %collective-permute-start.4 = (f32[224,128]{1,0:T(8,128)S(1)}, f32[224,128]{1,0:T(8,128)S(1)}, u32[]{:S(2)}, u32[]{:S(2)}) collective-permute-start(f32[224,128]{1,0:T(8,128)S(1)} %get-tuple-element.29), channel_id=1, source_target_pairs={{0,1},{1,0},{2,3},{3,2},{4,5},{5,4},{6,7},{7,6},{8,9},{9,8},{10,11... | collective-permute-start | bytes 344072 | tf_op jit(solution)/shard_map/ppermute | solution.py:413
  53.7 3.4 %collective-permute-start.6 = (f32[224,128]{1,0:T(8,128)S(1)}, f32[224,128]{1,0:T(8,128)S(1)}, u32[]{:S(2)}, u32[]{:S(2)}) collective-permute-start(f32[224,128]{1,0:T(8,128)S(1)} %get-tuple-element.31), channel_id=1, source_target_pairs={{0,1},{1,0},{2,3},{3,2},{4,5},{5,4},{6,7},{7,6},{8,9},{9,8},{10,11... | collective-permute-start | bytes 344072 | tf_op jit(solution)/shard_map/ppermute | solution.py:413
  54.6 5.8 %collective-permute-start.3 = (s16[240,128]{1,0:T(8,128)(2,1)S(1)}, s16[240,128]{1,0:T(8,128)(2,1)S(1)}, u32[]{:S(2)}, u32[]{:S(2)}) collective-permute-start(s16[240,128]{1,0:T(8,128)(2,1)S(1)} %pad_add_fusion.5), channel_id=1, source_target_pairs={{0,6},{1,7},{2,4},{3,5},{4,2},{5,3},{6,0},{7,1},{8,14},{9,15},{10,... | collective-permute-start | bytes 184328 | tf_op jit(solution)/shard_map/ppermute | solution.py:413
  55.7 4.7 %collective-permute-start.5 = (s16[240,128]{1,0:T(8,128)(2,1)S(1)}, s16[240,128]{1,0:T(8,128)(2,1)S(1)}, u32[]{:S(2)}, u32[]{:S(2)}) collective-permute-start(s16[240,128]{1,0:T(8,128)(2,1)S(1)} %pad_add_fusion.4), channel_id=1, source_target_pairs={{0,2},{1,3},{2,0},{3,1},{4,6},{5,7},{6,4},{7,5},{8,10},{9,11},{10,... | collective-permute-start | bytes 184328 | tf_op jit(solution)/shard_map/ppermute | solution.py:413
  57.3 4.3 %collective-permute-start.7 = (s16[240,128]{1,0:T(8,128)(2,1)S(1)}, s16[240,128]{1,0:T(8,128)(2,1)S(1)}, u32[]{:S(2)}, u32[]{:S(2)}) collective-permute-start(s16[240,128]{1,0:T(8,128)(2,1)S(1)} %pad_add_fusion.3), channel_id=1, source_target_pairs={{0,4},{1,5},{2,6},{3,7},{4,0},{5,1},{6,2},{7,3},{8,12},{9,13},{10,... | collective-permute-start | bytes 184328 | tf_op jit(solution)/shard_map/ppermute | solution.py:413
  61.7 4.3 %collective-permute-start.8 = (s16[240,128]{1,0:T(8,128)(2,1)S(1)}, s16[240,128]{1,0:T(8,128)(2,1)S(1)}, u32[]{:S(2)}, u32[]{:S(2)}) collective-permute-start(s16[240,128]{1,0:T(8,128)(2,1)S(1)} %pad_add_fusion.2), channel_id=1, source_target_pairs={{0,8},{1,9},{2,10},{3,11},{4,12},{5,13},{6,14},{7,15},{8,0},{9,1},... | collective-permute-start | bytes 184328 | tf_op jit(solution)/shard_map/ppermute | solution.py:413
  66.2 6.3 %collective-permute-start.9 = (s16[240,128]{1,0:T(8,128)(2,1)S(1)}, s16[240,128]{1,0:T(8,128)(2,1)S(1)}, u32[]{:S(2)}, u32[]{:S(2)}) collective-permute-start(s16[240,128]{1,0:T(8,128)(2,1)S(1)} %pad_add_fusion.1), channel_id=1, source_target_pairs={{0,16},{1,17},{2,18},{3,19},{4,20},{5,21},{6,22},{7,23},{8,24},{9,... | collective-permute-start | bytes 184328 | tf_op jit(solution)/shard_map/ppermute | solution.py:413
  72.8 4.3 %collective-permute-start.14 = (s16[240,128]{1,0:T(8,128)(2,1)S(1)}, s16[240,128]{1,0:T(8,128)(2,1)S(1)}, u32[]{:S(2)}, u32[]{:S(2)}) collective-permute-start(s16[240,128]{1,0:T(8,128)(2,1)S(1)} %pad_add_fusion), channel_id=1, source_target_pairs={{0,4},{1,5},{2,6},{3,7},{4,0},{5,1},{6,2},{7,3},{8,12},{9,13},{10,... | collective-permute-start | bytes 184328 | tf_op jit(solution)/shard_map/ppermute | solution.py:413
  74.0 6.1 %collective-permute-start.16 = (s16[240,128]{1,0:T(8,128)(2,1)S(1)}, s16[240,128]{1,0:T(8,128)(2,1)S(1)}, u32[]{:S(2)}, u32[]{:S(2)}) collective-permute-start(s16[240,128]{1,0:T(8,128)(2,1)S(1)} %pad_add_fusion), channel_id=1, source_target_pairs={{0,1},{1,0},{2,3},{3,2},{4,5},{5,4},{6,7},{7,6},{8,9},{9,8},{10,11... | collective-permute-start | bytes 184328 | tf_op jit(solution)/shard_map/ppermute | solution.py:413
  74.0 4.8 %collective-permute-start.12 = (s16[240,128]{1,0:T(8,128)(2,1)S(1)}, s16[240,128]{1,0:T(8,128)(2,1)S(1)}, u32[]{:S(2)}, u32[]{:S(2)}) collective-permute-start(s16[240,128]{1,0:T(8,128)(2,1)S(1)} %pad_add_fusion), channel_id=1, source_target_pairs={{0,2},{1,3},{2,0},{3,1},{4,6},{5,7},{6,4},{7,5},{8,10},{9,11},{10,... | collective-permute-start | bytes 184328 | tf_op jit(solution)/shard_map/ppermute | solution.py:413
  74.0 6.0 %collective-permute-start.10 = (s16[240,128]{1,0:T(8,128)(2,1)S(1)}, s16[240,128]{1,0:T(8,128)(2,1)S(1)}, u32[]{:S(2)}, u32[]{:S(2)}) collective-permute-start(s16[240,128]{1,0:T(8,128)(2,1)S(1)} %pad_add_fusion), channel_id=1, source_target_pairs={{0,6},{1,7},{2,4},{3,5},{4,2},{5,3},{6,0},{7,1},{8,14},{9,15},{10,... | collective-permute-start | bytes 184328 | tf_op jit(solution)/shard_map/ppermute | solution.py:413
  77.1 3.1 %collective-permute-start.15 = (s16[240,128]{1,0:T(8,128)(2,1)S(1)}, s16[240,128]{1,0:T(8,128)(2,1)S(1)}, u32[]{:S(2)}, u32[]{:S(2)}) collective-permute-start(s16[240,128]{1,0:T(8,128)(2,1)S(1)} %collective-permute-done.14), channel_id=1, source_target_pairs={{0,1},{1,0},{2,3},{3,2},{4,5},{5,4},{6,7},{7,6},{8,9},{9,8},{10,11... | collective-permute-start | bytes 184328 | tf_op jit(solution)/shard_map/ppermute | solution.py:413
  78.8 1.4 %collective-permute-start.13 = (s16[240,128]{1,0:T(8,128)(2,1)S(1)}, s16[240,128]{1,0:T(8,128)(2,1)S(1)}, u32[]{:S(2)}, u32[]{:S(2)}) collective-permute-start(s16[240,128]{1,0:T(8,128)(2,1)S(1)} %collective-permute-done.12), channel_id=1, source_target_pairs={{0,1},{1,0},{2,3},{3,2},{4,5},{5,4},{6,7},{7,6},{8,9},{9,8},{10,11... | collective-permute-start | bytes 184328 | tf_op jit(solution)/shard_map/ppermute | solution.py:413
  80.1 1.3 %collective-permute-start.11 = (s16[240,128]{1,0:T(8,128)(2,1)S(1)}, s16[240,128]{1,0:T(8,128)(2,1)S(1)}, u32[]{:S(2)}, u32[]{:S(2)}) collective-permute-start(s16[240,128]{1,0:T(8,128)(2,1)S(1)} %collective-permute-done.10), channel_id=1, source_target_pairs={{0,1},{1,0},{2,3},{3,2},{4,5},{5,4},{6,7},{7,6},{8,9},{9,8},{10,11... | collective-permute-start | bytes 184328 | tf_op jit(solution)/shard_map/ppermute | solution.py:413

commit v14 on v13

--- a/solution.py
+++ b/solution.py
@@ -172,10 +172,10 @@
 
     def copies(batch):
         rows = pl.ds(batch * BATCH, BATCH)
-        return (
-            pltpu.make_async_copy(weights_ref.at[rows], weights_held.at[rows], weights_sem.at[batch]),
-            pltpu.make_async_copy(context_ref.at[rows], context_held.at[rows], context_sem.at[batch]),
-        )
+        tiles = [batch * BATCH + place for place in range(BATCH)]
+        return [
+            pltpu.make_async_copy(weights_ref.at[tile], weights_held.at[tile], weights_sem.at[tile]) for tile in tiles
+        ] + [pltpu.make_async_copy(context_ref.at[rows], context_held.at[rows], context_sem.at[batch])]
 
     def start(batch):
         for copy in copies(batch):
@@ -186,6 +186,7 @@
             copy.wait()
 
     start(0)
+    start(1)
 
     def multiply(batch, place, into_ref):
         tile = batch * BATCH + place
@@ -211,16 +212,16 @@
     y_ref[...] = jnp.zeros_like(y_ref)
     parts = 2 * users // LANES
     wait(0)
-    start(1)
+    start(2)
     for place in range(BATCH):
         multiply(0, place, even_ref)
 
     def turn(batch, from_ref, into_ref):
         wait(batch + 1)
 
-        @pl.when(batch + 2 < batches)
+        @pl.when(batch + 3 < batches)
         def _():
-            start(batch + 2)
+            start(batch + 3)
 
         for part in range(max(parts, BATCH)):
             if part < BATCH:
@@ -290,7 +291,7 @@
             pltpu.VMEM(weights.shape, weights.dtype),
             pltpu.VMEM(contexts.shape, contexts.dtype),
             pltpu.VMEM(user_basis.shape, user_basis.dtype),
-            pltpu.SemaphoreType.DMA((tiles // BATCH,)),
+            pltpu.SemaphoreType.DMA((tiles,)),
             pltpu.SemaphoreType.DMA((tiles // BATCH,)),
             pltpu.SemaphoreType.DMA,
         ],

time: 88.4 us -> 86.7 us (0.981)
  Pallas kernels: 28.2 us -> 26.7 us
    pallas_call x1, Pallas kernels: 14.1 us -> 12.6 us  [tile_sums(): pl.pallas_call(tiles_kernel, out_shape=out_shape, in_specs=[SMEM] * 3 + [...]
where the time goes in v14:
time: 86.7 us; the launch traced here: 86.3 us
  Pallas kernels  26.7 us (31%)
  waiting for transfers between devices  23.2 us (27%)
  starting transfers between devices  20.4 us (24%)
  blocking collectives  10.5 us (12%)
  local copies, waits for them, and re-layouts  2.9 us (3%)
  between operations  1.62 us (2%)
  other arithmetic  1.07 us (1%)
    ppermute x17, starting transfers between devices, swap(): return lax.ppermute(value, 'users', [(i, i ^ mask) for i in range(devices)])  16.7 us
    ppermute x17, waiting for transfers between devices, swap(): return lax.ppermute(value, 'users', [(i, i ^ mask) for i in range(devices)])  14.3 us
    pallas_call x1, Pallas kernels, tile_sums(): pl.pallas_call(tiles_kernel, out_shape=out_shape, in_specs=[SMEM] * 3 + [...  12.6 us
    all_to_all x1, blocking collectives, body(): lax.all_to_all(requests, 'users', 0, 0, axis_index_groups=sides, tiled=True)  10.5 us
    all_to_all x1, waiting for transfers between devices, body(): lax.all_to_all(found, 'users', 0, 0, axis_index_groups=sides, tiled=True)  8.82 us
    pallas_call x1, Pallas kernels, finish(): pl.pallas_call(functools.partial(finish_kernel, users * devices), out_sha...  6.43 us
    pallas_call x1, Pallas kernels, context_values(): pl.pallas_call(context_kernel, out_shape=jax.ShapeDtypeStruct((tiles, ROW...  3.72 us
    all_to_all x1, starting transfers between devices, body(): lax.all_to_all(found, 'users', 0, 0, axis_index_groups=sides, tiled=True)  3.65 us
  transfers between devices with their start and end apart: 18, of which 10 were waited for; matrix products, arithmetic and copies ran while one was open for 2% of the time, Pallas kernels for 7%

profile of v14, /device:TPU:0, one launch (start us, length us, event | category | flops | bytes accessed | tf_op | source)
XLA Modules:
  0.0 86.3 jit_solution(13435038407304559494)
XLA Ops:
  0.6 4.1 %collective-permute-start = (bf16[16,64,128]{2,1,0:T(8,128)(2,1)}, bf16[16,64,128]{2,1,0:T(8,128)(2,1)S(1)}, u32[]{:S(2)}, u32[]{:S(2)}) collective-permute-start(bf16[16,64,128]{2,1,0:T(8,128)(2,1)} %own_ref.1), channel_id=1, source_target_pairs={{0,16},{1,17},{2,18},{3,19},{4,20},{5,21},{6,22},{7,23},{8,24},{9,... | collective-permute-start | bytes 786440 | tf_op jit(solution)/shard_map/ppermute | solution.py:414
  4.7 2.2 %route.1 = (s32[16,1,128]{2,1,0:T(1,128)S(1)}, s32[64]{0:T(128)S(1)}, bf16[16,64,128]{2,1,0:T(8,128)(2,1)S(1)}) custom-call(s32[1]{0:T(128)} %bitcast.me_ref, s32[64]{0:T(128)} %bitcast.136, s32[64]{0:T(128)} %slot_ref.1, bf16[16,64,128]{2,1,0:T(8,128)(2,1)} %own_ref.1), custom_call_target="tpu_custom_call" | custom-call | tf_op jit(solution)/shard_map/route/pallas_call | solution.py:85
  7.0 10.5 %all_to_all.10.asked_ref = s32[16,1,128]{2,1,0:T(1,128)S(1)} all-to-all(s32[16,1,128]{2,1,0:T(1,128)S(1)} %get-tuple-element.18), channel_id=1, replica_groups={{0,1,2,3,4,5,6,7,8,9,10,11,12,13,14,15},{16,17,18,19,20,21,22,23,24,25,..., dimensions={0} | all-to-all | bytes 16384 | tf_op jit(solution)/shard_map/all_to_all | solution.py:472
  17.4 1.7 %collect.1 = bf16[64,64,128]{2,1,0:T(8,128)(2,1)} custom-call(s32[16,1,128]{2,1,0:T(1,128)S(1)} %all_to_all.10.asked_ref, bf16[16,64,128]{2,1,0:T(8,128)(2,1)S(1)} %get-tuple-element.19.own_ref, bf16[16,64,128]{2,1,0:T(8,128)(2,1)S(1)} %collective-permute-done.mirror_ref), custom_call_target="tpu_custom_call" | custom-call | tf_op jit(solution)/shard_map/collect/pallas_call | solution.py:108
  19.1 3.7 %all-to-all-start.1 = ((bf16[64,64,128]{2,1,0:T(8,128)(2,1)}), bf16[64,64,128]{2,1,0:T(8,128)(2,1)S(1)}, u32[]{:S(2)}, u32[]{:S(2)}) async-start(bf16[64,64,128]{2,1,0:T(8,128)(2,1)} %collect.1), calls=%async_computation.1 | async-start | bytes 2097152 | tf_op jit(solution)/shard_map/all_to_all | solution.py:475
  23.5 0.9 %reshape.232 = f32[8,64,8]{2,1,0:T(8,128)S(1)} reshape(bf16[8,512]{1,0:T(8,128)(2,1)} %param.15) | data formatting | bytes 24576 | tf_op jit(solution)/shard_map/transpose | solution.py:477
  24.3 0.2 copy.13
  24.5 0.9 %copy-done.1 = s32[64,512]{1,0:T(8,128)S(1)} copy-done((s32[64,512]{1,0:T(8,128)S(1)}, s32[64,512]{1,0:T(8,128)}, u32[]{:S(2)}) %copy-start.1) | copy-done | bytes 131096
  25.4 3.7 %contexts.1.context_ref = f32[64,8,512]{2,1,0:T(8,128)S(1)} custom-call(s32[64]{0:T(128)} %cblock_ref, f32[64,8,8]{2,1,0:T(8,128)S(1)} %bitcast.129, s32[64,512]{1,0:T(8,128)S(1)} %copy-done.1), custom_call_target="tpu_custom_call" | custom-call | flops 10000000 | bytes 20000000 | tf_op jit(solution)/shard_map/contexts/pallas_call | solution.py:136
  29.1 1.0 %copy-done = f32[64,8,512]{2,1,0:T(8,128)} copy-done((f32[64,8,512]{2,1,0:T(8,128)}, f32[64,8,512]{2,1,0:T(8,128)S(1)}, u32[]{:S(2)}) %copy-start) | copy-done | bytes 1048600
  30.1 8.8 %all-to-all-done.1.blocks_ref = bf16[64,64,128]{2,1,0:T(8,128)(2,1)S(1)} async-done(((bf16[64,64,128]{2,1,0:T(8,128)(2,1)}), bf16[64,64,128]{2,1,0:T(8,128)(2,1)S(1)}, u32[]{:S(2)}, u32[]{:S(2)}) %all-to-all-start.1) | async-done | bytes 1048608 | tf_op jit(solution)/shard_map/all_to_all | solution.py:475
  38.9 12.6 %tile_sums.1 = (f32[224,128]{1,0:T(8,128)S(1)}, f32[224,128]{1,0:T(8,128)S(1)}, f32[224,128]{1,0:T(8,128)S(1)}, f32[224,128]{1,0:T(8,128)S(1)}, f32[224,128]{1,0...) custom-call(s32[64]{0:T(128)S(1)} %get-tuple-element.17.where_ref, ...), custom_call_target="tpu_custom_call" | custom-call | flops 2000000000 | bytes 12000000 | tf_op jit(solution)/shard_map/tile_sums/pallas_call | solution.py:280
  51.6 0.5 collective-permute-start.1
  52.2 0.4 collective-permute-start.6
  52.6 0.3 collective-permute-done.2
  53.0 1.0 %collective-permute-start.3 = (s16[240,128]{1,0:T(8,128)(2,1)S(1)}, s16[240,128]{1,0:T(8,128)(2,1)S(1)}, u32[]{:S(2)}, u32[]{:S(2)}) collective-permute-start(s16[240,128]{1,0:T(8,128)(2,1)S(1)} %pad_add_fusion.5), channel_id=1, source_target_pairs={{0,6},{1,7},{2,4},{3,5},{4,2},{5,3},{6,0},{7,1},{8,14},{9,15},{10,... | collective-permute-start | bytes 184328 | tf_op jit(solution)/shard_map/ppermute | solution.py:414
  54.2 1.4 %collective-permute-start.5 = (s16[240,128]{1,0:T(8,128)(2,1)S(1)}, s16[240,128]{1,0:T(8,128)(2,1)S(1)}, u32[]{:S(2)}, u32[]{:S(2)}) collective-permute-start(s16[240,128]{1,0:T(8,128)(2,1)S(1)} %pad_add_fusion.4), channel_id=1, source_target_pairs={{0,2},{1,3},{2,0},{3,1},{4,6},{5,7},{6,4},{7,5},{8,10},{9,11},{10,... | collective-permute-start | bytes 184328 | tf_op jit(solution)/shard_map/ppermute | solution.py:414
  55.7 1.2 %collective-permute-start.7 = (s16[240,128]{1,0:T(8,128)(2,1)S(1)}, s16[240,128]{1,0:T(8,128)(2,1)S(1)}, u32[]{:S(2)}, u32[]{:S(2)}) collective-permute-start(s16[240,128]{1,0:T(8,128)(2,1)S(1)} %pad_add_fusion.3), channel_id=1, source_target_pairs={{0,4},{1,5},{2,6},{3,7},{4,0},{5,1},{6,2},{7,3},{8,12},{9,13},{10,... | collective-permute-start | bytes 184328 | tf_op jit(solution)/shard_map/ppermute | solution.py:414
  57.0 1.9 %collective-permute-done.3 = s16[240,128]{1,0:T(8,128)(2,1)S(1)} collective-permute-done((s16[240,128]{1,0:T(8,128)(2,1)S(1)}, s16[240,128]{1,0:T(8,128)(2,1)S(1)}, u32[]{:S(2)}, u32[]{:S(2)}) %collective-permute-start.3) | collective-permute-done | bytes 61472 | tf_op jit(solution)/shard_map/ppermute | solution.py:414
  58.9 1.1 %collective-permute-done.7 = s16[240,128]{1,0:T(8,128)(2,1)S(1)} collective-permute-done((s16[240,128]{1,0:T(8,128)(2,1)S(1)}, s16[240,128]{1,0:T(8,128)(2,1)S(1)}, u32[]{:S(2)}, u32[]{:S(2)}) %collective-permute-start.7) | collective-permute-done | bytes 61472 | tf_op jit(solution)/shard_map/ppermute | solution.py:414
  60.0 0.1 fusion.35
  60.2 0.6 collective-permute-start.8
  60.8 3.7 %collective-permute-done.8 = s16[240,128]{1,0:T(8,128)(2,1)S(1)} collective-permute-done((s16[240,128]{1,0:T(8,128)(2,1)S(1)}, s16[240,128]{1,0:T(8,128)(2,1)S(1)}, u32[]{:S(2)}, u32[]{:S(2)}) %collective-permute-start.8) | collective-permute-done | bytes 61472 | tf_op jit(solution)/shard_map/ppermute | solution.py:414
  64.7 3.7 %collective-permute-start.9 = (s16[240,128]{1,0:T(8,128)(2,1)S(1)}, s16[240,128]{1,0:T(8,128)(2,1)S(1)}, u32[]{:S(2)}, u32[]{:S(2)}) collective-permute-start(s16[240,128]{1,0:T(8,128)(2,1)S(1)} %pad_add_fusion.1), channel_id=1, source_target_pairs={{0,16},{1,17},{2,18},{3,19},{4,20},{5,21},{6,22},{7,23},{8,24},{9,... | collective-permute-start | bytes 184328 | tf_op jit(solution)/shard_map/ppermute | solution.py:414
  68.4 2.7 %collective-permute-done.9 = s16[240,128]{1,0:T(8,128)(2,1)S(1)} collective-permute-done((s16[240,128]{1,0:T(8,128)(2,1)S(1)}, s16[240,128]{1,0:T(8,128)(2,1)S(1)}, u32[]{:S(2)}, u32[]{:S(2)}) %collective-permute-start.9) | collective-permute-done | bytes 61472 | tf_op jit(solution)/shard_map/ppermute | solution.py:414
  71.3 1.2 %collective-permute-start.14 = (s16[240,128]{1,0:T(8,128)(2,1)S(1)}, s16[240,128]{1,0:T(8,128)(2,1)S(1)}, u32[]{:S(2)}, u32[]{:S(2)}) collective-permute-start(s16[240,128]{1,0:T(8,128)(2,1)S(1)} %pad_add_fusion), channel_id=1, source_target_pairs={{0,4},{1,5},{2,6},{3,7},{4,0},{5,1},{6,2},{7,3},{8,12},{9,13},{10,... | collective-permute-start | bytes 184328 | tf_op jit(solution)/shard_map/ppermute | solution.py:414
  72.5 2.4 %collective-permute-start.10 = (s16[240,128]{1,0:T(8,128)(2,1)S(1)}, s16[240,128]{1,0:T(8,128)(2,1)S(1)}, u32[]{:S(2)}, u32[]{:S(2)}) collective-permute-start(s16[240,128]{1,0:T(8,128)(2,1)S(1)} %pad_add_fusion), channel_id=1, source_target_pairs={{0,6},{1,7},{2,4},{3,5},{4,2},{5,3},{6,0},{7,1},{8,14},{9,15},{10,... | collective-permute-start | bytes 184328 | tf_op jit(solution)/shard_map/ppermute | solution.py:414
  74.8 0.7 collective-permute-done.14
  75.6 1.7 %collective-permute-done.12 = s16[240,128]{1,0:T(8,128)(2,1)S(1)} collective-permute-done((s16[240,128]{1,0:T(8,128)(2,1)S(1)}, s16[240,128]{1,0:T(8,128)(2,1)S(1)}, u32[]{:S(2)}, u32[]{:S(2)}) %collective-permute-start.12) | collective-permute-done | bytes 61472 | tf_op jit(solution)/shard_map/ppermute | solution.py:414
  77.3 1.2 %collective-permute-done.10 = s16[240,128]{1,0:T(8,128)(2,1)S(1)} collective-permute-done((s16[240,128]{1,0:T(8,128)(2,1)S(1)}, s16[240,128]{1,0:T(8,128)(2,1)S(1)}, u32[]{:S(2)}, u32[]{:S(2)}) %collective-permute-start.10) | collective-permute-done | bytes 61472 | tf_op jit(solution)/shard_map/ppermute | solution.py:414
  78.8 1.0 %collective-permute-done.11 = s16[240,128]{1,0:T(8,128)(2,1)S(1)} collective-permute-done((s16[240,128]{1,0:T(8,128)(2,1)S(1)}, s16[240,128]{1,0:T(8,128)(2,1)S(1)}, u32[]{:S(2)}, u32[]{:S(2)}) %collective-permute-start.11) | collective-permute-done | bytes 61472 | tf_op jit(solution)/shard_map/ppermute | solution.py:414
  79.8 6.4 %finish.1 = (f32[512,128]{1,0:T(8,128)}, f32[128,512]{1,0:T(8,128)}) custom-call(s32[1]{0:T(128)} %bitcast.me_ref, bf16[1024,512]{1,0:T(8,128)(2,1)S(1)} %get-tuple-element.23.stack_ref, f32[224,128]{1,0:T(8,128)S(1)} %bitcast_multiply_fusion.7.rest_0_, f32[224,128]{1,0:T(8,128)S(1)} %bitcast_multiply_fusion.6.rest_1_, ...), custom_call_target="tpu_custom_call" | custom-call | tf_op jit(solution)/shard_map/finish/pallas_call | solution.py:394
  (65 shorter events, 1.2 us)
Async XLA Ops:
  0.6 16.8 %collective-permute-start = (bf16[16,64,128]{2,1,0:T(8,128)(2,1)}, bf16[16,64,128]{2,1,0:T(8,128)(2,1)S(1)}, u32[]{:S(2)}, u32[]{:S(2)}) collective-permute-start(bf16[16,64,128]{2,1,0:T(8,128)(2,1)} %own_ref.1), channel_id=1, source_target_pairs={{0,16},{1,17},{2,18},{3,19},{4,20},{5,21},{6,22},{7,23},{8,24},{9,... | collective-permute-start | bytes 786440 | tf_op jit(solution)/shard_map/ppermute | solution.py:414
  19.1 19.8 %all-to-all-start.1 = ((bf16[64,64,128]{2,1,0:T(8,128)(2,1)}), bf16[64,64,128]{2,1,0:T(8,128)(2,1)S(1)}, u32[]{:S(2)}, u32[]{:S(2)}) async-start(bf16[64,64,128]{2,1,0:T(8,128)(2,1)} %collect.1), calls=%async_computation.1 | async-start | bytes 2097152 | tf_op jit(solution)/shard_map/all_to_all | solution.py:475
  24.5 0.9 %copy-start.1 = (s32[64,512]{1,0:T(8,128)S(1)}, s32[64,512]{1,0:T(8,128)}, u32[]{:S(2)}) copy-start(s32[64,512]{1,0:T(8,128)} %marks_ref.1) | copy-start | bytes 393220
  29.1 1.0 %copy-start = (f32[64,8,512]{2,1,0:T(8,128)}, f32[64,8,512]{2,1,0:T(8,128)S(1)}, u32[]{:S(2)}) copy-start(f32[64,8,512]{2,1,0:T(8,128)S(1)} %contexts.1.context_ref) | copy-start | bytes 3145732
  51.5 1.4 %collective-permute-start.2 = (f32[224,128]{1,0:T(8,128)S(1)}, f32[224,128]{1,0:T(8,128)S(1)}, u32[]{:S(2)}, u32[]{:S(2)}) collective-permute-start(f32[224,128]{1,0:T(8,128)S(1)} %get-tuple-element.27), channel_id=1, source_target_pairs={{0,1},{1,0},{2,3},{3,2},{4,5},{5,4},{6,7},{7,6},{8,9},{9,8},{10,11... | collective-permute-start | bytes 344072 | tf_op jit(solution)/shard_map/ppermute | solution.py:414
  51.6 8.4 %collective-permute-start.1 = (f32[224,128]{1,0:T(8,128)S(1)}, f32[224,128]{1,0:T(8,128)S(1)}, u32[]{:S(2)}, u32[]{:S(2)}) collective-permute-start(f32[224,128]{1,0:T(8,128)S(1)} %get-tuple-element.25), channel_id=1, source_target_pairs={{0,1},{1,0},{2,3},{3,2},{4,5},{5,4},{6,7},{7,6},{8,9},{9,8},{10,11... | collective-permute-start | bytes 344072 | tf_op jit(solution)/shard_map/ppermute | solution.py:414
  52.1 2.0 %collective-permute-start.4 = (f32[224,128]{1,0:T(8,128)S(1)}, f32[224,128]{1,0:T(8,128)S(1)}, u32[]{:S(2)}, u32[]{:S(2)}) collective-permute-start(f32[224,128]{1,0:T(8,128)S(1)} %get-tuple-element.29), channel_id=1, source_target_pairs={{0,1},{1,0},{2,3},{3,2},{4,5},{5,4},{6,7},{7,6},{8,9},{9,8},{10,11... | collective-permute-start | bytes 344072 | tf_op jit(solution)/shard_map/ppermute | solution.py:414
  52.2 3.4 %collective-permute-start.6 = (f32[224,128]{1,0:T(8,128)S(1)}, f32[224,128]{1,0:T(8,128)S(1)}, u32[]{:S(2)}, u32[]{:S(2)}) collective-permute-start(f32[224,128]{1,0:T(8,128)S(1)} %get-tuple-element.31), channel_id=1, source_target_pairs={{0,1},{1,0},{2,3},{3,2},{4,5},{5,4},{6,7},{7,6},{8,9},{9,8},{10,11... | collective-permute-start | bytes 344072 | tf_op jit(solution)/shard_map/ppermute | solution.py:414
  53.0 5.8 %collective-permute-start.3 = (s16[240,128]{1,0:T(8,128)(2,1)S(1)}, s16[240,128]{1,0:T(8,128)(2,1)S(1)}, u32[]{:S(2)}, u32[]{:S(2)}) collective-permute-start(s16[240,128]{1,0:T(8,128)(2,1)S(1)} %pad_add_fusion.5), channel_id=1, source_target_pairs={{0,6},{1,7},{2,4},{3,5},{4,2},{5,3},{6,0},{7,1},{8,14},{9,15},{10,... | collective-permute-start | bytes 184328 | tf_op jit(solution)/shard_map/ppermute | solution.py:414
  54.2 4.7 %collective-permute-start.5 = (s16[240,128]{1,0:T(8,128)(2,1)S(1)}, s16[240,128]{1,0:T(8,128)(2,1)S(1)}, u32[]{:S(2)}, u32[]{:S(2)}) collective-permute-start(s16[240,128]{1,0:T(8,128)(2,1)S(1)} %pad_add_fusion.4), channel_id=1, source_target_pairs={{0,2},{1,3},{2,0},{3,1},{4,6},{5,7},{6,4},{7,5},{8,10},{9,11},{10,... | collective-permute-start | bytes 184328 | tf_op jit(solution)/shard_map/ppermute | solution.py:414
  55.7 4.3 %collective-permute-start.7 = (s16[240,128]{1,0:T(8,128)(2,1)S(1)}, s16[240,128]{1,0:T(8,128)(2,1)S(1)}, u32[]{:S(2)}, u32[]{:S(2)}) collective-permute-start(s16[240,128]{1,0:T(8,128)(2,1)S(1)} %pad_add_fusion.3), channel_id=1, source_target_pairs={{0,4},{1,5},{2,6},{3,7},{4,0},{5,1},{6,2},{7,3},{8,12},{9,13},{10,... | collective-permute-start | bytes 184328 | tf_op jit(solution)/shard_map/ppermute | solution.py:414
  60.2 4.3 %collective-permute-start.8 = (s16[240,128]{1,0:T(8,128)(2,1)S(1)}, s16[240,128]{1,0:T(8,128)(2,1)S(1)}, u32[]{:S(2)}, u32[]{:S(2)}) collective-permute-start(s16[240,128]{1,0:T(8,128)(2,1)S(1)} %pad_add_fusion.2), channel_id=1, source_target_pairs={{0,8},{1,9},{2,10},{3,11},{4,12},{5,13},{6,14},{7,15},{8,0},{9,1},... | collective-permute-start | bytes 184328 | tf_op jit(solution)/shard_map/ppermute | solution.py:414
  64.7 6.3 %collective-permute-start.9 = (s16[240,128]{1,0:T(8,128)(2,1)S(1)}, s16[240,128]{1,0:T(8,128)(2,1)S(1)}, u32[]{:S(2)}, u32[]{:S(2)}) collective-permute-start(s16[240,128]{1,0:T(8,128)(2,1)S(1)} %pad_add_fusion.1), channel_id=1, source_target_pairs={{0,16},{1,17},{2,18},{3,19},{4,20},{5,21},{6,22},{7,23},{8,24},{9,... | collective-permute-start | bytes 184328 | tf_op jit(solution)/shard_map/ppermute | solution.py:414
  71.3 4.3 %collective-permute-start.14 = (s16[240,128]{1,0:T(8,128)(2,1)S(1)}, s16[240,128]{1,0:T(8,128)(2,1)S(1)}, u32[]{:S(2)}, u32[]{:S(2)}) collective-permute-start(s16[240,128]{1,0:T(8,128)(2,1)S(1)} %pad_add_fusion), channel_id=1, source_target_pairs={{0,4},{1,5},{2,6},{3,7},{4,0},{5,1},{6,2},{7,3},{8,12},{9,13},{10,... | collective-permute-start | bytes 184328 | tf_op jit(solution)/shard_map/ppermute | solution.py:414
  72.5 6.1 %collective-permute-start.16 = (s16[240,128]{1,0:T(8,128)(2,1)S(1)}, s16[240,128]{1,0:T(8,128)(2,1)S(1)}, u32[]{:S(2)}, u32[]{:S(2)}) collective-permute-start(s16[240,128]{1,0:T(8,128)(2,1)S(1)} %pad_add_fusion), channel_id=1, source_target_pairs={{0,1},{1,0},{2,3},{3,2},{4,5},{5,4},{6,7},{7,6},{8,9},{9,8},{10,11... | collective-permute-start | bytes 184328 | tf_op jit(solution)/shard_map/ppermute | solution.py:414
  72.5 4.8 %collective-permute-start.12 = (s16[240,128]{1,0:T(8,128)(2,1)S(1)}, s16[240,128]{1,0:T(8,128)(2,1)S(1)}, u32[]{:S(2)}, u32[]{:S(2)}) collective-permute-start(s16[240,128]{1,0:T(8,128)(2,1)S(1)} %pad_add_fusion), channel_id=1, source_target_pairs={{0,2},{1,3},{2,0},{3,1},{4,6},{5,7},{6,4},{7,5},{8,10},{9,11},{10,... | collective-permute-start | bytes 184328 | tf_op jit(solution)/shard_map/ppermute | solution.py:414
  72.5 6.1 %collective-permute-start.10 = (s16[240,128]{1,0:T(8,128)(2,1)S(1)}, s16[240,128]{1,0:T(8,128)(2,1)S(1)}, u32[]{:S(2)}, u32[]{:S(2)}) collective-permute-start(s16[240,128]{1,0:T(8,128)(2,1)S(1)} %pad_add_fusion), channel_id=1, source_target_pairs={{0,6},{1,7},{2,4},{3,5},{4,2},{5,3},{6,0},{7,1},{8,14},{9,15},{10,... | collective-permute-start | bytes 184328 | tf_op jit(solution)/shard_map/ppermute | solution.py:414
  75.6 3.1 %collective-permute-start.15 = (s16[240,128]{1,0:T(8,128)(2,1)S(1)}, s16[240,128]{1,0:T(8,128)(2,1)S(1)}, u32[]{:S(2)}, u32[]{:S(2)}) collective-permute-start(s16[240,128]{1,0:T(8,128)(2,1)S(1)} %collective-permute-done.14), channel_id=1, source_target_pairs={{0,1},{1,0},{2,3},{3,2},{4,5},{5,4},{6,7},{7,6},{8,9},{9,8},{10,11... | collective-permute-start | bytes 184328 | tf_op jit(solution)/shard_map/ppermute | solution.py:414
  77.3 1.4 %collective-permute-start.13 = (s16[240,128]{1,0:T(8,128)(2,1)S(1)}, s16[240,128]{1,0:T(8,128)(2,1)S(1)}, u32[]{:S(2)}, u32[]{:S(2)}) collective-permute-start(s16[240,128]{1,0:T(8,128)(2,1)S(1)} %collective-permute-done.12), channel_id=1, source_target_pairs={{0,1},{1,0},{2,3},{3,2},{4,5},{5,4},{6,7},{7,6},{8,9},{9,8},{10,11... | collective-permute-start | bytes 184328 | tf_op jit(solution)/shard_map/ppermute | solution.py:414
  78.5 1.3 %collective-permute-start.11 = (s16[240,128]{1,0:T(8,128)(2,1)S(1)}, s16[240,128]{1,0:T(8,128)(2,1)S(1)}, u32[]{:S(2)}, u32[]{:S(2)}) collective-permute-start(s16[240,128]{1,0:T(8,128)(2,1)S(1)} %collective-permute-done.10), channel_id=1, source_target_pairs={{0,1},{1,0},{2,3},{3,2},{4,5},{5,4},{6,7},{7,6},{8,9},{9,8},{10,11... | collective-permute-start | bytes 184328 | tf_op jit(solution)/shard_map/ppermute | solution.py:414

commit v15 on v14

--- a/solution.py
+++ b/solution.py
@@ -190,8 +190,7 @@
 
     def multiply(batch, place, into_ref):
         tile = batch * BATCH + place
-        product = dot(blocks_ref[where_ref[tile]], weights_held[tile])
-        into_ref[place] = product.astype(jnp.bfloat16).astype(jnp.float32)
+        into_ref[place] = dot(blocks_ref[where_ref[tile]], weights_held[tile])
 
     def add(batch, part, from_ref):
         lanes = slice(part // 2 * LANES, (part // 2 + 1) * LANES)

time: 86.7 us -> 86.5 us (level)
  no operation moved by 1% of the time
where the time goes in v15:
time: 86.5 us; the launch traced here: 86.1 us
  Pallas kernels  26.5 us (31%)
  waiting for transfers between devices  23.1 us (27%)
  starting transfers between devices  20.4 us (24%)
  blocking collectives  10.5 us (12%)
  local copies, waits for them, and re-layouts  2.9 us (3%)
  between operations  1.62 us (2%)
  other arithmetic  1.07 us (1%)
    ppermute x17, starting transfers between devices, swap(): return lax.ppermute(value, 'users', [(i, i ^ mask) for i in range(devices)])  16.7 us
    ppermute x17, waiting for transfers between devices, swap(): return lax.ppermute(value, 'users', [(i, i ^ mask) for i in range(devices)])  14.3 us
    pallas_call x1, Pallas kernels, tile_sums(): pl.pallas_call(tiles_kernel, out_shape=out_shape, in_specs=[SMEM] * 3 + [...  12.4 us
    all_to_all x1, blocking collectives, body(): lax.all_to_all(requests, 'users', 0, 0, axis_index_groups=sides, tiled=True)  10.5 us
    all_to_all x1, waiting for transfers between devices, body(): lax.all_to_all(found, 'users', 0, 0, axis_index_groups=sides, tiled=True)  8.82 us
    pallas_call x1, Pallas kernels, finish(): pl.pallas_call(functools.partial(finish_kernel, users * devices), out_sha...  6.43 us
    pallas_call x1, Pallas kernels, context_values(): pl.pallas_call(context_kernel, out_shape=jax.ShapeDtypeStruct((tiles, ROW...  3.72 us
    all_to_all x1, starting transfers between devices, body(): lax.all_to_all(found, 'users', 0, 0, axis_index_groups=sides, tiled=True)  3.65 us
  transfers between devices with their start and end apart: 18, of which 10 were waited for; matrix products, arithmetic and copies ran while one was open for 2% of the time, Pallas kernels for 7%

profile of v15, /device:TPU:0, one launch (start us, length us, event | category | flops | bytes accessed | tf_op | source)
XLA Modules:
  0.0 86.1 jit_solution(388407984205377330)
XLA Ops:
  0.6 4.1 %collective-permute-start = (bf16[16,64,128]{2,1,0:T(8,128)(2,1)}, bf16[16,64,128]{2,1,0:T(8,128)(2,1)S(1)}, u32[]{:S(2)}, u32[]{:S(2)}) collective-permute-start(bf16[16,64,128]{2,1,0:T(8,128)(2,1)} %own_ref.1), channel_id=1, source_target_pairs={{0,16},{1,17},{2,18},{3,19},{4,20},{5,21},{6,22},{7,23},{8,24},{9,... | collective-permute-start | bytes 786440 | tf_op jit(solution)/shard_map/ppermute | solution.py:413
  4.7 2.2 %route.1 = (s32[16,1,128]{2,1,0:T(1,128)S(1)}, s32[64]{0:T(128)S(1)}, bf16[16,64,128]{2,1,0:T(8,128)(2,1)S(1)}) custom-call(s32[1]{0:T(128)} %bitcast.me_ref, s32[64]{0:T(128)} %bitcast.136, s32[64]{0:T(128)} %slot_ref.1, bf16[16,64,128]{2,1,0:T(8,128)(2,1)} %own_ref.1), custom_call_target="tpu_custom_call" | custom-call | tf_op jit(solution)/shard_map/route/pallas_call | solution.py:85
  7.0 10.5 %all_to_all.10.asked_ref = s32[16,1,128]{2,1,0:T(1,128)S(1)} all-to-all(s32[16,1,128]{2,1,0:T(1,128)S(1)} %get-tuple-element.18), channel_id=1, replica_groups={{0,1,2,3,4,5,6,7,8,9,10,11,12,13,14,15},{16,17,18,19,20,21,22,23,24,25,..., dimensions={0} | all-to-all | bytes 16384 | tf_op jit(solution)/shard_map/all_to_all | solution.py:471
  17.4 1.7 %collect.1 = bf16[64,64,128]{2,1,0:T(8,128)(2,1)} custom-call(s32[16,1,128]{2,1,0:T(1,128)S(1)} %all_to_all.10.asked_ref, bf16[16,64,128]{2,1,0:T(8,128)(2,1)S(1)} %get-tuple-element.19.own_ref, bf16[16,64,128]{2,1,0:T(8,128)(2,1)S(1)} %collective-permute-done.mirror_ref), custom_call_target="tpu_custom_call" | custom-call | tf_op jit(solution)/shard_map/collect/pallas_call | solution.py:108
  19.1 3.7 %all-to-all-start.1 = ((bf16[64,64,128]{2,1,0:T(8,128)(2,1)}), bf16[64,64,128]{2,1,0:T(8,128)(2,1)S(1)}, u32[]{:S(2)}, u32[]{:S(2)}) async-start(bf16[64,64,128]{2,1,0:T(8,128)(2,1)} %collect.1), calls=%async_computation.1 | async-start | bytes 2097152 | tf_op jit(solution)/shard_map/all_to_all | solution.py:474
  23.5 0.9 %reshape.232 = f32[8,64,8]{2,1,0:T(8,128)S(1)} reshape(bf16[8,512]{1,0:T(8,128)(2,1)} %param.15) | data formatting | bytes 24576 | tf_op jit(solution)/shard_map/transpose | solution.py:476
  24.3 0.2 copy.13
  24.5 0.9 %copy-done.1 = s32[64,512]{1,0:T(8,128)S(1)} copy-done((s32[64,512]{1,0:T(8,128)S(1)}, s32[64,512]{1,0:T(8,128)}, u32[]{:S(2)}) %copy-start.1) | copy-done | bytes 131096
  25.4 3.7 %contexts.1.context_ref = f32[64,8,512]{2,1,0:T(8,128)S(1)} custom-call(s32[64]{0:T(128)} %cblock_ref, f32[64,8,8]{2,1,0:T(8,128)S(1)} %bitcast.129, s32[64,512]{1,0:T(8,128)S(1)} %copy-done.1), custom_call_target="tpu_custom_call" | custom-call | flops 10000000 | bytes 20000000 | tf_op jit(solution)/shard_map/contexts/pallas_call | solution.py:136
  29.1 1.0 %copy-done = f32[64,8,512]{2,1,0:T(8,128)} copy-done((f32[64,8,512]{2,1,0:T(8,128)}, f32[64,8,512]{2,1,0:T(8,128)S(1)}, u32[]{:S(2)}) %copy-start) | copy-done | bytes 1048600
  30.1 8.8 %all-to-all-done.1.blocks_ref = bf16[64,64,128]{2,1,0:T(8,128)(2,1)S(1)} async-done(((bf16[64,64,128]{2,1,0:T(8,128)(2,1)}), bf16[64,64,128]{2,1,0:T(8,128)(2,1)S(1)}, u32[]{:S(2)}, u32[]{:S(2)}) %all-to-all-start.1) | async-done | bytes 1048608 | tf_op jit(solution)/shard_map/all_to_all | solution.py:474
  38.9 12.4 %tile_sums.1 = (f32[224,128]{1,0:T(8,128)S(1)}, f32[224,128]{1,0:T(8,128)S(1)}, f32[224,128]{1,0:T(8,128)S(1)}, f32[224,128]{1,0:T(8,128)S(1)}, f32[224,128]{1,0...) custom-call(s32[64]{0:T(128)S(1)} %get-tuple-element.17.where_ref, ...), custom_call_target="tpu_custom_call" | custom-call | flops 2000000000 | bytes 12000000 | tf_op jit(solution)/shard_map/tile_sums/pallas_call | solution.py:279
  51.4 0.5 collective-permute-start.1
  52.0 0.4 collective-permute-start.6
  52.4 0.3 collective-permute-done.2
  52.9 1.0 %collective-permute-start.3 = (s16[240,128]{1,0:T(8,128)(2,1)S(1)}, s16[240,128]{1,0:T(8,128)(2,1)S(1)}, u32[]{:S(2)}, u32[]{:S(2)}) collective-permute-start(s16[240,128]{1,0:T(8,128)(2,1)S(1)} %pad_add_fusion.5), channel_id=1, source_target_pairs={{0,6},{1,7},{2,4},{3,5},{4,2},{5,3},{6,0},{7,1},{8,14},{9,15},{10,... | collective-permute-start | bytes 184328 | tf_op jit(solution)/shard_map/ppermute | solution.py:413
  54.0 1.4 %collective-permute-start.5 = (s16[240,128]{1,0:T(8,128)(2,1)S(1)}, s16[240,128]{1,0:T(8,128)(2,1)S(1)}, u32[]{:S(2)}, u32[]{:S(2)}) collective-permute-start(s16[240,128]{1,0:T(8,128)(2,1)S(1)} %pad_add_fusion.4), channel_id=1, source_target_pairs={{0,2},{1,3},{2,0},{3,1},{4,6},{5,7},{6,4},{7,5},{8,10},{9,11},{10,... | collective-permute-start | bytes 184328 | tf_op jit(solution)/shard_map/ppermute | solution.py:413
  55.5 1.3 %collective-permute-start.7 = (s16[240,128]{1,0:T(8,128)(2,1)S(1)}, s16[240,128]{1,0:T(8,128)(2,1)S(1)}, u32[]{:S(2)}, u32[]{:S(2)}) collective-permute-start(s16[240,128]{1,0:T(8,128)(2,1)S(1)} %pad_add_fusion.3), channel_id=1, source_target_pairs={{0,4},{1,5},{2,6},{3,7},{4,0},{5,1},{6,2},{7,3},{8,12},{9,13},{10,... | collective-permute-start | bytes 184328 | tf_op jit(solution)/shard_map/ppermute | solution.py:413
  56.8 1.9 %collective-permute-done.3 = s16[240,128]{1,0:T(8,128)(2,1)S(1)} collective-permute-done((s16[240,128]{1,0:T(8,128)(2,1)S(1)}, s16[240,128]{1,0:T(8,128)(2,1)S(1)}, u32[]{:S(2)}, u32[]{:S(2)}) %collective-permute-start.3) | collective-permute-done | bytes 61472 | tf_op jit(solution)/shard_map/ppermute | solution.py:413
  58.7 1.1 %collective-permute-done.7 = s16[240,128]{1,0:T(8,128)(2,1)S(1)} collective-permute-done((s16[240,128]{1,0:T(8,128)(2,1)S(1)}, s16[240,128]{1,0:T(8,128)(2,1)S(1)}, u32[]{:S(2)}, u32[]{:S(2)}) %collective-permute-start.7) | collective-permute-done | bytes 61472 | tf_op jit(solution)/shard_map/ppermute | solution.py:413
  59.8 0.1 fusion.35
  60.0 0.6 collective-permute-start.8
  60.6 3.6 %collective-permute-done.8 = s16[240,128]{1,0:T(8,128)(2,1)S(1)} collective-permute-done((s16[240,128]{1,0:T(8,128)(2,1)S(1)}, s16[240,128]{1,0:T(8,128)(2,1)S(1)}, u32[]{:S(2)}, u32[]{:S(2)}) %collective-permute-start.8) | collective-permute-done | bytes 61472 | tf_op jit(solution)/shard_map/ppermute | solution.py:413
  64.5 3.7 %collective-permute-start.9 = (s16[240,128]{1,0:T(8,128)(2,1)S(1)}, s16[240,128]{1,0:T(8,128)(2,1)S(1)}, u32[]{:S(2)}, u32[]{:S(2)}) collective-permute-start(s16[240,128]{1,0:T(8,128)(2,1)S(1)} %pad_add_fusion.1), channel_id=1, source_target_pairs={{0,16},{1,17},{2,18},{3,19},{4,20},{5,21},{6,22},{7,23},{8,24},{9,... | collective-permute-start | bytes 184328 | tf_op jit(solution)/shard_map/ppermute | solution.py:413
  68.2 2.7 %collective-permute-done.9 = s16[240,128]{1,0:T(8,128)(2,1)S(1)} collective-permute-done((s16[240,128]{1,0:T(8,128)(2,1)S(1)}, s16[240,128]{1,0:T(8,128)(2,1)S(1)}, u32[]{:S(2)}, u32[]{:S(2)}) %collective-permute-start.9) | collective-permute-done | bytes 61472 | tf_op jit(solution)/shard_map/ppermute | solution.py:413
  71.1 1.2 %collective-permute-start.14 = (s16[240,128]{1,0:T(8,128)(2,1)S(1)}, s16[240,128]{1,0:T(8,128)(2,1)S(1)}, u32[]{:S(2)}, u32[]{:S(2)}) collective-permute-start(s16[240,128]{1,0:T(8,128)(2,1)S(1)} %pad_add_fusion), channel_id=1, source_target_pairs={{0,4},{1,5},{2,6},{3,7},{4,0},{5,1},{6,2},{7,3},{8,12},{9,13},{10,... | collective-permute-start | bytes 184328 | tf_op jit(solution)/shard_map/ppermute | solution.py:413
  72.3 2.3 %collective-permute-start.10 = (s16[240,128]{1,0:T(8,128)(2,1)S(1)}, s16[240,128]{1,0:T(8,128)(2,1)S(1)}, u32[]{:S(2)}, u32[]{:S(2)}) collective-permute-start(s16[240,128]{1,0:T(8,128)(2,1)S(1)} %pad_add_fusion), channel_id=1, source_target_pairs={{0,6},{1,7},{2,4},{3,5},{4,2},{5,3},{6,0},{7,1},{8,14},{9,15},{10,... | collective-permute-start | bytes 184328 | tf_op jit(solution)/shard_map/ppermute | solution.py:413
  74.6 0.7 collective-permute-done.14
  75.4 1.7 %collective-permute-done.12 = s16[240,128]{1,0:T(8,128)(2,1)S(1)} collective-permute-done((s16[240,128]{1,0:T(8,128)(2,1)S(1)}, s16[240,128]{1,0:T(8,128)(2,1)S(1)}, u32[]{:S(2)}, u32[]{:S(2)}) %collective-permute-start.12) | collective-permute-done | bytes 61472 | tf_op jit(solution)/shard_map/ppermute | solution.py:413
  77.1 1.2 %collective-permute-done.10 = s16[240,128]{1,0:T(8,128)(2,1)S(1)} collective-permute-done((s16[240,128]{1,0:T(8,128)(2,1)S(1)}, s16[240,128]{1,0:T(8,128)(2,1)S(1)}, u32[]{:S(2)}, u32[]{:S(2)}) %collective-permute-start.10) | collective-permute-done | bytes 61472 | tf_op jit(solution)/shard_map/ppermute | solution.py:413
  78.6 1.0 %collective-permute-done.11 = s16[240,128]{1,0:T(8,128)(2,1)S(1)} collective-permute-done((s16[240,128]{1,0:T(8,128)(2,1)S(1)}, s16[240,128]{1,0:T(8,128)(2,1)S(1)}, u32[]{:S(2)}, u32[]{:S(2)}) %collective-permute-start.11) | collective-permute-done | bytes 61472 | tf_op jit(solution)/shard_map/ppermute | solution.py:413
  79.6 6.4 %finish.1 = (f32[512,128]{1,0:T(8,128)}, f32[128,512]{1,0:T(8,128)}) custom-call(s32[1]{0:T(128)} %bitcast.me_ref, bf16[1024,512]{1,0:T(8,128)(2,1)S(1)} %get-tuple-element.23.stack_ref, f32[224,128]{1,0:T(8,128)S(1)} %bitcast_multiply_fusion.7.rest_0_, f32[224,128]{1,0:T(8,128)S(1)} %bitcast_multiply_fusion.6.rest_1_, ...), custom_call_target="tpu_custom_call" | custom-call | tf_op jit(solution)/shard_map/finish/pallas_call | solution.py:393
  (65 shorter events, 1.2 us)
Async XLA Ops:
  0.6 16.8 %collective-permute-start = (bf16[16,64,128]{2,1,0:T(8,128)(2,1)}, bf16[16,64,128]{2,1,0:T(8,128)(2,1)S(1)}, u32[]{:S(2)}, u32[]{:S(2)}) collective-permute-start(bf16[16,64,128]{2,1,0:T(8,128)(2,1)} %own_ref.1), channel_id=1, source_target_pairs={{0,16},{1,17},{2,18},{3,19},{4,20},{5,21},{6,22},{7,23},{8,24},{9,... | collective-permute-start | bytes 786440 | tf_op jit(solution)/shard_map/ppermute | solution.py:413
  19.1 19.8 %all-to-all-start.1 = ((bf16[64,64,128]{2,1,0:T(8,128)(2,1)}), bf16[64,64,128]{2,1,0:T(8,128)(2,1)S(1)}, u32[]{:S(2)}, u32[]{:S(2)}) async-start(bf16[64,64,128]{2,1,0:T(8,128)(2,1)} %collect.1), calls=%async_computation.1 | async-start | bytes 2097152 | tf_op jit(solution)/shard_map/all_to_all | solution.py:474
  24.5 0.9 %copy-start.1 = (s32[64,512]{1,0:T(8,128)S(1)}, s32[64,512]{1,0:T(8,128)}, u32[]{:S(2)}) copy-start(s32[64,512]{1,0:T(8,128)} %marks_ref.1) | copy-start | bytes 393220
  29.1 1.0 %copy-start = (f32[64,8,512]{2,1,0:T(8,128)}, f32[64,8,512]{2,1,0:T(8,128)S(1)}, u32[]{:S(2)}) copy-start(f32[64,8,512]{2,1,0:T(8,128)S(1)} %contexts.1.context_ref) | copy-start | bytes 3145732
  51.3 1.4 %collective-permute-start.2 = (f32[224,128]{1,0:T(8,128)S(1)}, f32[224,128]{1,0:T(8,128)S(1)}, u32[]{:S(2)}, u32[]{:S(2)}) collective-permute-start(f32[224,128]{1,0:T(8,128)S(1)} %get-tuple-element.27), channel_id=1, source_target_pairs={{0,1},{1,0},{2,3},{3,2},{4,5},{5,4},{6,7},{7,6},{8,9},{9,8},{10,11... | collective-permute-start | bytes 344072 | tf_op jit(solution)/shard_map/ppermute | solution.py:413
  51.4 8.4 %collective-permute-start.1 = (f32[224,128]{1,0:T(8,128)S(1)}, f32[224,128]{1,0:T(8,128)S(1)}, u32[]{:S(2)}, u32[]{:S(2)}) collective-permute-start(f32[224,128]{1,0:T(8,128)S(1)} %get-tuple-element.25), channel_id=1, source_target_pairs={{0,1},{1,0},{2,3},{3,2},{4,5},{5,4},{6,7},{7,6},{8,9},{9,8},{10,11... | collective-permute-start | bytes 344072 | tf_op jit(solution)/shard_map/ppermute | solution.py:413
  51.9 1.9 %collective-permute-start.4 = (f32[224,128]{1,0:T(8,128)S(1)}, f32[224,128]{1,0:T(8,128)S(1)}, u32[]{:S(2)}, u32[]{:S(2)}) collective-permute-start(f32[224,128]{1,0:T(8,128)S(1)} %get-tuple-element.29), channel_id=1, source_target_pairs={{0,1},{1,0},{2,3},{3,2},{4,5},{5,4},{6,7},{7,6},{8,9},{9,8},{10,11... | collective-permute-start | bytes 344072 | tf_op jit(solution)/shard_map/ppermute | solution.py:413
  52.0 3.4 %collective-permute-start.6 = (f32[224,128]{1,0:T(8,128)S(1)}, f32[224,128]{1,0:T(8,128)S(1)}, u32[]{:S(2)}, u32[]{:S(2)}) collective-permute-start(f32[224,128]{1,0:T(8,128)S(1)} %get-tuple-element.31), channel_id=1, source_target_pairs={{0,1},{1,0},{2,3},{3,2},{4,5},{5,4},{6,7},{7,6},{8,9},{9,8},{10,11... | collective-permute-start | bytes 344072 | tf_op jit(solution)/shard_map/ppermute | solution.py:413
  52.9 5.8 %collective-permute-start.3 = (s16[240,128]{1,0:T(8,128)(2,1)S(1)}, s16[240,128]{1,0:T(8,128)(2,1)S(1)}, u32[]{:S(2)}, u32[]{:S(2)}) collective-permute-start(s16[240,128]{1,0:T(8,128)(2,1)S(1)} %pad_add_fusion.5), channel_id=1, source_target_pairs={{0,6},{1,7},{2,4},{3,5},{4,2},{5,3},{6,0},{7,1},{8,14},{9,15},{10,... | collective-permute-start | bytes 184328 | tf_op jit(solution)/shard_map/ppermute | solution.py:413
  54.0 4.7 %collective-permute-start.5 = (s16[240,128]{1,0:T(8,128)(2,1)S(1)}, s16[240,128]{1,0:T(8,128)(2,1)S(1)}, u32[]{:S(2)}, u32[]{:S(2)}) collective-permute-start(s16[240,128]{1,0:T(8,128)(2,1)S(1)} %pad_add_fusion.4), channel_id=1, source_target_pairs={{0,2},{1,3},{2,0},{3,1},{4,6},{5,7},{6,4},{7,5},{8,10},{9,11},{10,... | collective-permute-start | bytes 184328 | tf_op jit(solution)/shard_map/ppermute | solution.py:413
  55.5 4.3 %collective-permute-start.7 = (s16[240,128]{1,0:T(8,128)(2,1)S(1)}, s16[240,128]{1,0:T(8,128)(2,1)S(1)}, u32[]{:S(2)}, u32[]{:S(2)}) collective-permute-start(s16[240,128]{1,0:T(8,128)(2,1)S(1)} %pad_add_fusion.3), channel_id=1, source_target_pairs={{0,4},{1,5},{2,6},{3,7},{4,0},{5,1},{6,2},{7,3},{8,12},{9,13},{10,... | collective-permute-start | bytes 184328 | tf_op jit(solution)/shard_map/ppermute | solution.py:413
  60.0 4.3 %collective-permute-start.8 = (s16[240,128]{1,0:T(8,128)(2,1)S(1)}, s16[240,128]{1,0:T(8,128)(2,1)S(1)}, u32[]{:S(2)}, u32[]{:S(2)}) collective-permute-start(s16[240,128]{1,0:T(8,128)(2,1)S(1)} %pad_add_fusion.2), channel_id=1, source_target_pairs={{0,8},{1,9},{2,10},{3,11},{4,12},{5,13},{6,14},{7,15},{8,0},{9,1},... | collective-permute-start | bytes 184328 | tf_op jit(solution)/shard_map/ppermute | solution.py:413
  64.5 6.4 %collective-permute-start.9 = (s16[240,128]{1,0:T(8,128)(2,1)S(1)}, s16[240,128]{1,0:T(8,128)(2,1)S(1)}, u32[]{:S(2)}, u32[]{:S(2)}) collective-permute-start(s16[240,128]{1,0:T(8,128)(2,1)S(1)} %pad_add_fusion.1), channel_id=1, source_target_pairs={{0,16},{1,17},{2,18},{3,19},{4,20},{5,21},{6,22},{7,23},{8,24},{9,... | collective-permute-start | bytes 184328 | tf_op jit(solution)/shard_map/ppermute | solution.py:413
  71.1 4.3 %collective-permute-start.14 = (s16[240,128]{1,0:T(8,128)(2,1)S(1)}, s16[240,128]{1,0:T(8,128)(2,1)S(1)}, u32[]{:S(2)}, u32[]{:S(2)}) collective-permute-start(s16[240,128]{1,0:T(8,128)(2,1)S(1)} %pad_add_fusion), channel_id=1, source_target_pairs={{0,4},{1,5},{2,6},{3,7},{4,0},{5,1},{6,2},{7,3},{8,12},{9,13},{10,... | collective-permute-start | bytes 184328 | tf_op jit(solution)/shard_map/ppermute | solution.py:413
  72.3 6.1 %collective-permute-start.16 = (s16[240,128]{1,0:T(8,128)(2,1)S(1)}, s16[240,128]{1,0:T(8,128)(2,1)S(1)}, u32[]{:S(2)}, u32[]{:S(2)}) collective-permute-start(s16[240,128]{1,0:T(8,128)(2,1)S(1)} %pad_add_fusion), channel_id=1, source_target_pairs={{0,1},{1,0},{2,3},{3,2},{4,5},{5,4},{6,7},{7,6},{8,9},{9,8},{10,11... | collective-permute-start | bytes 184328 | tf_op jit(solution)/shard_map/ppermute | solution.py:413
  72.3 4.8 %collective-permute-start.12 = (s16[240,128]{1,0:T(8,128)(2,1)S(1)}, s16[240,128]{1,0:T(8,128)(2,1)S(1)}, u32[]{:S(2)}, u32[]{:S(2)}) collective-permute-start(s16[240,128]{1,0:T(8,128)(2,1)S(1)} %pad_add_fusion), channel_id=1, source_target_pairs={{0,2},{1,3},{2,0},{3,1},{4,6},{5,7},{6,4},{7,5},{8,10},{9,11},{10,... | collective-permute-start | bytes 184328 | tf_op jit(solution)/shard_map/ppermute | solution.py:413
  72.3 6.1 %collective-permute-start.10 = (s16[240,128]{1,0:T(8,128)(2,1)S(1)}, s16[240,128]{1,0:T(8,128)(2,1)S(1)}, u32[]{:S(2)}, u32[]{:S(2)}) collective-permute-start(s16[240,128]{1,0:T(8,128)(2,1)S(1)} %pad_add_fusion), channel_id=1, source_target_pairs={{0,6},{1,7},{2,4},{3,5},{4,2},{5,3},{6,0},{7,1},{8,14},{9,15},{10,... | collective-permute-start | bytes 184328 | tf_op jit(solution)/shard_map/ppermute | solution.py:413
  75.4 3.1 %collective-permute-start.15 = (s16[240,128]{1,0:T(8,128)(2,1)S(1)}, s16[240,128]{1,0:T(8,128)(2,1)S(1)}, u32[]{:S(2)}, u32[]{:S(2)}) collective-permute-start(s16[240,128]{1,0:T(8,128)(2,1)S(1)} %collective-permute-done.14), channel_id=1, source_target_pairs={{0,1},{1,0},{2,3},{3,2},{4,5},{5,4},{6,7},{7,6},{8,9},{9,8},{10,11... | collective-permute-start | bytes 184328 | tf_op jit(solution)/shard_map/ppermute | solution.py:413
  77.1 1.4 %collective-permute-start.13 = (s16[240,128]{1,0:T(8,128)(2,1)S(1)}, s16[240,128]{1,0:T(8,128)(2,1)S(1)}, u32[]{:S(2)}, u32[]{:S(2)}) collective-permute-start(s16[240,128]{1,0:T(8,128)(2,1)S(1)} %collective-permute-done.12), channel_id=1, source_target_pairs={{0,1},{1,0},{2,3},{3,2},{4,5},{5,4},{6,7},{7,6},{8,9},{9,8},{10,11... | collective-permute-start | bytes 184328 | tf_op jit(solution)/shard_map/ppermute | solution.py:413
  78.3 1.3 %collective-permute-start.11 = (s16[240,128]{1,0:T(8,128)(2,1)S(1)}, s16[240,128]{1,0:T(8,128)(2,1)S(1)}, u32[]{:S(2)}, u32[]{:S(2)}) collective-permute-start(s16[240,128]{1,0:T(8,128)(2,1)S(1)} %collective-permute-done.10), channel_id=1, source_target_pairs={{0,1},{1,0},{2,3},{3,2},{4,5},{5,4},{6,7},{7,6},{8,9},{9,8},{10,11... | collective-permute-start | bytes 184328 | tf_op jit(solution)/shard_map/ppermute | solution.py:413

commit v16 on v14

--- a/solution.py
+++ b/solution.py
@@ -223,11 +223,10 @@
         def _():
             start(batch + 3)
 
-        for part in range(max(parts, BATCH)):
-            if part < BATCH:
-                multiply(batch + 1, part, into_ref)
-            if part < parts:
-                add(batch, part, from_ref)
+        for place in range(BATCH):
+            multiply(batch + 1, place, into_ref)
+        for part in range(parts):
+            add(batch, part, from_ref)
 
     def pair(index, _):
         turn(2 * index, even_ref, odd_ref)

time: 86.7 us -> 86.7 us (level)
  no operation moved by 1% of the time
where the time goes in v16:
time: 86.7 us; the launch traced here: 86.3 us
  Pallas kernels  26.7 us (31%)
  waiting for transfers between devices  23.2 us (27%)
  starting transfers between devices  20.4 us (24%)
  blocking collectives  10.5 us (12%)
  local copies, waits for them, and re-layouts  2.9 us (3%)
  between operations  1.62 us (2%)
  other arithmetic  1.07 us (1%)
    ppermute x17, starting transfers between devices, swap(): return lax.ppermute(value, 'users', [(i, i ^ mask) for i in range(devices)])  16.7 us
    ppermute x17, waiting for transfers between devices, swap(): return lax.ppermute(value, 'users', [(i, i ^ mask) for i in range(devices)])  14.3 us
    pallas_call x1, Pallas kernels, tile_sums(): pl.pallas_call(tiles_kernel, out_shape=out_shape, in_specs=[SMEM] * 3 + [...  12.6 us
    all_to_all x1, blocking collectives, body(): lax.all_to_all(requests, 'users', 0, 0, axis_index_groups=sides, tiled=True)  10.5 us
    all_to_all x1, waiting for transfers between devices, body(): lax.all_to_all(found, 'users', 0, 0, axis_index_groups=sides, tiled=True)  8.82 us
    pallas_call x1, Pallas kernels, finish(): pl.pallas_call(functools.partial(finish_kernel, users * devices), out_sha...  6.43 us
    pallas_call x1, Pallas kernels, context_values(): pl.pallas_call(context_kernel, out_shape=jax.ShapeDtypeStruct((tiles, ROW...  3.72 us
    all_to_all x1, starting transfers between devices, body(): lax.all_to_all(found, 'users', 0, 0, axis_index_groups=sides, tiled=True)  3.65 us
  transfers between devices with their start and end apart: 18, of which 10 were waited for; matrix products, arithmetic and copies ran while one was open for 2% of the time, Pallas kernels for 7%

profile of v16, /device:TPU:0, one launch (start us, length us, event | category | flops | bytes accessed | tf_op | source)
XLA Modules:
  0.0 86.3 jit_solution(13435038407304559494)
XLA Ops:
  0.6 4.1 %collective-permute-start = (bf16[16,64,128]{2,1,0:T(8,128)(2,1)}, bf16[16,64,128]{2,1,0:T(8,128)(2,1)S(1)}, u32[]{:S(2)}, u32[]{:S(2)}) collective-permute-start(bf16[16,64,128]{2,1,0:T(8,128)(2,1)} %own_ref.1), channel_id=1, source_target_pairs={{0,16},{1,17},{2,18},{3,19},{4,20},{5,21},{6,22},{7,23},{8,24},{9,... | collective-permute-start | bytes 786440 | tf_op jit(solution)/shard_map/ppermute | solution.py:413
  4.7 2.2 %route.1 = (s32[16,1,128]{2,1,0:T(1,128)S(1)}, s32[64]{0:T(128)S(1)}, bf16[16,64,128]{2,1,0:T(8,128)(2,1)S(1)}) custom-call(s32[1]{0:T(128)} %bitcast.me_ref, s32[64]{0:T(128)} %bitcast.136, s32[64]{0:T(128)} %slot_ref.1, bf16[16,64,128]{2,1,0:T(8,128)(2,1)} %own_ref.1), custom_call_target="tpu_custom_call" | custom-call | tf_op jit(solution)/shard_map/route/pallas_call | solution.py:85
  7.0 10.5 %all_to_all.10.asked_ref = s32[16,1,128]{2,1,0:T(1,128)S(1)} all-to-all(s32[16,1,128]{2,1,0:T(1,128)S(1)} %get-tuple-element.18), channel_id=1, replica_groups={{0,1,2,3,4,5,6,7,8,9,10,11,12,13,14,15},{16,17,18,19,20,21,22,23,24,25,..., dimensions={0} | all-to-all | bytes 16384 | tf_op jit(solution)/shard_map/all_to_all | solution.py:471
  17.4 1.7 %collect.1 = bf16[64,64,128]{2,1,0:T(8,128)(2,1)} custom-call(s32[16,1,128]{2,1,0:T(1,128)S(1)} %all_to_all.10.asked_ref, bf16[16,64,128]{2,1,0:T(8,128)(2,1)S(1)} %get-tuple-element.19.own_ref, bf16[16,64,128]{2,1,0:T(8,128)(2,1)S(1)} %collective-permute-done.mirror_ref), custom_call_target="tpu_custom_call" | custom-call | tf_op jit(solution)/shard_map/collect/pallas_call | solution.py:108
  19.1 3.7 %all-to-all-start.1 = ((bf16[64,64,128]{2,1,0:T(8,128)(2,1)}), bf16[64,64,128]{2,1,0:T(8,128)(2,1)S(1)}, u32[]{:S(2)}, u32[]{:S(2)}) async-start(bf16[64,64,128]{2,1,0:T(8,128)(2,1)} %collect.1), calls=%async_computation.1 | async-start | bytes 2097152 | tf_op jit(solution)/shard_map/all_to_all | solution.py:474
  23.5 0.9 %reshape.232 = f32[8,64,8]{2,1,0:T(8,128)S(1)} reshape(bf16[8,512]{1,0:T(8,128)(2,1)} %param.15) | data formatting | bytes 24576 | tf_op jit(solution)/shard_map/transpose | solution.py:476
  24.3 0.2 copy.13
  24.5 0.9 %copy-done.1 = s32[64,512]{1,0:T(8,128)S(1)} copy-done((s32[64,512]{1,0:T(8,128)S(1)}, s32[64,512]{1,0:T(8,128)}, u32[]{:S(2)}) %copy-start.1) | copy-done | bytes 131096
  25.4 3.7 %contexts.1.context_ref = f32[64,8,512]{2,1,0:T(8,128)S(1)} custom-call(s32[64]{0:T(128)} %cblock_ref, f32[64,8,8]{2,1,0:T(8,128)S(1)} %bitcast.129, s32[64,512]{1,0:T(8,128)S(1)} %copy-done.1), custom_call_target="tpu_custom_call" | custom-call | flops 10000000 | bytes 20000000 | tf_op jit(solution)/shard_map/contexts/pallas_call | solution.py:136
  29.1 1.0 %copy-done = f32[64,8,512]{2,1,0:T(8,128)} copy-done((f32[64,8,512]{2,1,0:T(8,128)}, f32[64,8,512]{2,1,0:T(8,128)S(1)}, u32[]{:S(2)}) %copy-start) | copy-done | bytes 1048600
  30.1 8.8 %all-to-all-done.1.blocks_ref = bf16[64,64,128]{2,1,0:T(8,128)(2,1)S(1)} async-done(((bf16[64,64,128]{2,1,0:T(8,128)(2,1)}), bf16[64,64,128]{2,1,0:T(8,128)(2,1)S(1)}, u32[]{:S(2)}, u32[]{:S(2)}) %all-to-all-start.1) | async-done | bytes 1048608 | tf_op jit(solution)/shard_map/all_to_all | solution.py:474
  38.9 12.6 %tile_sums.1 = (f32[224,128]{1,0:T(8,128)S(1)}, f32[224,128]{1,0:T(8,128)S(1)}, f32[224,128]{1,0:T(8,128)S(1)}, f32[224,128]{1,0:T(8,128)S(1)}, f32[224,128]{1,0...) custom-call(s32[64]{0:T(128)S(1)} %get-tuple-element.17.where_ref, ...), custom_call_target="tpu_custom_call" | custom-call | flops 2000000000 | bytes 12000000 | tf_op jit(solution)/shard_map/tile_sums/pallas_call | solution.py:279
  51.6 0.5 collective-permute-start.1
  52.2 0.4 collective-permute-start.6
  52.6 0.3 collective-permute-done.2
  53.0 1.0 %collective-permute-start.3 = (s16[240,128]{1,0:T(8,128)(2,1)S(1)}, s16[240,128]{1,0:T(8,128)(2,1)S(1)}, u32[]{:S(2)}, u32[]{:S(2)}) collective-permute-start(s16[240,128]{1,0:T(8,128)(2,1)S(1)} %pad_add_fusion.5), channel_id=1, source_target_pairs={{0,6},{1,7},{2,4},{3,5},{4,2},{5,3},{6,0},{7,1},{8,14},{9,15},{10,... | collective-permute-start | bytes 184328 | tf_op jit(solution)/shard_map/ppermute | solution.py:413
  54.2 1.4 %collective-permute-start.5 = (s16[240,128]{1,0:T(8,128)(2,1)S(1)}, s16[240,128]{1,0:T(8,128)(2,1)S(1)}, u32[]{:S(2)}, u32[]{:S(2)}) collective-permute-start(s16[240,128]{1,0:T(8,128)(2,1)S(1)} %pad_add_fusion.4), channel_id=1, source_target_pairs={{0,2},{1,3},{2,0},{3,1},{4,6},{5,7},{6,4},{7,5},{8,10},{9,11},{10,... | collective-permute-start | bytes 184328 | tf_op jit(solution)/shard_map/ppermute | solution.py:413
  55.7 1.2 %collective-permute-start.7 = (s16[240,128]{1,0:T(8,128)(2,1)S(1)}, s16[240,128]{1,0:T(8,128)(2,1)S(1)}, u32[]{:S(2)}, u32[]{:S(2)}) collective-permute-start(s16[240,128]{1,0:T(8,128)(2,1)S(1)} %pad_add_fusion.3), channel_id=1, source_target_pairs={{0,4},{1,5},{2,6},{3,7},{4,0},{5,1},{6,2},{7,3},{8,12},{9,13},{10,... | collective-permute-start | bytes 184328 | tf_op jit(solution)/shard_map/ppermute | solution.py:413
  57.0 1.9 %collective-permute-done.3 = s16[240,128]{1,0:T(8,128)(2,1)S(1)} collective-permute-done((s16[240,128]{1,0:T(8,128)(2,1)S(1)}, s16[240,128]{1,0:T(8,128)(2,1)S(1)}, u32[]{:S(2)}, u32[]{:S(2)}) %collective-permute-start.3) | collective-permute-done | bytes 61472 | tf_op jit(solution)/shard_map/ppermute | solution.py:413
  58.9 1.1 %collective-permute-done.7 = s16[240,128]{1,0:T(8,128)(2,1)S(1)} collective-permute-done((s16[240,128]{1,0:T(8,128)(2,1)S(1)}, s16[240,128]{1,0:T(8,128)(2,1)S(1)}, u32[]{:S(2)}, u32[]{:S(2)}) %collective-permute-start.7) | collective-permute-done | bytes 61472 | tf_op jit(solution)/shard_map/ppermute | solution.py:413
  60.0 0.1 fusion.35
  60.2 0.6 collective-permute-start.8
  60.8 3.7 %collective-permute-done.8 = s16[240,128]{1,0:T(8,128)(2,1)S(1)} collective-permute-done((s16[240,128]{1,0:T(8,128)(2,1)S(1)}, s16[240,128]{1,0:T(8,128)(2,1)S(1)}, u32[]{:S(2)}, u32[]{:S(2)}) %collective-permute-start.8) | collective-permute-done | bytes 61472 | tf_op jit(solution)/shard_map/ppermute | solution.py:413
  64.7 3.7 %collective-permute-start.9 = (s16[240,128]{1,0:T(8,128)(2,1)S(1)}, s16[240,128]{1,0:T(8,128)(2,1)S(1)}, u32[]{:S(2)}, u32[]{:S(2)}) collective-permute-start(s16[240,128]{1,0:T(8,128)(2,1)S(1)} %pad_add_fusion.1), channel_id=1, source_target_pairs={{0,16},{1,17},{2,18},{3,19},{4,20},{5,21},{6,22},{7,23},{8,24},{9,... | collective-permute-start | bytes 184328 | tf_op jit(solution)/shard_map/ppermute | solution.py:413
  68.4 2.7 %collective-permute-done.9 = s16[240,128]{1,0:T(8,128)(2,1)S(1)} collective-permute-done((s16[240,128]{1,0:T(8,128)(2,1)S(1)}, s16[240,128]{1,0:T(8,128)(2,1)S(1)}, u32[]{:S(2)}, u32[]{:S(2)}) %collective-permute-start.9) | collective-permute-done | bytes 61472 | tf_op jit(solution)/shard_map/ppermute | solution.py:413
  71.3 1.2 %collective-permute-start.14 = (s16[240,128]{1,0:T(8,128)(2,1)S(1)}, s16[240,128]{1,0:T(8,128)(2,1)S(1)}, u32[]{:S(2)}, u32[]{:S(2)}) collective-permute-start(s16[240,128]{1,0:T(8,128)(2,1)S(1)} %pad_add_fusion), channel_id=1, source_target_pairs={{0,4},{1,5},{2,6},{3,7},{4,0},{5,1},{6,2},{7,3},{8,12},{9,13},{10,... | collective-permute-start | bytes 184328 | tf_op jit(solution)/shard_map/ppermute | solution.py:413
  72.5 2.4 %collective-permute-start.10 = (s16[240,128]{1,0:T(8,128)(2,1)S(1)}, s16[240,128]{1,0:T(8,128)(2,1)S(1)}, u32[]{:S(2)}, u32[]{:S(2)}) collective-permute-start(s16[240,128]{1,0:T(8,128)(2,1)S(1)} %pad_add_fusion), channel_id=1, source_target_pairs={{0,6},{1,7},{2,4},{3,5},{4,2},{5,3},{6,0},{7,1},{8,14},{9,15},{10,... | collective-permute-start | bytes 184328 | tf_op jit(solution)/shard_map/ppermute | solution.py:413
  74.8 0.7 collective-permute-done.14
  75.6 1.7 %collective-permute-done.12 = s16[240,128]{1,0:T(8,128)(2,1)S(1)} collective-permute-done((s16[240,128]{1,0:T(8,128)(2,1)S(1)}, s16[240,128]{1,0:T(8,128)(2,1)S(1)}, u32[]{:S(2)}, u32[]{:S(2)}) %collective-permute-start.12) | collective-permute-done | bytes 61472 | tf_op jit(solution)/shard_map/ppermute | solution.py:413
  77.3 1.2 %collective-permute-done.10 = s16[240,128]{1,0:T(8,128)(2,1)S(1)} collective-permute-done((s16[240,128]{1,0:T(8,128)(2,1)S(1)}, s16[240,128]{1,0:T(8,128)(2,1)S(1)}, u32[]{:S(2)}, u32[]{:S(2)}) %collective-permute-start.10) | collective-permute-done | bytes 61472 | tf_op jit(solution)/shard_map/ppermute | solution.py:413
  78.8 1.0 %collective-permute-done.11 = s16[240,128]{1,0:T(8,128)(2,1)S(1)} collective-permute-done((s16[240,128]{1,0:T(8,128)(2,1)S(1)}, s16[240,128]{1,0:T(8,128)(2,1)S(1)}, u32[]{:S(2)}, u32[]{:S(2)}) %collective-permute-start.11) | collective-permute-done | bytes 61472 | tf_op jit(solution)/shard_map/ppermute | solution.py:413
  79.8 6.4 %finish.1 = (f32[512,128]{1,0:T(8,128)}, f32[128,512]{1,0:T(8,128)}) custom-call(s32[1]{0:T(128)} %bitcast.me_ref, bf16[1024,512]{1,0:T(8,128)(2,1)S(1)} %get-tuple-element.23.stack_ref, f32[224,128]{1,0:T(8,128)S(1)} %bitcast_multiply_fusion.7.rest_0_, f32[224,128]{1,0:T(8,128)S(1)} %bitcast_multiply_fusion.6.rest_1_, ...), custom_call_target="tpu_custom_call" | custom-call | tf_op jit(solution)/shard_map/finish/pallas_call | solution.py:393
  (65 shorter events, 1.2 us)
Async XLA Ops:
  0.6 16.8 %collective-permute-start = (bf16[16,64,128]{2,1,0:T(8,128)(2,1)}, bf16[16,64,128]{2,1,0:T(8,128)(2,1)S(1)}, u32[]{:S(2)}, u32[]{:S(2)}) collective-permute-start(bf16[16,64,128]{2,1,0:T(8,128)(2,1)} %own_ref.1), channel_id=1, source_target_pairs={{0,16},{1,17},{2,18},{3,19},{4,20},{5,21},{6,22},{7,23},{8,24},{9,... | collective-permute-start | bytes 786440 | tf_op jit(solution)/shard_map/ppermute | solution.py:413
  19.1 19.8 %all-to-all-start.1 = ((bf16[64,64,128]{2,1,0:T(8,128)(2,1)}), bf16[64,64,128]{2,1,0:T(8,128)(2,1)S(1)}, u32[]{:S(2)}, u32[]{:S(2)}) async-start(bf16[64,64,128]{2,1,0:T(8,128)(2,1)} %collect.1), calls=%async_computation.1 | async-start | bytes 2097152 | tf_op jit(solution)/shard_map/all_to_all | solution.py:474
  24.5 0.9 %copy-start.1 = (s32[64,512]{1,0:T(8,128)S(1)}, s32[64,512]{1,0:T(8,128)}, u32[]{:S(2)}) copy-start(s32[64,512]{1,0:T(8,128)} %marks_ref.1) | copy-start | bytes 393220
  29.1 1.0 %copy-start = (f32[64,8,512]{2,1,0:T(8,128)}, f32[64,8,512]{2,1,0:T(8,128)S(1)}, u32[]{:S(2)}) copy-start(f32[64,8,512]{2,1,0:T(8,128)S(1)} %contexts.1.context_ref) | copy-start | bytes 3145732
  51.5 1.4 %collective-permute-start.2 = (f32[224,128]{1,0:T(8,128)S(1)}, f32[224,128]{1,0:T(8,128)S(1)}, u32[]{:S(2)}, u32[]{:S(2)}) collective-permute-start(f32[224,128]{1,0:T(8,128)S(1)} %get-tuple-element.27), channel_id=1, source_target_pairs={{0,1},{1,0},{2,3},{3,2},{4,5},{5,4},{6,7},{7,6},{8,9},{9,8},{10,11... | collective-permute-start | bytes 344072 | tf_op jit(solution)/shard_map/ppermute | solution.py:413
  51.6 8.4 %collective-permute-start.1 = (f32[224,128]{1,0:T(8,128)S(1)}, f32[224,128]{1,0:T(8,128)S(1)}, u32[]{:S(2)}, u32[]{:S(2)}) collective-permute-start(f32[224,128]{1,0:T(8,128)S(1)} %get-tuple-element.25), channel_id=1, source_target_pairs={{0,1},{1,0},{2,3},{3,2},{4,5},{5,4},{6,7},{7,6},{8,9},{9,8},{10,11... | collective-permute-start | bytes 344072 | tf_op jit(solution)/shard_map/ppermute | solution.py:413
  52.1 2.0 %collective-permute-start.4 = (f32[224,128]{1,0:T(8,128)S(1)}, f32[224,128]{1,0:T(8,128)S(1)}, u32[]{:S(2)}, u32[]{:S(2)}) collective-permute-start(f32[224,128]{1,0:T(8,128)S(1)} %get-tuple-element.29), channel_id=1, source_target_pairs={{0,1},{1,0},{2,3},{3,2},{4,5},{5,4},{6,7},{7,6},{8,9},{9,8},{10,11... | collective-permute-start | bytes 344072 | tf_op jit(solution)/shard_map/ppermute | solution.py:413
  52.2 3.4 %collective-permute-start.6 = (f32[224,128]{1,0:T(8,128)S(1)}, f32[224,128]{1,0:T(8,128)S(1)}, u32[]{:S(2)}, u32[]{:S(2)}) collective-permute-start(f32[224,128]{1,0:T(8,128)S(1)} %get-tuple-element.31), channel_id=1, source_target_pairs={{0,1},{1,0},{2,3},{3,2},{4,5},{5,4},{6,7},{7,6},{8,9},{9,8},{10,11... | collective-permute-start | bytes 344072 | tf_op jit(solution)/shard_map/ppermute | solution.py:413
  53.0 5.8 %collective-permute-start.3 = (s16[240,128]{1,0:T(8,128)(2,1)S(1)}, s16[240,128]{1,0:T(8,128)(2,1)S(1)}, u32[]{:S(2)}, u32[]{:S(2)}) collective-permute-start(s16[240,128]{1,0:T(8,128)(2,1)S(1)} %pad_add_fusion.5), channel_id=1, source_target_pairs={{0,6},{1,7},{2,4},{3,5},{4,2},{5,3},{6,0},{7,1},{8,14},{9,15},{10,... | collective-permute-start | bytes 184328 | tf_op jit(solution)/shard_map/ppermute | solution.py:413
  54.2 4.7 %collective-permute-start.5 = (s16[240,128]{1,0:T(8,128)(2,1)S(1)}, s16[240,128]{1,0:T(8,128)(2,1)S(1)}, u32[]{:S(2)}, u32[]{:S(2)}) collective-permute-start(s16[240,128]{1,0:T(8,128)(2,1)S(1)} %pad_add_fusion.4), channel_id=1, source_target_pairs={{0,2},{1,3},{2,0},{3,1},{4,6},{5,7},{6,4},{7,5},{8,10},{9,11},{10,... | collective-permute-start | bytes 184328 | tf_op jit(solution)/shard_map/ppermute | solution.py:413
  55.7 4.3 %collective-permute-start.7 = (s16[240,128]{1,0:T(8,128)(2,1)S(1)}, s16[240,128]{1,0:T(8,128)(2,1)S(1)}, u32[]{:S(2)}, u32[]{:S(2)}) collective-permute-start(s16[240,128]{1,0:T(8,128)(2,1)S(1)} %pad_add_fusion.3), channel_id=1, source_target_pairs={{0,4},{1,5},{2,6},{3,7},{4,0},{5,1},{6,2},{7,3},{8,12},{9,13},{10,... | collective-permute-start | bytes 184328 | tf_op jit(solution)/shard_map/ppermute | solution.py:413
  60.2 4.3 %collective-permute-start.8 = (s16[240,128]{1,0:T(8,128)(2,1)S(1)}, s16[240,128]{1,0:T(8,128)(2,1)S(1)}, u32[]{:S(2)}, u32[]{:S(2)}) collective-permute-start(s16[240,128]{1,0:T(8,128)(2,1)S(1)} %pad_add_fusion.2), channel_id=1, source_target_pairs={{0,8},{1,9},{2,10},{3,11},{4,12},{5,13},{6,14},{7,15},{8,0},{9,1},... | collective-permute-start | bytes 184328 | tf_op jit(solution)/shard_map/ppermute | solution.py:413
  64.7 6.3 %collective-permute-start.9 = (s16[240,128]{1,0:T(8,128)(2,1)S(1)}, s16[240,128]{1,0:T(8,128)(2,1)S(1)}, u32[]{:S(2)}, u32[]{:S(2)}) collective-permute-start(s16[240,128]{1,0:T(8,128)(2,1)S(1)} %pad_add_fusion.1), channel_id=1, source_target_pairs={{0,16},{1,17},{2,18},{3,19},{4,20},{5,21},{6,22},{7,23},{8,24},{9,... | collective-permute-start | bytes 184328 | tf_op jit(solution)/shard_map/ppermute | solution.py:413
  71.3 4.3 %collective-permute-start.14 = (s16[240,128]{1,0:T(8,128)(2,1)S(1)}, s16[240,128]{1,0:T(8,128)(2,1)S(1)}, u32[]{:S(2)}, u32[]{:S(2)}) collective-permute-start(s16[240,128]{1,0:T(8,128)(2,1)S(1)} %pad_add_fusion), channel_id=1, source_target_pairs={{0,4},{1,5},{2,6},{3,7},{4,0},{5,1},{6,2},{7,3},{8,12},{9,13},{10,... | collective-permute-start | bytes 184328 | tf_op jit(solution)/shard_map/ppermute | solution.py:413
  72.5 6.1 %collective-permute-start.16 = (s16[240,128]{1,0:T(8,128)(2,1)S(1)}, s16[240,128]{1,0:T(8,128)(2,1)S(1)}, u32[]{:S(2)}, u32[]{:S(2)}) collective-permute-start(s16[240,128]{1,0:T(8,128)(2,1)S(1)} %pad_add_fusion), channel_id=1, source_target_pairs={{0,1},{1,0},{2,3},{3,2},{4,5},{5,4},{6,7},{7,6},{8,9},{9,8},{10,11... | collective-permute-start | bytes 184328 | tf_op jit(solution)/shard_map/ppermute | solution.py:413
  72.5 4.8 %collective-permute-start.12 = (s16[240,128]{1,0:T(8,128)(2,1)S(1)}, s16[240,128]{1,0:T(8,128)(2,1)S(1)}, u32[]{:S(2)}, u32[]{:S(2)}) collective-permute-start(s16[240,128]{1,0:T(8,128)(2,1)S(1)} %pad_add_fusion), channel_id=1, source_target_pairs={{0,2},{1,3},{2,0},{3,1},{4,6},{5,7},{6,4},{7,5},{8,10},{9,11},{10,... | collective-permute-start | bytes 184328 | tf_op jit(solution)/shard_map/ppermute | solution.py:413
  72.5 6.1 %collective-permute-start.10 = (s16[240,128]{1,0:T(8,128)(2,1)S(1)}, s16[240,128]{1,0:T(8,128)(2,1)S(1)}, u32[]{:S(2)}, u32[]{:S(2)}) collective-permute-start(s16[240,128]{1,0:T(8,128)(2,1)S(1)} %pad_add_fusion), channel_id=1, source_target_pairs={{0,6},{1,7},{2,4},{3,5},{4,2},{5,3},{6,0},{7,1},{8,14},{9,15},{10,... | collective-permute-start | bytes 184328 | tf_op jit(solution)/shard_map/ppermute | solution.py:413
  75.6 3.1 %collective-permute-start.15 = (s16[240,128]{1,0:T(8,128)(2,1)S(1)}, s16[240,128]{1,0:T(8,128)(2,1)S(1)}, u32[]{:S(2)}, u32[]{:S(2)}) collective-permute-start(s16[240,128]{1,0:T(8,128)(2,1)S(1)} %collective-permute-done.14), channel_id=1, source_target_pairs={{0,1},{1,0},{2,3},{3,2},{4,5},{5,4},{6,7},{7,6},{8,9},{9,8},{10,11... | collective-permute-start | bytes 184328 | tf_op jit(solution)/shard_map/ppermute | solution.py:413
  77.3 1.4 %collective-permute-start.13 = (s16[240,128]{1,0:T(8,128)(2,1)S(1)}, s16[240,128]{1,0:T(8,128)(2,1)S(1)}, u32[]{:S(2)}, u32[]{:S(2)}) collective-permute-start(s16[240,128]{1,0:T(8,128)(2,1)S(1)} %collective-permute-done.12), channel_id=1, source_target_pairs={{0,1},{1,0},{2,3},{3,2},{4,5},{5,4},{6,7},{7,6},{8,9},{9,8},{10,11... | collective-permute-start | bytes 184328 | tf_op jit(solution)/shard_map/ppermute | solution.py:413
  78.5 1.3 %collective-permute-start.11 = (s16[240,128]{1,0:T(8,128)(2,1)S(1)}, s16[240,128]{1,0:T(8,128)(2,1)S(1)}, u32[]{:S(2)}, u32[]{:S(2)}) collective-permute-start(s16[240,128]{1,0:T(8,128)(2,1)S(1)} %collective-permute-done.10), channel_id=1, source_target_pairs={{0,1},{1,0},{2,3},{3,2},{4,5},{5,4},{6,7},{7,6},{8,9},{9,8},{10,11... | collective-permute-start | bytes 184328 | tf_op jit(solution)/shard_map/ppermute | solution.py:413

commit v17 on v16

--- a/solution.py
+++ b/solution.py
@@ -190,8 +190,7 @@
 
     def multiply(batch, place, into_ref):
         tile = batch * BATCH + place
-        product = dot(blocks_ref[where_ref[tile]], weights_held[tile])
-        into_ref[place] = product.astype(jnp.bfloat16).astype(jnp.float32)
+        into_ref[place] = dot(blocks_ref[where_ref[tile]], weights_held[tile]).astype(into_ref.dtype)
 
     def add(batch, part, from_ref):
         lanes = slice(part // 2 * LANES, (part // 2 + 1) * LANES)
@@ -199,7 +198,10 @@
         strips = [slice(i, i + ROWS) for i in range(0, rank_i, ROWS)]
         totals = [[y_ref[r, strip, lanes] for strip in strips] for r in ranks]
         for place in range(BATCH):
-            parts_of = [from_ref[place, strip, lanes] for strip in strips]
+            parts_of = []
+            for i in range(0, rank_i, 2 * ROWS):
+                wide = from_ref[place, i : i + 2 * ROWS, lanes].astype(jnp.float32)
+                parts_of += [wide[:ROWS], wide[ROWS:]]
             for i, r in enumerate(ranks):
                 values = context_held[batch * BATCH + place, r : r + 1, lanes]
                 values = jnp.broadcast_to(values, (ROWS, LANES))
@@ -285,8 +287,8 @@
             pltpu.VMEM((rank_c, rank_i, users), jnp.float32),
             pltpu.VMEM((2 * ranks, ranks), jnp.float32),
             pltpu.VMEM((rows, LANES), jnp.float32),
-            pltpu.VMEM((BATCH, rank_i, users), jnp.float32),
-            pltpu.VMEM((BATCH, rank_i, users), jnp.float32),
+            pltpu.VMEM((BATCH, rank_i, users), jnp.bfloat16),
+            pltpu.VMEM((BATCH, rank_i, users), jnp.bfloat16),
             pltpu.VMEM(weights.shape, weights.dtype),
             pltpu.VMEM(contexts.shape, contexts.dtype),
             pltpu.VMEM(user_basis.shape, user_basis.dtype),

time: 86.7 us -> 86.5 us (level)
  no operation moved by 1% of the time
where the time goes in v17:
time: 86.5 us; the launch traced here: 86.1 us
  Pallas kernels  26.5 us (31%)
  waiting for transfers between devices  23.1 us (27%)
  starting transfers between devices  20.4 us (24%)
  blocking collectives  10.5 us (12%)
  local copies, waits for them, and re-layouts  2.9 us (3%)
  between operations  1.63 us (2%)
  other arithmetic  1.07 us (1%)
    ppermute x17, starting transfers between devices, swap(): return lax.ppermute(value, 'users', [(i, i ^ mask) for i in range(devices)])  16.7 us
    ppermute x17, waiting for transfers between devices, swap(): return lax.ppermute(value, 'users', [(i, i ^ mask) for i in range(devices)])  14.3 us
    pallas_call x1, Pallas kernels, tile_sums(): pl.pallas_call(tiles_kernel, out_shape=out_shape, in_specs=[SMEM] * 3 + [...  12.4 us
    all_to_all x1, blocking collectives, body(): lax.all_to_all(requests, 'users', 0, 0, axis_index_groups=sides, tiled=True)  10.5 us
    all_to_all x1, waiting for transfers between devices, body(): lax.all_to_all(found, 'users', 0, 0, axis_index_groups=sides, tiled=True)  8.82 us
    pallas_call x1, Pallas kernels, finish(): pl.pallas_call(functools.partial(finish_kernel, users * devices), out_sha...  6.43 us
    pallas_call x1, Pallas kernels, context_values(): pl.pallas_call(context_kernel, out_shape=jax.ShapeDtypeStruct((tiles, ROW...  3.72 us
    all_to_all x1, starting transfers between devices, body(): lax.all_to_all(found, 'users', 0, 0, axis_index_groups=sides, tiled=True)  3.65 us
  transfers between devices with their start and end apart: 18, of which 10 were waited for; matrix products, arithmetic and copies ran while one was open for 2% of the time, Pallas kernels for 7%

profile of v17, /device:TPU:0, one launch (start us, length us, event | category | flops | bytes accessed | tf_op | source)
XLA Modules:
  0.0 86.1 jit_solution(3343562262898652675)
XLA Ops:
  0.6 4.1 %collective-permute-start = (bf16[16,64,128]{2,1,0:T(8,128)(2,1)}, bf16[16,64,128]{2,1,0:T(8,128)(2,1)S(1)}, u32[]{:S(2)}, u32[]{:S(2)}) collective-permute-start(bf16[16,64,128]{2,1,0:T(8,128)(2,1)} %own_ref.1), channel_id=1, source_target_pairs={{0,16},{1,17},{2,18},{3,19},{4,20},{5,21},{6,22},{7,23},{8,24},{9,... | collective-permute-start | bytes 786440 | tf_op jit(solution)/shard_map/ppermute | solution.py:415
  4.7 2.2 %route.1 = (s32[16,1,128]{2,1,0:T(1,128)S(1)}, s32[64]{0:T(128)S(1)}, bf16[16,64,128]{2,1,0:T(8,128)(2,1)S(1)}) custom-call(s32[1]{0:T(128)} %bitcast.me_ref, s32[64]{0:T(128)} %bitcast.136, s32[64]{0:T(128)} %slot_ref.1, bf16[16,64,128]{2,1,0:T(8,128)(2,1)} %own_ref.1), custom_call_target="tpu_custom_call" | custom-call | tf_op jit(solution)/shard_map/route/pallas_call | solution.py:85
  7.0 10.5 %all_to_all.10.asked_ref = s32[16,1,128]{2,1,0:T(1,128)S(1)} all-to-all(s32[16,1,128]{2,1,0:T(1,128)S(1)} %get-tuple-element.18), channel_id=1, replica_groups={{0,1,2,3,4,5,6,7,8,9,10,11,12,13,14,15},{16,17,18,19,20,21,22,23,24,25,..., dimensions={0} | all-to-all | bytes 16384 | tf_op jit(solution)/shard_map/all_to_all | solution.py:473
  17.4 1.7 %collect.1 = bf16[64,64,128]{2,1,0:T(8,128)(2,1)} custom-call(s32[16,1,128]{2,1,0:T(1,128)S(1)} %all_to_all.10.asked_ref, bf16[16,64,128]{2,1,0:T(8,128)(2,1)S(1)} %get-tuple-element.19.own_ref, bf16[16,64,128]{2,1,0:T(8,128)(2,1)S(1)} %collective-permute-done.mirror_ref), custom_call_target="tpu_custom_call" | custom-call | tf_op jit(solution)/shard_map/collect/pallas_call | solution.py:108
  19.1 3.7 %all-to-all-start.1 = ((bf16[64,64,128]{2,1,0:T(8,128)(2,1)}), bf16[64,64,128]{2,1,0:T(8,128)(2,1)S(1)}, u32[]{:S(2)}, u32[]{:S(2)}) async-start(bf16[64,64,128]{2,1,0:T(8,128)(2,1)} %collect.1), calls=%async_computation.1 | async-start | bytes 2097152 | tf_op jit(solution)/shard_map/all_to_all | solution.py:476
  23.5 0.9 %reshape.232 = f32[8,64,8]{2,1,0:T(8,128)S(1)} reshape(bf16[8,512]{1,0:T(8,128)(2,1)} %param.15) | data formatting | bytes 24576 | tf_op jit(solution)/shard_map/transpose | solution.py:478
  24.3 0.2 copy.13
  24.5 0.9 %copy-done.1 = s32[64,512]{1,0:T(8,128)S(1)} copy-done((s32[64,512]{1,0:T(8,128)S(1)}, s32[64,512]{1,0:T(8,128)}, u32[]{:S(2)}) %copy-start.1) | copy-done | bytes 131096
  25.4 3.7 %contexts.1.context_ref = f32[64,8,512]{2,1,0:T(8,128)S(1)} custom-call(s32[64]{0:T(128)} %cblock_ref, f32[64,8,8]{2,1,0:T(8,128)S(1)} %bitcast.129, s32[64,512]{1,0:T(8,128)S(1)} %copy-done.1), custom_call_target="tpu_custom_call" | custom-call | flops 10000000 | bytes 20000000 | tf_op jit(solution)/shard_map/contexts/pallas_call | solution.py:136
  29.1 1.0 %copy-done = f32[64,8,512]{2,1,0:T(8,128)} copy-done((f32[64,8,512]{2,1,0:T(8,128)}, f32[64,8,512]{2,1,0:T(8,128)S(1)}, u32[]{:S(2)}) %copy-start) | copy-done | bytes 1048600
  30.1 8.8 %all-to-all-done.1.blocks_ref = bf16[64,64,128]{2,1,0:T(8,128)(2,1)S(1)} async-done(((bf16[64,64,128]{2,1,0:T(8,128)(2,1)}), bf16[64,64,128]{2,1,0:T(8,128)(2,1)S(1)}, u32[]{:S(2)}, u32[]{:S(2)}) %all-to-all-start.1) | async-done | bytes 1048608 | tf_op jit(solution)/shard_map/all_to_all | solution.py:476
  38.9 12.4 %tile_sums.1 = (f32[224,128]{1,0:T(8,128)S(1)}, f32[224,128]{1,0:T(8,128)S(1)}, f32[224,128]{1,0:T(8,128)S(1)}, f32[224,128]{1,0:T(8,128)S(1)}, f32[224,128]{1,0...) custom-call(s32[64]{0:T(128)S(1)} %get-tuple-element.17.where_ref, ...), custom_call_target="tpu_custom_call" | custom-call | flops 2000000000 | bytes 12000000 | tf_op jit(solution)/shard_map/tile_sums/pallas_call | solution.py:281
  51.5 0.5 collective-permute-start.1
  52.0 0.4 collective-permute-start.6
  52.5 0.3 collective-permute-done.2
  52.9 1.0 %collective-permute-start.3 = (s16[240,128]{1,0:T(8,128)(2,1)S(1)}, s16[240,128]{1,0:T(8,128)(2,1)S(1)}, u32[]{:S(2)}, u32[]{:S(2)}) collective-permute-start(s16[240,128]{1,0:T(8,128)(2,1)S(1)} %pad_add_fusion.5), channel_id=1, source_target_pairs={{0,6},{1,7},{2,4},{3,5},{4,2},{5,3},{6,0},{7,1},{8,14},{9,15},{10,... | collective-permute-start | bytes 184328 | tf_op jit(solution)/shard_map/ppermute | solution.py:415
  54.0 1.4 %collective-permute-start.5 = (s16[240,128]{1,0:T(8,128)(2,1)S(1)}, s16[240,128]{1,0:T(8,128)(2,1)S(1)}, u32[]{:S(2)}, u32[]{:S(2)}) collective-permute-start(s16[240,128]{1,0:T(8,128)(2,1)S(1)} %pad_add_fusion.4), channel_id=1, source_target_pairs={{0,2},{1,3},{2,0},{3,1},{4,6},{5,7},{6,4},{7,5},{8,10},{9,11},{10,... | collective-permute-start | bytes 184328 | tf_op jit(solution)/shard_map/ppermute | solution.py:415
  55.5 1.3 %collective-permute-start.7 = (s16[240,128]{1,0:T(8,128)(2,1)S(1)}, s16[240,128]{1,0:T(8,128)(2,1)S(1)}, u32[]{:S(2)}, u32[]{:S(2)}) collective-permute-start(s16[240,128]{1,0:T(8,128)(2,1)S(1)} %pad_add_fusion.3), channel_id=1, source_target_pairs={{0,4},{1,5},{2,6},{3,7},{4,0},{5,1},{6,2},{7,3},{8,12},{9,13},{10,... | collective-permute-start | bytes 184328 | tf_op jit(solution)/shard_map/ppermute | solution.py:415
  56.8 1.9 %collective-permute-done.3 = s16[240,128]{1,0:T(8,128)(2,1)S(1)} collective-permute-done((s16[240,128]{1,0:T(8,128)(2,1)S(1)}, s16[240,128]{1,0:T(8,128)(2,1)S(1)}, u32[]{:S(2)}, u32[]{:S(2)}) %collective-permute-start.3) | collective-permute-done | bytes 61472 | tf_op jit(solution)/shard_map/ppermute | solution.py:415
  58.7 1.1 %collective-permute-done.7 = s16[240,128]{1,0:T(8,128)(2,1)S(1)} collective-permute-done((s16[240,128]{1,0:T(8,128)(2,1)S(1)}, s16[240,128]{1,0:T(8,128)(2,1)S(1)}, u32[]{:S(2)}, u32[]{:S(2)}) %collective-permute-start.7) | collective-permute-done | bytes 61472 | tf_op jit(solution)/shard_map/ppermute | solution.py:415
  59.8 0.1 fusion.35
  60.0 0.6 collective-permute-start.8
  60.6 3.7 %collective-permute-done.8 = s16[240,128]{1,0:T(8,128)(2,1)S(1)} collective-permute-done((s16[240,128]{1,0:T(8,128)(2,1)S(1)}, s16[240,128]{1,0:T(8,128)(2,1)S(1)}, u32[]{:S(2)}, u32[]{:S(2)}) %collective-permute-start.8) | collective-permute-done | bytes 61472 | tf_op jit(solution)/shard_map/ppermute | solution.py:415
  64.5 3.6 %collective-permute-start.9 = (s16[240,128]{1,0:T(8,128)(2,1)S(1)}, s16[240,128]{1,0:T(8,128)(2,1)S(1)}, u32[]{:S(2)}, u32[]{:S(2)}) collective-permute-start(s16[240,128]{1,0:T(8,128)(2,1)S(1)} %pad_add_fusion.1), channel_id=1, source_target_pairs={{0,16},{1,17},{2,18},{3,19},{4,20},{5,21},{6,22},{7,23},{8,24},{9,... | collective-permute-start | bytes 184328 | tf_op jit(solution)/shard_map/ppermute | solution.py:415
  68.1 2.7 %collective-permute-done.9 = s16[240,128]{1,0:T(8,128)(2,1)S(1)} collective-permute-done((s16[240,128]{1,0:T(8,128)(2,1)S(1)}, s16[240,128]{1,0:T(8,128)(2,1)S(1)}, u32[]{:S(2)}, u32[]{:S(2)}) %collective-permute-start.9) | collective-permute-done | bytes 61472 | tf_op jit(solution)/shard_map/ppermute | solution.py:415
  71.1 1.2 %collective-permute-start.14 = (s16[240,128]{1,0:T(8,128)(2,1)S(1)}, s16[240,128]{1,0:T(8,128)(2,1)S(1)}, u32[]{:S(2)}, u32[]{:S(2)}) collective-permute-start(s16[240,128]{1,0:T(8,128)(2,1)S(1)} %pad_add_fusion), channel_id=1, source_target_pairs={{0,4},{1,5},{2,6},{3,7},{4,0},{5,1},{6,2},{7,3},{8,12},{9,13},{10,... | collective-permute-start | bytes 184328 | tf_op jit(solution)/shard_map/ppermute | solution.py:415
  72.3 2.3 %collective-permute-start.10 = (s16[240,128]{1,0:T(8,128)(2,1)S(1)}, s16[240,128]{1,0:T(8,128)(2,1)S(1)}, u32[]{:S(2)}, u32[]{:S(2)}) collective-permute-start(s16[240,128]{1,0:T(8,128)(2,1)S(1)} %pad_add_fusion), channel_id=1, source_target_pairs={{0,6},{1,7},{2,4},{3,5},{4,2},{5,3},{6,0},{7,1},{8,14},{9,15},{10,... | collective-permute-start | bytes 184328 | tf_op jit(solution)/shard_map/ppermute | solution.py:415
  74.6 0.7 collective-permute-done.14
  75.4 1.7 %collective-permute-done.12 = s16[240,128]{1,0:T(8,128)(2,1)S(1)} collective-permute-done((s16[240,128]{1,0:T(8,128)(2,1)S(1)}, s16[240,128]{1,0:T(8,128)(2,1)S(1)}, u32[]{:S(2)}, u32[]{:S(2)}) %collective-permute-start.12) | collective-permute-done | bytes 61472 | tf_op jit(solution)/shard_map/ppermute | solution.py:415
  77.1 1.2 %collective-permute-done.10 = s16[240,128]{1,0:T(8,128)(2,1)S(1)} collective-permute-done((s16[240,128]{1,0:T(8,128)(2,1)S(1)}, s16[240,128]{1,0:T(8,128)(2,1)S(1)}, u32[]{:S(2)}, u32[]{:S(2)}) %collective-permute-start.10) | collective-permute-done | bytes 61472 | tf_op jit(solution)/shard_map/ppermute | solution.py:415
  78.6 1.0 %collective-permute-done.11 = s16[240,128]{1,0:T(8,128)(2,1)S(1)} collective-permute-done((s16[240,128]{1,0:T(8,128)(2,1)S(1)}, s16[240,128]{1,0:T(8,128)(2,1)S(1)}, u32[]{:S(2)}, u32[]{:S(2)}) %collective-permute-start.11) | collective-permute-done | bytes 61472 | tf_op jit(solution)/shard_map/ppermute | solution.py:415
  79.6 6.4 %finish.1 = (f32[512,128]{1,0:T(8,128)}, f32[128,512]{1,0:T(8,128)}) custom-call(s32[1]{0:T(128)} %bitcast.me_ref, bf16[1024,512]{1,0:T(8,128)(2,1)S(1)} %get-tuple-element.23.stack_ref, f32[224,128]{1,0:T(8,128)S(1)} %bitcast_multiply_fusion.7.rest_0_, f32[224,128]{1,0:T(8,128)S(1)} %bitcast_multiply_fusion.6.rest_1_, ...), custom_call_target="tpu_custom_call" | custom-call | tf_op jit(solution)/shard_map/finish/pallas_call | solution.py:395
  (65 shorter events, 1.2 us)
Async XLA Ops:
  0.6 16.8 %collective-permute-start = (bf16[16,64,128]{2,1,0:T(8,128)(2,1)}, bf16[16,64,128]{2,1,0:T(8,128)(2,1)S(1)}, u32[]{:S(2)}, u32[]{:S(2)}) collective-permute-start(bf16[16,64,128]{2,1,0:T(8,128)(2,1)} %own_ref.1), channel_id=1, source_target_pairs={{0,16},{1,17},{2,18},{3,19},{4,20},{5,21},{6,22},{7,23},{8,24},{9,... | collective-permute-start | bytes 786440 | tf_op jit(solution)/shard_map/ppermute | solution.py:415
  19.1 19.8 %all-to-all-start.1 = ((bf16[64,64,128]{2,1,0:T(8,128)(2,1)}), bf16[64,64,128]{2,1,0:T(8,128)(2,1)S(1)}, u32[]{:S(2)}, u32[]{:S(2)}) async-start(bf16[64,64,128]{2,1,0:T(8,128)(2,1)} %collect.1), calls=%async_computation.1 | async-start | bytes 2097152 | tf_op jit(solution)/shard_map/all_to_all | solution.py:476
  24.5 0.9 %copy-start.1 = (s32[64,512]{1,0:T(8,128)S(1)}, s32[64,512]{1,0:T(8,128)}, u32[]{:S(2)}) copy-start(s32[64,512]{1,0:T(8,128)} %marks_ref.1) | copy-start | bytes 393220
  29.1 1.0 %copy-start = (f32[64,8,512]{2,1,0:T(8,128)}, f32[64,8,512]{2,1,0:T(8,128)S(1)}, u32[]{:S(2)}) copy-start(f32[64,8,512]{2,1,0:T(8,128)S(1)} %contexts.1.context_ref) | copy-start | bytes 3145732
  51.4 1.4 %collective-permute-start.2 = (f32[224,128]{1,0:T(8,128)S(1)}, f32[224,128]{1,0:T(8,128)S(1)}, u32[]{:S(2)}, u32[]{:S(2)}) collective-permute-start(f32[224,128]{1,0:T(8,128)S(1)} %get-tuple-element.27), channel_id=1, source_target_pairs={{0,1},{1,0},{2,3},{3,2},{4,5},{5,4},{6,7},{7,6},{8,9},{9,8},{10,11... | collective-permute-start | bytes 344072 | tf_op jit(solution)/shard_map/ppermute | solution.py:415
  51.5 8.4 %collective-permute-start.1 = (f32[224,128]{1,0:T(8,128)S(1)}, f32[224,128]{1,0:T(8,128)S(1)}, u32[]{:S(2)}, u32[]{:S(2)}) collective-permute-start(f32[224,128]{1,0:T(8,128)S(1)} %get-tuple-element.25), channel_id=1, source_target_pairs={{0,1},{1,0},{2,3},{3,2},{4,5},{5,4},{6,7},{7,6},{8,9},{9,8},{10,11... | collective-permute-start | bytes 344072 | tf_op jit(solution)/shard_map/ppermute | solution.py:415
  52.0 1.9 %collective-permute-start.4 = (f32[224,128]{1,0:T(8,128)S(1)}, f32[224,128]{1,0:T(8,128)S(1)}, u32[]{:S(2)}, u32[]{:S(2)}) collective-permute-start(f32[224,128]{1,0:T(8,128)S(1)} %get-tuple-element.29), channel_id=1, source_target_pairs={{0,1},{1,0},{2,3},{3,2},{4,5},{5,4},{6,7},{7,6},{8,9},{9,8},{10,11... | collective-permute-start | bytes 344072 | tf_op jit(solution)/shard_map/ppermute | solution.py:415
  52.0 3.4 %collective-permute-start.6 = (f32[224,128]{1,0:T(8,128)S(1)}, f32[224,128]{1,0:T(8,128)S(1)}, u32[]{:S(2)}, u32[]{:S(2)}) collective-permute-start(f32[224,128]{1,0:T(8,128)S(1)} %get-tuple-element.31), channel_id=1, source_target_pairs={{0,1},{1,0},{2,3},{3,2},{4,5},{5,4},{6,7},{7,6},{8,9},{9,8},{10,11... | collective-permute-start | bytes 344072 | tf_op jit(solution)/shard_map/ppermute | solution.py:415
  52.9 5.8 %collective-permute-start.3 = (s16[240,128]{1,0:T(8,128)(2,1)S(1)}, s16[240,128]{1,0:T(8,128)(2,1)S(1)}, u32[]{:S(2)}, u32[]{:S(2)}) collective-permute-start(s16[240,128]{1,0:T(8,128)(2,1)S(1)} %pad_add_fusion.5), channel_id=1, source_target_pairs={{0,6},{1,7},{2,4},{3,5},{4,2},{5,3},{6,0},{7,1},{8,14},{9,15},{10,... | collective-permute-start | bytes 184328 | tf_op jit(solution)/shard_map/ppermute | solution.py:415
  54.0 4.7 %collective-permute-start.5 = (s16[240,128]{1,0:T(8,128)(2,1)S(1)}, s16[240,128]{1,0:T(8,128)(2,1)S(1)}, u32[]{:S(2)}, u32[]{:S(2)}) collective-permute-start(s16[240,128]{1,0:T(8,128)(2,1)S(1)} %pad_add_fusion.4), channel_id=1, source_target_pairs={{0,2},{1,3},{2,0},{3,1},{4,6},{5,7},{6,4},{7,5},{8,10},{9,11},{10,... | collective-permute-start | bytes 184328 | tf_op jit(solution)/shard_map/ppermute | solution.py:415
  55.5 4.3 %collective-permute-start.7 = (s16[240,128]{1,0:T(8,128)(2,1)S(1)}, s16[240,128]{1,0:T(8,128)(2,1)S(1)}, u32[]{:S(2)}, u32[]{:S(2)}) collective-permute-start(s16[240,128]{1,0:T(8,128)(2,1)S(1)} %pad_add_fusion.3), channel_id=1, source_target_pairs={{0,4},{1,5},{2,6},{3,7},{4,0},{5,1},{6,2},{7,3},{8,12},{9,13},{10,... | collective-permute-start | bytes 184328 | tf_op jit(solution)/shard_map/ppermute | solution.py:415
  60.0 4.3 %collective-permute-start.8 = (s16[240,128]{1,0:T(8,128)(2,1)S(1)}, s16[240,128]{1,0:T(8,128)(2,1)S(1)}, u32[]{:S(2)}, u32[]{:S(2)}) collective-permute-start(s16[240,128]{1,0:T(8,128)(2,1)S(1)} %pad_add_fusion.2), channel_id=1, source_target_pairs={{0,8},{1,9},{2,10},{3,11},{4,12},{5,13},{6,14},{7,15},{8,0},{9,1},... | collective-permute-start | bytes 184328 | tf_op jit(solution)/shard_map/ppermute | solution.py:415
  64.5 6.3 %collective-permute-start.9 = (s16[240,128]{1,0:T(8,128)(2,1)S(1)}, s16[240,128]{1,0:T(8,128)(2,1)S(1)}, u32[]{:S(2)}, u32[]{:S(2)}) collective-permute-start(s16[240,128]{1,0:T(8,128)(2,1)S(1)} %pad_add_fusion.1), channel_id=1, source_target_pairs={{0,16},{1,17},{2,18},{3,19},{4,20},{5,21},{6,22},{7,23},{8,24},{9,... | collective-permute-start | bytes 184328 | tf_op jit(solution)/shard_map/ppermute | solution.py:415
  71.1 4.3 %collective-permute-start.14 = (s16[240,128]{1,0:T(8,128)(2,1)S(1)}, s16[240,128]{1,0:T(8,128)(2,1)S(1)}, u32[]{:S(2)}, u32[]{:S(2)}) collective-permute-start(s16[240,128]{1,0:T(8,128)(2,1)S(1)} %pad_add_fusion), channel_id=1, source_target_pairs={{0,4},{1,5},{2,6},{3,7},{4,0},{5,1},{6,2},{7,3},{8,12},{9,13},{10,... | collective-permute-start | bytes 184328 | tf_op jit(solution)/shard_map/ppermute | solution.py:415
  72.3 6.0 %collective-permute-start.16 = (s16[240,128]{1,0:T(8,128)(2,1)S(1)}, s16[240,128]{1,0:T(8,128)(2,1)S(1)}, u32[]{:S(2)}, u32[]{:S(2)}) collective-permute-start(s16[240,128]{1,0:T(8,128)(2,1)S(1)} %pad_add_fusion), channel_id=1, source_target_pairs={{0,1},{1,0},{2,3},{3,2},{4,5},{5,4},{6,7},{7,6},{8,9},{9,8},{10,11... | collective-permute-start | bytes 184328 | tf_op jit(solution)/shard_map/ppermute | solution.py:415
  72.3 4.8 %collective-permute-start.12 = (s16[240,128]{1,0:T(8,128)(2,1)S(1)}, s16[240,128]{1,0:T(8,128)(2,1)S(1)}, u32[]{:S(2)}, u32[]{:S(2)}) collective-permute-start(s16[240,128]{1,0:T(8,128)(2,1)S(1)} %pad_add_fusion), channel_id=1, source_target_pairs={{0,2},{1,3},{2,0},{3,1},{4,6},{5,7},{6,4},{7,5},{8,10},{9,11},{10,... | collective-permute-start | bytes 184328 | tf_op jit(solution)/shard_map/ppermute | solution.py:415
  72.3 6.0 %collective-permute-start.10 = (s16[240,128]{1,0:T(8,128)(2,1)S(1)}, s16[240,128]{1,0:T(8,128)(2,1)S(1)}, u32[]{:S(2)}, u32[]{:S(2)}) collective-permute-start(s16[240,128]{1,0:T(8,128)(2,1)S(1)} %pad_add_fusion), channel_id=1, source_target_pairs={{0,6},{1,7},{2,4},{3,5},{4,2},{5,3},{6,0},{7,1},{8,14},{9,15},{10,... | collective-permute-start | bytes 184328 | tf_op jit(solution)/shard_map/ppermute | solution.py:415
  75.4 3.1 %collective-permute-start.15 = (s16[240,128]{1,0:T(8,128)(2,1)S(1)}, s16[240,128]{1,0:T(8,128)(2,1)S(1)}, u32[]{:S(2)}, u32[]{:S(2)}) collective-permute-start(s16[240,128]{1,0:T(8,128)(2,1)S(1)} %collective-permute-done.14), channel_id=1, source_target_pairs={{0,1},{1,0},{2,3},{3,2},{4,5},{5,4},{6,7},{7,6},{8,9},{9,8},{10,11... | collective-permute-start | bytes 184328 | tf_op jit(solution)/shard_map/ppermute | solution.py:415
  77.1 1.4 %collective-permute-start.13 = (s16[240,128]{1,0:T(8,128)(2,1)S(1)}, s16[240,128]{1,0:T(8,128)(2,1)S(1)}, u32[]{:S(2)}, u32[]{:S(2)}) collective-permute-start(s16[240,128]{1,0:T(8,128)(2,1)S(1)} %collective-permute-done.12), channel_id=1, source_target_pairs={{0,1},{1,0},{2,3},{3,2},{4,5},{5,4},{6,7},{7,6},{8,9},{9,8},{10,11... | collective-permute-start | bytes 184328 | tf_op jit(solution)/shard_map/ppermute | solution.py:415
  78.3 1.3 %collective-permute-start.11 = (s16[240,128]{1,0:T(8,128)(2,1)S(1)}, s16[240,128]{1,0:T(8,128)(2,1)S(1)}, u32[]{:S(2)}, u32[]{:S(2)}) collective-permute-start(s16[240,128]{1,0:T(8,128)(2,1)S(1)} %collective-permute-done.10), channel_id=1, source_target_pairs={{0,1},{1,0},{2,3},{3,2},{4,5},{5,4},{6,7},{7,6},{8,9},{9,8},{10,11... | collective-permute-start | bytes 184328 | tf_op jit(solution)/shard_map/ppermute | solution.py:415

commit v18 on v17

--- a/solution.py
+++ b/solution.py
@@ -125,7 +125,7 @@
         for k in range(CB):
             column = jnp.broadcast_to(table[:, k : k + 1], (ROWS, users))
             total = jnp.where(marks == k, column, total)
-        context_ref[tile] = total
+        context_ref[tile] = jnp.broadcast_to(total[:, None, :], (ROWS, ROWS, users))
         return 0
 
     lax.fori_loop(0, tiles, one, 0, unroll=2)
@@ -135,7 +135,7 @@
     tiles, users = marks.shape
     return pl.pallas_call(
         context_kernel,
-        out_shape=jax.ShapeDtypeStruct((tiles, ROWS, users), jnp.float32),
+        out_shape=jax.ShapeDtypeStruct((tiles, ROWS, ROWS, users), jnp.float32),
         in_specs=[SMEM, VMEM, VMEM],
         out_specs=VMEM,
         compiler_params=limit(4),
@@ -203,8 +203,7 @@
                 wide = from_ref[place, i : i + 2 * ROWS, lanes].astype(jnp.float32)
                 parts_of += [wide[:ROWS], wide[ROWS:]]
             for i, r in enumerate(ranks):
-                values = context_held[batch * BATCH + place, r : r + 1, lanes]
-                values = jnp.broadcast_to(values, (ROWS, LANES))
+                values = context_held[batch * BATCH + place, r, :, lanes]
                 for j in range(len(strips)):
                     totals[i][j] = totals[i][j] + values * parts_of[j]
         for i, r in enumerate(ranks):
@@ -296,7 +295,7 @@
             pltpu.SemaphoreType.DMA((tiles // BATCH,)),
             pltpu.SemaphoreType.DMA,
         ],
-        compiler_params=limit(12 + held),
+        compiler_params=limit(12 + held + contexts.size * 4 // MIB),
         cost_estimate=pl.CostEstimate(flops=2 * 10**9, bytes_accessed=12 * 10**6, transcendentals=0),
         name="tile_sums",
     )(where, count, me, blocks, in_hbm(weights), in_hbm(contexts), in_hbm(user_basis))

time: 86.5 us -> 87.7 us (1.014)
  waiting for transfers between devices: 23.1 us -> 20.2 us
  local copies, waits for them, and re-layouts: 2.9 us -> 5.15 us
  Pallas kernels: 26.5 us -> 28.4 us
    all_to_all x1, waiting for transfers between devices: 8.82 us -> 5.9 us  [body(): lax.all_to_all(found, 'users', 0, 0, axis_index_groups=sides, tiled=True)]
    unnamed x4, local copies, waits for them, and re-layouts: 1.88 us -> 4.12 us
    pallas_call x1, Pallas kernels: 12.4 us -> 13.6 us  [tile_sums(): pl.pallas_call(tiles_kernel, out_shape=out_shape, in_specs=[SMEM] * 3 + [...]
  transfers between devices with their start and end apart: 18 -> 18, of which waited for: 10 -> 10; matrix products, arithmetic and copies ran while one was open for 2% -> 2% of each run, Pallas kernels for 7% -> 8%
where the time goes in v18:
time: 87.7 us; the launch traced here: 87.3 us
  Pallas kernels  28.4 us (32%)
  starting transfers between devices  20.3 us (23%)
  waiting for transfers between devices  20.2 us (23%)
  blocking collectives  10.5 us (12%)
  local copies, waits for them, and re-layouts  5.15 us (6%)
  between operations  1.63 us (2%)
  other arithmetic  1.07 us (1%)
    ppermute x17, starting transfers between devices, swap(): return lax.ppermute(value, 'users', [(i, i ^ mask) for i in range(devices)])  16.7 us
    ppermute x17, waiting for transfers between devices, swap(): return lax.ppermute(value, 'users', [(i, i ^ mask) for i in range(devices)])  14.3 us
    pallas_call x1, Pallas kernels, tile_sums(): pl.pallas_call(tiles_kernel, out_shape=out_shape, in_specs=[SMEM] * 3 + [...  13.6 us
    all_to_all x1, blocking collectives, body(): lax.all_to_all(requests, 'users', 0, 0, axis_index_groups=sides, tiled=True)  10.5 us
    pallas_call x1, Pallas kernels, finish(): pl.pallas_call(functools.partial(finish_kernel, users * devices), out_sha...  6.44 us
    all_to_all x1, waiting for transfers between devices, body(): lax.all_to_all(found, 'users', 0, 0, axis_index_groups=sides, tiled=True)  5.9 us
    pallas_call x1, Pallas kernels, context_values(): pl.pallas_call(context_kernel, out_shape=jax.ShapeDtypeStruct((tiles, ROW...  4.39 us
    unnamed x4, local copies, waits for them, and re-layouts  4.12 us
  transfers between devices with their start and end apart: 18, of which 10 were waited for; matrix products, arithmetic and copies ran while one was open for 2% of the time, Pallas kernels for 8%

profile of v18, /device:TPU:0, one launch (start us, length us, event | category | flops | bytes accessed | tf_op | source)
XLA Modules:
  0.0 87.3 jit_solution(1005548635918753737)
XLA Ops:
  0.6 4.1 %collective-permute-start = (bf16[16,64,128]{2,1,0:T(8,128)(2,1)}, bf16[16,64,128]{2,1,0:T(8,128)(2,1)S(1)}, u32[]{:S(2)}, u32[]{:S(2)}) collective-permute-start(bf16[16,64,128]{2,1,0:T(8,128)(2,1)} %own_ref.1), channel_id=1, source_target_pairs={{0,16},{1,17},{2,18},{3,19},{4,20},{5,21},{6,22},{7,23},{8,24},{9,... | collective-permute-start | bytes 786440 | tf_op jit(solution)/shard_map/ppermute | solution.py:414
  4.7 2.2 %route.1 = (s32[16,1,128]{2,1,0:T(1,128)S(1)}, s32[64]{0:T(128)S(1)}, bf16[16,64,128]{2,1,0:T(8,128)(2,1)S(1)}) custom-call(s32[1]{0:T(128)} %bitcast.me_ref, s32[64]{0:T(128)} %bitcast.136, s32[64]{0:T(128)} %slot_ref.1, bf16[16,64,128]{2,1,0:T(8,128)(2,1)} %own_ref.1), custom_call_target="tpu_custom_call" | custom-call | tf_op jit(solution)/shard_map/route/pallas_call | solution.py:85
  7.0 10.5 %all_to_all.10.asked_ref = s32[16,1,128]{2,1,0:T(1,128)S(1)} all-to-all(s32[16,1,128]{2,1,0:T(1,128)S(1)} %get-tuple-element.18), channel_id=1, replica_groups={{0,1,2,3,4,5,6,7,8,9,10,11,12,13,14,15},{16,17,18,19,20,21,22,23,24,25,..., dimensions={0} | all-to-all | bytes 16384 | tf_op jit(solution)/shard_map/all_to_all | solution.py:472
  17.4 1.8 %collect.1 = bf16[64,64,128]{2,1,0:T(8,128)(2,1)} custom-call(s32[16,1,128]{2,1,0:T(1,128)S(1)} %all_to_all.10.asked_ref, bf16[16,64,128]{2,1,0:T(8,128)(2,1)S(1)} %get-tuple-element.19.own_ref, bf16[16,64,128]{2,1,0:T(8,128)(2,1)S(1)} %collective-permute-done.mirror_ref), custom_call_target="tpu_custom_call" | custom-call | tf_op jit(solution)/shard_map/collect/pallas_call | solution.py:108
  19.2 3.7 %all-to-all-start.1 = ((bf16[64,64,128]{2,1,0:T(8,128)(2,1)}), bf16[64,64,128]{2,1,0:T(8,128)(2,1)S(1)}, u32[]{:S(2)}, u32[]{:S(2)}) async-start(bf16[64,64,128]{2,1,0:T(8,128)(2,1)} %collect.1), calls=%async_computation.1 | async-start | bytes 2097152 | tf_op jit(solution)/shard_map/all_to_all | solution.py:475
  23.5 0.9 reshape.232
  24.4 0.2 copy.13
  24.6 0.9 %copy-done.1 = s32[64,512]{1,0:T(8,128)S(1)} copy-done((s32[64,512]{1,0:T(8,128)S(1)}, s32[64,512]{1,0:T(8,128)}, u32[]{:S(2)}) %copy-start.1) | copy-done | bytes 131096
  25.5 4.4 %contexts.1.context_ref = f32[64,8,8,512]{3,2,1,0:T(8,128)S(1)} custom-call(s32[64]{0:T(128)} %cblock_ref, f32[64,8,8]{2,1,0:T(8,128)S(1)} %bitcast.129, s32[64,512]{1,0:T(8,128)S(1)} %copy-done.1), custom_call_target="tpu_custom_call" | custom-call | flops 10000000 | bytes 20000000 | tf_op jit(solution)/shard_map/contexts/pallas_call | solution.py:136
  29.9 3.2 %copy-done = f32[64,8,8,512]{3,2,1,0:T(8,128)} copy-done((f32[64,8,8,512]{3,2,1,0:T(8,128)}, f32[64,8,8,512]{3,2,1,0:T(8,128)S(1)}, u32[]{:S(2)}) %copy-start) | copy-done | bytes 8388632
  33.1 5.9 %all-to-all-done.1.blocks_ref = bf16[64,64,128]{2,1,0:T(8,128)(2,1)S(1)} async-done(((bf16[64,64,128]{2,1,0:T(8,128)(2,1)}), bf16[64,64,128]{2,1,0:T(8,128)(2,1)S(1)}, u32[]{:S(2)}, u32[]{:S(2)}) %all-to-all-start.1) | async-done | bytes 1048608 | tf_op jit(solution)/shard_map/all_to_all | solution.py:475
  39.0 13.6 %tile_sums.1 = (f32[224,128]{1,0:T(8,128)S(1)}, f32[224,128]{1,0:T(8,128)S(1)}, f32[224,128]{1,0:T(8,128)S(1)}, f32[224,128]{1,0:T(8,128)S(1)}, f32[224,128]{1,0...) custom-call(s32[64]{0:T(128)S(1)} %get-tuple-element.17.where_ref, ...), custom_call_target="tpu_custom_call" | custom-call | flops 2000000000 | bytes 12000000 | tf_op jit(solution)/shard_map/tile_sums/pallas_call | solution.py:280
  52.7 0.5 collective-permute-start.1
  53.2 0.4 collective-permute-start.6
  53.7 0.3 collective-permute-done.2
  54.1 1.0 %collective-permute-start.3 = (s16[240,128]{1,0:T(8,128)(2,1)S(1)}, s16[240,128]{1,0:T(8,128)(2,1)S(1)}, u32[]{:S(2)}, u32[]{:S(2)}) collective-permute-start(s16[240,128]{1,0:T(8,128)(2,1)S(1)} %pad_add_fusion.5), channel_id=1, source_target_pairs={{0,6},{1,7},{2,4},{3,5},{4,2},{5,3},{6,0},{7,1},{8,14},{9,15},{10,... | collective-permute-start | bytes 184328 | tf_op jit(solution)/shard_map/ppermute | solution.py:414
  55.2 1.4 %collective-permute-start.5 = (s16[240,128]{1,0:T(8,128)(2,1)S(1)}, s16[240,128]{1,0:T(8,128)(2,1)S(1)}, u32[]{:S(2)}, u32[]{:S(2)}) collective-permute-start(s16[240,128]{1,0:T(8,128)(2,1)S(1)} %pad_add_fusion.4), channel_id=1, source_target_pairs={{0,2},{1,3},{2,0},{3,1},{4,6},{5,7},{6,4},{7,5},{8,10},{9,11},{10,... | collective-permute-start | bytes 184328 | tf_op jit(solution)/shard_map/ppermute | solution.py:414
  56.8 1.3 %collective-permute-start.7 = (s16[240,128]{1,0:T(8,128)(2,1)S(1)}, s16[240,128]{1,0:T(8,128)(2,1)S(1)}, u32[]{:S(2)}, u32[]{:S(2)}) collective-permute-start(s16[240,128]{1,0:T(8,128)(2,1)S(1)} %pad_add_fusion.3), channel_id=1, source_target_pairs={{0,4},{1,5},{2,6},{3,7},{4,0},{5,1},{6,2},{7,3},{8,12},{9,13},{10,... | collective-permute-start | bytes 184328 | tf_op jit(solution)/shard_map/ppermute | solution.py:414
  58.0 1.9 %collective-permute-done.3 = s16[240,128]{1,0:T(8,128)(2,1)S(1)} collective-permute-done((s16[240,128]{1,0:T(8,128)(2,1)S(1)}, s16[240,128]{1,0:T(8,128)(2,1)S(1)}, u32[]{:S(2)}, u32[]{:S(2)}) %collective-permute-start.3) | collective-permute-done | bytes 61472 | tf_op jit(solution)/shard_map/ppermute | solution.py:414
  59.9 1.1 %collective-permute-done.7 = s16[240,128]{1,0:T(8,128)(2,1)S(1)} collective-permute-done((s16[240,128]{1,0:T(8,128)(2,1)S(1)}, s16[240,128]{1,0:T(8,128)(2,1)S(1)}, u32[]{:S(2)}, u32[]{:S(2)}) %collective-permute-start.7) | collective-permute-done | bytes 61472 | tf_op jit(solution)/shard_map/ppermute | solution.py:414
  61.1 0.1 fusion.35
  61.3 0.6 collective-permute-start.8
  61.9 3.7 %collective-permute-done.8 = s16[240,128]{1,0:T(8,128)(2,1)S(1)} collective-permute-done((s16[240,128]{1,0:T(8,128)(2,1)S(1)}, s16[240,128]{1,0:T(8,128)(2,1)S(1)}, u32[]{:S(2)}, u32[]{:S(2)}) %collective-permute-start.8) | collective-permute-done | bytes 61472 | tf_op jit(solution)/shard_map/ppermute | solution.py:414
  65.7 3.6 %collective-permute-start.9 = (s16[240,128]{1,0:T(8,128)(2,1)S(1)}, s16[240,128]{1,0:T(8,128)(2,1)S(1)}, u32[]{:S(2)}, u32[]{:S(2)}) collective-permute-start(s16[240,128]{1,0:T(8,128)(2,1)S(1)} %pad_add_fusion.1), channel_id=1, source_target_pairs={{0,16},{1,17},{2,18},{3,19},{4,20},{5,21},{6,22},{7,23},{8,24},{9,... | collective-permute-start | bytes 184328 | tf_op jit(solution)/shard_map/ppermute | solution.py:414
  69.4 2.7 %collective-permute-done.9 = s16[240,128]{1,0:T(8,128)(2,1)S(1)} collective-permute-done((s16[240,128]{1,0:T(8,128)(2,1)S(1)}, s16[240,128]{1,0:T(8,128)(2,1)S(1)}, u32[]{:S(2)}, u32[]{:S(2)}) %collective-permute-start.9) | collective-permute-done | bytes 61472 | tf_op jit(solution)/shard_map/ppermute | solution.py:414
  72.3 1.2 %collective-permute-start.14 = (s16[240,128]{1,0:T(8,128)(2,1)S(1)}, s16[240,128]{1,0:T(8,128)(2,1)S(1)}, u32[]{:S(2)}, u32[]{:S(2)}) collective-permute-start(s16[240,128]{1,0:T(8,128)(2,1)S(1)} %pad_add_fusion), channel_id=1, source_target_pairs={{0,4},{1,5},{2,6},{3,7},{4,0},{5,1},{6,2},{7,3},{8,12},{9,13},{10,... | collective-permute-start | bytes 184328 | tf_op jit(solution)/shard_map/ppermute | solution.py:414
  73.5 2.3 %collective-permute-start.10 = (s16[240,128]{1,0:T(8,128)(2,1)S(1)}, s16[240,128]{1,0:T(8,128)(2,1)S(1)}, u32[]{:S(2)}, u32[]{:S(2)}) collective-permute-start(s16[240,128]{1,0:T(8,128)(2,1)S(1)} %pad_add_fusion), channel_id=1, source_target_pairs={{0,6},{1,7},{2,4},{3,5},{4,2},{5,3},{6,0},{7,1},{8,14},{9,15},{10,... | collective-permute-start | bytes 184328 | tf_op jit(solution)/shard_map/ppermute | solution.py:414
  75.8 0.7 collective-permute-done.14
  76.6 1.7 %collective-permute-done.12 = s16[240,128]{1,0:T(8,128)(2,1)S(1)} collective-permute-done((s16[240,128]{1,0:T(8,128)(2,1)S(1)}, s16[240,128]{1,0:T(8,128)(2,1)S(1)}, u32[]{:S(2)}, u32[]{:S(2)}) %collective-permute-start.12) | collective-permute-done | bytes 61472 | tf_op jit(solution)/shard_map/ppermute | solution.py:414
  78.3 1.2 %collective-permute-done.10 = s16[240,128]{1,0:T(8,128)(2,1)S(1)} collective-permute-done((s16[240,128]{1,0:T(8,128)(2,1)S(1)}, s16[240,128]{1,0:T(8,128)(2,1)S(1)}, u32[]{:S(2)}, u32[]{:S(2)}) %collective-permute-start.10) | collective-permute-done | bytes 61472 | tf_op jit(solution)/shard_map/ppermute | solution.py:414
  79.8 1.0 %collective-permute-done.11 = s16[240,128]{1,0:T(8,128)(2,1)S(1)} collective-permute-done((s16[240,128]{1,0:T(8,128)(2,1)S(1)}, s16[240,128]{1,0:T(8,128)(2,1)S(1)}, u32[]{:S(2)}, u32[]{:S(2)}) %collective-permute-start.11) | collective-permute-done | bytes 61472 | tf_op jit(solution)/shard_map/ppermute | solution.py:414
  80.9 6.4 %finish.1 = (f32[512,128]{1,0:T(8,128)}, f32[128,512]{1,0:T(8,128)}) custom-call(s32[1]{0:T(128)} %bitcast.me_ref, bf16[1024,512]{1,0:T(8,128)(2,1)S(1)} %get-tuple-element.23.stack_ref, f32[224,128]{1,0:T(8,128)S(1)} %bitcast_multiply_fusion.7.rest_0_, f32[224,128]{1,0:T(8,128)S(1)} %bitcast_multiply_fusion.6.rest_1_, ...), custom_call_target="tpu_custom_call" | custom-call | tf_op jit(solution)/shard_map/finish/pallas_call | solution.py:394
  (65 shorter events, 1.2 us)
Async XLA Ops:
  0.6 16.8 %collective-permute-start = (bf16[16,64,128]{2,1,0:T(8,128)(2,1)}, bf16[16,64,128]{2,1,0:T(8,128)(2,1)S(1)}, u32[]{:S(2)}, u32[]{:S(2)}) collective-permute-start(bf16[16,64,128]{2,1,0:T(8,128)(2,1)} %own_ref.1), channel_id=1, source_target_pairs={{0,16},{1,17},{2,18},{3,19},{4,20},{5,21},{6,22},{7,23},{8,24},{9,... | collective-permute-start | bytes 786440 | tf_op jit(solution)/shard_map/ppermute | solution.py:414
  19.2 19.8 %all-to-all-start.1 = ((bf16[64,64,128]{2,1,0:T(8,128)(2,1)}), bf16[64,64,128]{2,1,0:T(8,128)(2,1)S(1)}, u32[]{:S(2)}, u32[]{:S(2)}) async-start(bf16[64,64,128]{2,1,0:T(8,128)(2,1)} %collect.1), calls=%async_computation.1 | async-start | bytes 2097152 | tf_op jit(solution)/shard_map/all_to_all | solution.py:475
  24.6 0.9 %copy-start.1 = (s32[64,512]{1,0:T(8,128)S(1)}, s32[64,512]{1,0:T(8,128)}, u32[]{:S(2)}) copy-start(s32[64,512]{1,0:T(8,128)} %marks_ref.1) | copy-start | bytes 393220
  29.9 3.2 %copy-start = (f32[64,8,8,512]{3,2,1,0:T(8,128)}, f32[64,8,8,512]{3,2,1,0:T(8,128)S(1)}, u32[]{:S(2)}) copy-start(f32[64,8,8,512]{3,2,1,0:T(8,128)S(1)} %contexts.1.context_ref) | copy-start | bytes 25165828
  52.6 1.4 %collective-permute-start.2 = (f32[224,128]{1,0:T(8,128)S(1)}, f32[224,128]{1,0:T(8,128)S(1)}, u32[]{:S(2)}, u32[]{:S(2)}) collective-permute-start(f32[224,128]{1,0:T(8,128)S(1)} %get-tuple-element.27), channel_id=1, source_target_pairs={{0,1},{1,0},{2,3},{3,2},{4,5},{5,4},{6,7},{7,6},{8,9},{9,8},{10,11... | collective-permute-start | bytes 344072 | tf_op jit(solution)/shard_map/ppermute | solution.py:414
  52.7 8.4 %collective-permute-start.1 = (f32[224,128]{1,0:T(8,128)S(1)}, f32[224,128]{1,0:T(8,128)S(1)}, u32[]{:S(2)}, u32[]{:S(2)}) collective-permute-start(f32[224,128]{1,0:T(8,128)S(1)} %get-tuple-element.25), channel_id=1, source_target_pairs={{0,1},{1,0},{2,3},{3,2},{4,5},{5,4},{6,7},{7,6},{8,9},{9,8},{10,11... | collective-permute-start | bytes 344072 | tf_op jit(solution)/shard_map/ppermute | solution.py:414
  53.2 1.9 %collective-permute-start.4 = (f32[224,128]{1,0:T(8,128)S(1)}, f32[224,128]{1,0:T(8,128)S(1)}, u32[]{:S(2)}, u32[]{:S(2)}) collective-permute-start(f32[224,128]{1,0:T(8,128)S(1)} %get-tuple-element.29), channel_id=1, source_target_pairs={{0,1},{1,0},{2,3},{3,2},{4,5},{5,4},{6,7},{7,6},{8,9},{9,8},{10,11... | collective-permute-start | bytes 344072 | tf_op jit(solution)/shard_map/ppermute | solution.py:414
  53.2 3.4 %collective-permute-start.6 = (f32[224,128]{1,0:T(8,128)S(1)}, f32[224,128]{1,0:T(8,128)S(1)}, u32[]{:S(2)}, u32[]{:S(2)}) collective-permute-start(f32[224,128]{1,0:T(8,128)S(1)} %get-tuple-element.31), channel_id=1, source_target_pairs={{0,1},{1,0},{2,3},{3,2},{4,5},{5,4},{6,7},{7,6},{8,9},{9,8},{10,11... | collective-permute-start | bytes 344072 | tf_op jit(solution)/shard_map/ppermute | solution.py:414
  54.1 5.8 %collective-permute-start.3 = (s16[240,128]{1,0:T(8,128)(2,1)S(1)}, s16[240,128]{1,0:T(8,128)(2,1)S(1)}, u32[]{:S(2)}, u32[]{:S(2)}) collective-permute-start(s16[240,128]{1,0:T(8,128)(2,1)S(1)} %pad_add_fusion.5), channel_id=1, source_target_pairs={{0,6},{1,7},{2,4},{3,5},{4,2},{5,3},{6,0},{7,1},{8,14},{9,15},{10,... | collective-permute-start | bytes 184328 | tf_op jit(solution)/shard_map/ppermute | solution.py:414
  55.2 4.7 %collective-permute-start.5 = (s16[240,128]{1,0:T(8,128)(2,1)S(1)}, s16[240,128]{1,0:T(8,128)(2,1)S(1)}, u32[]{:S(2)}, u32[]{:S(2)}) collective-permute-start(s16[240,128]{1,0:T(8,128)(2,1)S(1)} %pad_add_fusion.4), channel_id=1, source_target_pairs={{0,2},{1,3},{2,0},{3,1},{4,6},{5,7},{6,4},{7,5},{8,10},{9,11},{10,... | collective-permute-start | bytes 184328 | tf_op jit(solution)/shard_map/ppermute | solution.py:414
  56.8 4.3 %collective-permute-start.7 = (s16[240,128]{1,0:T(8,128)(2,1)S(1)}, s16[240,128]{1,0:T(8,128)(2,1)S(1)}, u32[]{:S(2)}, u32[]{:S(2)}) collective-permute-start(s16[240,128]{1,0:T(8,128)(2,1)S(1)} %pad_add_fusion.3), channel_id=1, source_target_pairs={{0,4},{1,5},{2,6},{3,7},{4,0},{5,1},{6,2},{7,3},{8,12},{9,13},{10,... | collective-permute-start | bytes 184328 | tf_op jit(solution)/shard_map/ppermute | solution.py:414
  61.3 4.3 %collective-permute-start.8 = (s16[240,128]{1,0:T(8,128)(2,1)S(1)}, s16[240,128]{1,0:T(8,128)(2,1)S(1)}, u32[]{:S(2)}, u32[]{:S(2)}) collective-permute-start(s16[240,128]{1,0:T(8,128)(2,1)S(1)} %pad_add_fusion.2), channel_id=1, source_target_pairs={{0,8},{1,9},{2,10},{3,11},{4,12},{5,13},{6,14},{7,15},{8,0},{9,1},... | collective-permute-start | bytes 184328 | tf_op jit(solution)/shard_map/ppermute | solution.py:414
  65.7 6.3 %collective-permute-start.9 = (s16[240,128]{1,0:T(8,128)(2,1)S(1)}, s16[240,128]{1,0:T(8,128)(2,1)S(1)}, u32[]{:S(2)}, u32[]{:S(2)}) collective-permute-start(s16[240,128]{1,0:T(8,128)(2,1)S(1)} %pad_add_fusion.1), channel_id=1, source_target_pairs={{0,16},{1,17},{2,18},{3,19},{4,20},{5,21},{6,22},{7,23},{8,24},{9,... | collective-permute-start | bytes 184328 | tf_op jit(solution)/shard_map/ppermute | solution.py:414
  72.3 4.3 %collective-permute-start.14 = (s16[240,128]{1,0:T(8,128)(2,1)S(1)}, s16[240,128]{1,0:T(8,128)(2,1)S(1)}, u32[]{:S(2)}, u32[]{:S(2)}) collective-permute-start(s16[240,128]{1,0:T(8,128)(2,1)S(1)} %pad_add_fusion), channel_id=1, source_target_pairs={{0,4},{1,5},{2,6},{3,7},{4,0},{5,1},{6,2},{7,3},{8,12},{9,13},{10,... | collective-permute-start | bytes 184328 | tf_op jit(solution)/shard_map/ppermute | solution.py:414
  73.5 6.1 %collective-permute-start.16 = (s16[240,128]{1,0:T(8,128)(2,1)S(1)}, s16[240,128]{1,0:T(8,128)(2,1)S(1)}, u32[]{:S(2)}, u32[]{:S(2)}) collective-permute-start(s16[240,128]{1,0:T(8,128)(2,1)S(1)} %pad_add_fusion), channel_id=1, source_target_pairs={{0,1},{1,0},{2,3},{3,2},{4,5},{5,4},{6,7},{7,6},{8,9},{9,8},{10,11... | collective-permute-start | bytes 184328 | tf_op jit(solution)/shard_map/ppermute | solution.py:414
  73.5 4.8 %collective-permute-start.12 = (s16[240,128]{1,0:T(8,128)(2,1)S(1)}, s16[240,128]{1,0:T(8,128)(2,1)S(1)}, u32[]{:S(2)}, u32[]{:S(2)}) collective-permute-start(s16[240,128]{1,0:T(8,128)(2,1)S(1)} %pad_add_fusion), channel_id=1, source_target_pairs={{0,2},{1,3},{2,0},{3,1},{4,6},{5,7},{6,4},{7,5},{8,10},{9,11},{10,... | collective-permute-start | bytes 184328 | tf_op jit(solution)/shard_map/ppermute | solution.py:414
  73.5 6.0 %collective-permute-start.10 = (s16[240,128]{1,0:T(8,128)(2,1)S(1)}, s16[240,128]{1,0:T(8,128)(2,1)S(1)}, u32[]{:S(2)}, u32[]{:S(2)}) collective-permute-start(s16[240,128]{1,0:T(8,128)(2,1)S(1)} %pad_add_fusion), channel_id=1, source_target_pairs={{0,6},{1,7},{2,4},{3,5},{4,2},{5,3},{6,0},{7,1},{8,14},{9,15},{10,... | collective-permute-start | bytes 184328 | tf_op jit(solution)/shard_map/ppermute | solution.py:414
  76.6 3.1 %collective-permute-start.15 = (s16[240,128]{1,0:T(8,128)(2,1)S(1)}, s16[240,128]{1,0:T(8,128)(2,1)S(1)}, u32[]{:S(2)}, u32[]{:S(2)}) collective-permute-start(s16[240,128]{1,0:T(8,128)(2,1)S(1)} %collective-permute-done.14), channel_id=1, source_target_pairs={{0,1},{1,0},{2,3},{3,2},{4,5},{5,4},{6,7},{7,6},{8,9},{9,8},{10,11... | collective-permute-start | bytes 184328 | tf_op jit(solution)/shard_map/ppermute | solution.py:414
  78.3 1.4 %collective-permute-start.13 = (s16[240,128]{1,0:T(8,128)(2,1)S(1)}, s16[240,128]{1,0:T(8,128)(2,1)S(1)}, u32[]{:S(2)}, u32[]{:S(2)}) collective-permute-start(s16[240,128]{1,0:T(8,128)(2,1)S(1)} %collective-permute-done.12), channel_id=1, source_target_pairs={{0,1},{1,0},{2,3},{3,2},{4,5},{5,4},{6,7},{7,6},{8,9},{9,8},{10,11... | collective-permute-start | bytes 184328 | tf_op jit(solution)/shard_map/ppermute | solution.py:414
  79.6 1.3 %collective-permute-start.11 = (s16[240,128]{1,0:T(8,128)(2,1)S(1)}, s16[240,128]{1,0:T(8,128)(2,1)S(1)}, u32[]{:S(2)}, u32[]{:S(2)}) collective-permute-start(s16[240,128]{1,0:T(8,128)(2,1)S(1)} %collective-permute-done.10), channel_id=1, source_target_pairs={{0,1},{1,0},{2,3},{3,2},{4,5},{5,4},{6,7},{7,6},{8,9},{9,8},{10,11... | collective-permute-start | bytes 184328 | tf_op jit(solution)/shard_map/ppermute | solution.py:414
